TPU v7x, 32 devices: a whole 2x2x4 slice. The times are simulated.
32 devices in a mesh: ta: 4 (over x, core), ha: 4 (over z), wa: 2 (over y).
Axes of the slice: x: 2, y: 2, z: 4, core: 2. Of those that a mesh axis runs over, the one named last changes fastest.
Arguments:
- tokens: bfloat16 [12, 32, 16, 1536], P('ta', 'ha', 'wa'), may hold values from -6 to 6
- modulation: float32 [3, 1536], replicated, may hold values from -4 to 4
- w_query: bfloat16 [1536, 1536], replicated
- w_key: bfloat16 [1536, 1536], replicated
- w_value: bfloat16 [1536, 1536], replicated, may hold values from -0.15625 to 0.15625
- w_out: bfloat16 [1536, 1536], replicated, may hold values from -0.15625 to 0.15625
- norm_q: float32 [1536], replicated, may hold values from 0.8 to 1.6
- norm_k: float32 [1536], replicated, may hold values from 0.8 to 1.6
Outputs:
- branch: bfloat16 [12, 32, 16, 1536], P('ta', 'ha', 'wa')
All inputs are finite; a program needn't handle non-finite values.
Results may differ from a plain program's by a relative error of at most 0.0051.
Values may be sent and summed in bfloat16 or wider, within the bound.
No kernel may reach another device: no remote copies, remote signals or barrier semaphores. Data moves between devices by JAX's collectives and lax.ppermute only.
A program may use at most 192 MiB of HBM per device.

v0:
```python
import jax
import jax.numpy as jnp
from jax import lax
from jax.sharding import PartitionSpec as P

HEADS = 12
HEAD_DIM = 128
D = 1536
TT = 3
TH = 8
TW = 8
CT = 3
CH = 8
CW = 8


def with_halo(value, sides, width):
    for axis, dim in sides:
        devices, length = (lax.axis_size(axis), value.shape[dim])
        up = [(i, (i + 1) % devices) for i in range(devices - 1)]
        down = [(j, i) for i, j in up]
        last = lax.slice_in_dim(value, length - width, length, axis=dim)
        first = lax.slice_in_dim(value, 0, width, axis=dim)
        before = lax.ppermute(last, axis, up)
        after = lax.ppermute(first, axis, down)
        value = jnp.concatenate([before, value, after], axis=dim)
    return value


def modulate(tokens, modulation):
    values = tokens.astype(jnp.float32)
    center = values - jnp.mean(values, axis=-1, keepdims=True)
    spread = jnp.mean(center * center, axis=-1, keepdims=True)
    return (center * lax.rsqrt(spread + 1e-06) * (1.0 + modulation[1]) + modulation[0]).astype(
        jnp.bfloat16
    )


def rms_gain(values, gain):
    return values * lax.rsqrt(jnp.mean(values * values, axis=-1, keepdims=True) + 1e-06) * gain


def rotate_pairs(values, frame_pos, row_pos, column_pos):
    half = HEAD_DIM // 2
    sixth = HEAD_DIM // 6
    first = half - 2 * sixth
    freq_first = 10000.0 ** (-jnp.arange(first, dtype=jnp.float32) / first)
    freq_rest = 10000.0 ** (-jnp.arange(sixth, dtype=jnp.float32) / sixth)
    shape = values.shape[:3]
    angle_frame = frame_pos[:, None] * freq_first
    angle_row = row_pos[:, None] * freq_rest
    angle_column = column_pos[:, None] * freq_rest
    angles = jnp.concatenate(
        [
            jnp.broadcast_to(angle_frame[:, None, None, :], shape + (first,)),
            jnp.broadcast_to(angle_row[None, :, None, :], shape + (sixth,)),
            jnp.broadcast_to(angle_column[None, None, :, :], shape + (sixth,)),
        ],
        axis=-1,
    )
    cosine = jnp.cos(angles)[:, :, :, None, :]
    sine = jnp.sin(angles)[:, :, :, None, :]
    pairs = values.reshape(shape + (HEADS, half, 2))
    even_part = pairs[..., 0]
    odd_part = pairs[..., 1]
    rotated = jnp.stack(
        [even_part * cosine - odd_part * sine, even_part * sine + odd_part * cosine], axis=-1
    )
    return rotated.reshape(values.shape)


def tile_rows(query, key_pad, value_pad, anchor, extent):
    tile_frames = CT // TT
    tile_rows_n = CH // TH
    tile_columns = CW // TW
    tile_size = TT * TH * TW
    window = 27 * tile_size

    def one_row(index):
        frame_tile = index // tile_rows_n
        row_tile = index % tile_rows_n
        query_row = query
        query_row = query_row.reshape(TT, TH, tile_columns, TW, HEADS, HEAD_DIM).transpose(
            4, 2, 0, 1, 3, 5
        )
        query_row = query_row.reshape(HEADS, tile_columns, tile_size, HEAD_DIM)
        key_tiles = jnp.stack([key_pad])
        value_tiles = jnp.stack([value_pad])
        key_tiles = key_tiles.reshape(tile_columns, window, HEADS, HEAD_DIM).transpose(2, 0, 1, 3)
        value_tiles = value_tiles.reshape(tile_columns, window, HEADS, HEAD_DIM).transpose(
            2, 0, 1, 3
        )
        frames_at = anchor[0] + frame_tile * TT - TT + jnp.arange(3 * TT, dtype=jnp.int32)
        rows_at = anchor[1] + row_tile * TH - TH + jnp.arange(3 * TH, dtype=jnp.int32)
        columns_at = (
            anchor[2]
            + jnp.arange(tile_columns, dtype=jnp.int32)[:, None] * TW
            - TW
            + jnp.arange(3 * TW, dtype=jnp.int32)[None, :]
        )
        frame_ok = (frames_at >= 0) & (frames_at < extent[0])
        row_ok = (rows_at >= 0) & (rows_at < extent[1])
        column_ok = (columns_at >= 0) & (columns_at < extent[2])
        valid = (
            frame_ok[None, :, None, None]
            & row_ok[None, None, :, None]
            & column_ok[:, None, None, :]
        )
        valid = valid.reshape(tile_columns, window)

        def one_head(operands):
            head_query, head_key, head_value = operands
            scores = jnp.einsum(
                "cqd,ckd->cqk", head_query, head_key, preferred_element_type=jnp.float32
            ) * HEAD_DIM ** (-0.5)
            scores = jnp.where(valid[:, None, :], scores, -1e30)
            peak = jnp.max(scores, axis=-1, keepdims=True)
            expo = jnp.exp(scores - peak)
            weights = (expo / jnp.sum(expo, axis=-1, keepdims=True)).astype(jnp.bfloat16)
            return jnp.einsum(
                "cqk,ckd->cqd", weights, head_value, preferred_element_type=jnp.float32
            ).astype(jnp.bfloat16)

        attended = lax.map(one_head, (query_row, key_tiles, value_tiles))
        attended = attended.reshape(HEADS, tile_columns, TT, TH, TW, HEAD_DIM).transpose(
            2, 3, 1, 4, 0, 5
        )
        return attended.reshape(TT, TH, CW, D)

    result = lax.map(one_row, jnp.arange(tile_frames * tile_rows_n, dtype=jnp.int32))
    result = result.reshape(tile_frames, tile_rows_n, TT, TH, CW, D).transpose(0, 2, 1, 3, 4, 5)
    return result.reshape(CT, CH, CW, D)


def body(tokens, modulation, w_query, w_key, w_value, w_out, norm_q, norm_k):
    anchor = (lax.axis_index("ta") * CT, lax.axis_index("ha") * CH, lax.axis_index("wa") * CW)
    extent = (lax.axis_size("ta") * CT, lax.axis_size("ha") * CH, lax.axis_size("wa") * CW)
    frame_pos = (anchor[0] + jnp.arange(CT, dtype=jnp.int32)).astype(jnp.float32)
    row_pos = (anchor[1] + jnp.arange(CH, dtype=jnp.int32)).astype(jnp.float32)
    column_pos = (anchor[2] + jnp.arange(CW, dtype=jnp.int32)).astype(jnp.float32)
    grid = (CT, CH, CW, D)
    normed = modulate(tokens, modulation)
    flat = normed.reshape(-1, D)
    key = rms_gain(jnp.dot(flat, w_key, preferred_element_type=jnp.float32), norm_k).reshape(grid)
    key = rotate_pairs(key, frame_pos, row_pos, column_pos).astype(jnp.bfloat16)
    value = (
        jnp.dot(flat, w_value, preferred_element_type=jnp.float32)
        .astype(jnp.bfloat16)
        .reshape(grid)
    )
    key_value = jnp.stack([key, value])
    framed = with_halo(key_value, (("ta", 1),), TT)
    padded = with_halo(framed, (("ha", 2), ("wa", 3)), TW)
    query = rms_gain(jnp.dot(flat, w_query, preferred_element_type=jnp.float32), norm_q).reshape(
        grid
    )
    query = rotate_pairs(query, frame_pos, row_pos, column_pos).astype(jnp.bfloat16)
    attended = tile_rows(query, padded[0], padded[1], anchor, extent)
    branch = (
        jnp.dot(attended.reshape(-1, D), w_out, preferred_element_type=jnp.float32) * modulation[2]
    )
    return branch.astype(jnp.bfloat16).reshape(grid)


def solution(mesh):
    in_specs = (P("ta", "ha", "wa", None), P(), P(), P(), P(), P(), P(), P())
    out_specs = P("ta", "ha", "wa", None)
    return jax.shard_map(body, mesh=mesh, in_specs=in_specs, out_specs=out_specs, check_vma=False)
```

profile of v0, /device:TPU:29, one launch (start us, length us, event | category | flops | bytes accessed | tf_op | source)
XLA Modules:
  0.0 629.4 jit_solution(9776995252536142989)
XLA Ops:
  5.6 3.5 multiply_reduce_fusion
  9.8 9.5 %reshape_reshape.7 = f32[3,8,8,12,64,2]{2,1,0,5,4,3:T(8,128)} reshape(f32[192,1536]{0,1:T(8,128)S(1)} %copy.38) | data formatting | bytes 2359296 | tf_op jit(solution)/shard_map/reshape;reshape | solution.py:63
  22.4 3.5 multiply_reduce_fusion.1
  26.6 9.6 %reshape_reshape.6 = f32[3,8,8,12,64,2]{2,1,0,5,4,3:T(8,128)} reshape(f32[192,1536]{0,1:T(8,128)S(1)} %copy.31) | data formatting | bytes 2359296 | tf_op jit(solution)/shard_map/reshape;reshape | solution.py:63
  36.2 3.5 convolution_convert_fusion
  39.8 20.9 %multiply_subtract_fusion = (bf16[3,8,8,12,64,1]{2,1,0,5,4,3:T(8,128)(2,1)}, bf16[3,8,8,12,64,1]{2,1,0,5,4,3:T(8,128)(2,1)}, bf16[3,8,8,12,64,1]{2,1,0,5,4,3:T(8,128)(2,1)}, bf16[3,8,8,12,64,1]{2,1,0,5,4,3:T(8,128)(2,1)}) fusion(f32[3,8,8,12,64,2]{2,1,0,5,4,3:T(8,128)} %reshape_reshape.7, f32[3,8,8,64]{2,1,0,3:T(8,128)S(1)} %copy-done.2, ...), kind=kLoop, calls=%fused_computation.22 | loop fusion | flops 2359296 | bytes 3637248 | tf_op jit(solution)/shard_map/sub | solution.py:67
  60.6 4.5 copy.40
  65.1 4.5 copy.39
  69.8 7.3 %copy.41 = bf16[3,8,8,12,64,2]{2,1,5,4,3,0:T(8,128)(2,1)} copy(bf16[3,8,8,12,64,2]{4,2,5,3,1,0:T(8,128)(2,1)S(1)} %pad_maximum_fusion.4) | data formatting | bytes 1179648 | tf_op jit(solution)/shard_map/stack | solution.py:66
  77.1 9.3 %copy.42 = bf16[1,3,8,8,1536]{4,3,2,1,0:T(8,128)(2,1)S(1)} copy(bf16[1,3,8,8,1536]{3,2,4,1,0:T(8,128)(2,1)} %bitcast.67) | data formatting | bytes 1179648 | tf_op jit(solution)/shard_map/convert_element_type | solution.py:145
  86.5 2.6 collective-permute-start.1
  89.1 3.0 collective-permute-start
  92.1 12.2 %collective-permute-done.1 = bf16[2,3,8,8,1536]{4,3,2,1,0:T(8,128)(2,1)S(1)} collective-permute-done((bf16[2,3,8,8,1536]{4,3,2,1,0:T(8,128)(2,1)S(1)}, bf16[2,3,8,8,1536]{4,3,2,1,0:T(8,128)(2,1)S(1)}, u32[]{:S(2)}, u32[]{:S(2)}) %collective-permute-start.1) | collective-permute-done | bytes 1179680 | tf_op jit(solution)/shard_map/ppermute | solution.py:25
  105.7 2.5 collective-permute-start.3
  109.5 63.8 %collective-permute-done.3 = bf16[2,9,8,8,1536]{4,3,2,1,0:T(8,128)(2,1)S(1)} collective-permute-done((bf16[2,9,8,8,1536]{4,3,2,1,0:T(8,128)(2,1)S(1)}, bf16[2,9,8,8,1536]{4,3,2,1,0:T(8,128)(2,1)S(1)}, u32[]{:S(2)}, u32[]{:S(2)}) %collective-permute-start.3) | collective-permute-done | bytes 3538976 | tf_op jit(solution)/shard_map/ppermute | solution.py:25
  173.3 4.5 collective-permute-done.2
  177.8 5.6 pad_maximum_fusion.1
  183.4 6.0 collective-permute-start.5
  190.8 5.2 copy.35
  196.0 5.2 copy.34
  201.1 2.5 pad_maximum_fusion.3
  203.7 7.8 %copy.36 = bf16[3,8,8,12,64,2]{3,2,5,4,1,0:T(8,128)(2,1)} copy(bf16[3,8,8,12,64,2]{4,2,5,3,1,0:T(8,128)(2,1)} %pad_maximum_fusion.3) | data formatting | bytes 1179648 | tf_op jit(solution)/shard_map/stack | solution.py:66
  211.4 7.3 %copy.37 = bf16[12,1,3,8,8,128]{5,4,3,2,0,1:T(8,128)(2,1)} copy(bf16[12,1,3,8,8,128]{0,4,5,3,2,1:T(8,128)(2,1)} %bitcast.68) | data formatting | bytes 1179648 | tf_op jit(solution)/shard_map/while/body/eval_jaxpr/transpose | solution.py:83
  218.8 185.6 %collective-permute-done.5 = bf16[2,9,24,8,1536]{4,3,2,1,0:T(8,128)(2,1)} collective-permute-done((bf16[2,9,24,8,1536]{4,3,2,1,0:T(8,128)(2,1)}, bf16[2,9,24,8,1536]{4,3,2,1,0:T(8,128)(2,1)}, u32[]{:S(2)}, u32[]{:S(2)}) %collective-permute-start.5) | collective-permute-done | bytes 10616864 | tf_op jit(solution)/shard_map/ppermute | solution.py:25
  404.4 8.0 %collective-permute-done.4 = bf16[2,9,24,8,1536]{4,3,2,1,0:T(8,128)(2,1)} collective-permute-done((bf16[2,9,24,8,1536]{4,3,2,1,0:T(8,128)(2,1)}, bf16[2,9,24,8,1536]{4,3,2,1,0:T(8,128)(2,1)}, u32[]{:S(2)}, u32[]{:S(2)}) %collective-permute-start.4) | collective-permute-done | bytes 10616864 | tf_op jit(solution)/shard_map/ppermute | solution.py:24
  412.4 33.2 %pad_maximum_fusion = bf16[2,9,24,24,1536]{4,3,2,1,0:T(8,128)(2,1)} fusion(bf16[2,9,24,8,1536]{4,3,2,1,0:T(8,128)(2,1)} %collective-permute-done.5, bf16[2,9,8,8,1536]{4,3,2,1,0:T(8,128)(2,1)} %copy-done, bf16[2,3,8,8,1536]{4,3,2,1,0:T(8,128)(2,1)S(1)} %collective-permute-done.1, bf16[1,3,8,8,1536]{4,3,2,1,0:T(8,128)(2,1)S(1)} %bitcast.72, ...), kind=kLoop, calls=%fused_computation.19 | loop fusion | flops 254803968 | bytes 63700992 | tf_op jit(solution)/shard_map/concatenate | solution.py:26
  445.6 22.0 %fusion.32 = (bf16[1,9,24,24,1536]{4,3,2,1,0:T(8,128)(2,1)}, bf16[1,9,24,24,1536]{4,3,2,1,0:T(8,128)(2,1)}) fusion(bf16[2,9,24,24,1536]{4,3,2,1,0:T(8,128)(2,1)} %pad_maximum_fusion), kind=kLoop, calls=%fused_computation.67 | loop fusion | bytes 63700992 | tf_op jit(solution)/shard_map/slice | solution.py:158
  467.6 29.0 %stack_squeeze.8 = bf16[1,5184,12,128]{3,2,1,0:T(8,128)(2,1)} reshape(bf16[1,9,24,24,1536]{4,3,2,1,0:T(8,128)(2,1)} %get-tuple-element.121) | data formatting | bytes 31850496 | tf_op jit(solution)/shard_map/while/body/eval_jaxpr/reshape;while/body/eval_jaxpr/stack;squeeze | solution.py:89
  496.6 16.9 %copy.44 = bf16[12,1,5184,128]{3,2,1,0:T(8,128)(2,1)} copy(bf16[12,1,5184,128]{3,0,2,1:T(8,128)(2,1)} %bitcast.65) | data formatting | bytes 31850496
  513.5 29.0 %stack_squeeze.9 = bf16[1,5184,12,128]{3,2,1,0:T(8,128)(2,1)} reshape(bf16[1,9,24,24,1536]{4,3,2,1,0:T(8,128)(2,1)} %get-tuple-element.120) | data formatting | bytes 31850496 | tf_op jit(solution)/shard_map/while/body/eval_jaxpr/reshape;while/body/eval_jaxpr/stack;squeeze | solution.py:90
  542.5 16.9 %copy.45 = bf16[12,1,5184,128]{3,2,1,0:T(8,128)(2,1)} copy(bf16[12,1,5184,128]{3,0,2,1:T(8,128)(2,1)} %bitcast.66) | data formatting | bytes 31850496
  559.3 65.7 %while.18 = (s32[]{:T(128)}, bf16[12,1,192,128]{3,2,1,0:T(8,128)(2,1)S(1)}, bf16[12,1,192,128]{3,2,1,0:T(8,128)(2,1)}, bf16[12,1,5184,128]{3,2,1,0:T(8,128)(2,1)...) while((s32[]{:T(128)}, ...), condition=%wide.region_7.8_spmd.clone, body=%wide.region_4.7_spmd.clone.sunk | while | flops 517599936 | bytes 14773069 | solution.py:124
  562.4 2.4 fusion.48
  565.0 2.2 fusion.46
  567.9 2.4 fusion.48
  573.4 2.4 fusion.48
  576.0 2.2 fusion.46
  578.9 2.4 fusion.48
  581.5 2.2 fusion.46
  584.3 2.4 fusion.48
  589.8 2.4 fusion.48
  595.3 2.4 fusion.48
  600.8 2.4 fusion.48
  606.2 2.4 fusion.48
  611.7 2.4 fusion.48
  617.2 2.4 fusion.48
  622.6 2.4 fusion.48
  625.1 4.3 fusion.22
  (97 shorter events, 44.9 us)
Async XLA Ops:
  0.0 9.2 %copy-start.5 = (f32[1536]{0:T(1024)S(1)}, f32[1536]{0:T(1024)}, u32[]{:S(2)}) copy-start(f32[1536]{0:T(1024)} %param.17) | copy-start | bytes 18436
  19.4 6.6 %copy-start.6 = (f32[1536]{0:T(1024)S(1)}, f32[1536]{0:T(1024)}, u32[]{:S(2)}) copy-start(f32[1536]{0:T(1024)} %param.16) | copy-start | bytes 18436
  36.2 3.5 copy-start.2
  36.2 3.6 copy-start.3
  86.5 17.8 %collective-permute-start.1 = (bf16[2,3,8,8,1536]{4,3,2,1,0:T(8,128)(2,1)S(1)}, bf16[2,3,8,8,1536]{4,3,2,1,0:T(8,128)(2,1)S(1)}, u32[]{:S(2)}, u32[]{:S(2)}) collective-permute-start(bf16[2,3,8,8,1536]{4,3,2,1,0:T(8,128)(2,1)S(1)} %pad_maximum_fusion.5), channel_id=1, source_target_pairs={{8,0},{16,8},{24,16},{9,1},{17,9},{25,17},{10,2},{18,10},{26,18},{... | collective-permute-start | bytes 3538952 | tf_op jit(solution)/shard_map/ppermute | solution.py:25
  89.1 16.1 %collective-permute-start = (bf16[2,3,8,8,1536]{4,3,2,1,0:T(8,128)(2,1)S(1)}, bf16[2,3,8,8,1536]{4,3,2,1,0:T(8,128)(2,1)S(1)}, u32[]{:S(2)}, u32[]{:S(2)}) collective-permute-start(bf16[2,3,8,8,1536]{4,3,2,1,0:T(8,128)(2,1)S(1)} %pad_maximum_fusion.5), channel_id=1, source_target_pairs={{0,8},{8,16},{16,24},{1,9},{9,17},{17,25},{2,10},{10,18},{18,26},{... | collective-permute-start | bytes 3538952 | tf_op jit(solution)/shard_map/ppermute | solution.py:24
  105.7 67.6 %collective-permute-start.3 = (bf16[2,9,8,8,1536]{4,3,2,1,0:T(8,128)(2,1)S(1)}, bf16[2,9,8,8,1536]{4,3,2,1,0:T(8,128)(2,1)S(1)}, u32[]{:S(2)}, u32[]{:S(2)}) collective-permute-start(bf16[2,9,8,8,1536]{4,3,2,1,0:T(8,128)(2,1)S(1)} %pad_maximum_fusion.2), channel_id=1, source_target_pairs={{2,0},{4,2},{6,4},{3,1},{5,3},{7,5},{10,8},{12,10},{14,12},{11,9},... | collective-permute-start | bytes 10616840 | tf_op jit(solution)/shard_map/ppermute | solution.py:25
  108.2 69.6 %collective-permute-start.2 = (bf16[2,9,8,8,1536]{4,3,2,1,0:T(8,128)(2,1)S(1)}, bf16[2,9,8,8,1536]{4,3,2,1,0:T(8,128)(2,1)S(1)}, u32[]{:S(2)}, u32[]{:S(2)}) collective-permute-start(bf16[2,9,8,8,1536]{4,3,2,1,0:T(8,128)(2,1)S(1)} %pad_maximum_fusion.2), channel_id=1, source_target_pairs={{0,2},{2,4},{4,6},{1,3},{3,5},{5,7},{8,10},{10,12},{12,14},{9,11},... | collective-permute-start | bytes 10616840 | tf_op jit(solution)/shard_map/ppermute | solution.py:24
  173.3 10.2 %copy-start = (bf16[2,9,8,8,1536]{4,3,2,1,0:T(8,128)(2,1)}, bf16[2,9,8,8,1536]{4,3,2,1,0:T(8,128)(2,1)S(1)}, u32[]{:S(2)}) copy-start(bf16[2,9,8,8,1536]{4,3,2,1,0:T(8,128)(2,1)S(1)} %collective-permute-done.3) | copy-start | bytes 10616836
  177.8 5.7 copy-start.1
  183.4 221.0 %collective-permute-start.5 = (bf16[2,9,24,8,1536]{4,3,2,1,0:T(8,128)(2,1)}, bf16[2,9,24,8,1536]{4,3,2,1,0:T(8,128)(2,1)}, u32[]{:S(2)}, u32[]{:S(2)}) collective-permute-start(bf16[2,9,24,8,1536]{4,3,2,1,0:T(8,128)(2,1)} %pad_maximum_fusion.1), channel_id=1, source_target_pairs={{1,0},{3,2},{5,4},{7,6},{9,8},{11,10},{13,12},{15,14},{17,16},{19,... | collective-permute-start | bytes 31850504 | tf_op jit(solution)/shard_map/ppermute | solution.py:25
  189.5 223.0 %collective-permute-start.4 = (bf16[2,9,24,8,1536]{4,3,2,1,0:T(8,128)(2,1)}, bf16[2,9,24,8,1536]{4,3,2,1,0:T(8,128)(2,1)}, u32[]{:S(2)}, u32[]{:S(2)}) collective-permute-start(bf16[2,9,24,8,1536]{4,3,2,1,0:T(8,128)(2,1)} %pad_maximum_fusion.1), channel_id=1, source_target_pairs={{0,1},{2,3},{4,5},{6,7},{8,9},{10,11},{12,13},{14,15},{16,17},{18,... | collective-permute-start | bytes 31850504 | tf_op jit(solution)/shard_map/ppermute | solution.py:24
  542.5 16.9 %copy-start.4 = (bf16[12,1,192,128]{3,2,1,0:T(8,128)(2,1)S(1)}, bf16[12,1,192,128]{3,2,1,0:T(8,128)(2,1)}, u32[]{:S(2)}) copy-start(bf16[12,1,192,128]{3,2,1,0:T(8,128)(2,1)} %custom-call) | copy-start | bytes 1769476
  559.3 65.8 %copy-start.7 = (f32[1536]{0:T(1024)S(1)}, f32[1536]{0:T(1024)}, u32[]{:S(2)}) copy-start(f32[1536]{0:T(1024)} %get-tuple-element.101) | copy-start | bytes 18436
where the time goes:
time: 633 us; the launch traced here: 629 us
  waiting for transfers between devices  275 us (43%)
  local copies, waits for them, and re-layouts  189 us (30%)
  other arithmetic  79.2 us (13%)
  matrix products  69.1 us (11%)
  starting transfers between devices  16.7 us (3%)
    ppermute x3, waiting for transfers between devices, with_halo(): after = lax.ppermute(first, axis, down)  262 us
    concatenate x3, other arithmetic, with_halo(): value = jnp.concatenate([before, value, after], axis=dim)  39.3 us
    unnamed x18, local copies, waits for them, and re-layouts  33.8 us
    another operation x1, local copies, waits for them, and re-layouts, one_row(): key_tiles.reshape(tile_columns, window, HEADS, HEAD_DIM)  29 us
    another operation x1, local copies, waits for them, and re-layouts, one_row(): value_tiles.reshape(tile_columns, window, HEADS, HEAD_DIM)  29 us
    dot_general x12, matrix products, one_head(): jnp.einsum('cqk,ckd->cqd', weights, head_value, preferred_element_type=jn...  28.2 us
    dot_general x12, matrix products, one_head(): jnp.einsum('cqd,ckd->cqk', head_query, head_key, preferred_element_type=j...  26 us
    slice x1, local copies, waits for them, and re-layouts, body(): attended = tile_rows(query, padded[0], padded[1], anchor, extent)  22 us
  transfers between devices with their start and end apart: 6, of which 6 were waited for; matrix products, arithmetic and copies ran while one was open for 4% of the time, Pallas kernels for 0%

commit v1 on v0

--- a/solution.py
+++ b/solution.py
@@ -1,6 +1,11 @@
+import functools
+
 import jax
 import jax.numpy as jnp
+import numpy as np
 from jax import lax
+from jax.experimental import pallas as pl
+from jax.experimental.pallas import tpu as pltpu
 from jax.sharding import PartitionSpec as P
 
 HEADS = 12
@@ -162,7 +167,391 @@
     return branch.astype(jnp.bfloat16).reshape(grid)
 
 
+TILE = TT * TH * TW
+GROUPS = 4
+GH = HEADS // GROUPS
+GW = GH * HEAD_DIM
+SCORE_SCALE = float(HEAD_DIM ** (-0.5) * np.log2(np.e))
+VMEM_LIMIT = 56 * 1024 * 1024
+
+
+def rope_tables(devices, per_device, low, count):
+    n = np.float32(count)
+    freq = np.float32(10000.0) ** (-np.arange(count, dtype=np.float32) / n)
+    angle = np.arange(devices * per_device, dtype=np.float32)[:, None] * freq[None, :]
+    cosine = np.zeros((devices * per_device, HEAD_DIM), np.float32)
+    sine = np.zeros((devices * per_device, HEAD_DIM), np.float32)
+    for j in range(count):
+        lane = 2 * (low + j)
+        cosine[:, lane] = cosine[:, lane + 1] = np.cos(angle[:, j])
+        sine[:, lane] = -np.sin(angle[:, j])
+        sine[:, lane + 1] = np.sin(angle[:, j])
+    tables = np.stack([cosine, sine]).reshape(2, devices, per_device, HEAD_DIM)
+    return jnp.asarray(tables.transpose(1, 0, 2, 3))
+
+
+def layer_norm(tok_ref, mod_ref):
+    values = tok_ref[...].astype(jnp.float32)
+    center = values - jnp.mean(values, axis=-1, keepdims=True)
+    spread = jnp.mean(center * center, axis=-1, keepdims=True)
+    shift, scale = mod_ref[0:1, :], mod_ref[1:2, :]
+    return (center * lax.rsqrt(spread + 1e-06) * (1.0 + scale) + shift).astype(jnp.bfloat16)
+
+
+def angle_tables(sc_ref, ft_ref, rt_ref, ct_ref):
+    out = []
+    for kind in range(2):
+        frame = ft_ref[sc_ref[1], kind]
+        row = rt_ref[sc_ref[2], kind]
+        column = ct_ref[sc_ref[3], kind]
+        full = frame[:, None, None, :] + row[None, :, None, :] + column[None, None, :, :]
+        out.append(full.reshape(TILE, HEAD_DIM))
+    return out
+
+
+def rope(x, cosine, sine, even):
+    swapped = jnp.where(even, pltpu.roll(x, HEAD_DIM - 1, 1), pltpu.roll(x, 1, 1))
+    return x * cosine + swapped * sine
+
+
+def fold_squares(prod):
+    total = None
+    for h in range(GH):
+        piece = prod[:, h * HEAD_DIM : (h + 1) * HEAD_DIM]
+        total = piece * piece if total is None else total + piece * piece
+    return total
+
+
+def finish_normed(sc_ref, tables, buf, gains, ssq, write):
+    cosine, sine = angle_tables(sc_ref, *tables)
+    even = lax.broadcasted_iota(jnp.int32, (TILE, HEAD_DIM), 1) % 2 == 0
+    inv = lax.rsqrt(jnp.sum(ssq[...], axis=-1, keepdims=True) / D + 1e-06)
+    for m in range(GROUPS):
+        for h in range(GH):
+            lanes = slice(h * HEAD_DIM, (h + 1) * HEAD_DIM)
+            x = buf[m, :, lanes] * inv * gains[m, :, lanes]
+            write(m, h, rope(x, cosine, sine, even).astype(jnp.bfloat16))
+
+
+def kv_kernel(sc_ref, tok_ref, mod_ref, nk_ref, ft_ref, rt_ref, ct_ref, wk_ref, wv_ref, o0, o1, o2, o3, normed_ref, buf, gains, ssq):
+    outs = (o0, o1, o2, o3)
+    i = pl.program_id(0)
+
+    @pl.when(i == 0)
+    def _():
+        normed_ref[...] = layer_norm(tok_ref, mod_ref)
+        ssq[...] = jnp.zeros_like(ssq)
+
+    @pl.when(i < GROUPS)
+    def _():
+        prod = jnp.dot(normed_ref[...], wk_ref[...], preferred_element_type=jnp.float32)
+        buf[i] = prod
+        gains[i] = nk_ref[...]
+        ssq[...] += fold_squares(prod)
+
+    @pl.when(i == GROUPS - 1)
+    def _():
+        def write(m, h, x):
+            outs[m][0, h] = x
+
+        finish_normed(sc_ref, (ft_ref, rt_ref, ct_ref), buf, gains, ssq, write)
+
+    for m in range(GROUPS):
+
+        @pl.when(i == GROUPS + m)
+        def _():
+            prod = jnp.dot(normed_ref[...], wv_ref[...], preferred_element_type=jnp.float32)
+            for h in range(GH):
+                outs[m][1, h] = prod[:, h * HEAD_DIM : (h + 1) * HEAD_DIM].astype(jnp.bfloat16)
+
+
+def q_kernel(sc_ref, normed_ref, nq_ref, ft_ref, rt_ref, ct_ref, wq_ref, o0, o1, o2, o3, buf, gains, ssq):
+    outs = (o0, o1, o2, o3)
+    i = pl.program_id(0)
+
+    @pl.when(i == 0)
+    def _():
+        ssq[...] = jnp.zeros_like(ssq)
+
+    prod = jnp.dot(normed_ref[...], wq_ref[...], preferred_element_type=jnp.float32)
+    buf[i] = prod
+    gains[i] = nq_ref[...]
+    ssq[...] += fold_squares(prod)
+
+    @pl.when(i == GROUPS - 1)
+    def _():
+        def write(m, h, x):
+            outs[m][h] = x
+
+        finish_normed(sc_ref, (ft_ref, rt_ref, ct_ref), buf, gains, ssq, write)
+
+
+def whole_spec(shape):
+    return pl.BlockSpec(shape, lambda i, sc: (0,) * len(shape))
+
+
+def project_kv(sc, tokens, modulation, norm_k, tables, w_key, w_value):
+    kv_shape = (2, GH, TILE, HEAD_DIM)
+    return pl.pallas_call(
+        kv_kernel,
+        grid_spec=pltpu.PrefetchScalarGridSpec(
+            num_scalar_prefetch=1,
+            grid=(2 * GROUPS,),
+            in_specs=[
+                whole_spec((TILE, D)),
+                whole_spec((3, D)),
+                pl.BlockSpec((1, GW), lambda i, sc: (0, jnp.minimum(i, GROUPS - 1) ^ sc[0])),
+                *[whole_spec(t.shape) for t in tables],
+                pl.BlockSpec((D, GW), lambda i, sc: (0, jnp.minimum(i, GROUPS - 1) ^ sc[0])),
+                pl.BlockSpec((D, GW), lambda i, sc: (0, jnp.maximum(i - GROUPS, 0) ^ sc[0])),
+            ],
+            out_specs=[whole_spec(kv_shape)] * GROUPS + [whole_spec((TILE, D))],
+            scratch_shapes=[
+                pltpu.VMEM((GROUPS, TILE, GW), jnp.float32),
+                pltpu.VMEM((GROUPS, 1, GW), jnp.float32),
+                pltpu.VMEM((TILE, HEAD_DIM), jnp.float32),
+            ],
+        ),
+        out_shape=[jax.ShapeDtypeStruct(kv_shape, jnp.bfloat16)] * GROUPS
+        + [jax.ShapeDtypeStruct((TILE, D), jnp.bfloat16)],
+        compiler_params=pltpu.CompilerParams(vmem_limit_bytes=VMEM_LIMIT),
+        cost_estimate=pl.CostEstimate(flops=4 * TILE * D * D, bytes_accessed=4 * D * D, transcendentals=0),
+        name="project_kv",
+    )(sc, tokens, modulation, norm_k, *tables, w_key, w_value)
+
+
+def project_q(sc, normed, norm_q, tables, w_query):
+    q_shape = (GH, TILE, HEAD_DIM)
+    return pl.pallas_call(
+        q_kernel,
+        grid_spec=pltpu.PrefetchScalarGridSpec(
+            num_scalar_prefetch=1,
+            grid=(GROUPS,),
+            in_specs=[
+                whole_spec((TILE, D)),
+                pl.BlockSpec((1, GW), lambda i, sc: (0, i ^ sc[0])),
+                *[whole_spec(t.shape) for t in tables],
+                pl.BlockSpec((D, GW), lambda i, sc: (0, i ^ sc[0])),
+            ],
+            out_specs=[whole_spec(q_shape)] * GROUPS,
+            scratch_shapes=[
+                pltpu.VMEM((GROUPS, TILE, GW), jnp.float32),
+                pltpu.VMEM((GROUPS, 1, GW), jnp.float32),
+                pltpu.VMEM((TILE, HEAD_DIM), jnp.float32),
+            ],
+        ),
+        out_shape=[jax.ShapeDtypeStruct(q_shape, jnp.bfloat16)] * GROUPS,
+        compiler_params=pltpu.CompilerParams(vmem_limit_bytes=VMEM_LIMIT),
+        cost_estimate=pl.CostEstimate(flops=2 * TILE * D * D, bytes_accessed=2 * D * D, transcendentals=0),
+        name="project_q",
+    )(sc, normed, norm_q, *tables, w_query)
+
+
+def pair_of(refs, kind):
+    return jnp.concatenate([ref[kind, 0] for ref in refs], axis=0)
+
+
+def attend_block(query, keys, values, peak_ref, acc_ref, s, first):
+    scores = lax.dot_general(query, keys, (((1,), (1,)), ((), ())), preferred_element_type=jnp.float32) * SCORE_SCALE
+    peak = jnp.max(scores, axis=-1, keepdims=True)
+    if not first:
+        old = peak_ref[0, s][:, :1]
+        peak = jnp.maximum(old, peak)
+    expo = jnp.exp2(scores - peak).astype(jnp.bfloat16)
+    ones = jnp.ones((values.shape[0], HEAD_DIM), jnp.bfloat16)
+    part = jnp.dot(expo, jnp.concatenate([values, ones], axis=1), preferred_element_type=jnp.float32)
+    if not first:
+        part = acc_ref[0, s] * jnp.exp2(old - peak) + part
+    acc_ref[0, s] = part
+    peak_ref[0, s] = jnp.broadcast_to(peak, (2 * TILE, HEAD_DIM))
+
+
+def own_row_kernel(sc_ref, *refs):
+    q, same, other = refs[0:4], refs[4:8], refs[8:12]
+    peak_ref, acc_ref = refs[12:]
+    for s in range(2):
+        query = jnp.concatenate([q[2 * s][0], q[2 * s + 1][0]], axis=0)
+        for n, keys in enumerate((same, other)):
+            pair = keys[2 * s : 2 * s + 2]
+            attend_block(query, pair_of(pair, 0), pair_of(pair, 1), peak_ref, acc_ref, s, n == 0)
+
+        @pl.when(sc_ref[4] == s)
+        def _():
+            pair = other[2 * (1 - s) : 2 * (1 - s) + 2]
+            attend_block(query, pair_of(pair, 0), pair_of(pair, 1), peak_ref, acc_ref, s, False)
+
+
+def halo_kernel(slot, final, sc_ref, *refs):
+    q = refs[0:4]
+    rows = [(refs[4 + 4 * r : 6 + 4 * r], refs[6 + 4 * r : 8 + 4 * r]) for r in range(2)]
+    peak_in, acc_in = refs[12:14]
+    if final:
+        outs, (peak_ref, acc_ref) = refs[14:18], refs[18:20]
+    else:
+        peak_ref, acc_ref = refs[14:16]
+    peak_ref[...] = peak_in[...]
+    acc_ref[...] = acc_in[...]
+    for r, (same, other) in enumerate(rows):
+
+        @pl.when(sc_ref[5 + r] == 1)
+        def _():
+            query = jnp.concatenate([q[2 * slot][0], q[2 * slot + 1][0]], axis=0)
+            for pair in (same, other):
+                attend_block(query, pair_of(pair, 0), pair_of(pair, 1), peak_ref, acc_ref, slot, False)
+
+            @pl.when(sc_ref[4] == 1 - slot)
+            def _():
+                far = jnp.concatenate([q[2 * (1 - slot)][0], q[2 * (1 - slot) + 1][0]], axis=0)
+                attend_block(far, pair_of(other, 0), pair_of(other, 1), peak_ref, acc_ref, 1 - slot, False)
+
+    if final:
+        for m in range(GROUPS):
+            rows_at = slice((m % 2) * TILE, (m % 2 + 1) * TILE)
+            acc = acc_ref[0, m // 2, rows_at]
+            outs[m][0] = (acc[:, :HEAD_DIM] / acc[:, HEAD_DIM:]).astype(jnp.bfloat16)
+
+
+Q_SPEC = pl.BlockSpec((1, TILE, HEAD_DIM), lambda h, sc: (h, 0, 0))
+KV_SPEC = pl.BlockSpec((2, 1, TILE, HEAD_DIM), lambda h, sc: (0, h, 0, 0))
+PEAK_SPEC = pl.BlockSpec((1, 2, 2 * TILE, HEAD_DIM), lambda h, sc: (h, 0, 0, 0))
+ACC_SPEC = pl.BlockSpec((1, 2, 2 * TILE, 2 * HEAD_DIM), lambda h, sc: (h, 0, 0, 0))
+STATE_SHAPES = [
+    jax.ShapeDtypeStruct((GH, 2, 2 * TILE, HEAD_DIM), jnp.float32),
+    jax.ShapeDtypeStruct((GH, 2, 2 * TILE, 2 * HEAD_DIM), jnp.float32),
+]
+
+
+def attend_cost(blocks):
+    pairs = GH * blocks * 4 * TILE * TILE
+    return pl.CostEstimate(flops=4 * pairs * HEAD_DIM, bytes_accessed=12 * TILE * GW * 2, transcendentals=pairs)
+
+
+def attend_own(sc, queries, same, other):
+    return pl.pallas_call(
+        own_row_kernel,
+        grid_spec=pltpu.PrefetchScalarGridSpec(
+            num_scalar_prefetch=1,
+            grid=(GH,),
+            in_specs=[Q_SPEC] * 4 + [KV_SPEC] * 8,
+            out_specs=[PEAK_SPEC, ACC_SPEC],
+        ),
+        out_shape=STATE_SHAPES,
+        compiler_params=pltpu.CompilerParams(vmem_limit_bytes=VMEM_LIMIT),
+        cost_estimate=attend_cost(5),
+        name="attend_own",
+    )(sc, *queries, *same, *other)
+
+
+def attend_halo(slot, final, sc, queries, tiles, state):
+    if final:
+        out_specs = [Q_SPEC] * GROUPS
+        out_shape = [jax.ShapeDtypeStruct((GH, TILE, HEAD_DIM), jnp.bfloat16)] * GROUPS
+        scratch = [
+            pltpu.VMEM((1, 2, 2 * TILE, HEAD_DIM), jnp.float32),
+            pltpu.VMEM((1, 2, 2 * TILE, 2 * HEAD_DIM), jnp.float32),
+        ]
+    else:
+        out_specs, out_shape, scratch = [PEAK_SPEC, ACC_SPEC], STATE_SHAPES, []
+    return pl.pallas_call(
+        functools.partial(halo_kernel, slot, final),
+        grid_spec=pltpu.PrefetchScalarGridSpec(
+            num_scalar_prefetch=1,
+            grid=(GH,),
+            in_specs=[Q_SPEC] * 4 + [KV_SPEC] * 8 + [PEAK_SPEC, ACC_SPEC],
+            out_specs=out_specs,
+            scratch_shapes=scratch,
+        ),
+        out_shape=out_shape,
+        compiler_params=pltpu.CompilerParams(vmem_limit_bytes=VMEM_LIMIT),
+        cost_estimate=attend_cost(5),
+        name="attend_halo",
+    )(sc, *queries, *tiles, *state)
+
+
+def out_kernel(sc_ref, a0, a1, a2, a3, mod_ref, w_ref, out_ref, acc):
+    i = pl.program_id(0)
+    for m, ref in enumerate((a0, a1, a2, a3)):
+
+        @pl.when(i == m)
+        def _():
+            rows = jnp.concatenate([ref[h] for h in range(GH)], axis=1)
+            part = jnp.dot(rows, w_ref[...], preferred_element_type=jnp.float32)
+            if m == 0:
+                acc[...] = part
+            elif m < GROUPS - 1:
+                acc[...] += part
+            else:
+                out_ref[...] = ((acc[...] + part) * mod_ref[2:3, :]).astype(jnp.bfloat16)
+
+
+def project_out(sc, attended, modulation, w_out):
+    return pl.pallas_call(
+        out_kernel,
+        grid_spec=pltpu.PrefetchScalarGridSpec(
+            num_scalar_prefetch=1,
+            grid=(GROUPS,),
+            in_specs=[whole_spec((GH, TILE, HEAD_DIM))] * GROUPS
+            + [whole_spec((3, D)), pl.BlockSpec((GW, D), lambda i, sc: (i ^ sc[0], 0))],
+            out_specs=whole_spec((TILE, D)),
+            scratch_shapes=[pltpu.VMEM((TILE, D), jnp.float32)],
+        ),
+        out_shape=jax.ShapeDtypeStruct((TILE, D), jnp.bfloat16),
+        compiler_params=pltpu.CompilerParams(vmem_limit_bytes=VMEM_LIMIT),
+        cost_estimate=pl.CostEstimate(flops=2 * TILE * D * D, bytes_accessed=2 * D * D, transcendentals=0),
+        name="project_out",
+    )(sc, *attended, modulation, w_out)
+
+
+def square_swap(value, m):
+    if m == 0:
+        return value
+    flip = (m >> 1) * 4 + (m & 1)
+    return lax.ppermute(value, ("ta", "wa"), [(i, i ^ flip) for i in range(8)])
+
+
+def core_swap(value):
+    return lax.ppermute(value, "ta", [(i, i ^ 1) for i in range(4)])
+
+
+def square_body(tokens, modulation, w_query, w_key, w_value, w_out, norm_q, norm_k):
+    ta, ha, wa = (lax.axis_index(name) for name in ("ta", "ha", "wa"))
+    rows_n = lax.axis_size("ha")
+    place_x, core = ta // 2, ta % 2
+    near_slot = 1 - (place_x ^ core)
+    sc = jnp.stack(
+        [2 * place_x + wa, ta, ha, wa, near_slot, (ha > 0).astype(jnp.int32), (ha < rows_n - 1).astype(jnp.int32)]
+    ).astype(jnp.int32)
+    half, sixth = HEAD_DIM // 2, HEAD_DIM // 6
+    first = half - 2 * sixth
+    tables = (
+        rope_tables(lax.axis_size("ta"), CT, 0, first),
+        rope_tables(rows_n, CH, first, sixth),
+        rope_tables(lax.axis_size("wa"), CW, first + sixth, sixth),
+    )
+    *kv, normed = project_kv(sc, tokens.reshape(TILE, D), modulation, norm_k.reshape(1, D), tables, w_key, w_value)
+    up = [(i, i + 1) for i in range(rows_n - 1)]
+    down = [(i + 1, i) for i in range(rows_n - 1)]
+    same = [square_swap(kv[m], m) for m in range(GROUPS)]
+    above = [lax.ppermute(tile, "ha", up) for tile in same]
+    below = [lax.ppermute(tile, "ha", down) for tile in same]
+    other = [core_swap(tile) for tile in same]
+    above_other = [core_swap(tile) for tile in above]
+    below_other = [core_swap(tile) for tile in below]
+    queries = project_q(sc, normed, norm_q.reshape(1, D), tables, w_query)
+    queries = [square_swap(queries[m], m) for m in range(GROUPS)]
+    state = attend_own(sc, queries, same, other)
+    for slot in range(2):
+        at = slice(2 * slot, 2 * slot + 2)
+        tiles = [*above[at], *above_other[at], *below[at], *below_other[at]]
+        state = attend_halo(slot, slot == 1, sc, queries, tiles, state)
+    attended = [square_swap(state[m], m) for m in range(GROUPS)]
+    branch = project_out(sc, attended, modulation, w_out)
+    return branch.reshape(CT, CH, CW, D)
+
+
 def solution(mesh):
+    square = mesh.shape["ta"] == 4 and mesh.shape["wa"] == 2
+    chosen = square_body if square else body
     in_specs = (P("ta", "ha", "wa", None), P(), P(), P(), P(), P(), P(), P())
     out_specs = P("ta", "ha", "wa", None)
-    return jax.shard_map(body, mesh=mesh, in_specs=in_specs, out_specs=out_specs, check_vma=False)
+    return jax.shard_map(chosen, mesh=mesh, in_specs=in_specs, out_specs=out_specs, check_vma=False)

time: 633 us -> 136 us (0.21)
  the two profiles are of different devices: /device:TPU:29 before, /device:TPU:16 now
where the time goes in v1:
time: 136 us; the launch traced here: 135 us
  Pallas kernels  57.9 us (43%)
  waiting for transfers between devices  36.3 us (27%)
  starting transfers between devices  35.2 us (26%)
  local copies, waits for them, and re-layouts  5.58 us (4%)
    pallas_call x2, Pallas kernels, attend_halo(): pl.pallas_call(functools.partial(halo_kernel, slot, final), grid_spec=plt...  23 us
    ppermute x9, waiting for transfers between devices, square_swap(): return lax.ppermute(value, ('ta', 'wa'), [(i, i ^ flip) for i in range(8)])  21.8 us
    ppermute x9, starting transfers between devices, square_swap(): return lax.ppermute(value, ('ta', 'wa'), [(i, i ^ flip) for i in range(8)])  12.5 us
    pallas_call x1, Pallas kernels, project_kv(): pl.pallas_call(kv_kernel, grid_spec=pltpu.PrefetchScalarGridSpec(num_scal...  11.9 us
    ppermute x4, starting transfers between devices, square_body(): above = [lax.ppermute(tile, 'ha', up) for tile in same]  11 us
    pallas_call x1, Pallas kernels, attend_own(): pl.pallas_call(own_row_kernel, grid_spec=pltpu.PrefetchScalarGridSpec(num...  10.6 us
    ppermute x4, starting transfers between devices, square_body(): below = [lax.ppermute(tile, 'ha', down) for tile in same]  9.43 us
    ppermute x4, waiting for transfers between devices, square_body(): below = [lax.ppermute(tile, 'ha', down) for tile in same]  9.37 us
  transfers between devices with their start and end apart: 29, of which 12 were waited for; matrix products, arithmetic and copies ran while one was open for 0% of the time, Pallas kernels for 18%

profile of v1, /device:TPU:16, one launch (start us, length us, event | category | flops | bytes accessed | tf_op | source)
XLA Modules:
  0.0 135.4 jit_solution(18198801281570508859)
XLA Ops:
  0.0 1.3 reshape.13.nk_ref
  1.3 1.3 reshape.14.nq_ref
  2.6 0.6 stack.39.sc_ref
  3.2 11.9 %project_kv.1 = (bf16[2,3,192,128]{3,2,1,0:T(8,128)(2,1)}, bf16[2,3,192,128]{3,2,1,0:T(8,128)(2,1)}, bf16[2,3,192,128]{3,2,1,0:T(8,128)(2,1)}, bf16[2,3,192,128]{3,2,1,0:T(8,128)(2,1)}, bf16[192,1536]{1,0:T(8,128)(2,1)}) custom-call(s32[7]{0:T(128)} %stack.39.sc_ref, bf16[192,1536]{1,0:T(8,128)(2,1)} %bitcast.9, f32[3,1536]{1,0:T(4,128)} %mod_ref.3, ...), custom_call_target="tpu_custom_call" | custom-call | flops 1811939328 | bytes 9437184 | tf_op jit(solution)/shard_map/project_kv/pallas_call | solution.py:295
  15.1 6.8 %project_q.1 = (bf16[3,192,128]{2,1,0:T(8,128)(2,1)}, bf16[3,192,128]{2,1,0:T(8,128)(2,1)}, bf16[3,192,128]{2,1,0:T(8,128)(2,1)}, bf16[3,192,128]{2,1,0:T(8,128)(2,1)}) custom-call(s32[7]{0:T(128)} %stack.39.sc_ref, bf16[192,1536]{1,0:T(8,128)(2,1)} %get-tuple-element.22.normed_ref, f32[1,1536]{1,0:T(1,128)} %reshape.14.nq_ref, ...), custom_call_target="tpu_custom_call" | custom-call | flops 905969664 | bytes 4718592 | tf_op jit(solution)/shard_map/project_q/pallas_call | solution.py:325
  21.8 1.5 %collective-permute-start = (bf16[3,192,128]{2,1,0:T(8,128)(2,1)}, bf16[3,192,128]{2,1,0:T(8,128)(2,1)S(1)}, u32[]{:S(2)}, u32[]{:S(2)}) collective-permute-start(bf16[3,192,128]{2,1,0:T(8,128)(2,1)} %get-tuple-element.24), channel_id=1, source_target_pairs={{0,1},{1,0},{8,9},{9,8},{16,17},{17,16},{24,25},{25,24},{2,3},{3,2... | collective-permute-start | bytes 442376 | tf_op jit(solution)/shard_map/ppermute | solution.py:509
  23.4 0.5 collective-permute-start.14
  23.9 1.5 %collective-permute-start.3 = (bf16[2,3,192,128]{3,2,1,0:T(8,128)(2,1)S(1)}, bf16[2,3,192,128]{3,2,1,0:T(8,128)(2,1)S(1)}, u32[]{:S(2)}, u32[]{:S(2)}) collective-permute-start(bf16[2,3,192,128]{3,2,1,0:T(8,128)(2,1)S(1)} %copy-done.31), channel_id=1, source_target_pairs={{0,16},{1,17},{8,24},{9,25},{16,0},{17,1},{24,8},{25,9},{2,18},{3,... | collective-permute-start | bytes 884744 | tf_op jit(solution)/shard_map/ppermute | solution.py:509
  25.4 1.5 %collective-permute-start.5 = (bf16[2,3,192,128]{3,2,1,0:T(8,128)(2,1)S(1)}, bf16[2,3,192,128]{3,2,1,0:T(8,128)(2,1)S(1)}, u32[]{:S(2)}, u32[]{:S(2)}) collective-permute-start(bf16[2,3,192,128]{3,2,1,0:T(8,128)(2,1)S(1)} %copy-done.30), channel_id=1, source_target_pairs={{0,17},{1,16},{8,25},{9,24},{16,1},{17,0},{24,9},{25,8},{2,19},{3,... | collective-permute-start | bytes 884744 | tf_op jit(solution)/shard_map/ppermute | solution.py:509
  26.9 1.5 %collective-permute-start.1 = (bf16[3,192,128]{2,1,0:T(8,128)(2,1)}, bf16[3,192,128]{2,1,0:T(8,128)(2,1)S(1)}, u32[]{:S(2)}, u32[]{:S(2)}) collective-permute-start(bf16[3,192,128]{2,1,0:T(8,128)(2,1)} %get-tuple-element.25), channel_id=1, source_target_pairs={{0,16},{1,17},{8,24},{9,25},{16,0},{17,1},{24,8},{25,9},{2,18},{3,... | collective-permute-start | bytes 442376 | tf_op jit(solution)/shard_map/ppermute | solution.py:509
  28.3 0.4 collective-permute-done.refs_1_
  28.8 2.4 %collective-permute-start.2 = (bf16[3,192,128]{2,1,0:T(8,128)(2,1)}, bf16[3,192,128]{2,1,0:T(8,128)(2,1)S(1)}, u32[]{:S(2)}, u32[]{:S(2)}) collective-permute-start(bf16[3,192,128]{2,1,0:T(8,128)(2,1)} %get-tuple-element.26), channel_id=1, source_target_pairs={{0,17},{1,16},{8,25},{9,24},{16,1},{17,0},{24,9},{25,8},{2,19},{3,... | collective-permute-start | bytes 442376 | tf_op jit(solution)/shard_map/ppermute | solution.py:509
  31.2 11.9 %collective-permute-done.1.refs_2_ = bf16[3,192,128]{2,1,0:T(8,128)(2,1)S(1)} collective-permute-done((bf16[3,192,128]{2,1,0:T(8,128)(2,1)}, bf16[3,192,128]{2,1,0:T(8,128)(2,1)S(1)}, u32[]{:S(2)}, u32[]{:S(2)}) %collective-permute-start.1) | collective-permute-done | bytes 147488 | tf_op jit(solution)/shard_map/ppermute | solution.py:509
  43.2 2.5 %collective-permute-done.2.refs_3_ = bf16[3,192,128]{2,1,0:T(8,128)(2,1)S(1)} collective-permute-done((bf16[3,192,128]{2,1,0:T(8,128)(2,1)}, bf16[3,192,128]{2,1,0:T(8,128)(2,1)S(1)}, u32[]{:S(2)}, u32[]{:S(2)}) %collective-permute-start.2) | collective-permute-done | bytes 147488 | tf_op jit(solution)/shard_map/ppermute | solution.py:509
  45.7 3.5 %collective-permute-start.13 = (bf16[2,3,192,128]{3,2,1,0:T(8,128)(2,1)S(1)}, bf16[2,3,192,128]{3,2,1,0:T(8,128)(2,1)S(1)}, u32[]{:S(2)}, u32[]{:S(2)}) collective-permute-start(bf16[2,3,192,128]{3,2,1,0:T(8,128)(2,1)S(1)} %copy-done.22), channel_id=1, source_target_pairs={{0,2},{2,4},{4,6},{1,3},{3,5},{5,7},{8,10},{10,12},{12,14},{9,11},... | collective-permute-start | bytes 884744 | tf_op jit(solution)/shard_map/ppermute | solution.py:535
  49.2 2.4 %collective-permute-start.18 = (bf16[2,3,192,128]{3,2,1,0:T(8,128)(2,1)S(1)}, bf16[2,3,192,128]{3,2,1,0:T(8,128)(2,1)S(1)}, u32[]{:S(2)}, u32[]{:S(2)}) collective-permute-start(bf16[2,3,192,128]{3,2,1,0:T(8,128)(2,1)S(1)} %copy-done.22), channel_id=1, source_target_pairs={{2,0},{4,2},{6,4},{3,1},{5,3},{7,5},{10,8},{12,10},{14,12},{11,9},... | collective-permute-start | bytes 884744 | tf_op jit(solution)/shard_map/ppermute | solution.py:536
  51.7 0.5 collective-permute-start.24
  52.2 0.1 collective-permute-start.25
  52.3 2.3 %collective-permute-done.13.refs_4_ = bf16[2,3,192,128]{3,2,1,0:T(8,128)(2,1)S(1)} collective-permute-done((bf16[2,3,192,128]{3,2,1,0:T(8,128)(2,1)S(1)}, bf16[2,3,192,128]{3,2,1,0:T(8,128)(2,1)S(1)}, u32[]{:S(2)}, u32[]{:S(2)}) %collective-permute-start.13) | collective-permute-done | bytes 294944 | tf_op jit(solution)/shard_map/ppermute | solution.py:535
  54.6 3.5 %collective-permute-start.15 = (bf16[2,3,192,128]{3,2,1,0:T(8,128)(2,1)S(1)}, bf16[2,3,192,128]{3,2,1,0:T(8,128)(2,1)S(1)}, u32[]{:S(2)}, u32[]{:S(2)}) collective-permute-start(bf16[2,3,192,128]{3,2,1,0:T(8,128)(2,1)S(1)} %collective-permute-done.14.refs_5_), channel_id=1, source_target_pairs={{0,2},{2,4},{4,6},{1,3},{3,5},{5,7},{8,10},{10,12},{12,14},{9,11},... | collective-permute-start | bytes 884744 | tf_op jit(solution)/shard_map/ppermute | solution.py:535
  58.1 2.4 %collective-permute-start.19 = (bf16[2,3,192,128]{3,2,1,0:T(8,128)(2,1)S(1)}, bf16[2,3,192,128]{3,2,1,0:T(8,128)(2,1)S(1)}, u32[]{:S(2)}, u32[]{:S(2)}) collective-permute-start(bf16[2,3,192,128]{3,2,1,0:T(8,128)(2,1)S(1)} %collective-permute-done.14.refs_5_), channel_id=1, source_target_pairs={{2,0},{4,2},{6,4},{3,1},{5,3},{7,5},{10,8},{12,10},{14,12},{11,9},... | collective-permute-start | bytes 884744 | tf_op jit(solution)/shard_map/ppermute | solution.py:536
  60.5 0.5 collective-permute-start.20
  61.0 2.4 %collective-permute-start.9 = (bf16[2,3,192,128]{3,2,1,0:T(8,128)(2,1)S(1)}, bf16[2,3,192,128]{3,2,1,0:T(8,128)(2,1)S(1)}, u32[]{:S(2)}, u32[]{:S(2)}) collective-permute-start(bf16[2,3,192,128]{3,2,1,0:T(8,128)(2,1)S(1)} %collective-permute-done.3.refs_6_), channel_id=1, source_target_pairs={{2,0},{4,2},{6,4},{3,1},{5,3},{7,5},{10,8},{12,10},{14,12},{11,9},... | collective-permute-start | bytes 884744 | tf_op jit(solution)/shard_map/ppermute | solution.py:536
  63.5 2.4 %collective-permute-start.10 = (bf16[2,3,192,128]{3,2,1,0:T(8,128)(2,1)S(1)}, bf16[2,3,192,128]{3,2,1,0:T(8,128)(2,1)S(1)}, u32[]{:S(2)}, u32[]{:S(2)}) collective-permute-start(bf16[2,3,192,128]{3,2,1,0:T(8,128)(2,1)S(1)} %collective-permute-done.5.refs_7_), channel_id=1, source_target_pairs={{2,0},{4,2},{6,4},{3,1},{5,3},{7,5},{10,8},{12,10},{14,12},{11,9},... | collective-permute-start | bytes 884744 | tf_op jit(solution)/shard_map/ppermute | solution.py:536
  65.9 1.9 %collective-permute-done.19.refs_9_ = bf16[2,3,192,128]{3,2,1,0:T(8,128)(2,1)S(1)} collective-permute-done((bf16[2,3,192,128]{3,2,1,0:T(8,128)(2,1)S(1)}, bf16[2,3,192,128]{3,2,1,0:T(8,128)(2,1)S(1)}, u32[]{:S(2)}, u32[]{:S(2)}) %collective-permute-start.19) | collective-permute-done | bytes 294944 | tf_op jit(solution)/shard_map/ppermute | solution.py:536
  67.8 1.9 %collective-permute-start.4 = (bf16[2,3,192,128]{3,2,1,0:T(8,128)(2,1)S(1)}, bf16[2,3,192,128]{3,2,1,0:T(8,128)(2,1)S(1)}, u32[]{:S(2)}, u32[]{:S(2)}) collective-permute-start(bf16[2,3,192,128]{3,2,1,0:T(8,128)(2,1)S(1)} %collective-permute-done.3.refs_6_), channel_id=1, source_target_pairs={{0,2},{2,4},{4,6},{1,3},{3,5},{5,7},{8,10},{10,12},{12,14},{9,11},... | collective-permute-start | bytes 884744 | tf_op jit(solution)/shard_map/ppermute | solution.py:535
  69.7 2.1 %collective-permute-start.6 = (bf16[2,3,192,128]{3,2,1,0:T(8,128)(2,1)S(1)}, bf16[2,3,192,128]{3,2,1,0:T(8,128)(2,1)S(1)}, u32[]{:S(2)}, u32[]{:S(2)}) collective-permute-start(bf16[2,3,192,128]{3,2,1,0:T(8,128)(2,1)S(1)} %collective-permute-done.5.refs_7_), channel_id=1, source_target_pairs={{0,2},{2,4},{4,6},{1,3},{3,5},{5,7},{8,10},{10,12},{12,14},{9,11},... | collective-permute-start | bytes 884744 | tf_op jit(solution)/shard_map/ppermute | solution.py:535
  71.9 2.2 %collective-permute-done.9.refs_8_ = bf16[2,3,192,128]{3,2,1,0:T(8,128)(2,1)S(1)} collective-permute-done((bf16[2,3,192,128]{3,2,1,0:T(8,128)(2,1)S(1)}, bf16[2,3,192,128]{3,2,1,0:T(8,128)(2,1)S(1)}, u32[]{:S(2)}, u32[]{:S(2)}) %collective-permute-start.9) | collective-permute-done | bytes 294944 | tf_op jit(solution)/shard_map/ppermute | solution.py:536
  74.1 5.2 %collective-permute-done.10.refs_9_ = bf16[2,3,192,128]{3,2,1,0:T(8,128)(2,1)S(1)} collective-permute-done((bf16[2,3,192,128]{3,2,1,0:T(8,128)(2,1)S(1)}, bf16[2,3,192,128]{3,2,1,0:T(8,128)(2,1)S(1)}, u32[]{:S(2)}, u32[]{:S(2)}) %collective-permute-start.10) | collective-permute-done | bytes 294944 | tf_op jit(solution)/shard_map/ppermute | solution.py:536
  79.4 0.5 collective-permute-start.12
  79.9 2.7 %collective-permute-done.6.refs_5_ = bf16[2,3,192,128]{3,2,1,0:T(8,128)(2,1)S(1)} collective-permute-done((bf16[2,3,192,128]{3,2,1,0:T(8,128)(2,1)S(1)}, bf16[2,3,192,128]{3,2,1,0:T(8,128)(2,1)S(1)}, u32[]{:S(2)}, u32[]{:S(2)}) %collective-permute-start.6) | collective-permute-done | bytes 294944 | tf_op jit(solution)/shard_map/ppermute | solution.py:535
  82.6 0.5 collective-permute-start.8
  83.1 10.6 %attend_own.1 = (f32[3,2,384,128]{3,2,1,0:T(8,128)}, f32[3,2,384,256]{3,2,1,0:T(8,128)}) custom-call(s32[7]{0:T(128)} %stack.39.sc_ref, bf16[3,192,128]{2,1,0:T(8,128)(2,1)} %get-tuple-element.23.refs_0_, bf16[3,192,128]{2,1,0:T(8,128)(2,1)} %copy-done, bf16[3,192,128]{2,1,0:T(8,128)(2,1)} %copy-done.1, bf16[3,192,128]{2,1,0:T(8,128)(2,1)} %copy-done.2, ...), custom_call_target="tpu_custom_call" | custom-call | flops 1132462080 | bytes 1769472 | tf_op jit(solution)/shard_map/attend_own/pallas_call | solution.py:430
  93.8 0.6 copy-done.18
  94.5 13.8 %attend_halo.2 = (f32[3,2,384,128]{3,2,1,0:T(8,128)}, f32[3,2,384,256]{3,2,1,0:T(8,128)}) custom-call(s32[7]{0:T(128)} %stack.39.sc_ref, bf16[3,192,128]{2,1,0:T(8,128)(2,1)} %get-tuple-element.23.refs_0_, bf16[3,192,128]{2,1,0:T(8,128)(2,1)} %copy-done, bf16[3,192,128]{2,1,0:T(8,128)(2,1)} %copy-done.1, bf16[3,192,128]{2,1,0:T(8,128)(2,1)} %copy-done.2, ...), custom_call_target="tpu_custom_call" | custom-call | flops 1132462080 | bytes 1769472 | tf_op jit(solution)/shard_map/attend_halo/pallas_call | solution.py:455
  108.4 0.6 copy-done.13
  109.0 0.1 copy-done.14
  109.1 0.1 copy-done.15
  109.2 0.1 copy-done.17
  109.4 9.2 %attend_halo.3 = (bf16[3,192,128]{2,1,0:T(8,128)(2,1)}, bf16[3,192,128]{2,1,0:T(8,128)(2,1)}, bf16[3,192,128]{2,1,0:T(8,128)(2,1)}, bf16[3,192,128]{2,1,0:T(8,128)(2,1)}) custom-call(s32[7]{0:T(128)} %stack.39.sc_ref, bf16[3,192,128]{2,1,0:T(8,128)(2,1)} %get-tuple-element.23.refs_0_, bf16[3,192,128]{2,1,0:T(8,128)(2,1)} %copy-done, ...), custom_call_target="tpu_custom_call" | custom-call | flops 1132462080 | bytes 1769472 | tf_op jit(solution)/shard_map/attend_halo/pallas_call | solution.py:455
  118.5 1.5 %collective-permute-start.26 = (bf16[3,192,128]{2,1,0:T(8,128)(2,1)}, bf16[3,192,128]{2,1,0:T(8,128)(2,1)S(1)}, u32[]{:S(2)}, u32[]{:S(2)}) collective-permute-start(bf16[3,192,128]{2,1,0:T(8,128)(2,1)} %get-tuple-element.36), channel_id=1, source_target_pairs={{0,1},{1,0},{8,9},{9,8},{16,17},{17,16},{24,25},{25,24},{2,3},{3,2... | collective-permute-start | bytes 442376 | tf_op jit(solution)/shard_map/ppermute | solution.py:509
  120.1 1.5 %collective-permute-start.27 = (bf16[3,192,128]{2,1,0:T(8,128)(2,1)}, bf16[3,192,128]{2,1,0:T(8,128)(2,1)S(1)}, u32[]{:S(2)}, u32[]{:S(2)}) collective-permute-start(bf16[3,192,128]{2,1,0:T(8,128)(2,1)} %get-tuple-element.37), channel_id=1, source_target_pairs={{0,16},{1,17},{8,24},{9,25},{16,0},{17,1},{24,8},{25,9},{2,18},{3,... | collective-permute-start | bytes 442376 | tf_op jit(solution)/shard_map/ppermute | solution.py:509
  121.6 0.5 collective-permute-start.28
  122.1 2.6 %collective-permute-done.26.a1 = bf16[3,192,128]{2,1,0:T(8,128)(2,1)S(1)} collective-permute-done((bf16[3,192,128]{2,1,0:T(8,128)(2,1)}, bf16[3,192,128]{2,1,0:T(8,128)(2,1)S(1)}, u32[]{:S(2)}, u32[]{:S(2)}) %collective-permute-start.26) | collective-permute-done | bytes 147488 | tf_op jit(solution)/shard_map/ppermute | solution.py:509
  124.7 2.3 %collective-permute-done.27.a2 = bf16[3,192,128]{2,1,0:T(8,128)(2,1)S(1)} collective-permute-done((bf16[3,192,128]{2,1,0:T(8,128)(2,1)}, bf16[3,192,128]{2,1,0:T(8,128)(2,1)S(1)}, u32[]{:S(2)}, u32[]{:S(2)}) %collective-permute-start.27) | collective-permute-done | bytes 147488 | tf_op jit(solution)/shard_map/ppermute | solution.py:509
  127.0 2.0 %collective-permute-done.28.a3 = bf16[3,192,128]{2,1,0:T(8,128)(2,1)S(1)} collective-permute-done((bf16[3,192,128]{2,1,0:T(8,128)(2,1)}, bf16[3,192,128]{2,1,0:T(8,128)(2,1)S(1)}, u32[]{:S(2)}, u32[]{:S(2)}) %collective-permute-start.28) | collective-permute-done | bytes 147488 | tf_op jit(solution)/shard_map/ppermute | solution.py:509
  129.0 0.7 copy-done.21
  129.7 5.7 %project_out.1 = bf16[192,1536]{1,0:T(8,128)(2,1)} custom-call(s32[7]{0:T(128)} %stack.39.sc_ref, bf16[3,192,128]{2,1,0:T(8,128)(2,1)} %get-tuple-element.35.a0, bf16[3,192,128]{2,1,0:T(8,128)(2,1)} %copy-done.19, bf16[3,192,128]{2,1,0:T(8,128)(2,1)} %copy-done.20, bf16[3,192,128]{2,1,0:T(8,128)(2,1)} %copy-done.21, f32[3,1536]{1,0:T(4,128)} %mod_ref.3, ...), custom_call_target="tpu_custom_call" | custom-call | flops 905969664 | bytes 4718592 | tf_op jit(solution)/shard_map/project_out/pallas_call | solution.py:488
  (85 shorter events, 0.5 us)
Async XLA Ops:
  15.1 28.1 %copy-start.22 = (bf16[2,3,192,128]{3,2,1,0:T(8,128)(2,1)S(1)}, bf16[2,3,192,128]{3,2,1,0:T(8,128)(2,1)}, u32[]{:S(2)}) copy-start(bf16[2,3,192,128]{3,2,1,0:T(8,128)(2,1)} %get-tuple-element.29.refs_4_) | copy-start | bytes 884740
  21.8 6.9 %collective-permute-start = (bf16[3,192,128]{2,1,0:T(8,128)(2,1)}, bf16[3,192,128]{2,1,0:T(8,128)(2,1)S(1)}, u32[]{:S(2)}, u32[]{:S(2)}) collective-permute-start(bf16[3,192,128]{2,1,0:T(8,128)(2,1)} %get-tuple-element.24), channel_id=1, source_target_pairs={{0,1},{1,0},{8,9},{9,8},{16,17},{17,16},{24,25},{25,24},{2,3},{3,2... | collective-permute-start | bytes 442376 | tf_op jit(solution)/shard_map/ppermute | solution.py:509
  23.4 25.8 %collective-permute-start.14 = (bf16[2,3,192,128]{3,2,1,0:T(8,128)(2,1)S(1)}, bf16[2,3,192,128]{3,2,1,0:T(8,128)(2,1)S(1)}, u32[]{:S(2)}, u32[]{:S(2)}) collective-permute-start(bf16[2,3,192,128]{3,2,1,0:T(8,128)(2,1)S(1)} %copy-done.32), channel_id=1, source_target_pairs={{0,1},{1,0},{8,9},{9,8},{16,17},{17,16},{24,25},{25,24},{2,3},{3,2... | collective-permute-start | bytes 884744 | tf_op jit(solution)/shard_map/ppermute | solution.py:509
  23.9 27.7 %collective-permute-start.3 = (bf16[2,3,192,128]{3,2,1,0:T(8,128)(2,1)S(1)}, bf16[2,3,192,128]{3,2,1,0:T(8,128)(2,1)S(1)}, u32[]{:S(2)}, u32[]{:S(2)}) collective-permute-start(bf16[2,3,192,128]{3,2,1,0:T(8,128)(2,1)S(1)} %copy-done.31), channel_id=1, source_target_pairs={{0,16},{1,17},{8,24},{9,25},{16,0},{17,1},{24,8},{25,9},{2,18},{3,... | collective-permute-start | bytes 884744 | tf_op jit(solution)/shard_map/ppermute | solution.py:509
  25.4 26.3 %collective-permute-start.5 = (bf16[2,3,192,128]{3,2,1,0:T(8,128)(2,1)S(1)}, bf16[2,3,192,128]{3,2,1,0:T(8,128)(2,1)S(1)}, u32[]{:S(2)}, u32[]{:S(2)}) collective-permute-start(bf16[2,3,192,128]{3,2,1,0:T(8,128)(2,1)S(1)} %copy-done.30), channel_id=1, source_target_pairs={{0,17},{1,16},{8,25},{9,24},{16,1},{17,0},{24,9},{25,8},{2,19},{3,... | collective-permute-start | bytes 884744 | tf_op jit(solution)/shard_map/ppermute | solution.py:509
  26.9 16.3 %collective-permute-start.1 = (bf16[3,192,128]{2,1,0:T(8,128)(2,1)}, bf16[3,192,128]{2,1,0:T(8,128)(2,1)S(1)}, u32[]{:S(2)}, u32[]{:S(2)}) collective-permute-start(bf16[3,192,128]{2,1,0:T(8,128)(2,1)} %get-tuple-element.25), channel_id=1, source_target_pairs={{0,16},{1,17},{8,24},{9,25},{16,0},{17,1},{24,8},{25,9},{2,18},{3,... | collective-permute-start | bytes 442376 | tf_op jit(solution)/shard_map/ppermute | solution.py:509
  28.8 54.3 %copy-start = (bf16[3,192,128]{2,1,0:T(8,128)(2,1)}, bf16[3,192,128]{2,1,0:T(8,128)(2,1)S(1)}, u32[]{:S(2)}) copy-start(bf16[3,192,128]{2,1,0:T(8,128)(2,1)S(1)} %collective-permute-done.refs_1_) | copy-start | bytes 442372
  28.8 16.9 %collective-permute-start.2 = (bf16[3,192,128]{2,1,0:T(8,128)(2,1)}, bf16[3,192,128]{2,1,0:T(8,128)(2,1)S(1)}, u32[]{:S(2)}, u32[]{:S(2)}) collective-permute-start(bf16[3,192,128]{2,1,0:T(8,128)(2,1)} %get-tuple-element.26), channel_id=1, source_target_pairs={{0,17},{1,16},{8,25},{9,24},{16,1},{17,0},{24,9},{25,8},{2,19},{3,... | collective-permute-start | bytes 442376 | tf_op jit(solution)/shard_map/ppermute | solution.py:509
  43.2 39.9 %copy-start.1 = (bf16[3,192,128]{2,1,0:T(8,128)(2,1)}, bf16[3,192,128]{2,1,0:T(8,128)(2,1)S(1)}, u32[]{:S(2)}) copy-start(bf16[3,192,128]{2,1,0:T(8,128)(2,1)S(1)} %collective-permute-done.1.refs_2_) | copy-start | bytes 442372
  43.2 9.0 %collective-permute-start.22 = (bf16[2,3,192,128]{3,2,1,0:T(8,128)(2,1)S(1)}, bf16[2,3,192,128]{3,2,1,0:T(8,128)(2,1)S(1)}, u32[]{:S(2)}, u32[]{:S(2)}) collective-permute-start(bf16[2,3,192,128]{3,2,1,0:T(8,128)(2,1)S(1)} %copy-done.22), channel_id=1, source_target_pairs={{0,8},{8,0},{16,24},{24,16},{1,9},{9,1},{17,25},{25,17},{2,10},{10... | collective-permute-start | bytes 884744 | tf_op jit(solution)/shard_map/ppermute | solution.py:513
  45.7 37.4 %copy-start.2 = (bf16[3,192,128]{2,1,0:T(8,128)(2,1)}, bf16[3,192,128]{2,1,0:T(8,128)(2,1)S(1)}, u32[]{:S(2)}) copy-start(bf16[3,192,128]{2,1,0:T(8,128)(2,1)S(1)} %collective-permute-done.2.refs_3_) | copy-start | bytes 442372
  45.7 8.9 %collective-permute-start.13 = (bf16[2,3,192,128]{3,2,1,0:T(8,128)(2,1)S(1)}, bf16[2,3,192,128]{3,2,1,0:T(8,128)(2,1)S(1)}, u32[]{:S(2)}, u32[]{:S(2)}) collective-permute-start(bf16[2,3,192,128]{3,2,1,0:T(8,128)(2,1)S(1)} %copy-done.22), channel_id=1, source_target_pairs={{0,2},{2,4},{4,6},{1,3},{3,5},{5,7},{8,10},{10,12},{12,14},{9,11},... | collective-permute-start | bytes 884744 | tf_op jit(solution)/shard_map/ppermute | solution.py:535
  49.2 33.9 %copy-start.23 = (bf16[2,3,192,128]{3,2,1,0:T(8,128)(2,1)}, bf16[2,3,192,128]{3,2,1,0:T(8,128)(2,1)S(1)}, u32[]{:S(2)}) copy-start(bf16[2,3,192,128]{3,2,1,0:T(8,128)(2,1)S(1)} %collective-permute-done.14.refs_5_) | copy-start | bytes 884740
  49.2 8.8 %collective-permute-start.18 = (bf16[2,3,192,128]{3,2,1,0:T(8,128)(2,1)S(1)}, bf16[2,3,192,128]{3,2,1,0:T(8,128)(2,1)S(1)}, u32[]{:S(2)}, u32[]{:S(2)}) collective-permute-start(bf16[2,3,192,128]{3,2,1,0:T(8,128)(2,1)S(1)} %copy-done.22), channel_id=1, source_target_pairs={{2,0},{4,2},{6,4},{3,1},{5,3},{7,5},{10,8},{12,10},{14,12},{11,9},... | collective-permute-start | bytes 884744 | tf_op jit(solution)/shard_map/ppermute | solution.py:536
  51.6 31.5 %copy-start.24 = (bf16[2,3,192,128]{3,2,1,0:T(8,128)(2,1)}, bf16[2,3,192,128]{3,2,1,0:T(8,128)(2,1)S(1)}, u32[]{:S(2)}) copy-start(bf16[2,3,192,128]{3,2,1,0:T(8,128)(2,1)S(1)} %collective-permute-done.3.refs_6_) | copy-start | bytes 884740
  51.6 8.8 %collective-permute-start.23 = (bf16[2,3,192,128]{3,2,1,0:T(8,128)(2,1)S(1)}, bf16[2,3,192,128]{3,2,1,0:T(8,128)(2,1)S(1)}, u32[]{:S(2)}, u32[]{:S(2)}) collective-permute-start(bf16[2,3,192,128]{3,2,1,0:T(8,128)(2,1)S(1)} %collective-permute-done.14.refs_5_), channel_id=1, source_target_pairs={{0,8},{8,0},{16,24},{24,16},{1,9},{9,1},{17,25},{25,17},{2,10},{10... | collective-permute-start | bytes 884744 | tf_op jit(solution)/shard_map/ppermute | solution.py:513
  51.7 31.4 %copy-start.25 = (bf16[2,3,192,128]{3,2,1,0:T(8,128)(2,1)}, bf16[2,3,192,128]{3,2,1,0:T(8,128)(2,1)S(1)}, u32[]{:S(2)}) copy-start(bf16[2,3,192,128]{3,2,1,0:T(8,128)(2,1)S(1)} %collective-permute-done.5.refs_7_) | copy-start | bytes 884740
  51.7 8.8 %collective-permute-start.24 = (bf16[2,3,192,128]{3,2,1,0:T(8,128)(2,1)S(1)}, bf16[2,3,192,128]{3,2,1,0:T(8,128)(2,1)S(1)}, u32[]{:S(2)}, u32[]{:S(2)}) collective-permute-start(bf16[2,3,192,128]{3,2,1,0:T(8,128)(2,1)S(1)} %collective-permute-done.3.refs_6_), channel_id=1, source_target_pairs={{0,8},{8,0},{16,24},{24,16},{1,9},{9,1},{17,25},{25,17},{2,10},{10... | collective-permute-start | bytes 884744 | tf_op jit(solution)/shard_map/ppermute | solution.py:513
  52.2 30.9 %copy-start.26 = (bf16[2,3,192,128]{3,2,1,0:T(8,128)(2,1)}, bf16[2,3,192,128]{3,2,1,0:T(8,128)(2,1)S(1)}, u32[]{:S(2)}) copy-start(bf16[2,3,192,128]{3,2,1,0:T(8,128)(2,1)S(1)} %collective-permute-done.22.refs_8_) | copy-start | bytes 884740
  52.2 8.9 %collective-permute-start.25 = (bf16[2,3,192,128]{3,2,1,0:T(8,128)(2,1)S(1)}, bf16[2,3,192,128]{3,2,1,0:T(8,128)(2,1)S(1)}, u32[]{:S(2)}, u32[]{:S(2)}) collective-permute-start(bf16[2,3,192,128]{3,2,1,0:T(8,128)(2,1)S(1)} %collective-permute-done.5.refs_7_), channel_id=1, source_target_pairs={{0,8},{8,0},{16,24},{24,16},{1,9},{9,1},{17,25},{25,17},{2,10},{10... | collective-permute-start | bytes 884744 | tf_op jit(solution)/shard_map/ppermute | solution.py:513
  54.6 39.2 %copy-start.3 = (bf16[2,3,192,128]{3,2,1,0:T(8,128)(2,1)}, bf16[2,3,192,128]{3,2,1,0:T(8,128)(2,1)S(1)}, u32[]{:S(2)}) copy-start(bf16[2,3,192,128]{3,2,1,0:T(8,128)(2,1)S(1)} %collective-permute-done.13.refs_4_) | copy-start | bytes 884740
  54.6 8.9 %collective-permute-start.15 = (bf16[2,3,192,128]{3,2,1,0:T(8,128)(2,1)S(1)}, bf16[2,3,192,128]{3,2,1,0:T(8,128)(2,1)S(1)}, u32[]{:S(2)}, u32[]{:S(2)}) collective-permute-start(bf16[2,3,192,128]{3,2,1,0:T(8,128)(2,1)S(1)} %collective-permute-done.14.refs_5_), channel_id=1, source_target_pairs={{0,2},{2,4},{4,6},{1,3},{3,5},{5,7},{8,10},{10,12},{12,14},{9,11},... | collective-permute-start | bytes 884744 | tf_op jit(solution)/shard_map/ppermute | solution.py:535
  58.0 35.7 %copy-start.4 = (bf16[2,3,192,128]{3,2,1,0:T(8,128)(2,1)}, bf16[2,3,192,128]{3,2,1,0:T(8,128)(2,1)S(1)}, u32[]{:S(2)}) copy-start(bf16[2,3,192,128]{3,2,1,0:T(8,128)(2,1)S(1)} %collective-permute-done.18.refs_8_) | copy-start | bytes 884740
  58.1 9.7 %collective-permute-start.19 = (bf16[2,3,192,128]{3,2,1,0:T(8,128)(2,1)S(1)}, bf16[2,3,192,128]{3,2,1,0:T(8,128)(2,1)S(1)}, u32[]{:S(2)}, u32[]{:S(2)}) collective-permute-start(bf16[2,3,192,128]{3,2,1,0:T(8,128)(2,1)S(1)} %collective-permute-done.14.refs_5_), channel_id=1, source_target_pairs={{2,0},{4,2},{6,4},{3,1},{5,3},{7,5},{10,8},{12,10},{14,12},{11,9},... | collective-permute-start | bytes 884744 | tf_op jit(solution)/shard_map/ppermute | solution.py:536
  60.4 22.7 %copy-start.27 = (bf16[2,3,192,128]{3,2,1,0:T(8,128)(2,1)}, bf16[2,3,192,128]{3,2,1,0:T(8,128)(2,1)S(1)}, u32[]{:S(2)}) copy-start(bf16[2,3,192,128]{3,2,1,0:T(8,128)(2,1)S(1)} %collective-permute-done.23.refs_9_) | copy-start | bytes 884740
  60.4 9.3 %collective-permute-start.16 = (bf16[2,3,192,128]{3,2,1,0:T(8,128)(2,1)S(1)}, bf16[2,3,192,128]{3,2,1,0:T(8,128)(2,1)S(1)}, u32[]{:S(2)}, u32[]{:S(2)}) collective-permute-start(bf16[2,3,192,128]{3,2,1,0:T(8,128)(2,1)S(1)} %collective-permute-done.13.refs_4_), channel_id=1, source_target_pairs={{0,8},{8,0},{16,24},{24,16},{1,9},{9,1},{17,25},{25,17},{2,10},{10... | collective-permute-start | bytes 884744 | tf_op jit(solution)/shard_map/ppermute | solution.py:513
  60.5 22.6 %copy-start.28 = (bf16[2,3,192,128]{3,2,1,0:T(8,128)(2,1)}, bf16[2,3,192,128]{3,2,1,0:T(8,128)(2,1)S(1)}, u32[]{:S(2)}) copy-start(bf16[2,3,192,128]{3,2,1,0:T(8,128)(2,1)S(1)} %collective-permute-done.24.refs_10_) | copy-start | bytes 884740
  60.5 11.3 %collective-permute-start.20 = (bf16[2,3,192,128]{3,2,1,0:T(8,128)(2,1)S(1)}, bf16[2,3,192,128]{3,2,1,0:T(8,128)(2,1)S(1)}, u32[]{:S(2)}, u32[]{:S(2)}) collective-permute-start(bf16[2,3,192,128]{3,2,1,0:T(8,128)(2,1)S(1)} %collective-permute-done.18.refs_8_), channel_id=1, source_target_pairs={{0,8},{8,0},{16,24},{24,16},{1,9},{9,1},{17,25},{25,17},{2,10},{10... | collective-permute-start | bytes 884744 | tf_op jit(solution)/shard_map/ppermute | solution.py:513
  61.0 13.1 %collective-permute-start.9 = (bf16[2,3,192,128]{3,2,1,0:T(8,128)(2,1)S(1)}, bf16[2,3,192,128]{3,2,1,0:T(8,128)(2,1)S(1)}, u32[]{:S(2)}, u32[]{:S(2)}) collective-permute-start(bf16[2,3,192,128]{3,2,1,0:T(8,128)(2,1)S(1)} %collective-permute-done.3.refs_6_), channel_id=1, source_target_pairs={{2,0},{4,2},{6,4},{3,1},{5,3},{7,5},{10,8},{12,10},{14,12},{11,9},... | collective-permute-start | bytes 884744 | tf_op jit(solution)/shard_map/ppermute | solution.py:536
  63.5 30.3 %copy-start.6 = (bf16[2,3,192,128]{3,2,1,0:T(8,128)(2,1)}, bf16[2,3,192,128]{3,2,1,0:T(8,128)(2,1)S(1)}, u32[]{:S(2)}) copy-start(bf16[2,3,192,128]{3,2,1,0:T(8,128)(2,1)S(1)} %collective-permute-done.15.refs_5_) | copy-start | bytes 884740
  63.5 15.9 %collective-permute-start.10 = (bf16[2,3,192,128]{3,2,1,0:T(8,128)(2,1)S(1)}, bf16[2,3,192,128]{3,2,1,0:T(8,128)(2,1)S(1)}, u32[]{:S(2)}, u32[]{:S(2)}) collective-permute-start(bf16[2,3,192,128]{3,2,1,0:T(8,128)(2,1)S(1)} %collective-permute-done.5.refs_7_), channel_id=1, source_target_pairs={{2,0},{4,2},{6,4},{3,1},{5,3},{7,5},{10,8},{12,10},{14,12},{11,9},... | collective-permute-start | bytes 884744 | tf_op jit(solution)/shard_map/ppermute | solution.py:536
  67.8 26.0 %copy-start.8 = (bf16[2,3,192,128]{3,2,1,0:T(8,128)(2,1)}, bf16[2,3,192,128]{3,2,1,0:T(8,128)(2,1)S(1)}, u32[]{:S(2)}) copy-start(bf16[2,3,192,128]{3,2,1,0:T(8,128)(2,1)S(1)} %collective-permute-done.19.refs_9_) | copy-start | bytes 884740
  67.8 11.6 %collective-permute-start.4 = (bf16[2,3,192,128]{3,2,1,0:T(8,128)(2,1)S(1)}, bf16[2,3,192,128]{3,2,1,0:T(8,128)(2,1)S(1)}, u32[]{:S(2)}, u32[]{:S(2)}) collective-permute-start(bf16[2,3,192,128]{3,2,1,0:T(8,128)(2,1)S(1)} %collective-permute-done.3.refs_6_), channel_id=1, source_target_pairs={{0,2},{2,4},{4,6},{1,3},{3,5},{5,7},{8,10},{10,12},{12,14},{9,11},... | collective-permute-start | bytes 884744 | tf_op jit(solution)/shard_map/ppermute | solution.py:535
  69.7 24.1 %copy-start.10 = (bf16[2,3,192,128]{3,2,1,0:T(8,128)(2,1)}, bf16[2,3,192,128]{3,2,1,0:T(8,128)(2,1)S(1)}, u32[]{:S(2)}) copy-start(bf16[2,3,192,128]{3,2,1,0:T(8,128)(2,1)S(1)} %collective-permute-done.16.refs_6_) | copy-start | bytes 884740
  69.7 12.8 %collective-permute-start.6 = (bf16[2,3,192,128]{3,2,1,0:T(8,128)(2,1)S(1)}, bf16[2,3,192,128]{3,2,1,0:T(8,128)(2,1)S(1)}, u32[]{:S(2)}, u32[]{:S(2)}) collective-permute-start(bf16[2,3,192,128]{3,2,1,0:T(8,128)(2,1)S(1)} %collective-permute-done.5.refs_7_), channel_id=1, source_target_pairs={{0,2},{2,4},{4,6},{1,3},{3,5},{5,7},{8,10},{10,12},{12,14},{9,11},... | collective-permute-start | bytes 884744 | tf_op jit(solution)/shard_map/ppermute | solution.py:535
  71.9 10.7 %collective-permute-start.17 = (bf16[2,3,192,128]{3,2,1,0:T(8,128)(2,1)S(1)}, bf16[2,3,192,128]{3,2,1,0:T(8,128)(2,1)S(1)}, u32[]{:S(2)}, u32[]{:S(2)}) collective-permute-start(bf16[2,3,192,128]{3,2,1,0:T(8,128)(2,1)S(1)} %collective-permute-done.15.refs_5_), channel_id=1, source_target_pairs={{0,8},{8,0},{16,24},{24,16},{1,9},{9,1},{17,25},{25,17},{2,10},{10... | collective-permute-start | bytes 884744 | tf_op jit(solution)/shard_map/ppermute | solution.py:513
  74.1 34.1 %copy-start.5 = (bf16[2,3,192,128]{3,2,1,0:T(8,128)(2,1)}, bf16[2,3,192,128]{3,2,1,0:T(8,128)(2,1)S(1)}, u32[]{:S(2)}) copy-start(bf16[2,3,192,128]{3,2,1,0:T(8,128)(2,1)S(1)} %collective-permute-done.9.refs_8_) | copy-start | bytes 884740
  74.1 19.6 %collective-permute-start.21 = (bf16[2,3,192,128]{3,2,1,0:T(8,128)(2,1)S(1)}, bf16[2,3,192,128]{3,2,1,0:T(8,128)(2,1)S(1)}, u32[]{:S(2)}, u32[]{:S(2)}) collective-permute-start(bf16[2,3,192,128]{3,2,1,0:T(8,128)(2,1)S(1)} %collective-permute-done.19.refs_9_), channel_id=1, source_target_pairs={{0,8},{8,0},{16,24},{24,16},{1,9},{9,1},{17,25},{25,17},{2,10},{10... | collective-permute-start | bytes 884744 | tf_op jit(solution)/shard_map/ppermute | solution.py:513
  79.4 28.9 %copy-start.7 = (bf16[2,3,192,128]{3,2,1,0:T(8,128)(2,1)}, bf16[2,3,192,128]{3,2,1,0:T(8,128)(2,1)S(1)}, u32[]{:S(2)}) copy-start(bf16[2,3,192,128]{3,2,1,0:T(8,128)(2,1)S(1)} %collective-permute-done.10.refs_9_) | copy-start | bytes 884740
  79.4 28.9 %collective-permute-start.11 = (bf16[2,3,192,128]{3,2,1,0:T(8,128)(2,1)S(1)}, bf16[2,3,192,128]{3,2,1,0:T(8,128)(2,1)S(1)}, u32[]{:S(2)}, u32[]{:S(2)}) collective-permute-start(bf16[2,3,192,128]{3,2,1,0:T(8,128)(2,1)S(1)} %collective-permute-done.9.refs_8_), channel_id=1, source_target_pairs={{0,8},{8,0},{16,24},{24,16},{1,9},{9,1},{17,25},{25,17},{2,10},{10... | collective-permute-start | bytes 884744 | tf_op jit(solution)/shard_map/ppermute | solution.py:513
  79.4 28.9 %copy-start.9 = (bf16[2,3,192,128]{3,2,1,0:T(8,128)(2,1)}, bf16[2,3,192,128]{3,2,1,0:T(8,128)(2,1)S(1)}, u32[]{:S(2)}) copy-start(bf16[2,3,192,128]{3,2,1,0:T(8,128)(2,1)S(1)} %collective-permute-done.4.refs_4_) | copy-start | bytes 884740
  79.4 28.9 %collective-permute-start.12 = (bf16[2,3,192,128]{3,2,1,0:T(8,128)(2,1)S(1)}, bf16[2,3,192,128]{3,2,1,0:T(8,128)(2,1)S(1)}, u32[]{:S(2)}, u32[]{:S(2)}) collective-permute-start(bf16[2,3,192,128]{3,2,1,0:T(8,128)(2,1)S(1)} %collective-permute-done.10.refs_9_), channel_id=1, source_target_pairs={{0,8},{8,0},{16,24},{24,16},{1,9},{9,1},{17,25},{25,17},{2,10},{10... | collective-permute-start | bytes 884744 | tf_op jit(solution)/shard_map/ppermute | solution.py:513
  82.5 25.8 %copy-start.11 = (bf16[2,3,192,128]{3,2,1,0:T(8,128)(2,1)}, bf16[2,3,192,128]{3,2,1,0:T(8,128)(2,1)S(1)}, u32[]{:S(2)}) copy-start(bf16[2,3,192,128]{3,2,1,0:T(8,128)(2,1)S(1)} %collective-permute-done.6.refs_5_) | copy-start | bytes 884740
  82.6 25.8 %collective-permute-start.7 = (bf16[2,3,192,128]{3,2,1,0:T(8,128)(2,1)S(1)}, bf16[2,3,192,128]{3,2,1,0:T(8,128)(2,1)S(1)}, u32[]{:S(2)}, u32[]{:S(2)}) collective-permute-start(bf16[2,3,192,128]{3,2,1,0:T(8,128)(2,1)S(1)} %collective-permute-done.4.refs_4_), channel_id=1, source_target_pairs={{0,8},{8,0},{16,24},{24,16},{1,9},{9,1},{17,25},{25,17},{2,10},{10... | collective-permute-start | bytes 884744 | tf_op jit(solution)/shard_map/ppermute | solution.py:513
  82.6 25.8 %collective-permute-start.8 = (bf16[2,3,192,128]{3,2,1,0:T(8,128)(2,1)S(1)}, bf16[2,3,192,128]{3,2,1,0:T(8,128)(2,1)S(1)}, u32[]{:S(2)}, u32[]{:S(2)}) collective-permute-start(bf16[2,3,192,128]{3,2,1,0:T(8,128)(2,1)S(1)} %collective-permute-done.6.refs_5_), channel_id=1, source_target_pairs={{0,8},{8,0},{16,24},{24,16},{1,9},{9,1},{17,25},{25,17},{2,10},{10... | collective-permute-start | bytes 884744 | tf_op jit(solution)/shard_map/ppermute | solution.py:513
  118.5 6.2 %collective-permute-start.26 = (bf16[3,192,128]{2,1,0:T(8,128)(2,1)}, bf16[3,192,128]{2,1,0:T(8,128)(2,1)S(1)}, u32[]{:S(2)}, u32[]{:S(2)}) collective-permute-start(bf16[3,192,128]{2,1,0:T(8,128)(2,1)} %get-tuple-element.36), channel_id=1, source_target_pairs={{0,1},{1,0},{8,9},{9,8},{16,17},{17,16},{24,25},{25,24},{2,3},{3,2... | collective-permute-start | bytes 442376 | tf_op jit(solution)/shard_map/ppermute | solution.py:509
  120.1 6.9 %collective-permute-start.27 = (bf16[3,192,128]{2,1,0:T(8,128)(2,1)}, bf16[3,192,128]{2,1,0:T(8,128)(2,1)S(1)}, u32[]{:S(2)}, u32[]{:S(2)}) collective-permute-start(bf16[3,192,128]{2,1,0:T(8,128)(2,1)} %get-tuple-element.37), channel_id=1, source_target_pairs={{0,16},{1,17},{8,24},{9,25},{16,0},{17,1},{24,8},{25,9},{2,18},{3,... | collective-permute-start | bytes 442376 | tf_op jit(solution)/shard_map/ppermute | solution.py:509
  121.6 7.4 %collective-permute-start.28 = (bf16[3,192,128]{2,1,0:T(8,128)(2,1)}, bf16[3,192,128]{2,1,0:T(8,128)(2,1)S(1)}, u32[]{:S(2)}, u32[]{:S(2)}) collective-permute-start(bf16[3,192,128]{2,1,0:T(8,128)(2,1)} %get-tuple-element.38), channel_id=1, source_target_pairs={{0,17},{1,16},{8,25},{9,24},{16,1},{17,0},{24,9},{25,8},{2,19},{3,... | collective-permute-start | bytes 442376 | tf_op jit(solution)/shard_map/ppermute | solution.py:509
  (14 other events, 93.9 us)

commit v2 on v0

--- a/solution.py
+++ b/solution.py
@@ -1,6 +1,11 @@
+import functools
+
 import jax
 import jax.numpy as jnp
+import numpy as np
 from jax import lax
+from jax.experimental import pallas as pl
+from jax.experimental.pallas import tpu as pltpu
 from jax.sharding import PartitionSpec as P
 
 HEADS = 12
@@ -162,7 +167,395 @@
     return branch.astype(jnp.bfloat16).reshape(grid)
 
 
+TILE = TT * TH * TW
+GROUPS = 4
+GH = HEADS // GROUPS
+GW = GH * HEAD_DIM
+SCORE_SCALE = float(HEAD_DIM ** (-0.5) * np.log2(np.e))
+
+
+def rope_tables(devices, per_device, low, count):
+    n = np.float32(count)
+    freq = np.float32(10000.0) ** (-np.arange(count, dtype=np.float32) / n)
+    angle = np.arange(devices * per_device, dtype=np.float32)[:, None] * freq[None, :]
+    cosine = np.zeros((devices * per_device, HEAD_DIM), np.float32)
+    sine = np.zeros((devices * per_device, HEAD_DIM), np.float32)
+    for j in range(count):
+        lane = 2 * (low + j)
+        cosine[:, lane] = cosine[:, lane + 1] = np.cos(angle[:, j])
+        sine[:, lane] = -np.sin(angle[:, j])
+        sine[:, lane + 1] = np.sin(angle[:, j])
+    tables = np.stack([cosine, sine]).reshape(2, devices, per_device, HEAD_DIM)
+    return jnp.asarray(tables.transpose(1, 0, 2, 3))
+
+
+def layer_norm(tokens, mod_ref):
+    values = tokens.astype(jnp.float32)
+    center = values - jnp.mean(values, axis=-1, keepdims=True)
+    spread = jnp.mean(center * center, axis=-1, keepdims=True)
+    shift, scale = mod_ref[0:1, :], mod_ref[1:2, :]
+    return (center * lax.rsqrt(spread + 1e-06) * (1.0 + scale) + shift).astype(jnp.bfloat16)
+
+
+def angle_tables(place, ft_ref, rt_ref, ct_ref):
+    out = []
+    for kind in range(2):
+        frame = ft_ref[place[0], kind]
+        row = rt_ref[place[1], kind]
+        column = ct_ref[place[2], kind]
+        full = frame[:, None, None, :] + row[None, :, None, :] + column[None, None, :, :]
+        out.append(full.reshape(TILE, HEAD_DIM))
+    return out
+
+
+def rope(x, cosine, sine, even):
+    swapped = jnp.where(even, pltpu.roll(x, HEAD_DIM - 1, 1), pltpu.roll(x, 1, 1))
+    return x * cosine + swapped * sine
+
+
+def fold_squares(prod):
+    total = None
+    for h in range(GH):
+        piece = prod[:, h * HEAD_DIM : (h + 1) * HEAD_DIM]
+        total = piece * piece if total is None else total + piece * piece
+    return total
+
+
+def group_of(sc_ref, m):
+    return pl.multiple_of((sc_ref[0] ^ m) * GW, GW)
+
+
+def finish_normed(sc_ref, tables, buf, gain_ref, ssq, write):
+    cosine, sine = angle_tables((sc_ref[1], sc_ref[2], sc_ref[3]), *tables)
+    even = lax.broadcasted_iota(jnp.int32, (TILE, HEAD_DIM), 1) % 2 == 0
+    inv = lax.rsqrt(jnp.sum(ssq, axis=-1, keepdims=True) / D + 1e-06)
+    for m in range(GROUPS):
+        gain = gain_ref[:, pl.ds(group_of(sc_ref, m), GW)]
+        for h in range(GH):
+            lanes = slice(h * HEAD_DIM, (h + 1) * HEAD_DIM)
+            x = buf[m, :, lanes] * inv * gain[:, lanes]
+            write(m, h, rope(x, cosine, sine, even).astype(jnp.bfloat16))
+
+
+def kv_kernel(sc_ref, tok_hbm, mod_hbm, nk_hbm, ft_hbm, rt_hbm, ct_hbm, wk_hbm, wv_hbm, *refs):
+    outs, normed_ref, (tok_ref, mod_ref, nk_ref, ft_ref, rt_ref, ct_ref, wbuf, buf, gain_ref, sems) = refs[:4], refs[4], refs[5:]
+    small = [
+        pltpu.make_async_copy(source, target, sems.at[2, n])
+        for n, (source, target) in enumerate(
+            zip((tok_hbm, mod_hbm, nk_hbm, ft_hbm, rt_hbm, ct_hbm), (tok_ref, mod_ref, nk_ref, ft_ref, rt_ref, ct_ref))
+        )
+    ]
+    for copy in small:
+        copy.start()
+    copies = []
+    for kind, w_hbm in enumerate((wk_hbm, wv_hbm)):
+        for m in range(GROUPS):
+            copies.append(
+                pltpu.make_async_copy(
+                    w_hbm.at[:, pl.ds(group_of(sc_ref, m), GW)], wbuf.at[kind, m], sems.at[kind, m]
+                )
+            )
+            copies[-1].start()
+    for copy in small:
+        copy.wait()
+    gain_ref[...] = nk_ref[...].reshape(1, D)
+    normed = layer_norm(tok_ref[...], mod_ref)
+    normed_ref[...] = normed
+    ssq = None
+    for m in range(GROUPS):
+        copies[m].wait()
+        prod = jnp.dot(normed, wbuf[0, m], preferred_element_type=jnp.float32)
+        buf[m] = prod
+        squares = fold_squares(prod)
+        ssq = squares if ssq is None else ssq + squares
+
+    def write(m, h, x):
+        outs[m][0, h] = x
+
+    finish_normed(sc_ref, (ft_ref, rt_ref, ct_ref), buf, gain_ref, ssq, write)
+    for m in range(GROUPS):
+        copies[GROUPS + m].wait()
+        prod = jnp.dot(normed, wbuf[1, m], preferred_element_type=jnp.float32)
+        for h in range(GH):
+            outs[m][1, h] = prod[:, h * HEAD_DIM : (h + 1) * HEAD_DIM].astype(jnp.bfloat16)
+
+
+def q_kernel(sc_ref, normed_ref, nq_ref, ft_ref, rt_ref, ct_ref, wq_ref, o0, o1, o2, o3, buf, gain_ref):
+    outs = (o0, o1, o2, o3)
+    gain_ref[...] = nq_ref[...].reshape(1, D)
+    ssq = None
+    for m in range(GROUPS):
+        prod = jnp.dot(
+            normed_ref[...], wq_ref[:, pl.ds(group_of(sc_ref, m), GW)], preferred_element_type=jnp.float32
+        )
+        buf[m] = prod
+        squares = fold_squares(prod)
+        ssq = squares if ssq is None else ssq + squares
+
+    def write(m, h, x):
+        outs[m][h] = x
+
+    finish_normed(sc_ref, (ft_ref, rt_ref, ct_ref), buf, gain_ref, ssq, write)
+
+
+SMEM = pl.BlockSpec(memory_space=pltpu.SMEM)
+VMEM = pl.BlockSpec(memory_space=pltpu.VMEM)
+HBM = pl.BlockSpec(memory_space=pl.ANY)
+
+
+def limit(mib):
+    return pltpu.CompilerParams(vmem_limit_bytes=mib * 1024 * 1024)
+
+
+def project_kv(sc, tokens, modulation, norm_k, tables, w_key, w_value):
+    kv_shape = (2, GH, TILE, HEAD_DIM)
+    return pl.pallas_call(
+        kv_kernel,
+        in_specs=[SMEM] + [HBM] * 8,
+        out_specs=[VMEM] * (GROUPS + 1),
+        scratch_shapes=[
+            pltpu.VMEM((TILE, D), jnp.bfloat16),
+            pltpu.VMEM((3, D), jnp.float32),
+            pltpu.VMEM((D,), jnp.float32),
+            *[pltpu.VMEM(t.shape, jnp.float32) for t in tables],
+            pltpu.VMEM((2, GROUPS, D, GW), jnp.bfloat16),
+            pltpu.VMEM((GROUPS, TILE, GW), jnp.float32),
+            pltpu.VMEM((1, D), jnp.float32),
+            pltpu.SemaphoreType.DMA((3, 6)),
+        ],
+        out_shape=[jax.ShapeDtypeStruct(kv_shape, jnp.bfloat16)] * GROUPS
+        + [jax.ShapeDtypeStruct((TILE, D), jnp.bfloat16)],
+        compiler_params=limit(60),
+        cost_estimate=pl.CostEstimate(flops=4 * TILE * D * D, bytes_accessed=4 * D * D, transcendentals=0),
+        name="project_kv",
+    )(sc, tokens, modulation, norm_k, *tables, w_key, w_value)
+
+
+def project_q(sc, normed, norm_q, tables, w_query):
+    q_shape = (GH, TILE, HEAD_DIM)
+    return pl.pallas_call(
+        q_kernel,
+        in_specs=[SMEM] + [VMEM] * 6,
+        out_specs=[VMEM] * GROUPS,
+        scratch_shapes=[pltpu.VMEM((GROUPS, TILE, GW), jnp.float32), pltpu.VMEM((1, D), jnp.float32)],
+        out_shape=[jax.ShapeDtypeStruct(q_shape, jnp.bfloat16)] * GROUPS,
+        compiler_params=limit(20),
+        cost_estimate=pl.CostEstimate(flops=2 * TILE * D * D, bytes_accessed=2 * D * D, transcendentals=0),
+        name="project_q",
+    )(sc, normed, norm_q, *tables, w_query)
+
+
+def query_of(refs, s):
+    return jnp.concatenate([refs[2 * s][0], refs[2 * s + 1][0]], axis=0)
+
+
+def raw_scores(query, keys):
+    return lax.dot_general(query, keys, (((1,), (1,)), ((), ())), preferred_element_type=jnp.float32)
+
+
+def weigh(scores, peak, values):
+    expo = jnp.exp2((scores - peak) * SCORE_SCALE).astype(jnp.bfloat16)
+    ones = jnp.ones((values.shape[0], HEAD_DIM), jnp.bfloat16)
+    both = jnp.dot(expo, jnp.concatenate([values, ones], axis=1), preferred_element_type=jnp.float32)
+    return both[:, :HEAD_DIM], both[:, HEAD_DIM:]
+
+
+def attend(query, segments, state=None):
+    scores = [raw_scores(query, keys) for keys, _, _ in segments]
+    found = [jnp.max(s, axis=-1, keepdims=True) for s in scores]
+    found = [f if there is None else jnp.where(there, f, -1e30) for f, (_, _, there) in zip(found, segments)]
+    peak = functools.reduce(jnp.maximum, found if state is None else [state[0], *found])
+    total = norm = None
+    if state is not None:
+        decay = jnp.exp2((state[0] - peak) * SCORE_SCALE)
+        total, norm = state[1] * decay, state[2] * decay
+    for s, (_, values, there) in zip(scores, segments):
+        part, weight = weigh(s, peak if there is None else jnp.where(there, peak, 1e30), values)
+        total, norm = (part, weight) if total is None else (total + part, norm + weight)
+    return peak, total, norm
+
+
+def stack_keys(slots, kind):
+    return jnp.concatenate([ref[kind, 0] for pair in slots for ref in pair], axis=0)
+
+
+def segment(slots, there):
+    return stack_keys(slots, 0), stack_keys(slots, 1), there
+
+
+def first_kernel(sc_ref, *refs):
+    q = refs[0:4]
+    same, other = [refs[4:6], refs[6:8]], [refs[8:10], refs[10:12]]
+    rows = [(refs[12 + 4 * r : 14 + 4 * r], refs[14 + 4 * r : 16 + 4 * r], sc_ref[5 + r] == 1) for r in range(2)]
+    stat_ref, acc_ref = refs[20:]
+    low = lax.broadcasted_iota(jnp.int32, (2 * TILE, HEAD_DIM), 1) < HEAD_DIM // 2
+
+    def store(s, state):
+        peak, total, norm = state
+        acc_ref[0, s] = total
+        stat_ref[0, s] = jnp.where(low, peak, norm)
+
+    halo = [segment([mine, theirs], there) for mine, theirs, there in rows]
+
+    @pl.when(sc_ref[4] == 0)
+    def _():
+        store(0, attend(query_of(q, 0), [segment([same[0], other[0], other[1]], None), *halo]))
+        store(1, attend(query_of(q, 1), [segment([same[1], other[1]], None)]))
+
+    @pl.when(sc_ref[4] == 1)
+    def _():
+        store(0, attend(query_of(q, 0), [segment([same[0], other[0]], None), *halo]))
+        far = [segment([theirs], there) for _, theirs, there in rows]
+        store(1, attend(query_of(q, 1), [segment([same[1], other[1], other[0]], None), *far]))
+
+
+def last_kernel(sc_ref, *refs):
+    q = refs[0:4]
+    rows = [(refs[4 + 4 * r : 6 + 4 * r], refs[6 + 4 * r : 8 + 4 * r], sc_ref[5 + r] == 1) for r in range(2)]
+    stat_in, acc_in = refs[12:14]
+    outs = refs[14:18]
+
+    def state(s):
+        stat = stat_in[0, s]
+        return stat[:, :1], acc_in[0, s], stat[:, HEAD_DIM // 2 : HEAD_DIM // 2 + 1]
+
+    def write(s, result):
+        attended = (result[1] / result[2]).astype(jnp.bfloat16)
+        outs[2 * s][0] = attended[:TILE]
+        outs[2 * s + 1][0] = attended[TILE:]
+
+    @pl.when(sc_ref[4] == 0)
+    def _():
+        write(0, attend(query_of(q, 0), [segment([theirs], there) for _, theirs, there in rows], state(0)))
+
+    @pl.when(sc_ref[4] == 1)
+    def _():
+        write(0, state(0))
+
+    write(1, attend(query_of(q, 1), [segment([mine, theirs], there) for mine, theirs, there in rows], state(1)))
+
+
+Q_SPEC = pl.BlockSpec((1, TILE, HEAD_DIM), lambda h, sc: (h, 0, 0))
+KV_SPEC = pl.BlockSpec((2, 1, TILE, HEAD_DIM), lambda h, sc: (0, h, 0, 0))
+STATE_SPEC = pl.BlockSpec((1, 2, 2 * TILE, HEAD_DIM), lambda h, sc: (h, 0, 0, 0))
+STATE_SHAPE = jax.ShapeDtypeStruct((GH, 2, 2 * TILE, HEAD_DIM), jnp.float32)
+
+
+def attend_cost(blocks):
+    pairs = GH * blocks * 4 * TILE * TILE
+    return pl.CostEstimate(flops=4 * pairs * HEAD_DIM, bytes_accessed=12 * TILE * GW * 2, transcendentals=pairs)
+
+
+def attend_first(sc, queries, tiles):
+    return pl.pallas_call(
+        first_kernel,
+        grid_spec=pltpu.PrefetchScalarGridSpec(
+            num_scalar_prefetch=1,
+            grid=(GH,),
+            in_specs=[Q_SPEC] * 4 + [KV_SPEC] * 16,
+            out_specs=[STATE_SPEC] * 2,
+        ),
+        out_shape=[STATE_SHAPE] * 2,
+        compiler_params=limit(32),
+        cost_estimate=attend_cost(10),
+        name="attend_first",
+    )(sc, *queries, *tiles)
+
+
+def attend_last(sc, queries, tiles, state):
+    return pl.pallas_call(
+        last_kernel,
+        grid_spec=pltpu.PrefetchScalarGridSpec(
+            num_scalar_prefetch=1,
+            grid=(GH,),
+            in_specs=[Q_SPEC] * 4 + [KV_SPEC] * 8 + [STATE_SPEC] * 2,
+            out_specs=[Q_SPEC] * GROUPS,
+        ),
+        out_shape=[jax.ShapeDtypeStruct((GH, TILE, HEAD_DIM), jnp.bfloat16)] * GROUPS,
+        compiler_params=limit(32),
+        cost_estimate=attend_cost(5),
+        name="attend_last",
+    )(sc, *queries, *tiles, *state)
+
+
+def out_kernel(sc_ref, a0, a1, a2, a3, mod_ref, w_ref, out_ref):
+    total = None
+    for m, ref in enumerate((a0, a1, a2, a3)):
+        rows = jnp.concatenate([ref[h] for h in range(GH)], axis=1)
+        part = jnp.dot(rows, w_ref[pl.ds(group_of(sc_ref, m), GW), :], preferred_element_type=jnp.float32)
+        total = part if total is None else total + part
+    out_ref[...] = (total * mod_ref[2:3, :]).astype(jnp.bfloat16)
+
+
+def project_out(sc, attended, modulation, w_out):
+    return pl.pallas_call(
+        out_kernel,
+        in_specs=[SMEM] + [VMEM] * 6,
+        out_specs=VMEM,
+        out_shape=jax.ShapeDtypeStruct((TILE, D), jnp.bfloat16),
+        compiler_params=limit(20),
+        cost_estimate=pl.CostEstimate(flops=2 * TILE * D * D, bytes_accessed=2 * D * D, transcendentals=0),
+        name="project_out",
+    )(sc, *attended, modulation, w_out)
+
+
+def square_swap(value, m):
+    if m == 0:
+        return value
+    flip = (m >> 1) * 4 + (m & 1)
+    return lax.ppermute(value, ("ta", "wa"), [(i, i ^ flip) for i in range(8)])
+
+
+def core_swap(value):
+    return lax.ppermute(value, "ta", [(i, i ^ 1) for i in range(4)])
+
+
+def square_body(tokens, modulation, w_query, w_key, w_value, w_out, norm_q, norm_k):
+    ta, ha, wa = (lax.axis_index(name) for name in ("ta", "ha", "wa"))
+    rows_n = lax.axis_size("ha")
+    place_x, core = ta // 2, ta % 2
+    near_slot = 1 - (place_x ^ core)
+    sc = jnp.stack(
+        [2 * place_x + wa, ta, ha, wa, near_slot, (ha > 0).astype(jnp.int32), (ha < rows_n - 1).astype(jnp.int32)]
+    ).astype(jnp.int32)
+    half, sixth = HEAD_DIM // 2, HEAD_DIM // 6
+    first = half - 2 * sixth
+    tables = (
+        rope_tables(lax.axis_size("ta"), CT, 0, first),
+        rope_tables(rows_n, CH, first, sixth),
+        rope_tables(lax.axis_size("wa"), CW, first + sixth, sixth),
+    )
+    *kv, normed = project_kv(sc, tokens.reshape(TILE, D), modulation, norm_k, tables, w_key, w_value)
+    up = [(i, i + 1) for i in range(rows_n - 1)]
+    down = [(i + 1, i) for i in range(rows_n - 1)]
+    def rows_of(tile):
+        return lax.ppermute(tile, "ha", up), lax.ppermute(tile, "ha", down)
+
+    def after(value, *others):
+        return lax.optimization_barrier((value, *others))[0]
+
+    same = [kv[0], square_swap(kv[1], 1), square_swap(kv[2], 2)]
+    halo = [rows_of(tile) for tile in same]
+    same.append(square_swap(after(kv[3], same[1], same[2]), 3))
+    halo.append(rows_of(same[3]))
+    queries = project_q(sc, after(normed, same[1]), norm_q, tables, w_query)
+    queries = [square_swap(queries[m], m) for m in range(GROUPS)]
+    other = [core_swap(tile) for tile in same]
+    halo_other = [[core_swap(tile) for tile in pair] for pair in halo]
+
+    def halo_slot(slot):
+        return [part[m][r] for r in range(2) for part in (halo, halo_other) for m in (2 * slot, 2 * slot + 1)]
+
+    state = attend_first(sc, queries, [*same, *other, *halo_slot(0)])
+    attended = attend_last(sc, queries, halo_slot(1), state)
+    attended = [square_swap(attended[m], m) for m in range(GROUPS)]
+    branch = project_out(sc, attended, modulation, w_out)
+    return branch.reshape(CT, CH, CW, D)
+
+
 def solution(mesh):
+    square = mesh.shape["ta"] == 4 and mesh.shape["wa"] == 2
+    chosen = square_body if square else body
     in_specs = (P("ta", "ha", "wa", None), P(), P(), P(), P(), P(), P(), P())
     out_specs = P("ta", "ha", "wa", None)
-    return jax.shard_map(body, mesh=mesh, in_specs=in_specs, out_specs=out_specs, check_vma=False)
+    return jax.shard_map(chosen, mesh=mesh, in_specs=in_specs, out_specs=out_specs, check_vma=False)

time: 633 us -> 94.9 us (0.15)
  the two profiles are of different devices: /device:TPU:29 before, /device:TPU:0 now
where the time goes in v2:
time: 94.9 us; the launch traced here: 94.5 us
  starting transfers between devices  36.9 us (39%)
  Pallas kernels  30.6 us (32%)
  waiting for transfers between devices  22.6 us (24%)
  local copies, waits for them, and re-layouts  4.11 us (4%)
    ppermute x8, starting transfers between devices, rows_of(): return (lax.ppermute(tile, 'ha', up), lax.ppermute(tile, 'ha', down))  20.8 us
    ppermute x9, starting transfers between devices, square_swap(): return lax.ppermute(value, ('ta', 'wa'), [(i, i ^ flip) for i in range(8)])  14.2 us
    ppermute x9, waiting for transfers between devices, square_swap(): return lax.ppermute(value, ('ta', 'wa'), [(i, i ^ flip) for i in range(8)])  13 us
    pallas_call x1, Pallas kernels, attend_first(): pl.pallas_call(first_kernel, grid_spec=pltpu.PrefetchScalarGridSpec(num_s...  10.7 us
    ppermute x8, waiting for transfers between devices, rows_of(): return (lax.ppermute(tile, 'ha', up), lax.ppermute(tile, 'ha', down))  9.57 us
    pallas_call x1, Pallas kernels, project_kv(): pl.pallas_call(kv_kernel, in_specs=[SMEM] + [HBM] * 8, out_specs=[VMEM] *...  7.93 us
    pallas_call x1, Pallas kernels, attend_last(): pl.pallas_call(last_kernel, grid_spec=pltpu.PrefetchScalarGridSpec(num_sc...  6.53 us
    unnamed x24, local copies, waits for them, and re-layouts  3.44 us
  transfers between devices with their start and end apart: 29, of which 9 were waited for; matrix products, arithmetic and copies ran while one was open for 0% of the time, Pallas kernels for 14%

profile of v2, /device:TPU:0, one launch (start us, length us, event | category | flops | bytes accessed | tf_op | source)
XLA Modules:
  0.0 94.5 jit_solution(18385692687308946914)
XLA Ops:
  0.0 0.7 stack.39.sc_ref
  0.7 0.0 copy-start.7
  0.7 7.9 %project_kv.1 = (bf16[2,3,192,128]{3,2,1,0:T(8,128)(2,1)}, bf16[2,3,192,128]{3,2,1,0:T(8,128)(2,1)}, bf16[2,3,192,128]{3,2,1,0:T(8,128)(2,1)}, bf16[2,3,192,128]{3,2,1,0:T(8,128)(2,1)}, bf16[192,1536]{1,0:T(8,128)(2,1)}) custom-call(s32[7]{0:T(128)} %stack.39.sc_ref, bf16[192,1536]{1,0:T(8,128)(2,1)} %bitcast.11, f32[3,1536]{1,0:T(4,128)} %mod_ref.1, ...), custom_call_target="tpu_custom_call" | custom-call | flops 1811939328 | bytes 9437184 | tf_op jit(solution)/shard_map/project_kv/pallas_call | solution.py:312
  8.6 3.0 %collective-permute-start = (bf16[2,3,192,128]{3,2,1,0:T(8,128)(2,1)}, bf16[2,3,192,128]{3,2,1,0:T(8,128)(2,1)S(1)}, u32[]{:S(2)}, u32[]{:S(2)}) collective-permute-start(bf16[2,3,192,128]{3,2,1,0:T(8,128)(2,1)} %get-tuple-element.23), channel_id=1, source_target_pairs={{0,1},{1,0},{8,9},{9,8},{16,17},{17,16},{24,25},{25,24},{2,3},{3,2... | collective-permute-start | bytes 884744 | tf_op jit(solution)/shard_map/ppermute | solution.py:506
  11.7 1.5 %collective-permute-start.4 = (bf16[2,3,192,128]{3,2,1,0:T(8,128)(2,1)}, bf16[2,3,192,128]{3,2,1,0:T(8,128)(2,1)S(1)}, u32[]{:S(2)}, u32[]{:S(2)}) collective-permute-start(bf16[2,3,192,128]{3,2,1,0:T(8,128)(2,1)} %get-tuple-element.29), channel_id=1, source_target_pairs={{0,16},{1,17},{8,24},{9,25},{16,0},{17,1},{24,8},{25,9},{2,18},{3,... | collective-permute-start | bytes 884744 | tf_op jit(solution)/shard_map/ppermute | solution.py:506
  13.2 3.5 %collective-permute-start.18 = (bf16[2,3,192,128]{3,2,1,0:T(8,128)(2,1)}, bf16[2,3,192,128]{3,2,1,0:T(8,128)(2,1)S(1)}, u32[]{:S(2)}, u32[]{:S(2)}) collective-permute-start(bf16[2,3,192,128]{3,2,1,0:T(8,128)(2,1)} %get-tuple-element.32.refs_4_), channel_id=1, source_target_pairs={{0,2},{2,4},{4,6},{1,3},{3,5},{5,7},{8,10},{10,12},{12,14},{9,11},... | collective-permute-start | bytes 884744 | tf_op jit(solution)/shard_map/ppermute | solution.py:532
  16.6 1.3 %collective-permute-start.22 = (bf16[2,3,192,128]{3,2,1,0:T(8,128)(2,1)}, bf16[2,3,192,128]{3,2,1,0:T(8,128)(2,1)S(1)}, u32[]{:S(2)}, u32[]{:S(2)}) collective-permute-start(bf16[2,3,192,128]{3,2,1,0:T(8,128)(2,1)} %get-tuple-element.32.refs_4_), channel_id=1, source_target_pairs={{2,0},{4,2},{6,4},{3,1},{5,3},{7,5},{10,8},{12,10},{14,12},{11,9},... | collective-permute-start | bytes 884744 | tf_op jit(solution)/shard_map/ppermute | solution.py:532
  17.9 0.1 collective-permute-start.14
  18.0 0.8 collective-permute-done.refs_5_
  18.9 0.0 copy-start
  18.9 2.3 %copy-done = bf16[1536,1536]{1,0:T(8,128)(2,1)S(1)} copy-done((bf16[1536,1536]{1,0:T(8,128)(2,1)S(1)}, bf16[1536,1536]{1,0:T(8,128)(2,1)}, u32[]{:S(2)}) %copy-start) | copy-done | bytes 4718616
  21.2 1.1 %copy-done.1 = bf16[192,1536]{1,0:T(8,128)(2,1)S(1)} copy-done((bf16[192,1536]{1,0:T(8,128)(2,1)S(1)}, bf16[192,1536]{1,0:T(8,128)(2,1)}, u32[]{:S(2)}) %copy-start.1) | copy-done | bytes 589848
  22.3 2.7 %project_q.1 = (bf16[3,192,128]{2,1,0:T(8,128)(2,1)S(1)}, bf16[3,192,128]{2,1,0:T(8,128)(2,1)S(1)}, bf16[3,192,128]{2,1,0:T(8,128)(2,1)S(1)}, bf16[3,192,128]{2,1,0:T(8,128)(2,1)S(1)}) custom-call(s32[7]{0:T(128)S(1)} %copy-done.6, bf16[192,1536]{1,0:T(8,128)(2,1)S(1)} %copy-done.1, f32[1536]{0:T(1024)S(1)} %copy-done.7, f32[4,2,3,128]{3,2,1,0:T(4,128)S(1)} %copy-done.4, ...), custom_call_target="tpu_custom_call" | custom-call | flops 905969664 | bytes 4718592 | tf_op jit(solution)/shard_map/project_q/pallas_call | solution.py:336
  25.0 1.8 %collective-permute-start.1 = (bf16[3,192,128]{2,1,0:T(8,128)(2,1)S(1)}, bf16[3,192,128]{2,1,0:T(8,128)(2,1)S(1)}, u32[]{:S(2)}, u32[]{:S(2)}) collective-permute-start(bf16[3,192,128]{2,1,0:T(8,128)(2,1)S(1)} %get-tuple-element.26), channel_id=1, source_target_pairs={{0,1},{1,0},{8,9},{9,8},{16,17},{17,16},{24,25},{25,24},{2,3},{3,2... | collective-permute-start | bytes 442376 | tf_op jit(solution)/shard_map/ppermute | solution.py:506
  26.8 1.5 %collective-permute-start.2 = (bf16[3,192,128]{2,1,0:T(8,128)(2,1)S(1)}, bf16[3,192,128]{2,1,0:T(8,128)(2,1)S(1)}, u32[]{:S(2)}, u32[]{:S(2)}) collective-permute-start(bf16[3,192,128]{2,1,0:T(8,128)(2,1)S(1)} %get-tuple-element.27), channel_id=1, source_target_pairs={{0,16},{1,17},{8,24},{9,25},{16,0},{17,1},{24,8},{25,9},{2,18},{3,... | collective-permute-start | bytes 442376 | tf_op jit(solution)/shard_map/ppermute | solution.py:506
  28.3 0.0 collective-permute-done.18.refs_12_
  28.3 0.2 collective-permute-start.6
  28.5 0.0 collective-permute-done.22.refs_16_
  28.6 3.7 %collective-permute-start.19 = (bf16[2,3,192,128]{3,2,1,0:T(8,128)(2,1)S(1)}, bf16[2,3,192,128]{3,2,1,0:T(8,128)(2,1)S(1)}, u32[]{:S(2)}, u32[]{:S(2)}) collective-permute-start(bf16[2,3,192,128]{3,2,1,0:T(8,128)(2,1)S(1)} %collective-permute-done.refs_5_), channel_id=1, source_target_pairs={{0,2},{2,4},{4,6},{1,3},{3,5},{5,7},{8,10},{10,12},{12,14},{9,11},... | collective-permute-start | bytes 884744 | tf_op jit(solution)/shard_map/ppermute | solution.py:532
  32.3 1.3 %collective-permute-start.23 = (bf16[2,3,192,128]{3,2,1,0:T(8,128)(2,1)S(1)}, bf16[2,3,192,128]{3,2,1,0:T(8,128)(2,1)S(1)}, u32[]{:S(2)}, u32[]{:S(2)}) collective-permute-start(bf16[2,3,192,128]{3,2,1,0:T(8,128)(2,1)S(1)} %collective-permute-done.refs_5_), channel_id=1, source_target_pairs={{2,0},{4,2},{6,4},{3,1},{5,3},{7,5},{10,8},{12,10},{14,12},{11,9},... | collective-permute-start | bytes 884744 | tf_op jit(solution)/shard_map/ppermute | solution.py:532
  33.6 0.1 collective-permute-start.15
  33.7 2.5 %collective-permute-start.3 = (bf16[3,192,128]{2,1,0:T(8,128)(2,1)S(1)}, bf16[3,192,128]{2,1,0:T(8,128)(2,1)S(1)}, u32[]{:S(2)}, u32[]{:S(2)}) collective-permute-start(bf16[3,192,128]{2,1,0:T(8,128)(2,1)S(1)} %get-tuple-element.28), channel_id=1, source_target_pairs={{0,17},{1,16},{8,25},{9,24},{16,1},{17,0},{24,9},{25,8},{2,19},{3,... | collective-permute-start | bytes 442376 | tf_op jit(solution)/shard_map/ppermute | solution.py:506
  36.2 4.9 %collective-permute-done.3.refs_3_ = bf16[3,192,128]{2,1,0:T(8,128)(2,1)S(1)} collective-permute-done((bf16[3,192,128]{2,1,0:T(8,128)(2,1)S(1)}, bf16[3,192,128]{2,1,0:T(8,128)(2,1)S(1)}, u32[]{:S(2)}, u32[]{:S(2)}) %collective-permute-start.3) | collective-permute-done | bytes 147488 | tf_op jit(solution)/shard_map/ppermute | solution.py:506
  41.1 0.5 collective-permute-start.20
  41.7 0.1 collective-permute-start.24
  41.7 0.7 collective-permute-done.23.refs_17_
  42.5 1.3 %collective-permute-start.10 = (bf16[2,3,192,128]{3,2,1,0:T(8,128)(2,1)S(1)}, bf16[2,3,192,128]{3,2,1,0:T(8,128)(2,1)S(1)}, u32[]{:S(2)}, u32[]{:S(2)}) collective-permute-start(bf16[2,3,192,128]{3,2,1,0:T(8,128)(2,1)S(1)} %collective-permute-done.4.refs_6_), channel_id=1, source_target_pairs={{2,0},{4,2},{6,4},{3,1},{5,3},{7,5},{10,8},{12,10},{14,12},{11,9},... | collective-permute-start | bytes 884744 | tf_op jit(solution)/shard_map/ppermute | solution.py:532
  43.8 4.6 %collective-permute-start.5 = (bf16[2,3,192,128]{3,2,1,0:T(8,128)(2,1)S(1)}, bf16[2,3,192,128]{3,2,1,0:T(8,128)(2,1)S(1)}, u32[]{:S(2)}, u32[]{:S(2)}) collective-permute-start(bf16[2,3,192,128]{3,2,1,0:T(8,128)(2,1)S(1)} %collective-permute-done.4.refs_6_), channel_id=1, source_target_pairs={{0,2},{2,4},{4,6},{1,3},{3,5},{5,7},{8,10},{10,12},{12,14},{9,11},... | collective-permute-start | bytes 884744 | tf_op jit(solution)/shard_map/ppermute | solution.py:532
  48.4 0.1 collective-permute-start.17
  48.5 0.5 collective-permute-start.21
  48.9 1.3 %collective-permute-start.11 = (bf16[2,3,192,128]{3,2,1,0:T(8,128)(2,1)S(1)}, bf16[2,3,192,128]{3,2,1,0:T(8,128)(2,1)S(1)}, u32[]{:S(2)}, u32[]{:S(2)}) collective-permute-start(bf16[2,3,192,128]{3,2,1,0:T(8,128)(2,1)S(1)} %collective-permute-done.6.refs_7_), channel_id=1, source_target_pairs={{2,0},{4,2},{6,4},{3,1},{5,3},{7,5},{10,8},{12,10},{14,12},{11,9},... | collective-permute-start | bytes 884744 | tf_op jit(solution)/shard_map/ppermute | solution.py:532
  50.2 3.8 %collective-permute-done.10.refs_8_ = bf16[2,3,192,128]{3,2,1,0:T(8,128)(2,1)S(1)} collective-permute-done((bf16[2,3,192,128]{3,2,1,0:T(8,128)(2,1)S(1)}, bf16[2,3,192,128]{3,2,1,0:T(8,128)(2,1)S(1)}, u32[]{:S(2)}, u32[]{:S(2)}) %collective-permute-start.10) | collective-permute-done | bytes 294944 | tf_op jit(solution)/shard_map/ppermute | solution.py:532
  54.0 3.8 %collective-permute-start.7 = (bf16[2,3,192,128]{3,2,1,0:T(8,128)(2,1)S(1)}, bf16[2,3,192,128]{3,2,1,0:T(8,128)(2,1)S(1)}, u32[]{:S(2)}, u32[]{:S(2)}) collective-permute-start(bf16[2,3,192,128]{3,2,1,0:T(8,128)(2,1)S(1)} %collective-permute-done.6.refs_7_), channel_id=1, source_target_pairs={{0,2},{2,4},{4,6},{1,3},{3,5},{5,7},{8,10},{10,12},{12,14},{9,11},... | collective-permute-start | bytes 884744 | tf_op jit(solution)/shard_map/ppermute | solution.py:532
  57.9 0.1 collective-permute-start.25
  58.0 0.5 collective-permute-start.12
  58.4 0.1 collective-permute-start.8
  58.5 1.7 %collective-permute-done.11.refs_9_ = bf16[2,3,192,128]{3,2,1,0:T(8,128)(2,1)S(1)} collective-permute-done((bf16[2,3,192,128]{3,2,1,0:T(8,128)(2,1)S(1)}, bf16[2,3,192,128]{3,2,1,0:T(8,128)(2,1)S(1)}, u32[]{:S(2)}, u32[]{:S(2)}) %collective-permute-start.11) | collective-permute-done | bytes 294944 | tf_op jit(solution)/shard_map/ppermute | solution.py:532
  60.2 3.4 %collective-permute-done.7.refs_5_ = bf16[2,3,192,128]{3,2,1,0:T(8,128)(2,1)S(1)} collective-permute-done((bf16[2,3,192,128]{3,2,1,0:T(8,128)(2,1)S(1)}, bf16[2,3,192,128]{3,2,1,0:T(8,128)(2,1)S(1)}, u32[]{:S(2)}, u32[]{:S(2)}) %collective-permute-start.7) | collective-permute-done | bytes 294944 | tf_op jit(solution)/shard_map/ppermute | solution.py:532
  63.6 10.7 %attend_first.1 = (f32[3,2,384,128]{3,2,1,0:T(8,128)S(1)}, f32[3,2,384,128]{3,2,1,0:T(8,128)S(1)}) custom-call(s32[7]{0:T(128)S(1)} %copy-done.6, bf16[3,192,128]{2,1,0:T(8,128)(2,1)S(1)} %get-tuple-element.25.refs_0_, bf16[3,192,128]{2,1,0:T(8,128)(2,1)S(1)} %collective-permute-done.1.refs_1_, bf16[3,192,128]{2,1,0:T(8,128)(2,1)S(1)} %collective-permute-done.2.refs_2_, ...), custom_call_target="tpu_custom_call" | custom-call | flops 2264924160 | bytes 1769472 | tf_op jit(solution)/shard_map/attend_first/pallas_call | solution.py:450
  74.3 0.0 copy-start.3
  74.4 6.5 %attend_last.1 = (bf16[3,192,128]{2,1,0:T(8,128)(2,1)S(1)}, bf16[3,192,128]{2,1,0:T(8,128)(2,1)S(1)}, bf16[3,192,128]{2,1,0:T(8,128)(2,1)S(1)}, bf16[3,192,128]{2,1,0:T(8,128)(2,1)S(1)}) custom-call(s32[7]{0:T(128)S(1)} %copy-done.6, bf16[3,192,128]{2,1,0:T(8,128)(2,1)S(1)} %get-tuple-element.25.refs_0_, ...), custom_call_target="tpu_custom_call" | custom-call | flops 1132462080 | bytes 1769472 | tf_op jit(solution)/shard_map/attend_last/pallas_call | solution.py:466
  80.9 1.3 %collective-permute-start.26 = (bf16[3,192,128]{2,1,0:T(8,128)(2,1)S(1)}, bf16[3,192,128]{2,1,0:T(8,128)(2,1)S(1)}, u32[]{:S(2)}, u32[]{:S(2)}) collective-permute-start(bf16[3,192,128]{2,1,0:T(8,128)(2,1)S(1)} %get-tuple-element.36), channel_id=1, source_target_pairs={{0,1},{1,0},{8,9},{9,8},{16,17},{17,16},{24,25},{25,24},{2,3},{3,2... | collective-permute-start | bytes 442376 | tf_op jit(solution)/shard_map/ppermute | solution.py:506
  82.2 1.7 %collective-permute-start.27 = (bf16[3,192,128]{2,1,0:T(8,128)(2,1)S(1)}, bf16[3,192,128]{2,1,0:T(8,128)(2,1)S(1)}, u32[]{:S(2)}, u32[]{:S(2)}) collective-permute-start(bf16[3,192,128]{2,1,0:T(8,128)(2,1)S(1)} %get-tuple-element.37), channel_id=1, source_target_pairs={{0,16},{1,17},{8,24},{9,25},{16,0},{17,1},{24,8},{25,9},{2,18},{3,... | collective-permute-start | bytes 442376 | tf_op jit(solution)/shard_map/ppermute | solution.py:506
  83.9 0.6 collective-permute-start.28
  84.5 2.9 %collective-permute-done.26.a1 = bf16[3,192,128]{2,1,0:T(8,128)(2,1)S(1)} collective-permute-done((bf16[3,192,128]{2,1,0:T(8,128)(2,1)S(1)}, bf16[3,192,128]{2,1,0:T(8,128)(2,1)S(1)}, u32[]{:S(2)}, u32[]{:S(2)}) %collective-permute-start.26) | collective-permute-done | bytes 147488 | tf_op jit(solution)/shard_map/ppermute | solution.py:506
  87.4 1.5 %collective-permute-done.27.a2 = bf16[3,192,128]{2,1,0:T(8,128)(2,1)S(1)} collective-permute-done((bf16[3,192,128]{2,1,0:T(8,128)(2,1)S(1)}, bf16[3,192,128]{2,1,0:T(8,128)(2,1)S(1)}, u32[]{:S(2)}, u32[]{:S(2)}) %collective-permute-start.27) | collective-permute-done | bytes 147488 | tf_op jit(solution)/shard_map/ppermute | solution.py:506
  88.9 2.8 %collective-permute-done.28.a3 = bf16[3,192,128]{2,1,0:T(8,128)(2,1)S(1)} collective-permute-done((bf16[3,192,128]{2,1,0:T(8,128)(2,1)S(1)}, bf16[3,192,128]{2,1,0:T(8,128)(2,1)S(1)}, u32[]{:S(2)}, u32[]{:S(2)}) %collective-permute-start.28) | collective-permute-done | bytes 147488 | tf_op jit(solution)/shard_map/ppermute | solution.py:506
  91.7 2.8 %project_out.1 = bf16[192,1536]{1,0:T(8,128)(2,1)} custom-call(s32[7]{0:T(128)S(1)} %copy-done.6, bf16[3,192,128]{2,1,0:T(8,128)(2,1)S(1)} %get-tuple-element.35.a0, bf16[3,192,128]{2,1,0:T(8,128)(2,1)S(1)} %collective-permute-done.26.a1, bf16[3,192,128]{2,1,0:T(8,128)(2,1)S(1)} %collective-permute-done.27.a2, ...), custom_call_target="tpu_custom_call" | custom-call | flops 905969664 | bytes 4718592 | tf_op jit(solution)/shard_map/project_out/pallas_call | solution.py:491
  (41 shorter events, 0.1 us)
Async XLA Ops:
  0.7 18.2 %copy-start.2 = (f32[4,2,8,128]{3,2,1,0:T(8,128)S(1)}, f32[4,2,8,128]{3,2,1,0:T(8,128)}, u32[]{:S(2)}) copy-start(f32[4,2,8,128]{3,2,1,0:T(8,128)} %constant.46.clone.rt_hbm.rt_ref) | copy-start | bytes 98308
  0.7 18.2 %copy-start.4 = (f32[4,2,3,128]{3,2,1,0:T(4,128)S(1)}, f32[4,2,3,128]{3,2,1,0:T(4,128)}, u32[]{:S(2)}) copy-start(f32[4,2,3,128]{3,2,1,0:T(4,128)} %constant.45.clone.ft_hbm.ft_ref) | copy-start | bytes 36868
  0.7 18.2 %copy-start.5 = (f32[2,2,8,128]{3,2,1,0:T(8,128)S(1)}, f32[2,2,8,128]{3,2,1,0:T(8,128)}, u32[]{:S(2)}) copy-start(f32[2,2,8,128]{3,2,1,0:T(8,128)} %constant.47.clone.ct_hbm.ct_ref) | copy-start | bytes 49156
  0.7 18.2 %copy-start.6 = (s32[7]{0:T(128)S(1)}, s32[7]{0:T(128)}, u32[]{:S(2)}) copy-start(s32[7]{0:T(128)} %stack.39.sc_ref) | copy-start | bytes 88
  0.7 18.2 %copy-start.7 = (f32[1536]{0:T(1024)S(1)}, f32[1536]{0:T(1024)}, u32[]{:S(2)}) copy-start(f32[1536]{0:T(1024)} %nq_ref.1) | copy-start | bytes 18436
  8.6 10.2 %collective-permute-start = (bf16[2,3,192,128]{3,2,1,0:T(8,128)(2,1)}, bf16[2,3,192,128]{3,2,1,0:T(8,128)(2,1)S(1)}, u32[]{:S(2)}, u32[]{:S(2)}) collective-permute-start(bf16[2,3,192,128]{3,2,1,0:T(8,128)(2,1)} %get-tuple-element.23), channel_id=1, source_target_pairs={{0,1},{1,0},{8,9},{9,8},{16,17},{17,16},{24,25},{25,24},{2,3},{3,2... | collective-permute-start | bytes 884744 | tf_op jit(solution)/shard_map/ppermute | solution.py:506
  11.7 15.1 %collective-permute-start.4 = (bf16[2,3,192,128]{3,2,1,0:T(8,128)(2,1)}, bf16[2,3,192,128]{3,2,1,0:T(8,128)(2,1)S(1)}, u32[]{:S(2)}, u32[]{:S(2)}) collective-permute-start(bf16[2,3,192,128]{3,2,1,0:T(8,128)(2,1)} %get-tuple-element.29), channel_id=1, source_target_pairs={{0,16},{1,17},{8,24},{9,25},{16,0},{17,1},{24,8},{25,9},{2,18},{3,... | collective-permute-start | bytes 884744 | tf_op jit(solution)/shard_map/ppermute | solution.py:506
  13.2 15.1 %collective-permute-start.18 = (bf16[2,3,192,128]{3,2,1,0:T(8,128)(2,1)}, bf16[2,3,192,128]{3,2,1,0:T(8,128)(2,1)S(1)}, u32[]{:S(2)}, u32[]{:S(2)}) collective-permute-start(bf16[2,3,192,128]{3,2,1,0:T(8,128)(2,1)} %get-tuple-element.32.refs_4_), channel_id=1, source_target_pairs={{0,2},{2,4},{4,6},{1,3},{3,5},{5,7},{8,10},{10,12},{12,14},{9,11},... | collective-permute-start | bytes 884744 | tf_op jit(solution)/shard_map/ppermute | solution.py:532
  16.6 11.9 %collective-permute-start.22 = (bf16[2,3,192,128]{3,2,1,0:T(8,128)(2,1)}, bf16[2,3,192,128]{3,2,1,0:T(8,128)(2,1)S(1)}, u32[]{:S(2)}, u32[]{:S(2)}) collective-permute-start(bf16[2,3,192,128]{3,2,1,0:T(8,128)(2,1)} %get-tuple-element.32.refs_4_), channel_id=1, source_target_pairs={{2,0},{4,2},{6,4},{3,1},{5,3},{7,5},{10,8},{12,10},{14,12},{11,9},... | collective-permute-start | bytes 884744 | tf_op jit(solution)/shard_map/ppermute | solution.py:532
  17.9 14.3 %collective-permute-start.14 = (bf16[2,3,192,128]{3,2,1,0:T(8,128)(2,1)}, bf16[2,3,192,128]{3,2,1,0:T(8,128)(2,1)S(1)}, u32[]{:S(2)}, u32[]{:S(2)}) collective-permute-start(bf16[2,3,192,128]{3,2,1,0:T(8,128)(2,1)} %get-tuple-element.32.refs_4_), channel_id=1, source_target_pairs={{0,8},{8,0},{16,24},{24,16},{1,9},{9,1},{17,25},{25,17},{2,10},{10... | collective-permute-start | bytes 884744 | tf_op jit(solution)/shard_map/ppermute | solution.py:510
  18.9 2.3 %copy-start = (bf16[1536,1536]{1,0:T(8,128)(2,1)S(1)}, bf16[1536,1536]{1,0:T(8,128)(2,1)}, u32[]{:S(2)}) copy-start(bf16[1536,1536]{1,0:T(8,128)(2,1)} %wq_ref.1) | copy-start | bytes 14155780
  21.2 1.1 %copy-start.1 = (bf16[192,1536]{1,0:T(8,128)(2,1)S(1)}, bf16[192,1536]{1,0:T(8,128)(2,1)}, u32[]{:S(2)}) copy-start(bf16[192,1536]{1,0:T(8,128)(2,1)} %get-tuple-element.24.normed_ref) | copy-start | bytes 1769476
  22.3 6.0 %copy-start.9 = (bf16[2,3,192,128]{3,2,1,0:T(8,128)(2,1)S(1)}, bf16[2,3,192,128]{3,2,1,0:T(8,128)(2,1)}, u32[]{:S(2)}) copy-start(bf16[2,3,192,128]{3,2,1,0:T(8,128)(2,1)} %get-tuple-element.31) | copy-start | bytes 884740
  22.3 41.3 %copy-start.8 = (bf16[2,3,192,128]{3,2,1,0:T(8,128)(2,1)S(1)}, bf16[2,3,192,128]{3,2,1,0:T(8,128)(2,1)}, u32[]{:S(2)}) copy-start(bf16[2,3,192,128]{3,2,1,0:T(8,128)(2,1)} %get-tuple-element.32.refs_4_) | copy-start | bytes 884740
  25.0 8.6 %collective-permute-start.1 = (bf16[3,192,128]{2,1,0:T(8,128)(2,1)S(1)}, bf16[3,192,128]{2,1,0:T(8,128)(2,1)S(1)}, u32[]{:S(2)}, u32[]{:S(2)}) collective-permute-start(bf16[3,192,128]{2,1,0:T(8,128)(2,1)S(1)} %get-tuple-element.26), channel_id=1, source_target_pairs={{0,1},{1,0},{8,9},{9,8},{16,17},{17,16},{24,25},{25,24},{2,3},{3,2... | collective-permute-start | bytes 442376 | tf_op jit(solution)/shard_map/ppermute | solution.py:506
  26.8 6.9 %collective-permute-start.2 = (bf16[3,192,128]{2,1,0:T(8,128)(2,1)S(1)}, bf16[3,192,128]{2,1,0:T(8,128)(2,1)S(1)}, u32[]{:S(2)}, u32[]{:S(2)}) collective-permute-start(bf16[3,192,128]{2,1,0:T(8,128)(2,1)S(1)} %get-tuple-element.27), channel_id=1, source_target_pairs={{0,16},{1,17},{8,24},{9,25},{16,0},{17,1},{24,8},{25,9},{2,18},{3,... | collective-permute-start | bytes 442376 | tf_op jit(solution)/shard_map/ppermute | solution.py:506
  28.3 12.8 %collective-permute-start.6 = (bf16[2,3,192,128]{3,2,1,0:T(8,128)(2,1)S(1)}, bf16[2,3,192,128]{3,2,1,0:T(8,128)(2,1)S(1)}, u32[]{:S(2)}, u32[]{:S(2)}) collective-permute-start(bf16[2,3,192,128]{3,2,1,0:T(8,128)(2,1)S(1)} %copy-done.9), channel_id=1, source_target_pairs={{0,17},{1,16},{8,25},{9,24},{16,1},{17,0},{24,9},{25,8},{2,19},{3,... | collective-permute-start | bytes 884744 | tf_op jit(solution)/shard_map/ppermute | solution.py:506
  28.6 13.1 %collective-permute-start.19 = (bf16[2,3,192,128]{3,2,1,0:T(8,128)(2,1)S(1)}, bf16[2,3,192,128]{3,2,1,0:T(8,128)(2,1)S(1)}, u32[]{:S(2)}, u32[]{:S(2)}) collective-permute-start(bf16[2,3,192,128]{3,2,1,0:T(8,128)(2,1)S(1)} %collective-permute-done.refs_5_), channel_id=1, source_target_pairs={{0,2},{2,4},{4,6},{1,3},{3,5},{5,7},{8,10},{10,12},{12,14},{9,11},... | collective-permute-start | bytes 884744 | tf_op jit(solution)/shard_map/ppermute | solution.py:532
  32.3 10.2 %collective-permute-start.23 = (bf16[2,3,192,128]{3,2,1,0:T(8,128)(2,1)S(1)}, bf16[2,3,192,128]{3,2,1,0:T(8,128)(2,1)S(1)}, u32[]{:S(2)}, u32[]{:S(2)}) collective-permute-start(bf16[2,3,192,128]{3,2,1,0:T(8,128)(2,1)S(1)} %collective-permute-done.refs_5_), channel_id=1, source_target_pairs={{2,0},{4,2},{6,4},{3,1},{5,3},{7,5},{10,8},{12,10},{14,12},{11,9},... | collective-permute-start | bytes 884744 | tf_op jit(solution)/shard_map/ppermute | solution.py:532
  33.6 10.1 %collective-permute-start.15 = (bf16[2,3,192,128]{3,2,1,0:T(8,128)(2,1)S(1)}, bf16[2,3,192,128]{3,2,1,0:T(8,128)(2,1)S(1)}, u32[]{:S(2)}, u32[]{:S(2)}) collective-permute-start(bf16[2,3,192,128]{3,2,1,0:T(8,128)(2,1)S(1)} %collective-permute-done.refs_5_), channel_id=1, source_target_pairs={{0,8},{8,0},{16,24},{24,16},{1,9},{9,1},{17,25},{25,17},{2,10},{10... | collective-permute-start | bytes 884744 | tf_op jit(solution)/shard_map/ppermute | solution.py:510
  33.7 7.4 %collective-permute-start.3 = (bf16[3,192,128]{2,1,0:T(8,128)(2,1)S(1)}, bf16[3,192,128]{2,1,0:T(8,128)(2,1)S(1)}, u32[]{:S(2)}, u32[]{:S(2)}) collective-permute-start(bf16[3,192,128]{2,1,0:T(8,128)(2,1)S(1)} %get-tuple-element.28), channel_id=1, source_target_pairs={{0,17},{1,16},{8,25},{9,24},{16,1},{17,0},{24,9},{25,8},{2,19},{3,... | collective-permute-start | bytes 442376 | tf_op jit(solution)/shard_map/ppermute | solution.py:506
  41.1 7.2 %collective-permute-start.16 = (bf16[2,3,192,128]{3,2,1,0:T(8,128)(2,1)S(1)}, bf16[2,3,192,128]{3,2,1,0:T(8,128)(2,1)S(1)}, u32[]{:S(2)}, u32[]{:S(2)}) collective-permute-start(bf16[2,3,192,128]{3,2,1,0:T(8,128)(2,1)S(1)} %collective-permute-done.4.refs_6_), channel_id=1, source_target_pairs={{0,8},{8,0},{16,24},{24,16},{1,9},{9,1},{17,25},{25,17},{2,10},{10... | collective-permute-start | bytes 884744 | tf_op jit(solution)/shard_map/ppermute | solution.py:510
  41.1 7.3 %collective-permute-start.20 = (bf16[2,3,192,128]{3,2,1,0:T(8,128)(2,1)S(1)}, bf16[2,3,192,128]{3,2,1,0:T(8,128)(2,1)S(1)}, u32[]{:S(2)}, u32[]{:S(2)}) collective-permute-start(bf16[2,3,192,128]{3,2,1,0:T(8,128)(2,1)S(1)} %collective-permute-done.18.refs_12_), channel_id=1, source_target_pairs={{0,8},{8,0},{16,24},{24,16},{1,9},{9,1},{17,25},{25,17},{2,10},{10... | collective-permute-start | bytes 884744 | tf_op jit(solution)/shard_map/ppermute | solution.py:510
  41.7 7.3 %collective-permute-start.24 = (bf16[2,3,192,128]{3,2,1,0:T(8,128)(2,1)S(1)}, bf16[2,3,192,128]{3,2,1,0:T(8,128)(2,1)S(1)}, u32[]{:S(2)}, u32[]{:S(2)}) collective-permute-start(bf16[2,3,192,128]{3,2,1,0:T(8,128)(2,1)S(1)} %collective-permute-done.22.refs_16_), channel_id=1, source_target_pairs={{0,8},{8,0},{16,24},{24,16},{1,9},{9,1},{17,25},{25,17},{2,10},{10... | collective-permute-start | bytes 884744 | tf_op jit(solution)/shard_map/ppermute | solution.py:510
  42.5 11.5 %collective-permute-start.10 = (bf16[2,3,192,128]{3,2,1,0:T(8,128)(2,1)S(1)}, bf16[2,3,192,128]{3,2,1,0:T(8,128)(2,1)S(1)}, u32[]{:S(2)}, u32[]{:S(2)}) collective-permute-start(bf16[2,3,192,128]{3,2,1,0:T(8,128)(2,1)S(1)} %collective-permute-done.4.refs_6_), channel_id=1, source_target_pairs={{2,0},{4,2},{6,4},{3,1},{5,3},{7,5},{10,8},{12,10},{14,12},{11,9},... | collective-permute-start | bytes 884744 | tf_op jit(solution)/shard_map/ppermute | solution.py:532
  43.8 14.1 %collective-permute-start.5 = (bf16[2,3,192,128]{3,2,1,0:T(8,128)(2,1)S(1)}, bf16[2,3,192,128]{3,2,1,0:T(8,128)(2,1)S(1)}, u32[]{:S(2)}, u32[]{:S(2)}) collective-permute-start(bf16[2,3,192,128]{3,2,1,0:T(8,128)(2,1)S(1)} %collective-permute-done.4.refs_6_), channel_id=1, source_target_pairs={{0,2},{2,4},{4,6},{1,3},{3,5},{5,7},{8,10},{10,12},{12,14},{9,11},... | collective-permute-start | bytes 884744 | tf_op jit(solution)/shard_map/ppermute | solution.py:532
  48.4 9.6 %collective-permute-start.17 = (bf16[2,3,192,128]{3,2,1,0:T(8,128)(2,1)S(1)}, bf16[2,3,192,128]{3,2,1,0:T(8,128)(2,1)S(1)}, u32[]{:S(2)}, u32[]{:S(2)}) collective-permute-start(bf16[2,3,192,128]{3,2,1,0:T(8,128)(2,1)S(1)} %collective-permute-done.6.refs_7_), channel_id=1, source_target_pairs={{0,8},{8,0},{16,24},{24,16},{1,9},{9,1},{17,25},{25,17},{2,10},{10... | collective-permute-start | bytes 884744 | tf_op jit(solution)/shard_map/ppermute | solution.py:510
  48.5 10.0 %collective-permute-start.21 = (bf16[2,3,192,128]{3,2,1,0:T(8,128)(2,1)S(1)}, bf16[2,3,192,128]{3,2,1,0:T(8,128)(2,1)S(1)}, u32[]{:S(2)}, u32[]{:S(2)}) collective-permute-start(bf16[2,3,192,128]{3,2,1,0:T(8,128)(2,1)S(1)} %collective-permute-done.19.refs_13_), channel_id=1, source_target_pairs={{0,8},{8,0},{16,24},{24,16},{1,9},{9,1},{17,25},{25,17},{2,10},{10... | collective-permute-start | bytes 884744 | tf_op jit(solution)/shard_map/ppermute | solution.py:510
  48.9 11.2 %collective-permute-start.11 = (bf16[2,3,192,128]{3,2,1,0:T(8,128)(2,1)S(1)}, bf16[2,3,192,128]{3,2,1,0:T(8,128)(2,1)S(1)}, u32[]{:S(2)}, u32[]{:S(2)}) collective-permute-start(bf16[2,3,192,128]{3,2,1,0:T(8,128)(2,1)S(1)} %collective-permute-done.6.refs_7_), channel_id=1, source_target_pairs={{2,0},{4,2},{6,4},{3,1},{5,3},{7,5},{10,8},{12,10},{14,12},{11,9},... | collective-permute-start | bytes 884744 | tf_op jit(solution)/shard_map/ppermute | solution.py:532
  54.0 9.5 %collective-permute-start.7 = (bf16[2,3,192,128]{3,2,1,0:T(8,128)(2,1)S(1)}, bf16[2,3,192,128]{3,2,1,0:T(8,128)(2,1)S(1)}, u32[]{:S(2)}, u32[]{:S(2)}) collective-permute-start(bf16[2,3,192,128]{3,2,1,0:T(8,128)(2,1)S(1)} %collective-permute-done.6.refs_7_), channel_id=1, source_target_pairs={{0,2},{2,4},{4,6},{1,3},{3,5},{5,7},{8,10},{10,12},{12,14},{9,11},... | collective-permute-start | bytes 884744 | tf_op jit(solution)/shard_map/ppermute | solution.py:532
  57.9 5.7 %collective-permute-start.25 = (bf16[2,3,192,128]{3,2,1,0:T(8,128)(2,1)S(1)}, bf16[2,3,192,128]{3,2,1,0:T(8,128)(2,1)S(1)}, u32[]{:S(2)}, u32[]{:S(2)}) collective-permute-start(bf16[2,3,192,128]{3,2,1,0:T(8,128)(2,1)S(1)} %collective-permute-done.23.refs_17_), channel_id=1, source_target_pairs={{0,8},{8,0},{16,24},{24,16},{1,9},{9,1},{17,25},{25,17},{2,10},{10... | collective-permute-start | bytes 884744 | tf_op jit(solution)/shard_map/ppermute | solution.py:510
  58.0 16.4 %collective-permute-start.12 = (bf16[2,3,192,128]{3,2,1,0:T(8,128)(2,1)S(1)}, bf16[2,3,192,128]{3,2,1,0:T(8,128)(2,1)S(1)}, u32[]{:S(2)}, u32[]{:S(2)}) collective-permute-start(bf16[2,3,192,128]{3,2,1,0:T(8,128)(2,1)S(1)} %collective-permute-done.10.refs_8_), channel_id=1, source_target_pairs={{0,8},{8,0},{16,24},{24,16},{1,9},{9,1},{17,25},{25,17},{2,10},{10... | collective-permute-start | bytes 884744 | tf_op jit(solution)/shard_map/ppermute | solution.py:510
  58.4 15.9 %collective-permute-start.8 = (bf16[2,3,192,128]{3,2,1,0:T(8,128)(2,1)S(1)}, bf16[2,3,192,128]{3,2,1,0:T(8,128)(2,1)S(1)}, u32[]{:S(2)}, u32[]{:S(2)}) collective-permute-start(bf16[2,3,192,128]{3,2,1,0:T(8,128)(2,1)S(1)} %collective-permute-done.5.refs_4_), channel_id=1, source_target_pairs={{0,8},{8,0},{16,24},{24,16},{1,9},{9,1},{17,25},{25,17},{2,10},{10... | collective-permute-start | bytes 884744 | tf_op jit(solution)/shard_map/ppermute | solution.py:510
  60.2 14.2 %collective-permute-start.13 = (bf16[2,3,192,128]{3,2,1,0:T(8,128)(2,1)S(1)}, bf16[2,3,192,128]{3,2,1,0:T(8,128)(2,1)S(1)}, u32[]{:S(2)}, u32[]{:S(2)}) collective-permute-start(bf16[2,3,192,128]{3,2,1,0:T(8,128)(2,1)S(1)} %collective-permute-done.11.refs_9_), channel_id=1, source_target_pairs={{0,8},{8,0},{16,24},{24,16},{1,9},{9,1},{17,25},{25,17},{2,10},{10... | collective-permute-start | bytes 884744 | tf_op jit(solution)/shard_map/ppermute | solution.py:510
  63.6 10.8 %collective-permute-start.9 = (bf16[2,3,192,128]{3,2,1,0:T(8,128)(2,1)S(1)}, bf16[2,3,192,128]{3,2,1,0:T(8,128)(2,1)S(1)}, u32[]{:S(2)}, u32[]{:S(2)}) collective-permute-start(bf16[2,3,192,128]{3,2,1,0:T(8,128)(2,1)S(1)} %collective-permute-done.7.refs_5_), channel_id=1, source_target_pairs={{0,8},{8,0},{16,24},{24,16},{1,9},{9,1},{17,25},{25,17},{2,10},{10... | collective-permute-start | bytes 884744 | tf_op jit(solution)/shard_map/ppermute | solution.py:510
  63.6 28.2 %slice-start = ((s8[4718592]{0:T(1024)(128)(4,1)}), s8[4194304]{0:T(1024)(128)(4,1)S(1)}, s32[]{:S(2)}) async-start(s8[4718592]{0:T(1024)(128)(4,1)} %bitcast.9), calls=%async_computation | async-start | bytes 8388608
  63.6 28.2 %slice-start.1 = ((s8[4718592]{0:T(1024)(128)(4,1)}), s8[524288]{0:T(1024)(128)(4,1)S(1)}, s32[]{:S(2)}) async-start(s8[4718592]{0:T(1024)(128)(4,1)} %bitcast.9), calls=%async_computation.1 | async-start | bytes 1048576
  74.3 17.4 %copy-start.3 = (f32[3,1536]{1,0:T(4,128)S(1)}, f32[3,1536]{1,0:T(4,128)}, u32[]{:S(2)}) copy-start(f32[3,1536]{1,0:T(4,128)} %mod_ref.1) | copy-start | bytes 55300
  80.9 6.5 %collective-permute-start.26 = (bf16[3,192,128]{2,1,0:T(8,128)(2,1)S(1)}, bf16[3,192,128]{2,1,0:T(8,128)(2,1)S(1)}, u32[]{:S(2)}, u32[]{:S(2)}) collective-permute-start(bf16[3,192,128]{2,1,0:T(8,128)(2,1)S(1)} %get-tuple-element.36), channel_id=1, source_target_pairs={{0,1},{1,0},{8,9},{9,8},{16,17},{17,16},{24,25},{25,24},{2,3},{3,2... | collective-permute-start | bytes 442376 | tf_op jit(solution)/shard_map/ppermute | solution.py:506
  82.2 6.7 %collective-permute-start.27 = (bf16[3,192,128]{2,1,0:T(8,128)(2,1)S(1)}, bf16[3,192,128]{2,1,0:T(8,128)(2,1)S(1)}, u32[]{:S(2)}, u32[]{:S(2)}) collective-permute-start(bf16[3,192,128]{2,1,0:T(8,128)(2,1)S(1)} %get-tuple-element.37), channel_id=1, source_target_pairs={{0,16},{1,17},{8,24},{9,25},{16,0},{17,1},{24,8},{25,9},{2,18},{3,... | collective-permute-start | bytes 442376 | tf_op jit(solution)/shard_map/ppermute | solution.py:506
  83.9 7.9 %collective-permute-start.28 = (bf16[3,192,128]{2,1,0:T(8,128)(2,1)S(1)}, bf16[3,192,128]{2,1,0:T(8,128)(2,1)S(1)}, u32[]{:S(2)}, u32[]{:S(2)}) collective-permute-start(bf16[3,192,128]{2,1,0:T(8,128)(2,1)S(1)} %get-tuple-element.38), channel_id=1, source_target_pairs={{0,17},{1,16},{8,25},{9,24},{16,1},{17,0},{24,9},{25,8},{2,19},{3,... | collective-permute-start | bytes 442376 | tf_op jit(solution)/shard_map/ppermute | solution.py:506

commit v3 on v2

--- a/solution.py
+++ b/solution.py
@@ -237,65 +237,74 @@
             write(m, h, rope(x, cosine, sine, even).astype(jnp.bfloat16))
 
 
+def start_all(pairs, sems):
+    copies = [pltpu.make_async_copy(source, target, sems.at[n]) for n, (source, target) in enumerate(pairs)]
+    for copy in copies:
+        copy.start()
+    return copies
+
+
+def wait_all(copies):
+    for copy in copies:
+        copy.wait()
+
+
+def weight_blocks(sc_ref, w_hbm, wbuf):
+    return [(w_hbm.at[:, pl.ds(group_of(sc_ref, m), GW)], wbuf.at[m]) for m in range(GROUPS)]
+
+
+def project_normed(sc_ref, normed, weights, wbuf, buf, gain_ref, tables, write):
+    ssq = None
+    for m in range(GROUPS):
+        weights[m].wait()
+        prod = jnp.dot(normed, wbuf[m], preferred_element_type=jnp.float32)
+        buf[m] = prod
+        squares = fold_squares(prod)
+        ssq = squares if ssq is None else ssq + squares
+    finish_normed(sc_ref, tables, buf, gain_ref, ssq, write)
+
+
 def kv_kernel(sc_ref, tok_hbm, mod_hbm, nk_hbm, ft_hbm, rt_hbm, ct_hbm, wk_hbm, wv_hbm, *refs):
-    outs, normed_ref, (tok_ref, mod_ref, nk_ref, ft_ref, rt_ref, ct_ref, wbuf, buf, gain_ref, sems) = refs[:4], refs[4], refs[5:]
-    small = [
-        pltpu.make_async_copy(source, target, sems.at[2, n])
-        for n, (source, target) in enumerate(
-            zip((tok_hbm, mod_hbm, nk_hbm, ft_hbm, rt_hbm, ct_hbm), (tok_ref, mod_ref, nk_ref, ft_ref, rt_ref, ct_ref))
-        )
-    ]
-    for copy in small:
-        copy.start()
-    copies = []
-    for kind, w_hbm in enumerate((wk_hbm, wv_hbm)):
-        for m in range(GROUPS):
-            copies.append(
-                pltpu.make_async_copy(
-                    w_hbm.at[:, pl.ds(group_of(sc_ref, m), GW)], wbuf.at[kind, m], sems.at[kind, m]
-                )
-            )
-            copies[-1].start()
-    for copy in small:
-        copy.wait()
+    kv_hbm, normed_hbm, refs = refs[:4], refs[4], refs[5:]
+    tok_ref, mod_ref, nk_ref, ft_ref, rt_ref, ct_ref, wk_buf, wv_buf, buf, gain_ref, normed_ref, kv_ref, sems, out_sems = refs
+    sources = (tok_hbm, mod_hbm, nk_hbm, ft_hbm, rt_hbm, ct_hbm)
+    small = start_all(zip(sources, refs), sems.at[2])
+    key_weights = start_all(weight_blocks(sc_ref, wk_hbm, wk_buf), sems.at[0])
+    value_weights = start_all(weight_blocks(sc_ref, wv_hbm, wv_buf), sems.at[1])
+    wait_all(small)
     gain_ref[...] = nk_ref[...].reshape(1, D)
     normed = layer_norm(tok_ref[...], mod_ref)
     normed_ref[...] = normed
-    ssq = None
+    results = start_all([(normed_ref, normed_hbm)], out_sems.at[2])
+
+    def write(m, h, x):
+        kv_ref[m, 0, h] = x
+
+    project_normed(sc_ref, normed, key_weights, wk_buf, buf, gain_ref, (ft_ref, rt_ref, ct_ref), write)
+    results += start_all([(kv_ref.at[m, 0], kv_hbm[m].at[0]) for m in range(GROUPS)], out_sems.at[0])
     for m in range(GROUPS):
-        copies[m].wait()
-        prod = jnp.dot(normed, wbuf[0, m], preferred_element_type=jnp.float32)
-        buf[m] = prod
-        squares = fold_squares(prod)
-        ssq = squares if ssq is None else ssq + squares
+        value_weights[m].wait()
+        prod = jnp.dot(normed, wv_buf[m], preferred_element_type=jnp.float32)
+        for h in range(GH):
+            kv_ref[m, 1, h] = prod[:, h * HEAD_DIM : (h + 1) * HEAD_DIM].astype(jnp.bfloat16)
+        results.append(pltpu.make_async_copy(kv_ref.at[m, 1], kv_hbm[m].at[1], out_sems.at[1, m]))
+        results[-1].start()
+    wait_all(results)
+
+
+def q_kernel(sc_ref, normed_hbm, nq_hbm, ft_hbm, rt_hbm, ct_hbm, wq_hbm, *refs):
+    q_hbm, refs = refs[:4], refs[4:]
+    normed_ref, nq_ref, ft_ref, rt_ref, ct_ref, wq_buf, buf, gain_ref, q_ref, sems, out_sems = refs
+    small = start_all(zip((normed_hbm, nq_hbm, ft_hbm, rt_hbm, ct_hbm), refs), sems.at[1])
+    weights = start_all(weight_blocks(sc_ref, wq_hbm, wq_buf), sems.at[0])
+    wait_all(small)
+    gain_ref[...] = nq_ref[...].reshape(1, D)
 
     def write(m, h, x):
-        outs[m][0, h] = x
-
-    finish_normed(sc_ref, (ft_ref, rt_ref, ct_ref), buf, gain_ref, ssq, write)
-    for m in range(GROUPS):
-        copies[GROUPS + m].wait()
-        prod = jnp.dot(normed, wbuf[1, m], preferred_element_type=jnp.float32)
-        for h in range(GH):
-            outs[m][1, h] = prod[:, h * HEAD_DIM : (h + 1) * HEAD_DIM].astype(jnp.bfloat16)
-
-
-def q_kernel(sc_ref, normed_ref, nq_ref, ft_ref, rt_ref, ct_ref, wq_ref, o0, o1, o2, o3, buf, gain_ref):
-    outs = (o0, o1, o2, o3)
-    gain_ref[...] = nq_ref[...].reshape(1, D)
-    ssq = None
-    for m in range(GROUPS):
-        prod = jnp.dot(
-            normed_ref[...], wq_ref[:, pl.ds(group_of(sc_ref, m), GW)], preferred_element_type=jnp.float32
-        )
-        buf[m] = prod
-        squares = fold_squares(prod)
-        ssq = squares if ssq is None else ssq + squares
-
-    def write(m, h, x):
-        outs[m][h] = x
-
-    finish_normed(sc_ref, (ft_ref, rt_ref, ct_ref), buf, gain_ref, ssq, write)
+        q_ref[m, h] = x
+
+    project_normed(sc_ref, normed_ref[...], weights, wq_buf, buf, gain_ref, (ft_ref, rt_ref, ct_ref), write)
+    wait_all(start_all([(q_ref.at[m], q_hbm[m]) for m in range(GROUPS)], out_sems))
 
 
 SMEM = pl.BlockSpec(memory_space=pltpu.SMEM)
@@ -307,23 +316,30 @@
     return pltpu.CompilerParams(vmem_limit_bytes=mib * 1024 * 1024)
 
 
+KV_SHAPE = (2, GH, TILE, HEAD_DIM)
+Q_SHAPE = (GH, TILE, HEAD_DIM)
+
+
 def project_kv(sc, tokens, modulation, norm_k, tables, w_key, w_value):
-    kv_shape = (2, GH, TILE, HEAD_DIM)
     return pl.pallas_call(
         kv_kernel,
         in_specs=[SMEM] + [HBM] * 8,
-        out_specs=[VMEM] * (GROUPS + 1),
+        out_specs=[HBM] * (GROUPS + 1),
         scratch_shapes=[
             pltpu.VMEM((TILE, D), jnp.bfloat16),
             pltpu.VMEM((3, D), jnp.float32),
             pltpu.VMEM((D,), jnp.float32),
             *[pltpu.VMEM(t.shape, jnp.float32) for t in tables],
-            pltpu.VMEM((2, GROUPS, D, GW), jnp.bfloat16),
+            pltpu.VMEM((GROUPS, D, GW), jnp.bfloat16),
+            pltpu.VMEM((GROUPS, D, GW), jnp.bfloat16),
             pltpu.VMEM((GROUPS, TILE, GW), jnp.float32),
             pltpu.VMEM((1, D), jnp.float32),
+            pltpu.VMEM((TILE, D), jnp.bfloat16),
+            pltpu.VMEM((GROUPS, *KV_SHAPE), jnp.bfloat16),
             pltpu.SemaphoreType.DMA((3, 6)),
+            pltpu.SemaphoreType.DMA((3, GROUPS)),
         ],
-        out_shape=[jax.ShapeDtypeStruct(kv_shape, jnp.bfloat16)] * GROUPS
+        out_shape=[jax.ShapeDtypeStruct(KV_SHAPE, jnp.bfloat16)] * GROUPS
         + [jax.ShapeDtypeStruct((TILE, D), jnp.bfloat16)],
         compiler_params=limit(60),
         cost_estimate=pl.CostEstimate(flops=4 * TILE * D * D, bytes_accessed=4 * D * D, transcendentals=0),
@@ -332,21 +348,30 @@
 
 
 def project_q(sc, normed, norm_q, tables, w_query):
-    q_shape = (GH, TILE, HEAD_DIM)
     return pl.pallas_call(
         q_kernel,
-        in_specs=[SMEM] + [VMEM] * 6,
-        out_specs=[VMEM] * GROUPS,
-        scratch_shapes=[pltpu.VMEM((GROUPS, TILE, GW), jnp.float32), pltpu.VMEM((1, D), jnp.float32)],
-        out_shape=[jax.ShapeDtypeStruct(q_shape, jnp.bfloat16)] * GROUPS,
-        compiler_params=limit(20),
+        in_specs=[SMEM] + [HBM] * 6,
+        out_specs=[HBM] * GROUPS,
+        scratch_shapes=[
+            pltpu.VMEM((TILE, D), jnp.bfloat16),
+            pltpu.VMEM((D,), jnp.float32),
+            *[pltpu.VMEM(t.shape, jnp.float32) for t in tables],
+            pltpu.VMEM((GROUPS, D, GW), jnp.bfloat16),
+            pltpu.VMEM((GROUPS, TILE, GW), jnp.float32),
+            pltpu.VMEM((1, D), jnp.float32),
+            pltpu.VMEM((GROUPS, *Q_SHAPE), jnp.bfloat16),
+            pltpu.SemaphoreType.DMA((2, 5)),
+            pltpu.SemaphoreType.DMA((GROUPS,)),
+        ],
+        out_shape=[jax.ShapeDtypeStruct(Q_SHAPE, jnp.bfloat16)] * GROUPS,
+        compiler_params=limit(60),
         cost_estimate=pl.CostEstimate(flops=2 * TILE * D * D, bytes_accessed=2 * D * D, transcendentals=0),
         name="project_q",
     )(sc, normed, norm_q, *tables, w_query)
 
 
-def query_of(refs, s):
-    return jnp.concatenate([refs[2 * s][0], refs[2 * s + 1][0]], axis=0)
+def query_of(refs, s, h):
+    return jnp.concatenate([refs[2 * s][h], refs[2 * s + 1][h]], axis=0)
 
 
 def raw_scores(query, keys):
@@ -375,107 +400,73 @@
     return peak, total, norm
 
 
-def stack_keys(slots, kind):
-    return jnp.concatenate([ref[kind, 0] for pair in slots for ref in pair], axis=0)
-
-
-def segment(slots, there):
-    return stack_keys(slots, 0), stack_keys(slots, 1), there
-
-
-def first_kernel(sc_ref, *refs):
-    q = refs[0:4]
-    same, other = [refs[4:6], refs[6:8]], [refs[8:10], refs[10:12]]
-    rows = [(refs[12 + 4 * r : 14 + 4 * r], refs[14 + 4 * r : 16 + 4 * r], sc_ref[5 + r] == 1) for r in range(2)]
-    stat_ref, acc_ref = refs[20:]
+def stack_keys(slots, kind, h):
+    return jnp.concatenate([ref[kind, h] for pair in slots for ref in pair], axis=0)
+
+
+def segment(slots, there, h):
+    return stack_keys(slots, 0, h), stack_keys(slots, 1, h), there
+
+
+def attend_kernel(plan, tile_places, state_slots, final, sc_ref, *refs):
+    q, refs = refs[:4], refs[4:]
+    tiles = {}
+    for name, places in tile_places:
+        tiles[name] = [ref if place is None else ref.at[place] for ref, place in zip(refs, places)]
+        refs = refs[2:]
+    state_in = {s: refs[2 * n : 2 * n + 2] for n, s in enumerate(state_slots)}
+    refs = refs[2 * len(state_slots) :]
     low = lax.broadcasted_iota(jnp.int32, (2 * TILE, HEAD_DIM), 1) < HEAD_DIM // 2
 
-    def store(s, state):
-        peak, total, norm = state
-        acc_ref[0, s] = total
-        stat_ref[0, s] = jnp.where(low, peak, norm)
-
-    halo = [segment([mine, theirs], there) for mine, theirs, there in rows]
-
-    @pl.when(sc_ref[4] == 0)
-    def _():
-        store(0, attend(query_of(q, 0), [segment([same[0], other[0], other[1]], None), *halo]))
-        store(1, attend(query_of(q, 1), [segment([same[1], other[1]], None)]))
-
-    @pl.when(sc_ref[4] == 1)
-    def _():
-        store(0, attend(query_of(q, 0), [segment([same[0], other[0]], None), *halo]))
-        far = [segment([theirs], there) for _, theirs, there in rows]
-        store(1, attend(query_of(q, 1), [segment([same[1], other[1], other[0]], None), *far]))
-
-
-def last_kernel(sc_ref, *refs):
-    q = refs[0:4]
-    rows = [(refs[4 + 4 * r : 6 + 4 * r], refs[6 + 4 * r : 8 + 4 * r], sc_ref[5 + r] == 1) for r in range(2)]
-    stat_in, acc_in = refs[12:14]
-    outs = refs[14:18]
-
-    def state(s):
-        stat = stat_in[0, s]
-        return stat[:, :1], acc_in[0, s], stat[:, HEAD_DIM // 2 : HEAD_DIM // 2 + 1]
-
-    def write(s, result):
-        attended = (result[1] / result[2]).astype(jnp.bfloat16)
-        outs[2 * s][0] = attended[:TILE]
-        outs[2 * s + 1][0] = attended[TILE:]
-
-    @pl.when(sc_ref[4] == 0)
-    def _():
-        write(0, attend(query_of(q, 0), [segment([theirs], there) for _, theirs, there in rows], state(0)))
-
-    @pl.when(sc_ref[4] == 1)
-    def _():
-        write(0, state(0))
-
-    write(1, attend(query_of(q, 1), [segment([mine, theirs], there) for mine, theirs, there in rows], state(1)))
-
-
-Q_SPEC = pl.BlockSpec((1, TILE, HEAD_DIM), lambda h, sc: (h, 0, 0))
-KV_SPEC = pl.BlockSpec((2, 1, TILE, HEAD_DIM), lambda h, sc: (0, h, 0, 0))
-STATE_SPEC = pl.BlockSpec((1, 2, 2 * TILE, HEAD_DIM), lambda h, sc: (h, 0, 0, 0))
-STATE_SHAPE = jax.ShapeDtypeStruct((GH, 2, 2 * TILE, HEAD_DIM), jnp.float32)
-
-
-def attend_cost(blocks):
-    pairs = GH * blocks * 4 * TILE * TILE
-    return pl.CostEstimate(flops=4 * pairs * HEAD_DIM, bytes_accessed=12 * TILE * GW * 2, transcendentals=pairs)
-
-
-def attend_first(sc, queries, tiles):
+    def state(s, h):
+        if s not in state_in:
+            return None
+        stat = state_in[s][0][h]
+        return stat[:, :1], state_in[s][1][h], stat[:, HEAD_DIM // 2 : HEAD_DIM // 2 + 1]
+
+    def one_head(slots, h):
+        for n, s in enumerate(sorted(slots)):
+            segments = [
+                segment([tiles[name] for name in names], None if row is None else sc_ref[5 + row] == 1, h)
+                for names, row in slots[s]
+            ]
+            peak, total, norm = attend(query_of(q, s, h), segments, state(s, h)) if segments else state(s, h)
+            if final:
+                attended = (total / norm).astype(jnp.bfloat16)
+                refs[2 * s][h] = attended[:TILE]
+                refs[2 * s + 1][h] = attended[TILE:]
+            else:
+                refs[2 * n][h] = jnp.where(low, peak, norm)
+                refs[2 * n + 1][h] = total
+
+    def run(slots):
+        for h in range(GH):
+            one_head(slots, h)
+    if plan[0] == plan[1]:
+        run(plan[0])
+    else:
+        for near in range(2):
+            pl.when(sc_ref[4] == near)(functools.partial(run, plan[near]))
+
+
+STATE_SHAPE = jax.ShapeDtypeStruct((GH, 2 * TILE, HEAD_DIM), jnp.float32)
+
+
+def attend_call(name, plan, sc, queries, tiles, state):
+    final = name == "attend_last"
+    state_slots = sorted(state)
+    places = tuple((key, tuple(place for _, place in pair)) for key, pair in tiles.items())
+    arrays = [array for pair in tiles.values() for array, _ in pair]
+    states = [array for s in state_slots for array in state[s]]
     return pl.pallas_call(
-        first_kernel,
-        grid_spec=pltpu.PrefetchScalarGridSpec(
-            num_scalar_prefetch=1,
-            grid=(GH,),
-            in_specs=[Q_SPEC] * 4 + [KV_SPEC] * 16,
-            out_specs=[STATE_SPEC] * 2,
-        ),
-        out_shape=[STATE_SHAPE] * 2,
+        functools.partial(attend_kernel, plan, places, tuple(state_slots), final),
+        in_specs=[SMEM] + [VMEM] * (GROUPS + len(arrays) + len(states)),
+        out_specs=[VMEM] * 4,
+        out_shape=[jax.ShapeDtypeStruct(Q_SHAPE, jnp.bfloat16) if final else STATE_SHAPE] * 4,
         compiler_params=limit(32),
-        cost_estimate=attend_cost(10),
-        name="attend_first",
-    )(sc, *queries, *tiles)
-
-
-def attend_last(sc, queries, tiles, state):
-    return pl.pallas_call(
-        last_kernel,
-        grid_spec=pltpu.PrefetchScalarGridSpec(
-            num_scalar_prefetch=1,
-            grid=(GH,),
-            in_specs=[Q_SPEC] * 4 + [KV_SPEC] * 8 + [STATE_SPEC] * 2,
-            out_specs=[Q_SPEC] * GROUPS,
-        ),
-        out_shape=[jax.ShapeDtypeStruct((GH, TILE, HEAD_DIM), jnp.bfloat16)] * GROUPS,
-        compiler_params=limit(32),
-        cost_estimate=attend_cost(5),
-        name="attend_last",
-    )(sc, *queries, *tiles, *state)
+        cost_estimate=pl.CostEstimate(flops=1000, bytes_accessed=1000, transcendentals=0),
+        name=name,
+    )(sc, *queries, *arrays, *states)
 
 
 def out_kernel(sc_ref, a0, a1, a2, a3, mod_ref, w_ref, out_ref):
@@ -510,13 +501,23 @@
     return lax.ppermute(value, "ta", [(i, i ^ 1) for i in range(4)])
 
 
+def row_swap(value, first, rows_n):
+    pairs = [(i, i + 1) for i in range(first, rows_n - 1, 2)]
+    return lax.ppermute(value, "ha", [edge for i, j in pairs for edge in ((i, j), (j, i))])
+
+
+def after(value, *others):
+    return lax.optimization_barrier((value, *others))[0]
+
+
 def square_body(tokens, modulation, w_query, w_key, w_value, w_out, norm_q, norm_k):
     ta, ha, wa = (lax.axis_index(name) for name in ("ta", "ha", "wa"))
     rows_n = lax.axis_size("ha")
     place_x, core = ta // 2, ta % 2
     near_slot = 1 - (place_x ^ core)
+    partner = [ha + 1 - 2 * (ha % 2), ha - 1 + 2 * (ha % 2)]
     sc = jnp.stack(
-        [2 * place_x + wa, ta, ha, wa, near_slot, (ha > 0).astype(jnp.int32), (ha < rows_n - 1).astype(jnp.int32)]
+        [2 * place_x + wa, ta, ha, wa, near_slot, *[((p >= 0) & (p < rows_n)).astype(jnp.int32) for p in partner]]
     ).astype(jnp.int32)
     half, sixth = HEAD_DIM // 2, HEAD_DIM // 6
     first = half - 2 * sixth
@@ -526,28 +527,54 @@
         rope_tables(lax.axis_size("wa"), CW, first + sixth, sixth),
     )
     *kv, normed = project_kv(sc, tokens.reshape(TILE, D), modulation, norm_k, tables, w_key, w_value)
-    up = [(i, i + 1) for i in range(rows_n - 1)]
-    down = [(i + 1, i) for i in range(rows_n - 1)]
+
     def rows_of(tile):
-        return lax.ppermute(tile, "ha", up), lax.ppermute(tile, "ha", down)
-
-    def after(value, *others):
-        return lax.optimization_barrier((value, *others))[0]
-
-    same = [kv[0], square_swap(kv[1], 1), square_swap(kv[2], 2)]
-    halo = [rows_of(tile) for tile in same]
-    same.append(square_swap(after(kv[3], same[1], same[2]), 3))
-    halo.append(rows_of(same[3]))
-    queries = project_q(sc, after(normed, same[1]), norm_q, tables, w_query)
-    queries = [square_swap(queries[m], m) for m in range(GROUPS)]
-    other = [core_swap(tile) for tile in same]
-    halo_other = [[core_swap(tile) for tile in pair] for pair in halo]
-
-    def halo_slot(slot):
-        return [part[m][r] for r in range(2) for part in (halo, halo_other) for m in (2 * slot, 2 * slot + 1)]
-
-    state = attend_first(sc, queries, [*same, *other, *halo_slot(0)])
-    attended = attend_last(sc, queries, halo_slot(1), state)
+        return [row_swap(tile, first, rows_n) for first in range(2)]
+
+    other0 = core_swap(kv[0])
+    halo0 = rows_of(kv[0])
+    side = [square_swap(kv[1], 1), square_swap(kv[2], 2)]
+    queries = list(project_q(sc, after(normed, other0), norm_q, tables, w_query))
+    middle = jnp.stack(after(side, queries[0], *halo0))
+    halo12, other12 = rows_of(middle), core_swap(middle)
+    mine3 = queries[3][None]
+    queries[1:3] = [square_swap(queries[m], m) for m in range(1, 3)]
+    corner = square_swap(jnp.concatenate([kv[3], after(mine3, queries[1], queries[2])]), 3)
+    queries[3], corner = corner[2], corner[:2]
+    halo3, other3 = rows_of(corner), core_swap(corner)
+    queries[0] = after(queries[0], *halo12)
+
+    def tiles_of(first, both, last):
+        return [(first, None), (both, 0), (both, 1), (last, None)]
+
+    same, other = tiles_of(kv[0], middle, corner), tiles_of(other0, other12, other3)
+    halo = [tiles_of(halo0[r], halo12[r], halo3[r]) for r in range(2)]
+    swapped = [[core_swap(tile) for tile in pair] for pair in (halo0, halo12)]
+
+    def call(name, plan, state):
+        tiles = {}
+        for s in range(2):
+            at = slice(2 * s, 2 * s + 2)
+            tiles[f"same{s}"], tiles[f"other{s}"] = same[at], other[at]
+            for r in range(2):
+                tiles[f"same{s}{r}"], tiles[f"other{s}{r}"] = halo[r][at], halo_other[r][at]
+        used = {n for p in plan for segs in p.values() for names, _ in segs for n in names}
+        return attend_call(name, plan, sc, queries, {n: t for n, t in tiles.items() if n in used}, state)
+
+    rows = [tuple(((f"same{s}{r}", f"other{s}{r}"), r) for r in range(2)) for s in range(2)]
+    far = [tuple(((f"other{s}{r}",), r) for r in range(2)) for s in range(2)]
+    own = [("same0", "other0"), ("same1", "other1")]
+    swapped_early = [*swapped, halo3]
+    halo_other = [tiles_of(*[pair[r] for pair in swapped_early]) for r in range(2)]
+    state = call(
+        "attend_own",
+        ({0: (((*own[0], "other1"), None),), 1: ((own[1], None),)}, {0: ((own[0], None),), 1: (((*own[1], "other0"), None),)}),
+        {},
+    )
+    state = call("attend_halo", ({0: rows[0], 1: ()}, {0: rows[0], 1: far[0]}), {0: state[:2], 1: state[2:]})
+    swapped.append([core_swap(after(tile, state[0])) for tile in halo3])
+    halo_other = [tiles_of(*[pair[r] for pair in swapped]) for r in range(2)]
+    attended = call("attend_last", ({0: far[1], 1: rows[1]}, {0: (), 1: rows[1]}), {0: state[:2], 1: state[2:]})
     attended = [square_swap(attended[m], m) for m in range(GROUPS)]
     branch = project_out(sc, attended, modulation, w_out)
     return branch.reshape(CT, CH, CW, D)

time: 94.9 us -> 79.9 us (0.84)
  starting transfers between devices: 36.9 us -> 26.9 us
  waiting for transfers between devices: 22.6 us -> 18.1 us
  local copies, waits for them, and re-layouts: 4.11 us -> 1.65 us
  Pallas kernels: 30.6 us -> 31.7 us
  other arithmetic: 0.01 us -> 1.01 us
    ppermute x8 -> x6, starting transfers between devices: 20.8 us -> 12.6 us  [row_swap(): lax.ppermute(value, 'ha', [edge for i, j in pairs for edge in ((i, j), (j...]
    ppermute x9 -> x8, waiting for transfers between devices: 13 us -> 7.7 us  [square_swap(): return lax.ppermute(value, ('ta', 'wa'), [(i, i ^ flip) for i in range(8)])]
    ppermute x12 -> x9, waiting for transfers between devices: 0.03 us -> 2.55 us  [core_swap(): return lax.ppermute(value, 'ta', [(i, i ^ 1) for i in range(4)])]
    unnamed x24 -> x16, local copies, waits for them, and re-layouts: 3.44 us -> 0.94 us
    ppermute x9 -> x8, starting transfers between devices: 14.2 us -> 11.7 us  [square_swap(): return lax.ppermute(value, ('ta', 'wa'), [(i, i ^ flip) for i in range(8)])]
    ppermute x8 -> x6, waiting for transfers between devices: 9.57 us -> 7.87 us  [row_swap(): lax.ppermute(value, 'ha', [edge for i, j in pairs for edge in ((i, j), (j...]
    pallas_call x4 -> x5, Pallas kernels: 27.8 us -> 29 us  [the longest x3 15.6 us: attend_call(): pl.pallas_call(functools.partial(attend_kernel, plan, places, tuple(state...]
    concatenate x0 -> x1, other arithmetic: none -> 0.95 us  [square_body(): jnp.concatenate([kv[3], after(mine3, queries[1], queries[2])])]
  transfers between devices with their start and end apart: 29 -> 23, of which waited for: 9 -> 8; matrix products, arithmetic and copies ran while one was open for 0% -> 1% of each run, Pallas kernels for 14% -> 22%
where the time goes in v3:
time: 79.9 us; the launch traced here: 79.7 us
  Pallas kernels  31.7 us (40%)
  starting transfers between devices  26.9 us (34%)
  waiting for transfers between devices  18.1 us (23%)
  local copies, waits for them, and re-layouts  1.65 us (2%)
  other arithmetic  1.01 us (1%)
    pallas_call x3, Pallas kernels, attend_call(): pl.pallas_call(functools.partial(attend_kernel, plan, places, tuple(state...  15.6 us
    ppermute x6, starting transfers between devices, row_swap(): lax.ppermute(value, 'ha', [edge for i, j in pairs for edge in ((i, j), (j...  12.6 us
    ppermute x8, starting transfers between devices, square_swap(): return lax.ppermute(value, ('ta', 'wa'), [(i, i ^ flip) for i in range(8)])  11.7 us
    ppermute x6, waiting for transfers between devices, row_swap(): lax.ppermute(value, 'ha', [edge for i, j in pairs for edge in ((i, j), (j...  7.87 us
    ppermute x8, waiting for transfers between devices, square_swap(): return lax.ppermute(value, ('ta', 'wa'), [(i, i ^ flip) for i in range(8)])  7.7 us
    pallas_call x1, Pallas kernels, project_kv(): pl.pallas_call(kv_kernel, in_specs=[SMEM] + [HBM] * 8, out_specs=[HBM] *...  7.63 us
    pallas_call x1, Pallas kernels, project_q(): pl.pallas_call(q_kernel, in_specs=[SMEM] + [HBM] * 6, out_specs=[HBM] * G...  5.77 us
    pallas_call x1, Pallas kernels, project_out(): pl.pallas_call(out_kernel, in_specs=[SMEM] + [VMEM] * 6, out_specs=VMEM,...  2.74 us
  transfers between devices with their start and end apart: 23, of which 8 were waited for; matrix products, arithmetic and copies ran while one was open for 1% of the time, Pallas kernels for 22%

profile of v3, /device:TPU:0, one launch (start us, length us, event | category | flops | bytes accessed | tf_op | source)
XLA Modules:
  0.0 79.7 jit_solution(589415696228386319)
XLA Ops:
  0.0 0.7 stack.48.sc_ref
  0.7 7.6 %project_kv.1 = (bf16[2,3,192,128]{3,2,1,0:T(8,128)(2,1)}, bf16[2,3,192,128]{3,2,1,0:T(8,128)(2,1)}, bf16[2,3,192,128]{3,2,1,0:T(8,128)(2,1)}, bf16[2,3,192,128]{3,2,1,0:T(8,128)(2,1)}, bf16[192,1536]{1,0:T(8,128)(2,1)}) custom-call(s32[7]{0:T(128)} %stack.48.sc_ref, bf16[192,1536]{1,0:T(8,128)(2,1)} %bitcast.16, f32[3,1536]{1,0:T(4,128)} %mod_ref.1, ...), custom_call_target="tpu_custom_call" | custom-call | flops 1811939328 | bytes 9437184 | tf_op jit(solution)/shard_map/project_kv/pallas_call | solution.py:324
  8.3 0.5 collective-permute-start
  8.9 2.6 %collective-permute-start.1 = (bf16[2,3,192,128]{3,2,1,0:T(8,128)(2,1)}, bf16[2,3,192,128]{3,2,1,0:T(8,128)(2,1)S(1)}, u32[]{:S(2)}, u32[]{:S(2)}) collective-permute-start(bf16[2,3,192,128]{3,2,1,0:T(8,128)(2,1)} %get-tuple-element.37), channel_id=1, source_target_pairs={{0,1},{1,0},{8,9},{9,8},{16,17},{17,16},{24,25},{25,24},{2,3},{3,2... | collective-permute-start | bytes 884744 | tf_op jit(solution)/shard_map/ppermute | solution.py:497
  11.5 1.5 %collective-permute-start.2 = (bf16[2,3,192,128]{3,2,1,0:T(8,128)(2,1)}, bf16[2,3,192,128]{3,2,1,0:T(8,128)(2,1)S(1)}, u32[]{:S(2)}, u32[]{:S(2)}) collective-permute-start(bf16[2,3,192,128]{3,2,1,0:T(8,128)(2,1)} %get-tuple-element.38), channel_id=1, source_target_pairs={{0,16},{1,17},{8,24},{9,25},{16,0},{17,1},{24,8},{25,9},{2,18},{3,... | collective-permute-start | bytes 884744 | tf_op jit(solution)/shard_map/ppermute | solution.py:497
  13.0 1.6 %collective-permute-start.3 = (bf16[2,3,192,128]{3,2,1,0:T(8,128)(2,1)}, bf16[2,3,192,128]{3,2,1,0:T(8,128)(2,1)S(1)}, u32[]{:S(2)}, u32[]{:S(2)}) collective-permute-start(bf16[2,3,192,128]{3,2,1,0:T(8,128)(2,1)} %get-tuple-element.34.refs_4_), channel_id=1, source_target_pairs={{0,2},{2,0},{4,6},{6,4},{1,3},{3,1},{5,7},{7,5},{8,10},{10,8},{12,... | collective-permute-start | bytes 884744 | tf_op jit(solution)/shard_map/ppermute | solution.py:506
  14.5 0.7 collective-permute-start.4
  15.2 5.8 %project_q.1 = (bf16[3,192,128]{2,1,0:T(8,128)(2,1)}, bf16[3,192,128]{2,1,0:T(8,128)(2,1)}, bf16[3,192,128]{2,1,0:T(8,128)(2,1)}, bf16[3,192,128]{2,1,0:T(8,128)(2,1)}) custom-call(s32[7]{0:T(128)} %stack.48.sc_ref, bf16[192,1536]{1,0:T(8,128)(2,1)} %get-tuple-element.35.normed_hbm, f32[1536]{0:T(1024)} %nq_hbm.1, f32[4,2,3,128]{3,2,1,0:T(4,128)} %constant.52.clone.ft_hbm, ...), custom_call_target="tpu_custom_call" | custom-call | flops 905969664 | bytes 4718592 | tf_op jit(solution)/shard_map/project_q/pallas_call | solution.py:351
  21.0 0.6 collective-permute-start.7
  21.6 0.0 collective-permute-done.1
  21.6 0.5 collective-permute-start.8
  22.1 0.1 pad_maximum_fusion.refs_5_.refs_8_
  22.2 4.5 %collective-permute-start.5 = (bf16[2,2,3,192,128]{4,3,2,1,0:T(8,128)(2,1)S(1)}, bf16[2,2,3,192,128]{4,3,2,1,0:T(8,128)(2,1)S(1)}, u32[]{:S(2)}, u32[]{:S(2)}) collective-permute-start(bf16[2,2,3,192,128]{4,3,2,1,0:T(8,128)(2,1)S(1)} %pad_maximum_fusion.refs_5_.refs_8_), channel_id=1, source_target_pairs={{0,2},{2,0},{4,6},{6,4},{1,3},{3,1},{5,7},{7,5},{8,10},{10,8},{12,... | collective-permute-start | bytes 1769480 | tf_op jit(solution)/shard_map/ppermute | solution.py:506
  26.7 0.7 collective-permute-start.6
  27.4 0.0 collective-permute-done.7.refs_1_
  27.4 1.0 %pad_maximum_fusion.1 = bf16[3,3,192,128]{3,2,1,0:T(8,128)(2,1)S(1)} fusion(bf16[1,3,192,128]{3,2,1,0:T(8,128)(2,1)} %bitcast.19, bf16[2,3,192,128]{3,2,1,0:T(8,128)(2,1)S(1)} %copy-done.5), kind=kLoop, calls=%fused_computation.1 | loop fusion | flops 221184 | bytes 884736 | tf_op jit(solution)/shard_map/concatenate | solution.py:542
  28.4 2.5 %collective-permute-start.9 = (bf16[3,3,192,128]{3,2,1,0:T(8,128)(2,1)S(1)}, bf16[3,3,192,128]{3,2,1,0:T(8,128)(2,1)S(1)}, u32[]{:S(2)}, u32[]{:S(2)}) collective-permute-start(bf16[3,3,192,128]{3,2,1,0:T(8,128)(2,1)S(1)} %pad_maximum_fusion.1), channel_id=1, source_target_pairs={{0,17},{1,16},{8,25},{9,24},{16,1},{17,0},{24,9},{25,8},{2,19},{3,... | collective-permute-start | bytes 1327112 | tf_op jit(solution)/shard_map/ppermute | solution.py:497
  30.8 0.0 collective-permute-start.15
  30.8 0.5 collective-permute-start.12
  31.3 7.9 %collective-permute-done.5.refs_5_.refs_4_ = bf16[2,2,3,192,128]{4,3,2,1,0:T(8,128)(2,1)S(1)} collective-permute-done((bf16[2,2,3,192,128]{4,3,2,1,0:T(8,128)(2,1)S(1)}, bf16[2,2,3,192,128]{4,3,2,1,0:T(8,128)(2,1)S(1)}, u32[]{:S(2)}, u32[]{:S(2)}) %collective-permute-start.5) | collective-permute-done | bytes 589856 | tf_op jit(solution)/shard_map/ppermute | solution.py:506
  39.2 0.5 collective-permute-start.14
  39.7 0.4 collective-permute-done.9
  40.2 0.1 collective-permute-start.16
  40.3 0.5 collective-permute-start.13
  40.7 0.0 collective-permute-done.15.refs_7_.refs_10_
  40.7 0.7 collective-permute-start.18
  41.4 1.0 %collective-permute-done.16.refs_11_ = bf16[2,3,192,128]{3,2,1,0:T(8,128)(2,1)S(1)} collective-permute-done((bf16[2,3,192,128]{3,2,1,0:T(8,128)(2,1)S(1)}, bf16[2,3,192,128]{3,2,1,0:T(8,128)(2,1)S(1)}, u32[]{:S(2)}, u32[]{:S(2)}) %collective-permute-start.16) | collective-permute-done | bytes 294944 | tf_op jit(solution)/shard_map/ppermute | solution.py:501
  42.5 4.5 %collective-permute-start.10 = (bf16[2,3,192,128]{3,2,1,0:T(8,128)(2,1)S(1)}, bf16[2,3,192,128]{3,2,1,0:T(8,128)(2,1)S(1)}, u32[]{:S(2)}, u32[]{:S(2)}) collective-permute-start(bf16[2,3,192,128]{3,2,1,0:T(8,128)(2,1)S(1)} %slice.9.refs_9_), channel_id=1, source_target_pairs={{0,2},{2,0},{4,6},{6,4},{1,3},{3,1},{5,7},{7,5},{8,10},{10,8},{12,... | collective-permute-start | bytes 884744 | tf_op jit(solution)/shard_map/ppermute | solution.py:506
  47.0 0.9 %copy-done = bf16[3,192,128]{2,1,0:T(8,128)(2,1)S(1)} copy-done((bf16[3,192,128]{2,1,0:T(8,128)(2,1)S(1)}, bf16[3,192,128]{2,1,0:T(8,128)(2,1)}, u32[]{:S(2)}) %copy-start) | copy-done | bytes 147480
  47.9 4.5 %attend_own.1 = (f32[3,384,128]{2,1,0:T(8,128)S(1)}, f32[3,384,128]{2,1,0:T(8,128)S(1)}, f32[3,384,128]{2,1,0:T(8,128)S(1)}, f32[3,384,128]{2,1,0:T(8,128)S(1)}) custom-call(s32[7]{0:T(128)S(1)} %copy-done.4, bf16[3,192,128]{2,1,0:T(8,128)(2,1)S(1)} %copy-done, bf16[3,192,128]{2,1,0:T(8,128)(2,1)S(1)} %collective-permute-done.7.refs_1_, ...), custom_call_target="tpu_custom_call" | custom-call | flops 1000 | bytes 1000 | tf_op jit(solution)/shard_map/attend_own/pallas_call | solution.py:461
  52.4 0.0 collective-permute-done.13.refs_10_
  52.4 0.0 collective-permute-done.14.refs_11_.refs_10_
  52.4 0.0 slice-start.1
  52.4 7.0 %attend_halo.1 = (f32[3,384,128]{2,1,0:T(8,128)S(1)}, f32[3,384,128]{2,1,0:T(8,128)S(1)}, f32[3,384,128]{2,1,0:T(8,128)S(1)}, f32[3,384,128]{2,1,0:T(8,128)S(1)}) custom-call(s32[7]{0:T(128)S(1)} %copy-done.4, bf16[3,192,128]{2,1,0:T(8,128)(2,1)S(1)} %copy-done.1, bf16[3,192,128]{2,1,0:T(8,128)(2,1)S(1)} %collective-permute-done.7.refs_1_, ...), custom_call_target="tpu_custom_call" | custom-call | flops 1000 | bytes 1000 | tf_op jit(solution)/shard_map/attend_halo/pallas_call | solution.py:461
  59.4 0.0 copy-start.3
  59.5 0.1 collective-permute-start.19
  59.5 0.0 collective-permute-done.10.refs_5_
  59.5 0.5 collective-permute-start.17
  60.0 1.1 %collective-permute-done.19.refs_11_ = bf16[2,3,192,128]{3,2,1,0:T(8,128)(2,1)S(1)} collective-permute-done((bf16[2,3,192,128]{3,2,1,0:T(8,128)(2,1)S(1)}, bf16[2,3,192,128]{3,2,1,0:T(8,128)(2,1)S(1)}, u32[]{:S(2)}, u32[]{:S(2)}) %collective-permute-start.19) | collective-permute-done | bytes 294944 | tf_op jit(solution)/shard_map/ppermute | solution.py:501
  61.1 0.4 collective-permute-done.17.refs_7_
  61.5 4.1 %attend_last.1 = (bf16[3,192,128]{2,1,0:T(8,128)(2,1)S(1)}, bf16[3,192,128]{2,1,0:T(8,128)(2,1)S(1)}, bf16[3,192,128]{2,1,0:T(8,128)(2,1)S(1)}, bf16[3,192,128]{2,1,0:T(8,128)(2,1)S(1)}) custom-call(s32[7]{0:T(128)S(1)} %copy-done.4, bf16[3,192,128]{2,1,0:T(8,128)(2,1)S(1)} %copy-done.1, bf16[3,192,128]{2,1,0:T(8,128)(2,1)S(1)} %collective-permute-done.7.refs_1_, ...), custom_call_target="tpu_custom_call" | custom-call | flops 1000 | bytes 1000 | tf_op jit(solution)/shard_map/attend_last/pallas_call | solution.py:461
  65.7 1.0 %collective-permute-start.20 = (bf16[3,192,128]{2,1,0:T(8,128)(2,1)S(1)}, bf16[3,192,128]{2,1,0:T(8,128)(2,1)S(1)}, u32[]{:S(2)}, u32[]{:S(2)}) collective-permute-start(bf16[3,192,128]{2,1,0:T(8,128)(2,1)S(1)} %get-tuple-element.58), channel_id=1, source_target_pairs={{0,1},{1,0},{8,9},{9,8},{16,17},{17,16},{24,25},{25,24},{2,3},{3,2... | collective-permute-start | bytes 442376 | tf_op jit(solution)/shard_map/ppermute | solution.py:497
  66.7 2.6 %collective-permute-start.21 = (bf16[3,192,128]{2,1,0:T(8,128)(2,1)S(1)}, bf16[3,192,128]{2,1,0:T(8,128)(2,1)S(1)}, u32[]{:S(2)}, u32[]{:S(2)}) collective-permute-start(bf16[3,192,128]{2,1,0:T(8,128)(2,1)S(1)} %get-tuple-element.59), channel_id=1, source_target_pairs={{0,16},{1,17},{8,24},{9,25},{16,0},{17,1},{24,8},{25,9},{2,18},{3,... | collective-permute-start | bytes 442376 | tf_op jit(solution)/shard_map/ppermute | solution.py:497
  69.3 0.4 collective-permute-start.22
  69.7 1.1 %collective-permute-done.20.a1 = bf16[3,192,128]{2,1,0:T(8,128)(2,1)S(1)} collective-permute-done((bf16[3,192,128]{2,1,0:T(8,128)(2,1)S(1)}, bf16[3,192,128]{2,1,0:T(8,128)(2,1)S(1)}, u32[]{:S(2)}, u32[]{:S(2)}) %collective-permute-start.20) | collective-permute-done | bytes 147488 | tf_op jit(solution)/shard_map/ppermute | solution.py:497
  70.9 2.7 %collective-permute-done.21.a2 = bf16[3,192,128]{2,1,0:T(8,128)(2,1)S(1)} collective-permute-done((bf16[3,192,128]{2,1,0:T(8,128)(2,1)S(1)}, bf16[3,192,128]{2,1,0:T(8,128)(2,1)S(1)}, u32[]{:S(2)}, u32[]{:S(2)}) %collective-permute-start.21) | collective-permute-done | bytes 147488 | tf_op jit(solution)/shard_map/ppermute | solution.py:497
  73.5 3.5 %collective-permute-done.22.a3 = bf16[3,192,128]{2,1,0:T(8,128)(2,1)S(1)} collective-permute-done((bf16[3,192,128]{2,1,0:T(8,128)(2,1)S(1)}, bf16[3,192,128]{2,1,0:T(8,128)(2,1)S(1)}, u32[]{:S(2)}, u32[]{:S(2)}) %collective-permute-start.22) | collective-permute-done | bytes 147488 | tf_op jit(solution)/shard_map/ppermute | solution.py:497
  77.0 2.7 %project_out.1 = bf16[192,1536]{1,0:T(8,128)(2,1)} custom-call(s32[7]{0:T(128)S(1)} %copy-done.4, bf16[3,192,128]{2,1,0:T(8,128)(2,1)S(1)} %get-tuple-element.57.a0, bf16[3,192,128]{2,1,0:T(8,128)(2,1)S(1)} %collective-permute-done.20.a1, bf16[3,192,128]{2,1,0:T(8,128)(2,1)S(1)} %collective-permute-done.21.a2, ...), custom_call_target="tpu_custom_call" | custom-call | flops 905969664 | bytes 4718592 | tf_op jit(solution)/shard_map/project_out/pallas_call | solution.py:482
  (26 shorter events, 0.1 us)
Async XLA Ops:
  8.3 19.1 %copy-start.5 = (bf16[2,3,192,128]{3,2,1,0:T(8,128)(2,1)S(1)}, bf16[2,3,192,128]{3,2,1,0:T(8,128)(2,1)}, u32[]{:S(2)}) copy-start(bf16[2,3,192,128]{3,2,1,0:T(8,128)(2,1)} %get-tuple-element.44) | copy-start | bytes 884740
  8.3 38.6 %copy-start.2 = (bf16[2,3,192,128]{3,2,1,0:T(8,128)(2,1)S(1)}, bf16[2,3,192,128]{3,2,1,0:T(8,128)(2,1)}, u32[]{:S(2)}) copy-start(bf16[2,3,192,128]{3,2,1,0:T(8,128)(2,1)} %get-tuple-element.34.refs_4_) | copy-start | bytes 884740
  8.3 38.6 %copy-start.4 = (s32[7]{0:T(128)S(1)}, s32[7]{0:T(128)}, u32[]{:S(2)}) copy-start(s32[7]{0:T(128)} %stack.48.sc_ref) | copy-start | bytes 88
  8.3 6.9 %collective-permute-start = (bf16[2,3,192,128]{3,2,1,0:T(8,128)(2,1)}, bf16[2,3,192,128]{3,2,1,0:T(8,128)(2,1)S(1)}, u32[]{:S(2)}, u32[]{:S(2)}) collective-permute-start(bf16[2,3,192,128]{3,2,1,0:T(8,128)(2,1)} %get-tuple-element.34.refs_4_), channel_id=1, source_target_pairs={{0,8},{8,0},{16,24},{24,16},{1,9},{9,1},{17,25},{25,17},{2,10},{10... | collective-permute-start | bytes 884744 | tf_op jit(solution)/shard_map/ppermute | solution.py:501
  8.9 12.7 %collective-permute-start.1 = (bf16[2,3,192,128]{3,2,1,0:T(8,128)(2,1)}, bf16[2,3,192,128]{3,2,1,0:T(8,128)(2,1)S(1)}, u32[]{:S(2)}, u32[]{:S(2)}) collective-permute-start(bf16[2,3,192,128]{3,2,1,0:T(8,128)(2,1)} %get-tuple-element.37), channel_id=1, source_target_pairs={{0,1},{1,0},{8,9},{9,8},{16,17},{17,16},{24,25},{25,24},{2,3},{3,2... | collective-permute-start | bytes 884744 | tf_op jit(solution)/shard_map/ppermute | solution.py:497
  11.5 10.7 %collective-permute-start.2 = (bf16[2,3,192,128]{3,2,1,0:T(8,128)(2,1)}, bf16[2,3,192,128]{3,2,1,0:T(8,128)(2,1)S(1)}, u32[]{:S(2)}, u32[]{:S(2)}) collective-permute-start(bf16[2,3,192,128]{3,2,1,0:T(8,128)(2,1)} %get-tuple-element.38), channel_id=1, source_target_pairs={{0,16},{1,17},{8,24},{9,25},{16,0},{17,1},{24,8},{25,9},{2,18},{3,... | collective-permute-start | bytes 884744 | tf_op jit(solution)/shard_map/ppermute | solution.py:497
  13.0 9.2 %collective-permute-start.3 = (bf16[2,3,192,128]{3,2,1,0:T(8,128)(2,1)}, bf16[2,3,192,128]{3,2,1,0:T(8,128)(2,1)S(1)}, u32[]{:S(2)}, u32[]{:S(2)}) collective-permute-start(bf16[2,3,192,128]{3,2,1,0:T(8,128)(2,1)} %get-tuple-element.34.refs_4_), channel_id=1, source_target_pairs={{0,2},{2,0},{4,6},{6,4},{1,3},{3,1},{5,7},{7,5},{8,10},{10,8},{12,... | collective-permute-start | bytes 884744 | tf_op jit(solution)/shard_map/ppermute | solution.py:506
  14.5 7.6 %collective-permute-start.4 = (bf16[2,3,192,128]{3,2,1,0:T(8,128)(2,1)}, bf16[2,3,192,128]{3,2,1,0:T(8,128)(2,1)S(1)}, u32[]{:S(2)}, u32[]{:S(2)}) collective-permute-start(bf16[2,3,192,128]{3,2,1,0:T(8,128)(2,1)} %get-tuple-element.34.refs_4_), channel_id=1, source_target_pairs={{2,4},{4,2},{3,5},{5,3},{10,12},{12,10},{11,13},{13,11},{18,20},{2... | collective-permute-start | bytes 884744 | tf_op jit(solution)/shard_map/ppermute | solution.py:506
  21.0 31.4 %copy-start.1 = (bf16[3,192,128]{2,1,0:T(8,128)(2,1)S(1)}, bf16[3,192,128]{2,1,0:T(8,128)(2,1)}, u32[]{:S(2)}) copy-start(bf16[3,192,128]{2,1,0:T(8,128)(2,1)} %get-tuple-element.41.refs_0_) | copy-start | bytes 442372
  21.0 6.4 %collective-permute-start.7 = (bf16[3,192,128]{2,1,0:T(8,128)(2,1)}, bf16[3,192,128]{2,1,0:T(8,128)(2,1)S(1)}, u32[]{:S(2)}, u32[]{:S(2)}) collective-permute-start(bf16[3,192,128]{2,1,0:T(8,128)(2,1)} %get-tuple-element.42), channel_id=1, source_target_pairs={{0,1},{1,0},{8,9},{9,8},{16,17},{17,16},{24,25},{25,24},{2,3},{3,2... | collective-permute-start | bytes 442376 | tf_op jit(solution)/shard_map/ppermute | solution.py:497
  21.6 5.8 %collective-permute-start.8 = (bf16[3,192,128]{2,1,0:T(8,128)(2,1)}, bf16[3,192,128]{2,1,0:T(8,128)(2,1)S(1)}, u32[]{:S(2)}, u32[]{:S(2)}) collective-permute-start(bf16[3,192,128]{2,1,0:T(8,128)(2,1)} %get-tuple-element.43), channel_id=1, source_target_pairs={{0,16},{1,17},{8,24},{9,25},{16,0},{17,1},{24,8},{25,9},{2,18},{3,... | collective-permute-start | bytes 442376 | tf_op jit(solution)/shard_map/ppermute | solution.py:497
  22.2 17.0 %collective-permute-start.5 = (bf16[2,2,3,192,128]{4,3,2,1,0:T(8,128)(2,1)S(1)}, bf16[2,2,3,192,128]{4,3,2,1,0:T(8,128)(2,1)S(1)}, u32[]{:S(2)}, u32[]{:S(2)}) collective-permute-start(bf16[2,2,3,192,128]{4,3,2,1,0:T(8,128)(2,1)S(1)} %pad_maximum_fusion.refs_5_.refs_8_), channel_id=1, source_target_pairs={{0,2},{2,0},{4,6},{6,4},{1,3},{3,1},{5,7},{7,5},{8,10},{10,8},{12,... | collective-permute-start | bytes 1769480 | tf_op jit(solution)/shard_map/ppermute | solution.py:506
  26.7 12.5 %collective-permute-start.6 = (bf16[2,2,3,192,128]{4,3,2,1,0:T(8,128)(2,1)S(1)}, bf16[2,2,3,192,128]{4,3,2,1,0:T(8,128)(2,1)S(1)}, u32[]{:S(2)}, u32[]{:S(2)}) collective-permute-start(bf16[2,2,3,192,128]{4,3,2,1,0:T(8,128)(2,1)S(1)} %pad_maximum_fusion.refs_5_.refs_8_), channel_id=1, source_target_pairs={{2,4},{4,2},{3,5},{5,3},{10,12},{12,10},{11,13},{13,11},{18,20},{2... | collective-permute-start | bytes 1769480 | tf_op jit(solution)/shard_map/ppermute | solution.py:506
  28.4 11.8 %collective-permute-start.9 = (bf16[3,3,192,128]{3,2,1,0:T(8,128)(2,1)S(1)}, bf16[3,3,192,128]{3,2,1,0:T(8,128)(2,1)S(1)}, u32[]{:S(2)}, u32[]{:S(2)}) collective-permute-start(bf16[3,3,192,128]{3,2,1,0:T(8,128)(2,1)S(1)} %pad_maximum_fusion.1), channel_id=1, source_target_pairs={{0,17},{1,16},{8,25},{9,24},{16,1},{17,0},{24,9},{25,8},{2,19},{3,... | collective-permute-start | bytes 1327112 | tf_op jit(solution)/shard_map/ppermute | solution.py:497
  30.8 9.9 %collective-permute-start.15 = (bf16[2,2,3,192,128]{4,3,2,1,0:T(8,128)(2,1)S(1)}, bf16[2,2,3,192,128]{4,3,2,1,0:T(8,128)(2,1)S(1)}, u32[]{:S(2)}, u32[]{:S(2)}) collective-permute-start(bf16[2,2,3,192,128]{4,3,2,1,0:T(8,128)(2,1)S(1)} %pad_maximum_fusion.refs_5_.refs_8_), channel_id=1, source_target_pairs={{0,8},{8,0},{16,24},{24,16},{1,9},{9,1},{17,25},{25,17},{2,10},{10... | collective-permute-start | bytes 1769480 | tf_op jit(solution)/shard_map/ppermute | solution.py:501
  30.8 9.4 %collective-permute-start.12 = (bf16[2,3,192,128]{3,2,1,0:T(8,128)(2,1)S(1)}, bf16[2,3,192,128]{3,2,1,0:T(8,128)(2,1)S(1)}, u32[]{:S(2)}, u32[]{:S(2)}) collective-permute-start(bf16[2,3,192,128]{3,2,1,0:T(8,128)(2,1)S(1)} %collective-permute-done.3.refs_4_), channel_id=1, source_target_pairs={{0,8},{8,0},{16,24},{24,16},{1,9},{9,1},{17,25},{25,17},{2,10},{10... | collective-permute-start | bytes 884744 | tf_op jit(solution)/shard_map/ppermute | solution.py:501
  39.2 13.2 %collective-permute-start.11 = (bf16[2,2,3,192,128]{4,3,2,1,0:T(8,128)(2,1)S(1)}, bf16[2,2,3,192,128]{4,3,2,1,0:T(8,128)(2,1)S(1)}, u32[]{:S(2)}, u32[]{:S(2)}) collective-permute-start(bf16[2,2,3,192,128]{4,3,2,1,0:T(8,128)(2,1)S(1)} %collective-permute-done.5.refs_5_.refs_4_), channel_id=1, source_target_pairs={{0,8},{8,0},{16,24},{24,16},{1,9},{9,1},{17,25},{25,17},{2,10},{10... | collective-permute-start | bytes 1769480 | tf_op jit(solution)/shard_map/ppermute | solution.py:501
  39.2 13.2 %collective-permute-start.14 = (bf16[2,2,3,192,128]{4,3,2,1,0:T(8,128)(2,1)S(1)}, bf16[2,2,3,192,128]{4,3,2,1,0:T(8,128)(2,1)S(1)}, u32[]{:S(2)}, u32[]{:S(2)}) collective-permute-start(bf16[2,2,3,192,128]{4,3,2,1,0:T(8,128)(2,1)S(1)} %collective-permute-done.6.refs_9_.refs_8_), channel_id=1, source_target_pairs={{0,8},{8,0},{16,24},{24,16},{1,9},{9,1},{17,25},{25,17},{2,10},{10... | collective-permute-start | bytes 1769480 | tf_op jit(solution)/shard_map/ppermute | solution.py:501
  40.2 2.3 %collective-permute-start.16 = (bf16[2,3,192,128]{3,2,1,0:T(8,128)(2,1)S(1)}, bf16[2,3,192,128]{3,2,1,0:T(8,128)(2,1)S(1)}, u32[]{:S(2)}, u32[]{:S(2)}) collective-permute-start(bf16[2,3,192,128]{3,2,1,0:T(8,128)(2,1)S(1)} %slice.9.refs_9_), channel_id=1, source_target_pairs={{0,8},{8,0},{16,24},{24,16},{1,9},{9,1},{17,25},{25,17},{2,10},{10... | collective-permute-start | bytes 884744 | tf_op jit(solution)/shard_map/ppermute | solution.py:501
  40.3 12.1 %collective-permute-start.13 = (bf16[2,3,192,128]{3,2,1,0:T(8,128)(2,1)S(1)}, bf16[2,3,192,128]{3,2,1,0:T(8,128)(2,1)S(1)}, u32[]{:S(2)}, u32[]{:S(2)}) collective-permute-start(bf16[2,3,192,128]{3,2,1,0:T(8,128)(2,1)S(1)} %collective-permute-done.4.refs_8_), channel_id=1, source_target_pairs={{0,8},{8,0},{16,24},{24,16},{1,9},{9,1},{17,25},{25,17},{2,10},{10... | collective-permute-start | bytes 884744 | tf_op jit(solution)/shard_map/ppermute | solution.py:501
  40.7 18.7 %collective-permute-start.18 = (bf16[2,3,192,128]{3,2,1,0:T(8,128)(2,1)S(1)}, bf16[2,3,192,128]{3,2,1,0:T(8,128)(2,1)S(1)}, u32[]{:S(2)}, u32[]{:S(2)}) collective-permute-start(bf16[2,3,192,128]{3,2,1,0:T(8,128)(2,1)S(1)} %slice.9.refs_9_), channel_id=1, source_target_pairs={{2,4},{4,2},{3,5},{5,3},{10,12},{12,10},{11,13},{13,11},{18,20},{2... | collective-permute-start | bytes 884744 | tf_op jit(solution)/shard_map/ppermute | solution.py:506
  42.5 17.1 %collective-permute-start.10 = (bf16[2,3,192,128]{3,2,1,0:T(8,128)(2,1)S(1)}, bf16[2,3,192,128]{3,2,1,0:T(8,128)(2,1)S(1)}, u32[]{:S(2)}, u32[]{:S(2)}) collective-permute-start(bf16[2,3,192,128]{3,2,1,0:T(8,128)(2,1)S(1)} %slice.9.refs_9_), channel_id=1, source_target_pairs={{0,2},{2,0},{4,6},{6,4},{1,3},{3,1},{5,7},{7,5},{8,10},{10,8},{12,... | collective-permute-start | bytes 884744 | tf_op jit(solution)/shard_map/ppermute | solution.py:506
  47.0 0.9 %copy-start = (bf16[3,192,128]{2,1,0:T(8,128)(2,1)S(1)}, bf16[3,192,128]{2,1,0:T(8,128)(2,1)}, u32[]{:S(2)}) copy-start(bf16[3,192,128]{2,1,0:T(8,128)(2,1)} %get-tuple-element.41.refs_0_) | copy-start | bytes 442372
  47.9 29.1 %slice-start = ((s8[4718592]{0:T(1024)(128)(4,1)}), s8[4194304]{0:T(1024)(128)(4,1)S(1)}, s32[]{:S(2)}) async-start(s8[4718592]{0:T(1024)(128)(4,1)} %bitcast.14), calls=%async_computation | async-start | bytes 8388608
  52.4 24.6 %slice-start.1 = ((s8[4718592]{0:T(1024)(128)(4,1)}), s8[524288]{0:T(1024)(128)(4,1)S(1)}, s32[]{:S(2)}) async-start(s8[4718592]{0:T(1024)(128)(4,1)} %bitcast.14), calls=%async_computation.1 | async-start | bytes 1048576
  59.4 17.5 %copy-start.3 = (f32[3,1536]{1,0:T(4,128)S(1)}, f32[3,1536]{1,0:T(4,128)}, u32[]{:S(2)}) copy-start(f32[3,1536]{1,0:T(4,128)} %mod_ref.1) | copy-start | bytes 55300
  59.5 1.6 %collective-permute-start.19 = (bf16[2,3,192,128]{3,2,1,0:T(8,128)(2,1)S(1)}, bf16[2,3,192,128]{3,2,1,0:T(8,128)(2,1)S(1)}, u32[]{:S(2)}, u32[]{:S(2)}) collective-permute-start(bf16[2,3,192,128]{3,2,1,0:T(8,128)(2,1)S(1)} %collective-permute-done.18.refs_9_), channel_id=1, source_target_pairs={{0,8},{8,0},{16,24},{24,16},{1,9},{9,1},{17,25},{25,17},{2,10},{10... | collective-permute-start | bytes 884744 | tf_op jit(solution)/shard_map/ppermute | solution.py:501
  59.5 2.0 %collective-permute-start.17 = (bf16[2,3,192,128]{3,2,1,0:T(8,128)(2,1)S(1)}, bf16[2,3,192,128]{3,2,1,0:T(8,128)(2,1)S(1)}, u32[]{:S(2)}, u32[]{:S(2)}) collective-permute-start(bf16[2,3,192,128]{3,2,1,0:T(8,128)(2,1)S(1)} %collective-permute-done.10.refs_5_), channel_id=1, source_target_pairs={{0,8},{8,0},{16,24},{24,16},{1,9},{9,1},{17,25},{25,17},{2,10},{10... | collective-permute-start | bytes 884744 | tf_op jit(solution)/shard_map/ppermute | solution.py:501
  65.7 5.2 %collective-permute-start.20 = (bf16[3,192,128]{2,1,0:T(8,128)(2,1)S(1)}, bf16[3,192,128]{2,1,0:T(8,128)(2,1)S(1)}, u32[]{:S(2)}, u32[]{:S(2)}) collective-permute-start(bf16[3,192,128]{2,1,0:T(8,128)(2,1)S(1)} %get-tuple-element.58), channel_id=1, source_target_pairs={{0,1},{1,0},{8,9},{9,8},{16,17},{17,16},{24,25},{25,24},{2,3},{3,2... | collective-permute-start | bytes 442376 | tf_op jit(solution)/shard_map/ppermute | solution.py:497
  66.7 6.8 %collective-permute-start.21 = (bf16[3,192,128]{2,1,0:T(8,128)(2,1)S(1)}, bf16[3,192,128]{2,1,0:T(8,128)(2,1)S(1)}, u32[]{:S(2)}, u32[]{:S(2)}) collective-permute-start(bf16[3,192,128]{2,1,0:T(8,128)(2,1)S(1)} %get-tuple-element.59), channel_id=1, source_target_pairs={{0,16},{1,17},{8,24},{9,25},{16,0},{17,1},{24,8},{25,9},{2,18},{3,... | collective-permute-start | bytes 442376 | tf_op jit(solution)/shard_map/ppermute | solution.py:497
  69.3 7.7 %collective-permute-start.22 = (bf16[3,192,128]{2,1,0:T(8,128)(2,1)S(1)}, bf16[3,192,128]{2,1,0:T(8,128)(2,1)S(1)}, u32[]{:S(2)}, u32[]{:S(2)}) collective-permute-start(bf16[3,192,128]{2,1,0:T(8,128)(2,1)S(1)} %get-tuple-element.60), channel_id=1, source_target_pairs={{0,17},{1,16},{8,25},{9,24},{16,1},{17,0},{24,9},{25,8},{2,19},{3,... | collective-permute-start | bytes 442376 | tf_op jit(solution)/shard_map/ppermute | solution.py:497

commit v4 on v3

--- a/solution.py
+++ b/solution.py
@@ -213,28 +213,13 @@
     return x * cosine + swapped * sine
 
 
-def fold_squares(prod):
-    total = None
-    for h in range(GH):
-        piece = prod[:, h * HEAD_DIM : (h + 1) * HEAD_DIM]
-        total = piece * piece if total is None else total + piece * piece
-    return total
-
-
-def group_of(sc_ref, m):
-    return pl.multiple_of((sc_ref[0] ^ m) * GW, GW)
-
-
-def finish_normed(sc_ref, tables, buf, gain_ref, ssq, write):
-    cosine, sine = angle_tables((sc_ref[1], sc_ref[2], sc_ref[3]), *tables)
-    even = lax.broadcasted_iota(jnp.int32, (TILE, HEAD_DIM), 1) % 2 == 0
-    inv = lax.rsqrt(jnp.sum(ssq, axis=-1, keepdims=True) / D + 1e-06)
-    for m in range(GROUPS):
-        gain = gain_ref[:, pl.ds(group_of(sc_ref, m), GW)]
-        for h in range(GH):
-            lanes = slice(h * HEAD_DIM, (h + 1) * HEAD_DIM)
-            x = buf[m, :, lanes] * inv * gain[:, lanes]
-            write(m, h, rope(x, cosine, sine, even).astype(jnp.bfloat16))
+def mesh_place():
+    ta, ha, wa = (lax.axis_index(name) for name in ("ta", "ha", "wa"))
+    return 2 * (ta // 2) + wa, ta, ha, wa
+
+
+def group_at(group, m):
+    return pl.multiple_of((group ^ m) * GW, GW)
 
 
 def start_all(pairs, sems):
@@ -249,62 +234,69 @@
         copy.wait()
 
 
-def weight_blocks(sc_ref, w_hbm, wbuf):
-    return [(w_hbm.at[:, pl.ds(group_of(sc_ref, m), GW)], wbuf.at[m]) for m in range(GROUPS)]
-
-
-def project_normed(sc_ref, normed, weights, wbuf, buf, gain_ref, tables, write):
+def weight_blocks(group, w_hbm, wbuf):
+    return [(w_hbm.at[:, pl.ds(group_at(group, m), GW)], wbuf.at[m]) for m in range(GROUPS)]
+
+
+def project_normed(group, normed, weights, wbuf, buf, gain_ref, angles, write):
+    cosine, sine = angles
+    even = lax.broadcasted_iota(jnp.int32, (TILE, HEAD_DIM), 1) % 2 == 0
     ssq = None
     for m in range(GROUPS):
         weights[m].wait()
         prod = jnp.dot(normed, wbuf[m], preferred_element_type=jnp.float32)
-        buf[m] = prod
-        squares = fold_squares(prod)
-        ssq = squares if ssq is None else ssq + squares
-    finish_normed(sc_ref, tables, buf, gain_ref, ssq, write)
-
-
-def kv_kernel(sc_ref, tok_hbm, mod_hbm, nk_hbm, ft_hbm, rt_hbm, ct_hbm, wk_hbm, wv_hbm, *refs):
-    kv_hbm, normed_hbm, refs = refs[:4], refs[4], refs[5:]
-    tok_ref, mod_ref, nk_ref, ft_ref, rt_ref, ct_ref, wk_buf, wv_buf, buf, gain_ref, normed_ref, kv_ref, sems, out_sems = refs
+        gain = gain_ref[:, pl.ds(group_at(group, m), GW)]
+        for h in range(GH):
+            lanes = slice(h * HEAD_DIM, (h + 1) * HEAD_DIM)
+            x = prod[:, lanes]
+            ssq = x * x if ssq is None else ssq + x * x
+            buf[m, :, lanes] = rope(x * gain[:, lanes], cosine, sine, even)
+    inv = lax.rsqrt(jnp.sum(ssq, axis=-1, keepdims=True) / D + 1e-06)
+    for m in range(GROUPS):
+        for h in range(GH):
+            write(m, h, (buf[m, :, h * HEAD_DIM : (h + 1) * HEAD_DIM] * inv).astype(jnp.bfloat16))
+
+
+def kv_kernel(tok_hbm, mod_hbm, nk_hbm, ft_hbm, rt_hbm, ct_hbm, wk_hbm, wv_hbm, *refs):
+    kv_ref, normed_ref, refs = refs[:4], refs[4], refs[5:]
+    tok_ref, mod_ref, nk_ref, ft_ref, rt_ref, ct_ref, wk_buf, wv_buf, buf, gain_ref, sems = refs
     sources = (tok_hbm, mod_hbm, nk_hbm, ft_hbm, rt_hbm, ct_hbm)
     small = start_all(zip(sources, refs), sems.at[2])
-    key_weights = start_all(weight_blocks(sc_ref, wk_hbm, wk_buf), sems.at[0])
-    value_weights = start_all(weight_blocks(sc_ref, wv_hbm, wv_buf), sems.at[1])
+    group, *place = mesh_place()
+    key_weights = start_all(weight_blocks(group, wk_hbm, wk_buf), sems.at[0])
+    value_weights = start_all(weight_blocks(group, wv_hbm, wv_buf), sems.at[1])
     wait_all(small)
+    angles = angle_tables(place, ft_ref, rt_ref, ct_ref)
     gain_ref[...] = nk_ref[...].reshape(1, D)
     normed = layer_norm(tok_ref[...], mod_ref)
     normed_ref[...] = normed
-    results = start_all([(normed_ref, normed_hbm)], out_sems.at[2])
 
     def write(m, h, x):
-        kv_ref[m, 0, h] = x
-
-    project_normed(sc_ref, normed, key_weights, wk_buf, buf, gain_ref, (ft_ref, rt_ref, ct_ref), write)
-    results += start_all([(kv_ref.at[m, 0], kv_hbm[m].at[0]) for m in range(GROUPS)], out_sems.at[0])
+        kv_ref[m][0, h] = x
+
+    project_normed(group, normed, key_weights, wk_buf, buf, gain_ref, angles, write)
     for m in range(GROUPS):
         value_weights[m].wait()
         prod = jnp.dot(normed, wv_buf[m], preferred_element_type=jnp.float32)
         for h in range(GH):
-            kv_ref[m, 1, h] = prod[:, h * HEAD_DIM : (h + 1) * HEAD_DIM].astype(jnp.bfloat16)
-        results.append(pltpu.make_async_copy(kv_ref.at[m, 1], kv_hbm[m].at[1], out_sems.at[1, m]))
-        results[-1].start()
-    wait_all(results)
-
-
-def q_kernel(sc_ref, normed_hbm, nq_hbm, ft_hbm, rt_hbm, ct_hbm, wq_hbm, *refs):
-    q_hbm, refs = refs[:4], refs[4:]
-    normed_ref, nq_ref, ft_ref, rt_ref, ct_ref, wq_buf, buf, gain_ref, q_ref, sems, out_sems = refs
+            kv_ref[m][1, h] = prod[:, h * HEAD_DIM : (h + 1) * HEAD_DIM].astype(jnp.bfloat16)
+
+
+def q_kernel(normed_hbm, nq_hbm, ft_hbm, rt_hbm, ct_hbm, wq_hbm, token_hbm, *refs):
+    q_ref, made_ref, refs = refs[:4], refs[4], refs[5:]
+    made_ref[...] = jnp.zeros_like(made_ref)
+    normed_ref, nq_ref, ft_ref, rt_ref, ct_ref, wq_buf, buf, gain_ref, sems = refs
     small = start_all(zip((normed_hbm, nq_hbm, ft_hbm, rt_hbm, ct_hbm), refs), sems.at[1])
-    weights = start_all(weight_blocks(sc_ref, wq_hbm, wq_buf), sems.at[0])
+    group, *place = mesh_place()
+    weights = start_all(weight_blocks(group, wq_hbm, wq_buf), sems.at[0])
     wait_all(small)
+    angles = angle_tables(place, ft_ref, rt_ref, ct_ref)
     gain_ref[...] = nq_ref[...].reshape(1, D)
 
     def write(m, h, x):
-        q_ref[m, h] = x
-
-    project_normed(sc_ref, normed_ref[...], weights, wq_buf, buf, gain_ref, (ft_ref, rt_ref, ct_ref), write)
-    wait_all(start_all([(q_ref.at[m], q_hbm[m]) for m in range(GROUPS)], out_sems))
+        q_ref[m][h] = x
+
+    project_normed(group, normed_ref[...], weights, wq_buf, buf, gain_ref, angles, write)
 
 
 SMEM = pl.BlockSpec(memory_space=pltpu.SMEM)
@@ -320,11 +312,11 @@
 Q_SHAPE = (GH, TILE, HEAD_DIM)
 
 
-def project_kv(sc, tokens, modulation, norm_k, tables, w_key, w_value):
+def project_kv(tokens, modulation, norm_k, tables, w_key, w_value):
     return pl.pallas_call(
         kv_kernel,
-        in_specs=[SMEM] + [HBM] * 8,
-        out_specs=[HBM] * (GROUPS + 1),
+        in_specs=[HBM] * 8,
+        out_specs=[VMEM] * (GROUPS + 1),
         scratch_shapes=[
             pltpu.VMEM((TILE, D), jnp.bfloat16),
             pltpu.VMEM((3, D), jnp.float32),
@@ -334,24 +326,20 @@
             pltpu.VMEM((GROUPS, D, GW), jnp.bfloat16),
             pltpu.VMEM((GROUPS, TILE, GW), jnp.float32),
             pltpu.VMEM((1, D), jnp.float32),
-            pltpu.VMEM((TILE, D), jnp.bfloat16),
-            pltpu.VMEM((GROUPS, *KV_SHAPE), jnp.bfloat16),
             pltpu.SemaphoreType.DMA((3, 6)),
-            pltpu.SemaphoreType.DMA((3, GROUPS)),
         ],
-        out_shape=[jax.ShapeDtypeStruct(KV_SHAPE, jnp.bfloat16)] * GROUPS
-        + [jax.ShapeDtypeStruct((TILE, D), jnp.bfloat16)],
-        compiler_params=limit(60),
+        out_shape=[pltpu.VMEM(KV_SHAPE, jnp.bfloat16)] * GROUPS + [pltpu.VMEM((TILE, D), jnp.bfloat16)],
+        compiler_params=limit(54),
         cost_estimate=pl.CostEstimate(flops=4 * TILE * D * D, bytes_accessed=4 * D * D, transcendentals=0),
         name="project_kv",
-    )(sc, tokens, modulation, norm_k, *tables, w_key, w_value)
-
-
-def project_q(sc, normed, norm_q, tables, w_query):
+    )(tokens, modulation, norm_k, *tables, w_key, w_value)
+
+
+def project_q(normed, norm_q, tables, w_query, token):
     return pl.pallas_call(
         q_kernel,
-        in_specs=[SMEM] + [HBM] * 6,
-        out_specs=[HBM] * GROUPS,
+        in_specs=[HBM] * 7,
+        out_specs=[VMEM] * (GROUPS + 1),
         scratch_shapes=[
             pltpu.VMEM((TILE, D), jnp.bfloat16),
             pltpu.VMEM((D,), jnp.float32),
@@ -359,15 +347,13 @@
             pltpu.VMEM((GROUPS, D, GW), jnp.bfloat16),
             pltpu.VMEM((GROUPS, TILE, GW), jnp.float32),
             pltpu.VMEM((1, D), jnp.float32),
-            pltpu.VMEM((GROUPS, *Q_SHAPE), jnp.bfloat16),
             pltpu.SemaphoreType.DMA((2, 5)),
-            pltpu.SemaphoreType.DMA((GROUPS,)),
         ],
-        out_shape=[jax.ShapeDtypeStruct(Q_SHAPE, jnp.bfloat16)] * GROUPS,
-        compiler_params=limit(60),
+        out_shape=[pltpu.VMEM(Q_SHAPE, jnp.bfloat16)] * GROUPS + [TOKEN],
+        compiler_params=limit(46),
         cost_estimate=pl.CostEstimate(flops=2 * TILE * D * D, bytes_accessed=2 * D * D, transcendentals=0),
         name="project_q",
-    )(sc, normed, norm_q, *tables, w_query)
+    )(normed, norm_q, *tables, w_query, token)
 
 
 def query_of(refs, s, h):
@@ -400,23 +386,15 @@
     return peak, total, norm
 
 
-def stack_keys(slots, kind, h):
-    return jnp.concatenate([ref[kind, h] for pair in slots for ref in pair], axis=0)
-
-
-def segment(slots, there, h):
-    return stack_keys(slots, 0, h), stack_keys(slots, 1, h), there
-
-
-def attend_kernel(plan, tile_places, state_slots, final, sc_ref, *refs):
-    q, refs = refs[:4], refs[4:]
-    tiles = {}
-    for name, places in tile_places:
-        tiles[name] = [ref if place is None else ref.at[place] for ref, place in zip(refs, places)]
-        refs = refs[2:]
+def attend_kernel(plan, arrays_n, state_slots, final, sc_ref, *refs):
+    q, arrays, refs = refs[:4], refs[4 : 4 + arrays_n], refs[4 + arrays_n :]
     state_in = {s: refs[2 * n : 2 * n + 2] for n, s in enumerate(state_slots)}
-    refs = refs[2 * len(state_slots) :]
+    *refs, token_ref = refs[2 * len(state_slots) :]
+    token_ref[...] = jnp.zeros_like(token_ref)
     low = lax.broadcasted_iota(jnp.int32, (2 * TILE, HEAD_DIM), 1) < HEAD_DIM // 2
+
+    def stack_keys(tiles, kind, h):
+        return jnp.concatenate([arrays[n][(*place, kind, h)] for n, place in tiles], axis=0)
 
     def state(s, h):
         if s not in state_in:
@@ -424,24 +402,22 @@
         stat = state_in[s][0][h]
         return stat[:, :1], state_in[s][1][h], stat[:, HEAD_DIM // 2 : HEAD_DIM // 2 + 1]
 
-    def one_head(slots, h):
-        for n, s in enumerate(sorted(slots)):
-            segments = [
-                segment([tiles[name] for name in names], None if row is None else sc_ref[5 + row] == 1, h)
-                for names, row in slots[s]
-            ]
-            peak, total, norm = attend(query_of(q, s, h), segments, state(s, h)) if segments else state(s, h)
-            if final:
-                attended = (total / norm).astype(jnp.bfloat16)
-                refs[2 * s][h] = attended[:TILE]
-                refs[2 * s + 1][h] = attended[TILE:]
-            else:
-                refs[2 * n][h] = jnp.where(low, peak, norm)
-                refs[2 * n + 1][h] = total
-
     def run(slots):
         for h in range(GH):
-            one_head(slots, h)
+            for n, s in enumerate(sorted(slots)):
+                segments = [
+                    (stack_keys(tiles, 0, h), stack_keys(tiles, 1, h), None if row is None else sc_ref[5 + row] == 1)
+                    for tiles, row in slots[s]
+                ]
+                peak, total, norm = attend(query_of(q, s, h), segments, state(s, h)) if segments else state(s, h)
+                if final:
+                    attended = (total / norm).astype(jnp.bfloat16)
+                    refs[2 * s][h] = attended[:TILE]
+                    refs[2 * s + 1][h] = attended[TILE:]
+                else:
+                    refs[2 * n][h] = jnp.where(low, peak, norm)
+                    refs[2 * n + 1][h] = total
+
     if plan[0] == plan[1]:
         run(plan[0])
     else:
@@ -449,45 +425,56 @@
             pl.when(sc_ref[4] == near)(functools.partial(run, plan[near]))
 
 
+TOKEN = jax.ShapeDtypeStruct((8, HEAD_DIM), jnp.float32)
 STATE_SHAPE = jax.ShapeDtypeStruct((GH, 2 * TILE, HEAD_DIM), jnp.float32)
 
 
-def attend_call(name, plan, sc, queries, tiles, state):
+def attend_call(name, plan, sc, queries, arrays, state):
     final = name == "attend_last"
     state_slots = sorted(state)
-    places = tuple((key, tuple(place for _, place in pair)) for key, pair in tiles.items())
-    arrays = [array for pair in tiles.values() for array, _ in pair]
     states = [array for s in state_slots for array in state[s]]
     return pl.pallas_call(
-        functools.partial(attend_kernel, plan, places, tuple(state_slots), final),
+        functools.partial(attend_kernel, plan, len(arrays), tuple(state_slots), final),
         in_specs=[SMEM] + [VMEM] * (GROUPS + len(arrays) + len(states)),
-        out_specs=[VMEM] * 4,
-        out_shape=[jax.ShapeDtypeStruct(Q_SHAPE, jnp.bfloat16) if final else STATE_SHAPE] * 4,
+        out_specs=[VMEM] * (5 if final else 2 * len(plan[0]) + 1),
+        out_shape=[*([jax.ShapeDtypeStruct(Q_SHAPE, jnp.bfloat16)] * 4 if final else [STATE_SHAPE] * (2 * len(plan[0]))), TOKEN],
         compiler_params=limit(32),
         cost_estimate=pl.CostEstimate(flops=1000, bytes_accessed=1000, transcendentals=0),
         name=name,
     )(sc, *queries, *arrays, *states)
 
 
-def out_kernel(sc_ref, a0, a1, a2, a3, mod_ref, w_ref, out_ref):
-    total = None
-    for m, ref in enumerate((a0, a1, a2, a3)):
-        rows = jnp.concatenate([ref[h] for h in range(GH)], axis=1)
-        part = jnp.dot(rows, w_ref[pl.ds(group_of(sc_ref, m), GW), :], preferred_element_type=jnp.float32)
-        total = part if total is None else total + part
-    out_ref[...] = (total * mod_ref[2:3, :]).astype(jnp.bfloat16)
-
-
-def project_out(sc, attended, modulation, w_out):
+OUT_PARTS = 3
+
+
+def out_kernel(a0, a1, a2, a3, mod_ref, w_ref, out_hbm, out_ref, sems):
+    group = mesh_place()[0]
+    rows = [jnp.concatenate([ref[h] for h in range(GH)], axis=1) for ref in (a0, a1, a2, a3)]
+    width = D // OUT_PARTS
+    copies = []
+    for n in range(OUT_PARTS):
+        lanes = slice(n * width, (n + 1) * width)
+        total = None
+        for m in range(GROUPS):
+            part = jnp.dot(rows[m], w_ref[pl.ds(group_at(group, m), GW), lanes], preferred_element_type=jnp.float32)
+            total = part if total is None else total + part
+        out_ref[:, lanes] = (total * mod_ref[2:3, lanes]).astype(jnp.bfloat16)
+        copies.append(pltpu.make_async_copy(out_ref.at[:, lanes], out_hbm.at[:, lanes], sems.at[n]))
+        copies[-1].start()
+    wait_all(copies)
+
+
+def project_out(attended, modulation, w_out):
     return pl.pallas_call(
         out_kernel,
-        in_specs=[SMEM] + [VMEM] * 6,
-        out_specs=VMEM,
+        in_specs=[VMEM] * 6,
+        out_specs=HBM,
+        scratch_shapes=[pltpu.VMEM((TILE, D), jnp.bfloat16), pltpu.SemaphoreType.DMA((OUT_PARTS,))],
         out_shape=jax.ShapeDtypeStruct((TILE, D), jnp.bfloat16),
         compiler_params=limit(20),
         cost_estimate=pl.CostEstimate(flops=2 * TILE * D * D, bytes_accessed=2 * D * D, transcendentals=0),
         name="project_out",
-    )(sc, *attended, modulation, w_out)
+    )(*attended, modulation, w_out)
 
 
 def square_swap(value, m):
@@ -508,6 +495,10 @@
 
 def after(value, *others):
     return lax.optimization_barrier((value, *others))[0]
+
+
+def hold(value, token):
+    return jnp.where(token[0] < 1.0, value, jnp.zeros((), value.dtype))
 
 
 def square_body(tokens, modulation, w_query, w_key, w_value, w_out, norm_q, norm_k):
@@ -526,7 +517,7 @@
         rope_tables(rows_n, CH, first, sixth),
         rope_tables(lax.axis_size("wa"), CW, first + sixth, sixth),
     )
-    *kv, normed = project_kv(sc, tokens.reshape(TILE, D), modulation, norm_k, tables, w_key, w_value)
+    *kv, normed = project_kv(tokens.reshape(TILE, D), modulation, norm_k, tables, w_key, w_value)
 
     def rows_of(tile):
         return [row_swap(tile, first, rows_n) for first in range(2)]
@@ -534,49 +525,82 @@
     other0 = core_swap(kv[0])
     halo0 = rows_of(kv[0])
     side = [square_swap(kv[1], 1), square_swap(kv[2], 2)]
-    queries = list(project_q(sc, after(normed, other0), norm_q, tables, w_query))
+    *queries, made = project_q(after(normed, other0), norm_q, tables, w_query, normed)
     middle = jnp.stack(after(side, queries[0], *halo0))
     halo12, other12 = rows_of(middle), core_swap(middle)
     mine3 = queries[3][None]
     queries[1:3] = [square_swap(queries[m], m) for m in range(1, 3)]
     corner = square_swap(jnp.concatenate([kv[3], after(mine3, queries[1], queries[2])]), 3)
+    queries[0] = after(queries[0], *halo12)
+    swapped0 = [core_swap(tile) for tile in halo0]
+    halo_parts = {"same": [halo0, halo12, None], "other": [swapped0, None, None]}
+    own = {"same": [(kv[0], ()), (middle, (0,)), (middle, (1,)), None], "other": [(other0, ()), (other12, (0,)), (other12, (1,)), None]}
+
+    def halo_tiles(row):
+        made = {}
+        for kind, parts in halo_parts.items():
+            c0, c12, c3 = [None if part is None else part[row] for part in parts]
+            made[kind] = [(c0, ()), (c12, (0,)), (c12, (1,)), (c3, ())]
+        return made
+
+    def own_keys(kinds):
+        return [(own[kind][m], kind, m) for kind, m in kinds], None
+
+    def row_keys(kinds, row):
+        return [(halo_tiles(row)[kind][m], kind, m) for kind, m in kinds], row
+
+    def call(name, plans, state):
+        numbers, arrays, numbered = {}, [], []
+        for slots in plans:
+            made = {}
+            for s, segments in slots.items():
+                made[s] = ()
+                for tiles, row in segments:
+                    ids = []
+                    for (array, place), kind, m in tiles:
+                        key = (id(array), place)
+                        if key not in numbers:
+                            known = [n for n, other in enumerate(arrays) if other is array]
+                            if not known:
+                                arrays.append(array)
+                                known = [len(arrays) - 1]
+                            numbers[key] = (known[0], place)
+                        ids.append(numbers[key])
+                    made[s] += ((tuple(ids), row),)
+            numbered.append(made)
+        return attend_call(name, tuple(numbered), sc, queries, arrays, state)
+
+    def both(*places):
+        return [(kind, m) for kind in ("same", "other") for m in places]
+
+    def rows_keys(kinds):
+        return [row_keys(kinds, r) for r in range(2)]
+
+    cross = [("other", 2), ("other", 3)], [("other", 0), ("other", 1)]
     queries[3], corner = corner[2], corner[:2]
-    halo3, other3 = rows_of(corner), core_swap(corner)
-    queries[0] = after(queries[0], *halo12)
-
-    def tiles_of(first, both, last):
-        return [(first, None), (both, 0), (both, 1), (last, None)]
-
-    same, other = tiles_of(kv[0], middle, corner), tiles_of(other0, other12, other3)
-    halo = [tiles_of(halo0[r], halo12[r], halo3[r]) for r in range(2)]
-    swapped = [[core_swap(tile) for tile in pair] for pair in (halo0, halo12)]
-
-    def call(name, plan, state):
-        tiles = {}
-        for s in range(2):
-            at = slice(2 * s, 2 * s + 2)
-            tiles[f"same{s}"], tiles[f"other{s}"] = same[at], other[at]
-            for r in range(2):
-                tiles[f"same{s}{r}"], tiles[f"other{s}{r}"] = halo[r][at], halo_other[r][at]
-        used = {n for p in plan for segs in p.values() for names, _ in segs for n in names}
-        return attend_call(name, plan, sc, queries, {n: t for n, t in tiles.items() if n in used}, state)
-
-    rows = [tuple(((f"same{s}{r}", f"other{s}{r}"), r) for r in range(2)) for s in range(2)]
-    far = [tuple(((f"other{s}{r}",), r) for r in range(2)) for s in range(2)]
-    own = [("same0", "other0"), ("same1", "other1")]
-    swapped_early = [*swapped, halo3]
-    halo_other = [tiles_of(*[pair[r] for pair in swapped_early]) for r in range(2)]
-    state = call(
+    own["same"][3], own["other"][3] = (corner, ()), (core_swap(corner), ())
+    halo_parts["other"][1] = [core_swap(tile) for tile in halo12]
+    *state, made = call(
         "attend_own",
-        ({0: (((*own[0], "other1"), None),), 1: ((own[1], None),)}, {0: ((own[0], None),), 1: (((*own[1], "other0"), None),)}),
+        (
+            {0: [own_keys(both(0, 1) + cross[0])], 1: [own_keys(both(2, 3))]},
+            {0: [own_keys(both(0, 1))], 1: [own_keys(both(2, 3) + cross[1])]},
+        ),
         {},
     )
-    state = call("attend_halo", ({0: rows[0], 1: ()}, {0: rows[0], 1: far[0]}), {0: state[:2], 1: state[2:]})
-    swapped.append([core_swap(after(tile, state[0])) for tile in halo3])
-    halo_other = [tiles_of(*[pair[r] for pair in swapped]) for r in range(2)]
-    attended = call("attend_last", ({0: far[1], 1: rows[1]}, {0: (), 1: rows[1]}), {0: state[:2], 1: state[2:]})
+    halo3 = rows_of(corner)
+    halo_parts["same"][2] = halo3
+    halo_parts["other"][2] = [core_swap(hold(tile, made)) for tile in halo3]
+    *state, made = call(
+        "attend_halo", ({0: rows_keys(both(0, 1)), 1: []},) * 2, {0: state[:2], 1: state[2:]}
+    )
+    *attended, made = call(
+        "attend_last",
+        ({0: rows_keys(cross[0]), 1: rows_keys(both(2, 3))}, {0: [], 1: rows_keys(both(2, 3) + cross[1])}),
+        {0: state[:2], 1: state[2:]},
+    )
     attended = [square_swap(attended[m], m) for m in range(GROUPS)]
-    branch = project_out(sc, attended, modulation, w_out)
+    branch = project_out(attended, modulation, w_out)
     return branch.reshape(CT, CH, CW, D)
 
 

time: 79.9 us -> 77.5 us (0.970)
  Pallas kernels: 31.7 us -> 27.9 us
  local copies, waits for them, and re-layouts: 1.65 us -> 4.72 us
  starting transfers between devices: 26.9 us -> 24.5 us
  waiting for transfers between devices: 18.1 us -> 19.5 us
  other arithmetic: 1.01 us -> 0.15 us
    ppermute x8, waiting for transfers between devices: 7.7 us -> 18.4 us  [square_swap(): return lax.ppermute(value, ('ta', 'wa'), [(i, i ^ flip) for i in range(8)])]
    ppermute x6, waiting for transfers between devices: 7.87 us -> 0.02 us  [row_swap(): lax.ppermute(value, 'ha', [edge for i, j in pairs for edge in ((i, j), (j...]
    pallas_call x6, Pallas kernels: 31.7 us -> 27.9 us  [the longest x3 15.5 us: attend_call(): pl.pallas_call(functools.partial(attend_kernel, plan, len(arrays), tuple(...]
    unnamed x16 -> x30, local copies, waits for them, and re-layouts: 0.94 us -> 3.69 us
    ppermute x8, starting transfers between devices: 11.7 us -> 9.76 us  [square_swap(): return lax.ppermute(value, ('ta', 'wa'), [(i, i ^ flip) for i in range(8)])]
    ppermute x9, waiting for transfers between devices: 2.55 us -> 1.1 us  [core_swap(): return lax.ppermute(value, 'ta', [(i, i ^ 1) for i in range(4)])]
    squeeze x1, local copies, waits for them, and re-layouts: 0.01 us -> 0.92 us  [square_body(): queries[3], corner = (corner[2], corner[:2])]
    concatenate x1, other arithmetic: 0.95 us -> 0.04 us  [square_body(): jnp.concatenate([kv[3], after(mine3, queries[1], queries[2])])]
  transfers between devices with their start and end apart: 23 -> 23, of which waited for: 8 -> 7; matrix products, arithmetic and copies ran while one was open for 1% -> 2% of each run, Pallas kernels for 22% -> 17%
where the time goes in v4:
time: 77.5 us; the launch traced here: 77.3 us
  Pallas kernels  27.9 us (36%)
  starting transfers between devices  24.5 us (32%)
  waiting for transfers between devices  19.5 us (25%)
  local copies, waits for them, and re-layouts  4.72 us (6%)
    ppermute x8, waiting for transfers between devices, square_swap(): return lax.ppermute(value, ('ta', 'wa'), [(i, i ^ flip) for i in range(8)])  18.4 us
    pallas_call x3, Pallas kernels, attend_call(): pl.pallas_call(functools.partial(attend_kernel, plan, len(arrays), tuple(...  15.5 us
    ppermute x6, starting transfers between devices, row_swap(): lax.ppermute(value, 'ha', [edge for i, j in pairs for edge in ((i, j), (j...  12.6 us
    ppermute x8, starting transfers between devices, square_swap(): return lax.ppermute(value, ('ta', 'wa'), [(i, i ^ flip) for i in range(8)])  9.76 us
    pallas_call x1, Pallas kernels, project_kv(): pl.pallas_call(kv_kernel, in_specs=[HBM] * 8, out_specs=[VMEM] * (GROUPS...  6.61 us
    pallas_call x1, Pallas kernels, project_q(): pl.pallas_call(q_kernel, in_specs=[HBM] * 7, out_specs=[VMEM] * (GROUPS +...  3.73 us
    unnamed x30, local copies, waits for them, and re-layouts  3.69 us
    ppermute x9, starting transfers between devices, core_swap(): return lax.ppermute(value, 'ta', [(i, i ^ 1) for i in range(4)])  2.12 us
  transfers between devices with their start and end apart: 23, of which 7 were waited for; matrix products, arithmetic and copies ran while one was open for 2% of the time, Pallas kernels for 17%

profile of v4, /device:TPU:0, one launch (start us, length us, event | category | flops | bytes accessed | tf_op | source)
XLA Modules:
  0.0 77.3 jit_solution(12254665215298418267)
XLA Ops:
  0.0 6.6 %project_kv.1 = (bf16[2,3,192,128]{3,2,1,0:T(8,128)(2,1)S(1)}, bf16[2,3,192,128]{3,2,1,0:T(8,128)(2,1)S(1)}, bf16[2,3,192,128]{3,2,1,0:T(8,128)(2,1)S(1)}, bf16[...) custom-call(bf16[192,1536]{1,0:T(8,128)(2,1)} %bitcast.19, f32[3,1536]{1,0:T(4,128)} %mod_ref.1, f32[1536]{0:T(1024)} %nk_hbm.1, ...), custom_call_target="tpu_custom_call" | custom-call | flops 1811939328 | bytes 9437184 | tf_op jit(solution)/shard_map/project_kv/pallas_call | solution.py:316
  6.6 0.5 collective-permute-start
  7.2 2.7 %collective-permute-start.3 = (bf16[2,3,192,128]{3,2,1,0:T(8,128)(2,1)S(1)}, bf16[2,3,192,128]{3,2,1,0:T(8,128)(2,1)S(1)}, u32[]{:S(2)}, u32[]{:S(2)}) collective-permute-start(bf16[2,3,192,128]{3,2,1,0:T(8,128)(2,1)S(1)} %get-tuple-element.33.refs_4_), channel_id=1, source_target_pairs={{0,2},{2,0},{4,6},{6,4},{1,3},{3,1},{5,7},{7,5},{8,10},{10,8},{12,... | collective-permute-start | bytes 884744 | tf_op jit(solution)/shard_map/ppermute | solution.py:493
  9.8 0.7 collective-permute-start.4
  10.5 1.6 %collective-permute-start.1 = (bf16[2,3,192,128]{3,2,1,0:T(8,128)(2,1)S(1)}, bf16[2,3,192,128]{3,2,1,0:T(8,128)(2,1)S(1)}, u32[]{:S(2)}, u32[]{:S(2)}) collective-permute-start(bf16[2,3,192,128]{3,2,1,0:T(8,128)(2,1)S(1)} %get-tuple-element.36), channel_id=1, source_target_pairs={{0,1},{1,0},{8,9},{9,8},{16,17},{17,16},{24,25},{25,24},{2,3},{3,2... | collective-permute-start | bytes 884744 | tf_op jit(solution)/shard_map/ppermute | solution.py:484
  12.1 1.5 %collective-permute-start.2 = (bf16[2,3,192,128]{3,2,1,0:T(8,128)(2,1)S(1)}, bf16[2,3,192,128]{3,2,1,0:T(8,128)(2,1)S(1)}, u32[]{:S(2)}, u32[]{:S(2)}) collective-permute-start(bf16[2,3,192,128]{3,2,1,0:T(8,128)(2,1)S(1)} %get-tuple-element.37), channel_id=1, source_target_pairs={{0,16},{1,17},{8,24},{9,25},{16,0},{17,1},{24,8},{25,9},{2,18},{3,... | collective-permute-start | bytes 884744 | tf_op jit(solution)/shard_map/ppermute | solution.py:484
  13.6 3.7 %project_q.1 = (bf16[3,192,128]{2,1,0:T(8,128)(2,1)S(1)}, bf16[3,192,128]{2,1,0:T(8,128)(2,1)S(1)}, bf16[3,192,128]{2,1,0:T(8,128)(2,1)S(1)}, bf16[3,192,128]{2,1,0:T(8,128)(2,1)S(1)}, f32[8,128]{1,0:T(8,128)}) custom-call(bf16[192,1536]{1,0:T(8,128)(2,1)S(1)} %get-tuple-element.34.normed_hbm.token_hbm, f32[1536]{0:T(1024)S(1)} %copy-done.11, ...), custom_call_target="tpu_custom_call" | custom-call | flops 905969664 | bytes 4718592 | tf_op jit(solution)/shard_map/project_q/pallas_call | solution.py:339
  17.4 0.6 collective-permute-start.7
  17.9 0.0 collective-permute-done.3.refs_4_
  17.9 1.2 %collective-permute-start.8 = (bf16[3,192,128]{2,1,0:T(8,128)(2,1)S(1)}, bf16[3,192,128]{2,1,0:T(8,128)(2,1)S(1)}, u32[]{:S(2)}, u32[]{:S(2)}) collective-permute-start(bf16[3,192,128]{2,1,0:T(8,128)(2,1)S(1)} %get-tuple-element.42), channel_id=1, source_target_pairs={{0,16},{1,17},{8,24},{9,25},{16,0},{17,1},{24,8},{25,9},{2,18},{3,... | collective-permute-start | bytes 442376 | tf_op jit(solution)/shard_map/ppermute | solution.py:484
  19.1 0.0 collective-permute-done.4.refs_8_
  19.1 0.5 collective-permute-done.1
  19.7 2.2 %collective-permute-done.2 = bf16[2,3,192,128]{3,2,1,0:T(8,128)(2,1)S(1)} collective-permute-done((bf16[2,3,192,128]{3,2,1,0:T(8,128)(2,1)S(1)}, bf16[2,3,192,128]{3,2,1,0:T(8,128)(2,1)S(1)}, u32[]{:S(2)}, u32[]{:S(2)}) %collective-permute-start.2) | collective-permute-done | bytes 294944 | tf_op jit(solution)/shard_map/ppermute | solution.py:484
  21.8 0.1 pad_maximum_fusion.refs_5_
  21.9 4.2 %collective-permute-start.5 = (bf16[2,2,3,192,128]{4,3,2,1,0:T(8,128)(2,1)S(1)}, bf16[2,2,3,192,128]{4,3,2,1,0:T(8,128)(2,1)S(1)}, u32[]{:S(2)}, u32[]{:S(2)}) collective-permute-start(bf16[2,2,3,192,128]{4,3,2,1,0:T(8,128)(2,1)S(1)} %pad_maximum_fusion.refs_5_), channel_id=1, source_target_pairs={{0,2},{2,0},{4,6},{6,4},{1,3},{3,1},{5,7},{7,5},{8,10},{10,8},{12,... | collective-permute-start | bytes 1769480 | tf_op jit(solution)/shard_map/ppermute | solution.py:493
  26.1 1.5 %collective-permute-start.9 = (bf16[3,3,192,128]{3,2,1,0:T(8,128)(2,1)S(1)}, bf16[3,3,192,128]{3,2,1,0:T(8,128)(2,1)S(1)}, u32[]{:S(2)}, u32[]{:S(2)}) collective-permute-start(bf16[3,3,192,128]{3,2,1,0:T(8,128)(2,1)S(1)} %pad_maximum_fusion.1), channel_id=1, source_target_pairs={{0,17},{1,16},{8,25},{9,24},{16,1},{17,0},{24,9},{25,8},{2,19},{3,... | collective-permute-start | bytes 1327112 | tf_op jit(solution)/shard_map/ppermute | solution.py:484
  27.6 0.7 collective-permute-start.6
  28.3 0.1 collective-permute-start.11
  28.4 8.3 %collective-permute-done.9 = bf16[3,3,192,128]{3,2,1,0:T(8,128)(2,1)S(1)} collective-permute-done((bf16[3,3,192,128]{3,2,1,0:T(8,128)(2,1)S(1)}, bf16[3,3,192,128]{3,2,1,0:T(8,128)(2,1)S(1)}, u32[]{:S(2)}, u32[]{:S(2)}) %collective-permute-start.9) | collective-permute-done | bytes 442400 | tf_op jit(solution)/shard_map/ppermute | solution.py:484
  36.6 0.8 copy-done.12
  37.4 0.1 collective-permute-start.12
  37.5 0.1 stack.48.sc_ref
  37.6 3.8 %collective-permute-start.13 = (bf16[2,3,192,128]{3,2,1,0:T(8,128)(2,1)S(1)}, bf16[2,3,192,128]{3,2,1,0:T(8,128)(2,1)S(1)}, u32[]{:S(2)}, u32[]{:S(2)}) collective-permute-start(bf16[2,3,192,128]{3,2,1,0:T(8,128)(2,1)S(1)} %slice.14.refs_9_), channel_id=1, source_target_pairs={{0,2},{2,0},{4,6},{6,4},{1,3},{3,1},{5,7},{7,5},{8,10},{10,8},{12,... | collective-permute-start | bytes 884744 | tf_op jit(solution)/shard_map/ppermute | solution.py:493
  41.4 0.0 collective-permute-done.5.refs_5_.refs_8_
  41.4 0.7 collective-permute-start.16
  42.1 0.9 %slice_bitcast_fusion.refs_3_ = bf16[3,192,128]{2,1,0:T(8,128)(2,1)S(1)} fusion(bf16[3,3,192,128]{3,2,1,0:T(8,128)(2,1)} %copy-done.12), kind=kLoop, calls=%fused_computation.4 | loop fusion | bytes 294912 | tf_op jit(solution)/shard_map/squeeze | solution.py:580
  43.0 0.0 collective-permute-done.6.refs_9_.refs_10_
  43.0 0.2 collective-permute-start.18
  43.2 0.3 collective-permute-start.10
  43.6 0.2 collective-permute-start.15
  43.8 1.0 %copy-done.4 = bf16[2,3,192,128]{3,2,1,0:T(8,128)(2,1)S(1)} copy-done((bf16[2,3,192,128]{3,2,1,0:T(8,128)(2,1)S(1)}, bf16[2,3,192,128]{3,2,1,0:T(8,128)(2,1)}, u32[]{:S(2)}) %copy-start.4) | copy-done | bytes 294936
  44.7 1.0 %copy-done.6 = bf16[2,3,192,128]{3,2,1,0:T(8,128)(2,1)S(1)} copy-done((bf16[2,3,192,128]{3,2,1,0:T(8,128)(2,1)S(1)}, bf16[2,3,192,128]{3,2,1,0:T(8,128)(2,1)}, u32[]{:S(2)}) %copy-start.6) | copy-done | bytes 294936
  45.7 4.9 %attend_own.1 = (f32[3,384,128]{2,1,0:T(8,128)S(1)}, f32[3,384,128]{2,1,0:T(8,128)S(1)}, f32[3,384,128]{2,1,0:T(8,128)S(1)}, f32[3,384,128]{2,1,0:T(8,128)S(1)}, f32[8,128]{1,0:T(8,128)S(1)}) custom-call(s32[7]{0:T(128)S(1)} %stack.48.sc_ref, bf16[3,192,128]{2,1,0:T(8,128)(2,1)S(1)} %get-tuple-element.40.refs_0_, ...), custom_call_target="tpu_custom_call" | custom-call | flops 1000 | bytes 1000 | tf_op jit(solution)/shard_map/attend_own/pallas_call | solution.py:436
  50.6 0.1 collective-permute-start.19
  50.7 0.0 slice-start
  50.7 0.5 collective-permute-start.14
  51.3 0.1 collective-permute-start.17
  51.4 1.1 %collective-permute-done.19.refs_10_.refs_13_ = bf16[2,3,192,128]{3,2,1,0:T(8,128)(2,1)S(1)} collective-permute-done((bf16[2,3,192,128]{3,2,1,0:T(8,128)(2,1)}, bf16[2,3,192,128]{3,2,1,0:T(8,128)(2,1)S(1)}, u32[]{:S(2)}, u32[]{:S(2)}) %collective-permute-start.19) | collective-permute-done | bytes 294944 | tf_op jit(solution)/shard_map/ppermute | solution.py:488
  52.5 1.0 %copy-done.2 = bf16[2,3,192,128]{3,2,1,0:T(8,128)(2,1)S(1)} copy-done((bf16[2,3,192,128]{3,2,1,0:T(8,128)(2,1)S(1)}, bf16[2,3,192,128]{3,2,1,0:T(8,128)(2,1)}, u32[]{:S(2)}) %copy-start.2) | copy-done | bytes 294936
  53.4 4.3 %attend_halo.1 = (f32[3,384,128]{2,1,0:T(8,128)S(1)}, f32[3,384,128]{2,1,0:T(8,128)S(1)}, f32[3,384,128]{2,1,0:T(8,128)S(1)}, f32[3,384,128]{2,1,0:T(8,128)S(1)}, f32[8,128]{1,0:T(8,128)}) custom-call(s32[7]{0:T(128)S(1)} %stack.48.sc_ref, bf16[3,192,128]{2,1,0:T(8,128)(2,1)S(1)} %get-tuple-element.40.refs_0_, ...), custom_call_target="tpu_custom_call" | custom-call | flops 1000 | bytes 1000 | tf_op jit(solution)/shard_map/attend_halo/pallas_call | solution.py:436
  57.8 6.3 %attend_last.1 = (bf16[3,192,128]{2,1,0:T(8,128)(2,1)S(1)}, bf16[3,192,128]{2,1,0:T(8,128)(2,1)S(1)}, bf16[3,192,128]{2,1,0:T(8,128)(2,1)S(1)}, bf16[3,192,128]{2,1,0:T(8,128)(2,1)S(1)}, f32[8,128]{1,0:T(8,128)}) custom-call(s32[7]{0:T(128)S(1)} %stack.48.sc_ref, bf16[3,192,128]{2,1,0:T(8,128)(2,1)S(1)} %get-tuple-element.40.refs_0_, ...), custom_call_target="tpu_custom_call" | custom-call | flops 1000 | bytes 1000 | tf_op jit(solution)/shard_map/attend_last/pallas_call | solution.py:436
  64.0 0.3 collective-permute-start.20
  64.3 2.3 %collective-permute-start.21 = (bf16[3,192,128]{2,1,0:T(8,128)(2,1)S(1)}, bf16[3,192,128]{2,1,0:T(8,128)(2,1)S(1)}, u32[]{:S(2)}, u32[]{:S(2)}) collective-permute-start(bf16[3,192,128]{2,1,0:T(8,128)(2,1)S(1)} %get-tuple-element.57), channel_id=1, source_target_pairs={{0,16},{1,17},{8,24},{9,25},{16,0},{17,1},{24,8},{25,9},{2,18},{3,... | collective-permute-start | bytes 442376 | tf_op jit(solution)/shard_map/ppermute | solution.py:484
  66.6 0.9 %collective-permute-start.22 = (bf16[3,192,128]{2,1,0:T(8,128)(2,1)S(1)}, bf16[3,192,128]{2,1,0:T(8,128)(2,1)S(1)}, u32[]{:S(2)}, u32[]{:S(2)}) collective-permute-start(bf16[3,192,128]{2,1,0:T(8,128)(2,1)S(1)} %get-tuple-element.58), channel_id=1, source_target_pairs={{0,17},{1,16},{8,25},{9,24},{16,1},{17,0},{24,9},{25,8},{2,19},{3,... | collective-permute-start | bytes 442376 | tf_op jit(solution)/shard_map/ppermute | solution.py:484
  67.5 3.1 %collective-permute-done.20.a1 = bf16[3,192,128]{2,1,0:T(8,128)(2,1)S(1)} collective-permute-done((bf16[3,192,128]{2,1,0:T(8,128)(2,1)S(1)}, bf16[3,192,128]{2,1,0:T(8,128)(2,1)S(1)}, u32[]{:S(2)}, u32[]{:S(2)}) %collective-permute-start.20) | collective-permute-done | bytes 147488 | tf_op jit(solution)/shard_map/ppermute | solution.py:484
  70.6 0.7 collective-permute-done.21.a2
  71.3 3.7 %collective-permute-done.22.a3 = bf16[3,192,128]{2,1,0:T(8,128)(2,1)S(1)} collective-permute-done((bf16[3,192,128]{2,1,0:T(8,128)(2,1)S(1)}, bf16[3,192,128]{2,1,0:T(8,128)(2,1)S(1)}, u32[]{:S(2)}, u32[]{:S(2)}) %collective-permute-start.22) | collective-permute-done | bytes 147488 | tf_op jit(solution)/shard_map/ppermute | solution.py:484
  75.0 2.1 %project_out.1 = bf16[192,1536]{1,0:T(8,128)(2,1)} custom-call(bf16[3,192,128]{2,1,0:T(8,128)(2,1)S(1)} %get-tuple-element.55.a0, bf16[3,192,128]{2,1,0:T(8,128)(2,1)S(1)} %collective-permute-done.20.a1, bf16[3,192,128]{2,1,0:T(8,128)(2,1)S(1)} %collective-permute-done.21.a2, bf16[3,192,128]{2,1,0:T(8,128)(2,1)S(1)} %collective-permute-done.22.a3, ...), custom_call_target="tpu_custom_call" | custom-call | flops 905969664 | bytes 4718592 | tf_op jit(solution)/shard_map/project_out/pallas_call | solution.py:468
  (42 shorter events, 0.2 us)
Async XLA Ops:
  0.0 13.6 %copy-start = (bf16[1536,1536]{1,0:T(8,128)(2,1)S(1)}, bf16[1536,1536]{1,0:T(8,128)(2,1)}, u32[]{:S(2)}) copy-start(bf16[1536,1536]{1,0:T(8,128)(2,1)} %wq_hbm.1) | copy-start | bytes 14155780
  0.0 13.6 %copy-start.7 = (f32[4,2,8,128]{3,2,1,0:T(8,128)S(1)}, f32[4,2,8,128]{3,2,1,0:T(8,128)}, u32[]{:S(2)}) copy-start(f32[4,2,8,128]{3,2,1,0:T(8,128)} %constant.57.clone.rt_hbm) | copy-start | bytes 98308
  0.0 13.6 %copy-start.9 = (f32[4,2,3,128]{3,2,1,0:T(4,128)S(1)}, f32[4,2,3,128]{3,2,1,0:T(4,128)}, u32[]{:S(2)}) copy-start(f32[4,2,3,128]{3,2,1,0:T(4,128)} %constant.56.clone.ft_hbm) | copy-start | bytes 36868
  0.0 13.6 %copy-start.10 = (f32[2,2,8,128]{3,2,1,0:T(8,128)S(1)}, f32[2,2,8,128]{3,2,1,0:T(8,128)}, u32[]{:S(2)}) copy-start(f32[2,2,8,128]{3,2,1,0:T(8,128)} %constant.58.clone.ct_hbm) | copy-start | bytes 49156
  0.0 13.6 %copy-start.11 = (f32[1536]{0:T(1024)S(1)}, f32[1536]{0:T(1024)}, u32[]{:S(2)}) copy-start(f32[1536]{0:T(1024)} %nq_hbm.1) | copy-start | bytes 18436
  6.6 15.2 %copy-start.3 = (bf16[2,3,192,128]{3,2,1,0:T(8,128)(2,1)}, bf16[2,3,192,128]{3,2,1,0:T(8,128)(2,1)S(1)}, u32[]{:S(2)}) copy-start(bf16[2,3,192,128]{3,2,1,0:T(8,128)(2,1)S(1)} %get-tuple-element.33.refs_4_) | copy-start | bytes 884740
  6.6 6.9 %collective-permute-start = (bf16[2,3,192,128]{3,2,1,0:T(8,128)(2,1)S(1)}, bf16[2,3,192,128]{3,2,1,0:T(8,128)(2,1)S(1)}, u32[]{:S(2)}, u32[]{:S(2)}) collective-permute-start(bf16[2,3,192,128]{3,2,1,0:T(8,128)(2,1)S(1)} %get-tuple-element.33.refs_4_), channel_id=1, source_target_pairs={{0,8},{8,0},{16,24},{24,16},{1,9},{9,1},{17,25},{25,17},{2,10},{10... | collective-permute-start | bytes 884744 | tf_op jit(solution)/shard_map/ppermute | solution.py:488
  7.2 10.8 %collective-permute-start.3 = (bf16[2,3,192,128]{3,2,1,0:T(8,128)(2,1)S(1)}, bf16[2,3,192,128]{3,2,1,0:T(8,128)(2,1)S(1)}, u32[]{:S(2)}, u32[]{:S(2)}) collective-permute-start(bf16[2,3,192,128]{3,2,1,0:T(8,128)(2,1)S(1)} %get-tuple-element.33.refs_4_), channel_id=1, source_target_pairs={{0,2},{2,0},{4,6},{6,4},{1,3},{3,1},{5,7},{7,5},{8,10},{10,8},{12,... | collective-permute-start | bytes 884744 | tf_op jit(solution)/shard_map/ppermute | solution.py:493
  9.8 9.3 %collective-permute-start.4 = (bf16[2,3,192,128]{3,2,1,0:T(8,128)(2,1)S(1)}, bf16[2,3,192,128]{3,2,1,0:T(8,128)(2,1)S(1)}, u32[]{:S(2)}, u32[]{:S(2)}) collective-permute-start(bf16[2,3,192,128]{3,2,1,0:T(8,128)(2,1)S(1)} %get-tuple-element.33.refs_4_), channel_id=1, source_target_pairs={{2,4},{4,2},{3,5},{5,3},{10,12},{12,10},{11,13},{13,11},{18,20},{2... | collective-permute-start | bytes 884744 | tf_op jit(solution)/shard_map/ppermute | solution.py:493
  10.5 9.1 %collective-permute-start.1 = (bf16[2,3,192,128]{3,2,1,0:T(8,128)(2,1)S(1)}, bf16[2,3,192,128]{3,2,1,0:T(8,128)(2,1)S(1)}, u32[]{:S(2)}, u32[]{:S(2)}) collective-permute-start(bf16[2,3,192,128]{3,2,1,0:T(8,128)(2,1)S(1)} %get-tuple-element.36), channel_id=1, source_target_pairs={{0,1},{1,0},{8,9},{9,8},{16,17},{17,16},{24,25},{25,24},{2,3},{3,2... | collective-permute-start | bytes 884744 | tf_op jit(solution)/shard_map/ppermute | solution.py:484
  12.1 9.7 %collective-permute-start.2 = (bf16[2,3,192,128]{3,2,1,0:T(8,128)(2,1)S(1)}, bf16[2,3,192,128]{3,2,1,0:T(8,128)(2,1)S(1)}, u32[]{:S(2)}, u32[]{:S(2)}) collective-permute-start(bf16[2,3,192,128]{3,2,1,0:T(8,128)(2,1)S(1)} %get-tuple-element.37), channel_id=1, source_target_pairs={{0,16},{1,17},{8,24},{9,25},{16,0},{17,1},{24,8},{25,9},{2,18},{3,... | collective-permute-start | bytes 884744 | tf_op jit(solution)/shard_map/ppermute | solution.py:484
  13.6 8.3 %copy-start.5 = (bf16[2,3,192,128]{3,2,1,0:T(8,128)(2,1)}, bf16[2,3,192,128]{3,2,1,0:T(8,128)(2,1)S(1)}, u32[]{:S(2)}) copy-start(bf16[2,3,192,128]{3,2,1,0:T(8,128)(2,1)S(1)} %collective-permute-done.refs_6_) | copy-start | bytes 884740
  17.4 8.7 %collective-permute-start.7 = (bf16[3,192,128]{2,1,0:T(8,128)(2,1)S(1)}, bf16[3,192,128]{2,1,0:T(8,128)(2,1)S(1)}, u32[]{:S(2)}, u32[]{:S(2)}) collective-permute-start(bf16[3,192,128]{2,1,0:T(8,128)(2,1)S(1)} %get-tuple-element.41), channel_id=1, source_target_pairs={{0,1},{1,0},{8,9},{9,8},{16,17},{17,16},{24,25},{25,24},{2,3},{3,2... | collective-permute-start | bytes 442376 | tf_op jit(solution)/shard_map/ppermute | solution.py:484
  17.9 8.1 %collective-permute-start.8 = (bf16[3,192,128]{2,1,0:T(8,128)(2,1)S(1)}, bf16[3,192,128]{2,1,0:T(8,128)(2,1)S(1)}, u32[]{:S(2)}, u32[]{:S(2)}) collective-permute-start(bf16[3,192,128]{2,1,0:T(8,128)(2,1)S(1)} %get-tuple-element.42), channel_id=1, source_target_pairs={{0,16},{1,17},{8,24},{9,25},{16,0},{17,1},{24,8},{25,9},{2,18},{3,... | collective-permute-start | bytes 442376 | tf_op jit(solution)/shard_map/ppermute | solution.py:484
  19.1 7.0 %copy-start.1 = (bf16[2,3,192,128]{3,2,1,0:T(8,128)(2,1)}, bf16[2,3,192,128]{3,2,1,0:T(8,128)(2,1)S(1)}, u32[]{:S(2)}) copy-start(bf16[2,3,192,128]{3,2,1,0:T(8,128)(2,1)S(1)} %collective-permute-done.4.refs_8_) | copy-start | bytes 884740
  21.9 19.5 %collective-permute-start.5 = (bf16[2,2,3,192,128]{4,3,2,1,0:T(8,128)(2,1)S(1)}, bf16[2,2,3,192,128]{4,3,2,1,0:T(8,128)(2,1)S(1)}, u32[]{:S(2)}, u32[]{:S(2)}) collective-permute-start(bf16[2,2,3,192,128]{4,3,2,1,0:T(8,128)(2,1)S(1)} %pad_maximum_fusion.refs_5_), channel_id=1, source_target_pairs={{0,2},{2,0},{4,6},{6,4},{1,3},{3,1},{5,7},{7,5},{8,10},{10,8},{12,... | collective-permute-start | bytes 1769480 | tf_op jit(solution)/shard_map/ppermute | solution.py:493
  26.1 10.5 %collective-permute-start.9 = (bf16[3,3,192,128]{3,2,1,0:T(8,128)(2,1)S(1)}, bf16[3,3,192,128]{3,2,1,0:T(8,128)(2,1)S(1)}, u32[]{:S(2)}, u32[]{:S(2)}) collective-permute-start(bf16[3,3,192,128]{3,2,1,0:T(8,128)(2,1)S(1)} %pad_maximum_fusion.1), channel_id=1, source_target_pairs={{0,17},{1,16},{8,25},{9,24},{16,1},{17,0},{24,9},{25,8},{2,19},{3,... | collective-permute-start | bytes 1327112 | tf_op jit(solution)/shard_map/ppermute | solution.py:484
  27.6 15.4 %collective-permute-start.6 = (bf16[2,2,3,192,128]{4,3,2,1,0:T(8,128)(2,1)S(1)}, bf16[2,2,3,192,128]{4,3,2,1,0:T(8,128)(2,1)S(1)}, u32[]{:S(2)}, u32[]{:S(2)}) collective-permute-start(bf16[2,2,3,192,128]{4,3,2,1,0:T(8,128)(2,1)S(1)} %pad_maximum_fusion.refs_5_), channel_id=1, source_target_pairs={{2,4},{4,2},{3,5},{5,3},{10,12},{12,10},{11,13},{13,11},{18,20},{2... | collective-permute-start | bytes 1769480 | tf_op jit(solution)/shard_map/ppermute | solution.py:493
  28.3 15.0 %collective-permute-start.11 = (bf16[2,2,3,192,128]{4,3,2,1,0:T(8,128)(2,1)S(1)}, bf16[2,2,3,192,128]{4,3,2,1,0:T(8,128)(2,1)S(1)}, u32[]{:S(2)}, u32[]{:S(2)}) collective-permute-start(bf16[2,2,3,192,128]{4,3,2,1,0:T(8,128)(2,1)S(1)} %pad_maximum_fusion.refs_5_), channel_id=1, source_target_pairs={{0,8},{8,0},{16,24},{24,16},{1,9},{9,1},{17,25},{25,17},{2,10},{10... | collective-permute-start | bytes 1769480 | tf_op jit(solution)/shard_map/ppermute | solution.py:488
  36.6 0.8 copy-start.12
  37.4 6.2 %collective-permute-start.12 = (bf16[2,3,192,128]{3,2,1,0:T(8,128)(2,1)S(1)}, bf16[2,3,192,128]{3,2,1,0:T(8,128)(2,1)}, u32[]{:S(2)}, u32[]{:S(2)}) collective-permute-start(bf16[2,3,192,128]{3,2,1,0:T(8,128)(2,1)S(1)} %slice.14.refs_9_), channel_id=1, source_target_pairs={{0,8},{8,0},{16,24},{24,16},{1,9},{9,1},{17,25},{25,17},{2,10},{10... | collective-permute-start | bytes 884744 | tf_op jit(solution)/shard_map/ppermute | solution.py:488
  37.6 13.0 %collective-permute-start.13 = (bf16[2,3,192,128]{3,2,1,0:T(8,128)(2,1)S(1)}, bf16[2,3,192,128]{3,2,1,0:T(8,128)(2,1)S(1)}, u32[]{:S(2)}, u32[]{:S(2)}) collective-permute-start(bf16[2,3,192,128]{3,2,1,0:T(8,128)(2,1)S(1)} %slice.14.refs_9_), channel_id=1, source_target_pairs={{0,2},{2,0},{4,6},{6,4},{1,3},{3,1},{5,7},{7,5},{8,10},{10,8},{12,... | collective-permute-start | bytes 884744 | tf_op jit(solution)/shard_map/ppermute | solution.py:493
  41.4 9.3 %collective-permute-start.16 = (bf16[2,3,192,128]{3,2,1,0:T(8,128)(2,1)S(1)}, bf16[2,3,192,128]{3,2,1,0:T(8,128)(2,1)S(1)}, u32[]{:S(2)}, u32[]{:S(2)}) collective-permute-start(bf16[2,3,192,128]{3,2,1,0:T(8,128)(2,1)S(1)} %slice.14.refs_9_), channel_id=1, source_target_pairs={{2,4},{4,2},{3,5},{5,3},{10,12},{12,10},{11,13},{13,11},{18,20},{2... | collective-permute-start | bytes 884744 | tf_op jit(solution)/shard_map/ppermute | solution.py:493
  43.0 8.3 %collective-permute-start.18 = (bf16[2,3,192,128]{3,2,1,0:T(8,128)(2,1)S(1)}, bf16[2,3,192,128]{3,2,1,0:T(8,128)(2,1)S(1)}, u32[]{:S(2)}, u32[]{:S(2)}) collective-permute-start(bf16[2,3,192,128]{3,2,1,0:T(8,128)(2,1)S(1)} %collective-permute-done.3.refs_4_), channel_id=1, source_target_pairs={{0,8},{8,0},{16,24},{24,16},{1,9},{9,1},{17,25},{25,17},{2,10},{10... | collective-permute-start | bytes 884744 | tf_op jit(solution)/shard_map/ppermute | solution.py:488
  43.2 9.2 %collective-permute-start.10 = (bf16[2,2,3,192,128]{4,3,2,1,0:T(8,128)(2,1)S(1)}, bf16[2,2,3,192,128]{4,3,2,1,0:T(8,128)(2,1)S(1)}, u32[]{:S(2)}, u32[]{:S(2)}) collective-permute-start(bf16[2,2,3,192,128]{4,3,2,1,0:T(8,128)(2,1)S(1)} %collective-permute-done.5.refs_5_.refs_8_), channel_id=1, source_target_pairs={{0,8},{8,0},{16,24},{24,16},{1,9},{9,1},{17,25},{25,17},{2,10},{10... | collective-permute-start | bytes 1769480 | tf_op jit(solution)/shard_map/ppermute | solution.py:488
  43.6 8.9 %collective-permute-start.15 = (bf16[2,2,3,192,128]{4,3,2,1,0:T(8,128)(2,1)S(1)}, bf16[2,2,3,192,128]{4,3,2,1,0:T(8,128)(2,1)S(1)}, u32[]{:S(2)}, u32[]{:S(2)}) collective-permute-start(bf16[2,2,3,192,128]{4,3,2,1,0:T(8,128)(2,1)S(1)} %collective-permute-done.6.refs_9_.refs_10_), channel_id=1, source_target_pairs={{0,8},{8,0},{16,24},{24,16},{1,9},{9,1},{17,25},{25,17},{2,10},{10... | collective-permute-start | bytes 1769480 | tf_op jit(solution)/shard_map/ppermute | solution.py:488
  43.8 1.0 %copy-start.4 = (bf16[2,3,192,128]{3,2,1,0:T(8,128)(2,1)S(1)}, bf16[2,3,192,128]{3,2,1,0:T(8,128)(2,1)}, u32[]{:S(2)}) copy-start(bf16[2,3,192,128]{3,2,1,0:T(8,128)(2,1)} %copy-done.3) | copy-start | bytes 884740
  44.7 1.0 %copy-start.6 = (bf16[2,3,192,128]{3,2,1,0:T(8,128)(2,1)S(1)}, bf16[2,3,192,128]{3,2,1,0:T(8,128)(2,1)}, u32[]{:S(2)}) copy-start(bf16[2,3,192,128]{3,2,1,0:T(8,128)(2,1)} %copy-done.5) | copy-start | bytes 884740
  50.6 1.9 %collective-permute-start.19 = (bf16[2,3,192,128]{3,2,1,0:T(8,128)(2,1)}, bf16[2,3,192,128]{3,2,1,0:T(8,128)(2,1)S(1)}, u32[]{:S(2)}, u32[]{:S(2)}) collective-permute-start(bf16[2,3,192,128]{3,2,1,0:T(8,128)(2,1)} %copy-done.1), channel_id=1, source_target_pairs={{0,8},{8,0},{16,24},{24,16},{1,9},{9,1},{17,25},{25,17},{2,10},{10... | collective-permute-start | bytes 884744 | tf_op jit(solution)/shard_map/ppermute | solution.py:488
  50.7 24.3 %slice-start = ((s8[4718592]{0:T(1024)(128)(4,1)}), s8[4194304]{0:T(1024)(128)(4,1)S(1)}, s32[]{:S(2)}) async-start(s8[4718592]{0:T(1024)(128)(4,1)} %bitcast.16), calls=%async_computation | async-start | bytes 8388608
  50.7 7.0 %collective-permute-start.14 = (bf16[2,3,192,128]{3,2,1,0:T(8,128)(2,1)S(1)}, bf16[2,3,192,128]{3,2,1,0:T(8,128)(2,1)S(1)}, u32[]{:S(2)}, u32[]{:S(2)}) collective-permute-start(bf16[2,3,192,128]{3,2,1,0:T(8,128)(2,1)S(1)} %get-tuple-element.60), channel_id=1, source_target_pairs={{0,8},{8,0},{16,24},{24,16},{1,9},{9,1},{17,25},{25,17},{2,10},{10... | collective-permute-start | bytes 884744 | tf_op jit(solution)/shard_map/ppermute | solution.py:488
  51.3 6.5 %collective-permute-start.17 = (bf16[2,3,192,128]{3,2,1,0:T(8,128)(2,1)S(1)}, bf16[2,3,192,128]{3,2,1,0:T(8,128)(2,1)S(1)}, u32[]{:S(2)}, u32[]{:S(2)}) collective-permute-start(bf16[2,3,192,128]{3,2,1,0:T(8,128)(2,1)S(1)} %get-tuple-element.59), channel_id=1, source_target_pairs={{0,8},{8,0},{16,24},{24,16},{1,9},{9,1},{17,25},{25,17},{2,10},{10... | collective-permute-start | bytes 884744 | tf_op jit(solution)/shard_map/ppermute | solution.py:488
  52.5 1.0 %copy-start.2 = (bf16[2,3,192,128]{3,2,1,0:T(8,128)(2,1)S(1)}, bf16[2,3,192,128]{3,2,1,0:T(8,128)(2,1)}, u32[]{:S(2)}) copy-start(bf16[2,3,192,128]{3,2,1,0:T(8,128)(2,1)} %copy-done.1) | copy-start | bytes 884740
  53.4 21.5 %slice-start.1 = ((s8[4718592]{0:T(1024)(128)(4,1)}), s8[524288]{0:T(1024)(128)(4,1)S(1)}, s32[]{:S(2)}) async-start(s8[4718592]{0:T(1024)(128)(4,1)} %bitcast.16), calls=%async_computation.1 | async-start | bytes 1048576
  57.8 17.2 %copy-start.8 = (f32[3,1536]{1,0:T(4,128)S(1)}, f32[3,1536]{1,0:T(4,128)}, u32[]{:S(2)}) copy-start(f32[3,1536]{1,0:T(4,128)} %mod_ref.1) | copy-start | bytes 55300
  64.0 6.6 %collective-permute-start.20 = (bf16[3,192,128]{2,1,0:T(8,128)(2,1)S(1)}, bf16[3,192,128]{2,1,0:T(8,128)(2,1)S(1)}, u32[]{:S(2)}, u32[]{:S(2)}) collective-permute-start(bf16[3,192,128]{2,1,0:T(8,128)(2,1)S(1)} %get-tuple-element.56), channel_id=1, source_target_pairs={{0,1},{1,0},{8,9},{9,8},{16,17},{17,16},{24,25},{25,24},{2,3},{3,2... | collective-permute-start | bytes 442376 | tf_op jit(solution)/shard_map/ppermute | solution.py:484
  64.3 7.0 %collective-permute-start.21 = (bf16[3,192,128]{2,1,0:T(8,128)(2,1)S(1)}, bf16[3,192,128]{2,1,0:T(8,128)(2,1)S(1)}, u32[]{:S(2)}, u32[]{:S(2)}) collective-permute-start(bf16[3,192,128]{2,1,0:T(8,128)(2,1)S(1)} %get-tuple-element.57), channel_id=1, source_target_pairs={{0,16},{1,17},{8,24},{9,25},{16,0},{17,1},{24,8},{25,9},{2,18},{3,... | collective-permute-start | bytes 442376 | tf_op jit(solution)/shard_map/ppermute | solution.py:484
  66.6 8.3 %collective-permute-start.22 = (bf16[3,192,128]{2,1,0:T(8,128)(2,1)S(1)}, bf16[3,192,128]{2,1,0:T(8,128)(2,1)S(1)}, u32[]{:S(2)}, u32[]{:S(2)}) collective-permute-start(bf16[3,192,128]{2,1,0:T(8,128)(2,1)S(1)} %get-tuple-element.58), channel_id=1, source_target_pairs={{0,17},{1,16},{8,25},{9,24},{16,1},{17,0},{24,9},{25,8},{2,19},{3,... | collective-permute-start | bytes 442376 | tf_op jit(solution)/shard_map/ppermute | solution.py:484

commit v5 on v4

--- a/solution.py
+++ b/solution.py
@@ -238,21 +238,35 @@
     return [(w_hbm.at[:, pl.ds(group_at(group, m), GW)], wbuf.at[m]) for m in range(GROUPS)]
 
 
-def project_normed(group, normed, weights, wbuf, buf, gain_ref, angles, write):
+def project_normed(group, normed, weights, wbuf, buf, gain_ref, angles, write, beside=()):
     cosine, sine = angles
     even = lax.broadcasted_iota(jnp.int32, (TILE, HEAD_DIM), 1) % 2 == 0
     ssq = None
-    for m in range(GROUPS):
-        weights[m].wait()
-        prod = jnp.dot(normed, wbuf[m], preferred_element_type=jnp.float32)
+
+    def rotate(m, prod, ssq):
         gain = gain_ref[:, pl.ds(group_at(group, m), GW)]
         for h in range(GH):
             lanes = slice(h * HEAD_DIM, (h + 1) * HEAD_DIM)
             x = prod[:, lanes]
             ssq = x * x if ssq is None else ssq + x * x
             buf[m, :, lanes] = rope(x * gain[:, lanes], cosine, sine, even)
+        return ssq
+
+    before = None
+    for m in range(GROUPS):
+        weights[m].wait()
+        prod = jnp.dot(normed, wbuf[m], preferred_element_type=jnp.float32)
+        if before is not None:
+            ssq = rotate(m - 1, before, ssq)
+        before = prod
+    steps = list(beside)
+    if steps:
+        steps.pop(0)()
+    ssq = rotate(GROUPS - 1, before, ssq)
     inv = lax.rsqrt(jnp.sum(ssq, axis=-1, keepdims=True) / D + 1e-06)
     for m in range(GROUPS):
+        if steps:
+            steps.pop(0)()
         for h in range(GH):
             write(m, h, (buf[m, :, h * HEAD_DIM : (h + 1) * HEAD_DIM] * inv).astype(jnp.bfloat16))
 
@@ -274,12 +288,14 @@
     def write(m, h, x):
         kv_ref[m][0, h] = x
 
-    project_normed(group, normed, key_weights, wk_buf, buf, gain_ref, angles, write)
-    for m in range(GROUPS):
+    def value_block(m):
         value_weights[m].wait()
         prod = jnp.dot(normed, wv_buf[m], preferred_element_type=jnp.float32)
         for h in range(GH):
             kv_ref[m][1, h] = prod[:, h * HEAD_DIM : (h + 1) * HEAD_DIM].astype(jnp.bfloat16)
+
+    beside = [functools.partial(value_block, m) for m in range(GROUPS)]
+    project_normed(group, normed, key_weights, wk_buf, buf, gain_ref, angles, write, beside)
 
 
 def q_kernel(normed_hbm, nq_hbm, ft_hbm, rt_hbm, ct_hbm, wq_hbm, token_hbm, *refs):
@@ -364,25 +380,32 @@
     return lax.dot_general(query, keys, (((1,), (1,)), ((), ())), preferred_element_type=jnp.float32)
 
 
-def weigh(scores, peak, values):
-    expo = jnp.exp2((scores - peak) * SCORE_SCALE).astype(jnp.bfloat16)
-    ones = jnp.ones((values.shape[0], HEAD_DIM), jnp.bfloat16)
-    both = jnp.dot(expo, jnp.concatenate([values, ones], axis=1), preferred_element_type=jnp.float32)
-    return both[:, :HEAD_DIM], both[:, HEAD_DIM:]
-
-
-def attend(query, segments, state=None):
-    scores = [raw_scores(query, keys) for keys, _, _ in segments]
+def score(query, segments):
+    keys = jnp.concatenate([segment[0] for segment in segments], axis=0)
+    scores = raw_scores(query, keys)
+    at, parts = 0, []
+    for segment in segments:
+        parts.append(scores[:, at : at + segment[0].shape[0]])
+        at += segment[0].shape[0]
+    return parts
+
+
+def attend(scores, segments, state):
     found = [jnp.max(s, axis=-1, keepdims=True) for s in scores]
     found = [f if there is None else jnp.where(there, f, -1e30) for f, (_, _, there) in zip(found, segments)]
     peak = functools.reduce(jnp.maximum, found if state is None else [state[0], *found])
-    total = norm = None
+    weights = []
+    for s, (_, _, there) in zip(scores, segments):
+        low = peak if there is None else jnp.where(there, peak, 1e30)
+        weights.append(jnp.exp2((s - low) * SCORE_SCALE).astype(jnp.bfloat16))
+    weights = jnp.concatenate(weights, axis=1)
+    values = jnp.concatenate([segment[1] for segment in segments], axis=0)
+    ones = jnp.ones((values.shape[0], HEAD_DIM), jnp.bfloat16)
+    both = jnp.dot(weights, jnp.concatenate([values, ones], axis=1), preferred_element_type=jnp.float32)
+    total, norm = both[:, :HEAD_DIM], both[:, HEAD_DIM:]
     if state is not None:
         decay = jnp.exp2((state[0] - peak) * SCORE_SCALE)
-        total, norm = state[1] * decay, state[2] * decay
-    for s, (_, values, there) in zip(scores, segments):
-        part, weight = weigh(s, peak if there is None else jnp.where(there, peak, 1e30), values)
-        total, norm = (part, weight) if total is None else (total + part, norm + weight)
+        total, norm = total + state[1] * decay, norm + state[2] * decay
     return peak, total, norm
 
 
@@ -403,20 +426,28 @@
         return stat[:, :1], state_in[s][1][h], stat[:, HEAD_DIM // 2 : HEAD_DIM // 2 + 1]
 
     def run(slots):
-        for h in range(GH):
-            for n, s in enumerate(sorted(slots)):
-                segments = [
-                    (stack_keys(tiles, 0, h), stack_keys(tiles, 1, h), None if row is None else sc_ref[5 + row] == 1)
-                    for tiles, row in slots[s]
-                ]
-                peak, total, norm = attend(query_of(q, s, h), segments, state(s, h)) if segments else state(s, h)
-                if final:
-                    attended = (total / norm).astype(jnp.bfloat16)
-                    refs[2 * s][h] = attended[:TILE]
-                    refs[2 * s + 1][h] = attended[TILE:]
-                else:
-                    refs[2 * n][h] = jnp.where(low, peak, norm)
-                    refs[2 * n + 1][h] = total
+        jobs = [(h, n, s) for h in range(GH) for n, s in enumerate(sorted(slots))]
+
+        def begin(job):
+            h, _, s = job
+            segments = [
+                (stack_keys(tiles, 0, h), stack_keys(tiles, 1, h), None if row is None else sc_ref[5 + row] == 1)
+                for tiles, row in slots[s]
+            ]
+            return segments, score(query_of(q, s, h), segments) if segments else None
+
+        begun = begin(jobs[0])
+        for place, (h, n, s) in enumerate(jobs):
+            segments, scores = begun
+            begun = begin(jobs[place + 1]) if place + 1 < len(jobs) else None
+            peak, total, norm = attend(scores, segments, state(s, h)) if segments else state(s, h)
+            if final:
+                attended = (total / norm).astype(jnp.bfloat16)
+                refs[2 * s][h] = attended[:TILE]
+                refs[2 * s + 1][h] = attended[TILE:]
+            else:
+                refs[2 * n][h] = jnp.where(low, peak, norm)
+                refs[2 * n + 1][h] = total
 
     if plan[0] == plan[1]:
         run(plan[0])
@@ -447,34 +478,54 @@
 OUT_PARTS = 3
 
 
-def out_kernel(a0, a1, a2, a3, mod_ref, w_ref, out_hbm, out_ref, sems):
+def heads_wide(ref):
+    return jnp.concatenate([ref[h] for h in range(GH)], axis=1)
+
+
+def part_kernel(a0, a1, a2, w_ref, out_ref):
     group = mesh_place()[0]
-    rows = [jnp.concatenate([ref[h] for h in range(GH)], axis=1) for ref in (a0, a1, a2, a3)]
+    total = None
+    for m, ref in enumerate((a0, a1, a2)):
+        rows = w_ref[pl.ds(group_at(group, m), GW), :]
+        part = jnp.dot(heads_wide(ref), rows, preferred_element_type=jnp.float32)
+        total = part if total is None else total + part
+    out_ref[...] = total
+
+
+def out_kernel(part_ref, a3, mod_ref, w_ref, out_hbm, out_ref, sems):
+    group = mesh_place()[0]
+    rows = heads_wide(a3)
     width = D // OUT_PARTS
     copies = []
     for n in range(OUT_PARTS):
         lanes = slice(n * width, (n + 1) * width)
-        total = None
-        for m in range(GROUPS):
-            part = jnp.dot(rows[m], w_ref[pl.ds(group_at(group, m), GW), lanes], preferred_element_type=jnp.float32)
-            total = part if total is None else total + part
-        out_ref[:, lanes] = (total * mod_ref[2:3, lanes]).astype(jnp.bfloat16)
+        last = jnp.dot(rows, w_ref[pl.ds(group_at(group, GROUPS - 1), GW), lanes], preferred_element_type=jnp.float32)
+        out_ref[:, lanes] = ((part_ref[:, lanes] + last) * mod_ref[2:3, lanes]).astype(jnp.bfloat16)
         copies.append(pltpu.make_async_copy(out_ref.at[:, lanes], out_hbm.at[:, lanes], sems.at[n]))
         copies[-1].start()
     wait_all(copies)
 
 
 def project_out(attended, modulation, w_out):
+    part = pl.pallas_call(
+        part_kernel,
+        in_specs=[VMEM] * 4,
+        out_specs=VMEM,
+        out_shape=pltpu.VMEM((TILE, D), jnp.float32),
+        compiler_params=limit(20),
+        cost_estimate=pl.CostEstimate(flops=2 * TILE * D * D, bytes_accessed=2 * D * D, transcendentals=0),
+        name="project_part",
+    )(*attended[:3], w_out)
     return pl.pallas_call(
         out_kernel,
-        in_specs=[VMEM] * 6,
+        in_specs=[VMEM] * 4,
         out_specs=HBM,
         scratch_shapes=[pltpu.VMEM((TILE, D), jnp.bfloat16), pltpu.SemaphoreType.DMA((OUT_PARTS,))],
         out_shape=jax.ShapeDtypeStruct((TILE, D), jnp.bfloat16),
         compiler_params=limit(20),
-        cost_estimate=pl.CostEstimate(flops=2 * TILE * D * D, bytes_accessed=2 * D * D, transcendentals=0),
+        cost_estimate=pl.CostEstimate(flops=2 * TILE * D * GW, bytes_accessed=2 * D * GW, transcendentals=0),
         name="project_out",
-    )(*attended, modulation, w_out)
+    )(part, attended[3], modulation, w_out)
 
 
 def square_swap(value, m):

time: 77.5 us -> 73.9 us (0.954)
  Pallas kernels: 27.9 us -> 25.8 us
  waiting for transfers between devices: 19.5 us -> 17.6 us
    ppermute x8, waiting for transfers between devices: 18.4 us -> 16.5 us  [square_swap(): return lax.ppermute(value, ('ta', 'wa'), [(i, i ^ flip) for i in range(8)])]
    pallas_call x1, Pallas kernels: 6.61 us -> 5.67 us  [project_kv(): pl.pallas_call(kv_kernel, in_specs=[HBM] * 8, out_specs=[VMEM] * (GROUPS...]
    pallas_call x3, Pallas kernels: 15.5 us -> 14.6 us  [attend_call(): pl.pallas_call(functools.partial(attend_kernel, plan, len(arrays), tuple(...]
    pallas_call x1 -> x2, Pallas kernels: 2.1 us -> 2.27 us  [the longest x1 1.17 us: project_out(): pl.pallas_call(out_kernel, in_specs=[VMEM] * 4, out_specs=HBM, scratch_sh...]
  transfers between devices with their start and end apart: 23 -> 23, of which waited for: 7 -> 7; matrix products, arithmetic and copies ran while one was open for 2% -> 2% of each run, Pallas kernels for 17% -> 18%
where the time goes in v5:
time: 73.9 us; the launch traced here: 73.7 us
  Pallas kernels  25.8 us (35%)
  starting transfers between devices  25 us (34%)
  waiting for transfers between devices  17.6 us (24%)
  local copies, waits for them, and re-layouts  4.72 us (6%)
    ppermute x8, waiting for transfers between devices, square_swap(): return lax.ppermute(value, ('ta', 'wa'), [(i, i ^ flip) for i in range(8)])  16.5 us
    pallas_call x3, Pallas kernels, attend_call(): pl.pallas_call(functools.partial(attend_kernel, plan, len(arrays), tuple(...  14.6 us
    ppermute x6, starting transfers between devices, row_swap(): lax.ppermute(value, 'ha', [edge for i, j in pairs for edge in ((i, j), (j...  12.6 us
    ppermute x8, starting transfers between devices, square_swap(): return lax.ppermute(value, ('ta', 'wa'), [(i, i ^ flip) for i in range(8)])  10.3 us
    pallas_call x1, Pallas kernels, project_kv(): pl.pallas_call(kv_kernel, in_specs=[HBM] * 8, out_specs=[VMEM] * (GROUPS...  5.67 us
    unnamed x30, local copies, waits for them, and re-layouts  3.69 us
    pallas_call x1, Pallas kernels, project_q(): pl.pallas_call(q_kernel, in_specs=[HBM] * 7, out_specs=[VMEM] * (GROUPS +...  3.25 us
    ppermute x9, starting transfers between devices, core_swap(): return lax.ppermute(value, 'ta', [(i, i ^ 1) for i in range(4)])  2.12 us
  transfers between devices with their start and end apart: 23, of which 7 were waited for; matrix products, arithmetic and copies ran while one was open for 2% of the time, Pallas kernels for 18%

profile of v5, /device:TPU:0, one launch (start us, length us, event | category | flops | bytes accessed | tf_op | source)
XLA Modules:
  0.0 73.7 jit_solution(4384984256814255920)
XLA Ops:
  0.0 5.7 %project_kv.1 = (bf16[2,3,192,128]{3,2,1,0:T(8,128)(2,1)S(1)}, bf16[2,3,192,128]{3,2,1,0:T(8,128)(2,1)S(1)}, bf16[2,3,192,128]{3,2,1,0:T(8,128)(2,1)S(1)}, bf16[...) custom-call(bf16[192,1536]{1,0:T(8,128)(2,1)} %bitcast.19, f32[3,1536]{1,0:T(4,128)} %mod_ref.1, f32[1536]{0:T(1024)} %nk_hbm.1, ...), custom_call_target="tpu_custom_call" | custom-call | flops 1811939328 | bytes 9437184 | tf_op jit(solution)/shard_map/project_kv/pallas_call | solution.py:332
  5.7 0.5 collective-permute-start
  6.2 2.7 %collective-permute-start.3 = (bf16[2,3,192,128]{3,2,1,0:T(8,128)(2,1)S(1)}, bf16[2,3,192,128]{3,2,1,0:T(8,128)(2,1)S(1)}, u32[]{:S(2)}, u32[]{:S(2)}) collective-permute-start(bf16[2,3,192,128]{3,2,1,0:T(8,128)(2,1)S(1)} %get-tuple-element.33.refs_4_), channel_id=1, source_target_pairs={{0,2},{2,0},{4,6},{6,4},{1,3},{3,1},{5,7},{7,5},{8,10},{10,8},{12,... | collective-permute-start | bytes 884744 | tf_op jit(solution)/shard_map/ppermute | solution.py:544
  8.9 0.7 collective-permute-start.4
  9.6 1.6 %collective-permute-start.1 = (bf16[2,3,192,128]{3,2,1,0:T(8,128)(2,1)S(1)}, bf16[2,3,192,128]{3,2,1,0:T(8,128)(2,1)S(1)}, u32[]{:S(2)}, u32[]{:S(2)}) collective-permute-start(bf16[2,3,192,128]{3,2,1,0:T(8,128)(2,1)S(1)} %get-tuple-element.36), channel_id=1, source_target_pairs={{0,1},{1,0},{8,9},{9,8},{16,17},{17,16},{24,25},{25,24},{2,3},{3,2... | collective-permute-start | bytes 884744 | tf_op jit(solution)/shard_map/ppermute | solution.py:535
  11.1 1.5 %collective-permute-start.2 = (bf16[2,3,192,128]{3,2,1,0:T(8,128)(2,1)S(1)}, bf16[2,3,192,128]{3,2,1,0:T(8,128)(2,1)S(1)}, u32[]{:S(2)}, u32[]{:S(2)}) collective-permute-start(bf16[2,3,192,128]{3,2,1,0:T(8,128)(2,1)S(1)} %get-tuple-element.37), channel_id=1, source_target_pairs={{0,16},{1,17},{8,24},{9,25},{16,0},{17,1},{24,8},{25,9},{2,18},{3,... | collective-permute-start | bytes 884744 | tf_op jit(solution)/shard_map/ppermute | solution.py:535
  12.6 0.0 collective-permute-done.refs_6_
  12.7 3.3 %project_q.1 = (bf16[3,192,128]{2,1,0:T(8,128)(2,1)S(1)}, bf16[3,192,128]{2,1,0:T(8,128)(2,1)S(1)}, bf16[3,192,128]{2,1,0:T(8,128)(2,1)S(1)}, bf16[3,192,128]{2,1,0:T(8,128)(2,1)S(1)}, f32[8,128]{1,0:T(8,128)}) custom-call(bf16[192,1536]{1,0:T(8,128)(2,1)S(1)} %get-tuple-element.34.normed_hbm.token_hbm, f32[1536]{0:T(1024)S(1)} %copy-done.11, ...), custom_call_target="tpu_custom_call" | custom-call | flops 905969664 | bytes 4718592 | tf_op jit(solution)/shard_map/project_q/pallas_call | solution.py:355
  15.9 0.6 collective-permute-start.7
  16.5 0.0 collective-permute-done.3.refs_4_
  16.5 1.6 %collective-permute-start.8 = (bf16[3,192,128]{2,1,0:T(8,128)(2,1)S(1)}, bf16[3,192,128]{2,1,0:T(8,128)(2,1)S(1)}, u32[]{:S(2)}, u32[]{:S(2)}) collective-permute-start(bf16[3,192,128]{2,1,0:T(8,128)(2,1)S(1)} %get-tuple-element.42), channel_id=1, source_target_pairs={{0,16},{1,17},{8,24},{9,25},{16,0},{17,1},{24,8},{25,9},{2,18},{3,... | collective-permute-start | bytes 442376 | tf_op jit(solution)/shard_map/ppermute | solution.py:535
  18.2 1.0 %collective-permute-done.1 = bf16[2,3,192,128]{3,2,1,0:T(8,128)(2,1)S(1)} collective-permute-done((bf16[2,3,192,128]{3,2,1,0:T(8,128)(2,1)S(1)}, bf16[2,3,192,128]{3,2,1,0:T(8,128)(2,1)S(1)}, u32[]{:S(2)}, u32[]{:S(2)}) %collective-permute-start.1) | collective-permute-done | bytes 294944 | tf_op jit(solution)/shard_map/ppermute | solution.py:535
  19.1 1.7 %collective-permute-done.2 = bf16[2,3,192,128]{3,2,1,0:T(8,128)(2,1)S(1)} collective-permute-done((bf16[2,3,192,128]{3,2,1,0:T(8,128)(2,1)S(1)}, bf16[2,3,192,128]{3,2,1,0:T(8,128)(2,1)S(1)}, u32[]{:S(2)}, u32[]{:S(2)}) %collective-permute-start.2) | collective-permute-done | bytes 294944 | tf_op jit(solution)/shard_map/ppermute | solution.py:535
  20.9 0.1 pad_maximum_fusion.refs_5_
  21.0 4.6 %collective-permute-start.5 = (bf16[2,2,3,192,128]{4,3,2,1,0:T(8,128)(2,1)S(1)}, bf16[2,2,3,192,128]{4,3,2,1,0:T(8,128)(2,1)S(1)}, u32[]{:S(2)}, u32[]{:S(2)}) collective-permute-start(bf16[2,2,3,192,128]{4,3,2,1,0:T(8,128)(2,1)S(1)} %pad_maximum_fusion.refs_5_), channel_id=1, source_target_pairs={{0,2},{2,0},{4,6},{6,4},{1,3},{3,1},{5,7},{7,5},{8,10},{10,8},{12,... | collective-permute-start | bytes 1769480 | tf_op jit(solution)/shard_map/ppermute | solution.py:544
  25.6 0.0 collective-permute-done.8.refs_2_
  25.7 1.5 %collective-permute-start.9 = (bf16[3,3,192,128]{3,2,1,0:T(8,128)(2,1)S(1)}, bf16[3,3,192,128]{3,2,1,0:T(8,128)(2,1)S(1)}, u32[]{:S(2)}, u32[]{:S(2)}) collective-permute-start(bf16[3,3,192,128]{3,2,1,0:T(8,128)(2,1)S(1)} %pad_maximum_fusion.1), channel_id=1, source_target_pairs={{0,17},{1,16},{8,25},{9,24},{16,1},{17,0},{24,9},{25,8},{2,19},{3,... | collective-permute-start | bytes 1327112 | tf_op jit(solution)/shard_map/ppermute | solution.py:535
  27.2 0.7 collective-permute-start.6
  27.8 0.1 collective-permute-start.11
  27.9 7.8 %collective-permute-done.9 = bf16[3,3,192,128]{3,2,1,0:T(8,128)(2,1)S(1)} collective-permute-done((bf16[3,3,192,128]{3,2,1,0:T(8,128)(2,1)S(1)}, bf16[3,3,192,128]{3,2,1,0:T(8,128)(2,1)S(1)}, u32[]{:S(2)}, u32[]{:S(2)}) %collective-permute-start.9) | collective-permute-done | bytes 442400 | tf_op jit(solution)/shard_map/ppermute | solution.py:535
  35.7 0.8 %copy-done.12 = bf16[3,3,192,128]{3,2,1,0:T(8,128)(2,1)} copy-done((bf16[3,3,192,128]{3,2,1,0:T(8,128)(2,1)}, bf16[3,3,192,128]{3,2,1,0:T(8,128)(2,1)S(1)}, u32[]{:S(2)}) %copy-start.12) | copy-done | bytes 442392
  36.5 0.1 collective-permute-start.12
  36.6 0.1 stack.48.sc_ref
  36.7 3.3 %collective-permute-start.13 = (bf16[2,3,192,128]{3,2,1,0:T(8,128)(2,1)S(1)}, bf16[2,3,192,128]{3,2,1,0:T(8,128)(2,1)S(1)}, u32[]{:S(2)}, u32[]{:S(2)}) collective-permute-start(bf16[2,3,192,128]{3,2,1,0:T(8,128)(2,1)S(1)} %slice.14.refs_9_), channel_id=1, source_target_pairs={{0,2},{2,0},{4,6},{6,4},{1,3},{3,1},{5,7},{7,5},{8,10},{10,8},{12,... | collective-permute-start | bytes 884744 | tf_op jit(solution)/shard_map/ppermute | solution.py:544
  40.0 0.7 collective-permute-start.16
  40.7 0.9 %slice_bitcast_fusion.refs_3_ = bf16[3,192,128]{2,1,0:T(8,128)(2,1)S(1)} fusion(bf16[3,3,192,128]{3,2,1,0:T(8,128)(2,1)} %copy-done.12), kind=kLoop, calls=%fused_computation.4 | loop fusion | bytes 294912 | tf_op jit(solution)/shard_map/squeeze | solution.py:631
  41.6 0.2 collective-permute-start.18
  41.9 0.3 collective-permute-start.10
  42.2 0.2 collective-permute-start.15
  42.4 1.0 %copy-done.4 = bf16[2,3,192,128]{3,2,1,0:T(8,128)(2,1)S(1)} copy-done((bf16[2,3,192,128]{3,2,1,0:T(8,128)(2,1)S(1)}, bf16[2,3,192,128]{3,2,1,0:T(8,128)(2,1)}, u32[]{:S(2)}) %copy-start.4) | copy-done | bytes 294936
  43.3 1.0 %copy-done.6 = bf16[2,3,192,128]{3,2,1,0:T(8,128)(2,1)S(1)} copy-done((bf16[2,3,192,128]{3,2,1,0:T(8,128)(2,1)S(1)}, bf16[2,3,192,128]{3,2,1,0:T(8,128)(2,1)}, u32[]{:S(2)}) %copy-start.6) | copy-done | bytes 294936
  44.3 4.3 %attend_own.1 = (f32[3,384,128]{2,1,0:T(8,128)S(1)}, f32[3,384,128]{2,1,0:T(8,128)S(1)}, f32[3,384,128]{2,1,0:T(8,128)S(1)}, f32[3,384,128]{2,1,0:T(8,128)S(1)}, f32[8,128]{1,0:T(8,128)S(1)}) custom-call(s32[7]{0:T(128)S(1)} %stack.48.sc_ref, bf16[3,192,128]{2,1,0:T(8,128)(2,1)S(1)} %get-tuple-element.40.refs_0_, ...), custom_call_target="tpu_custom_call" | custom-call | flops 1000 | bytes 1000 | tf_op jit(solution)/shard_map/attend_own/pallas_call | solution.py:467
  48.7 0.1 collective-permute-start.19
  48.8 0.0 slice-start
  48.8 0.5 collective-permute-start.14
  49.4 0.1 collective-permute-start.17
  49.5 1.1 %collective-permute-done.19.refs_10_.refs_13_ = bf16[2,3,192,128]{3,2,1,0:T(8,128)(2,1)S(1)} collective-permute-done((bf16[2,3,192,128]{3,2,1,0:T(8,128)(2,1)}, bf16[2,3,192,128]{3,2,1,0:T(8,128)(2,1)S(1)}, u32[]{:S(2)}, u32[]{:S(2)}) %collective-permute-start.19) | collective-permute-done | bytes 294944 | tf_op jit(solution)/shard_map/ppermute | solution.py:539
  50.5 1.0 %copy-done.2 = bf16[2,3,192,128]{3,2,1,0:T(8,128)(2,1)S(1)} copy-done((bf16[2,3,192,128]{3,2,1,0:T(8,128)(2,1)S(1)}, bf16[2,3,192,128]{3,2,1,0:T(8,128)(2,1)}, u32[]{:S(2)}) %copy-start.2) | copy-done | bytes 294936
  51.5 4.5 %attend_halo.1 = (f32[3,384,128]{2,1,0:T(8,128)S(1)}, f32[3,384,128]{2,1,0:T(8,128)S(1)}, f32[3,384,128]{2,1,0:T(8,128)S(1)}, f32[3,384,128]{2,1,0:T(8,128)S(1)}, f32[8,128]{1,0:T(8,128)}) custom-call(s32[7]{0:T(128)S(1)} %stack.48.sc_ref, bf16[3,192,128]{2,1,0:T(8,128)(2,1)S(1)} %get-tuple-element.40.refs_0_, ...), custom_call_target="tpu_custom_call" | custom-call | flops 1000 | bytes 1000 | tf_op jit(solution)/shard_map/attend_halo/pallas_call | solution.py:467
  56.0 5.7 %attend_last.1 = (bf16[3,192,128]{2,1,0:T(8,128)(2,1)S(1)}, bf16[3,192,128]{2,1,0:T(8,128)(2,1)S(1)}, bf16[3,192,128]{2,1,0:T(8,128)(2,1)S(1)}, bf16[3,192,128]{2,1,0:T(8,128)(2,1)S(1)}, f32[8,128]{1,0:T(8,128)}) custom-call(s32[7]{0:T(128)S(1)} %stack.48.sc_ref, bf16[3,192,128]{2,1,0:T(8,128)(2,1)S(1)} %get-tuple-element.40.refs_0_, ...), custom_call_target="tpu_custom_call" | custom-call | flops 1000 | bytes 1000 | tf_op jit(solution)/shard_map/attend_last/pallas_call | solution.py:467
  61.8 0.6 collective-permute-start.20
  62.4 1.8 %collective-permute-start.21 = (bf16[3,192,128]{2,1,0:T(8,128)(2,1)S(1)}, bf16[3,192,128]{2,1,0:T(8,128)(2,1)S(1)}, u32[]{:S(2)}, u32[]{:S(2)}) collective-permute-start(bf16[3,192,128]{2,1,0:T(8,128)(2,1)S(1)} %get-tuple-element.57), channel_id=1, source_target_pairs={{0,16},{1,17},{8,24},{9,25},{16,0},{17,1},{24,8},{25,9},{2,18},{3,... | collective-permute-start | bytes 442376 | tf_op jit(solution)/shard_map/ppermute | solution.py:535
  64.1 1.1 %collective-permute-start.22 = (bf16[3,192,128]{2,1,0:T(8,128)(2,1)S(1)}, bf16[3,192,128]{2,1,0:T(8,128)(2,1)S(1)}, u32[]{:S(2)}, u32[]{:S(2)}) collective-permute-start(bf16[3,192,128]{2,1,0:T(8,128)(2,1)S(1)} %get-tuple-element.58), channel_id=1, source_target_pairs={{0,17},{1,16},{8,25},{9,24},{16,1},{17,0},{24,9},{25,8},{2,19},{3,... | collective-permute-start | bytes 442376 | tf_op jit(solution)/shard_map/ppermute | solution.py:535
  65.2 2.7 %collective-permute-done.20.a1 = bf16[3,192,128]{2,1,0:T(8,128)(2,1)S(1)} collective-permute-done((bf16[3,192,128]{2,1,0:T(8,128)(2,1)S(1)}, bf16[3,192,128]{2,1,0:T(8,128)(2,1)S(1)}, u32[]{:S(2)}, u32[]{:S(2)}) %collective-permute-start.20) | collective-permute-done | bytes 147488 | tf_op jit(solution)/shard_map/ppermute | solution.py:535
  68.0 1.1 %collective-permute-done.21.a2 = bf16[3,192,128]{2,1,0:T(8,128)(2,1)S(1)} collective-permute-done((bf16[3,192,128]{2,1,0:T(8,128)(2,1)S(1)}, bf16[3,192,128]{2,1,0:T(8,128)(2,1)S(1)}, u32[]{:S(2)}, u32[]{:S(2)}) %collective-permute-start.21) | collective-permute-done | bytes 147488 | tf_op jit(solution)/shard_map/ppermute | solution.py:535
  69.1 1.1 %project_part.1.part_ref = f32[192,1536]{1,0:T(8,128)S(1)} custom-call(bf16[3,192,128]{2,1,0:T(8,128)(2,1)S(1)} %get-tuple-element.55.a0, bf16[3,192,128]{2,1,0:T(8,128)(2,1)S(1)} %collective-permute-done.20.a1, bf16[3,192,128]{2,1,0:T(8,128)(2,1)S(1)} %collective-permute-done.21.a2, bf16[1536,1536]{1,0:T(8,128)(2,1)S(1)} %bitcast.17), custom_call_target="tpu_custom_call" | custom-call | flops 905969664 | bytes 4718592 | tf_op jit(solution)/shard_map/project_part/pallas_call | solution.py:510
  70.1 2.2 %collective-permute-done.22.a3 = bf16[3,192,128]{2,1,0:T(8,128)(2,1)S(1)} collective-permute-done((bf16[3,192,128]{2,1,0:T(8,128)(2,1)S(1)}, bf16[3,192,128]{2,1,0:T(8,128)(2,1)S(1)}, u32[]{:S(2)}, u32[]{:S(2)}) %collective-permute-start.22) | collective-permute-done | bytes 147488 | tf_op jit(solution)/shard_map/ppermute | solution.py:535
  72.3 1.2 %project_out.1 = bf16[192,1536]{1,0:T(8,128)(2,1)} custom-call(f32[192,1536]{1,0:T(8,128)S(1)} %project_part.1.part_ref, bf16[3,192,128]{2,1,0:T(8,128)(2,1)S(1)} %collective-permute-done.22.a3, f32[3,1536]{1,0:T(4,128)S(1)} %copy-done.8, bf16[1536,1536]{1,0:T(8,128)(2,1)S(1)} %bitcast.17), custom_call_target="tpu_custom_call" | custom-call | flops 226492416 | bytes 1179648 | tf_op jit(solution)/shard_map/project_out/pallas_call | solution.py:519
  (43 shorter events, 0.2 us)
Async XLA Ops:
  0.0 12.6 %copy-start = (bf16[1536,1536]{1,0:T(8,128)(2,1)S(1)}, bf16[1536,1536]{1,0:T(8,128)(2,1)}, u32[]{:S(2)}) copy-start(bf16[1536,1536]{1,0:T(8,128)(2,1)} %wq_hbm.1) | copy-start | bytes 14155780
  0.0 12.6 %copy-start.7 = (f32[4,2,8,128]{3,2,1,0:T(8,128)S(1)}, f32[4,2,8,128]{3,2,1,0:T(8,128)}, u32[]{:S(2)}) copy-start(f32[4,2,8,128]{3,2,1,0:T(8,128)} %constant.57.clone.rt_hbm) | copy-start | bytes 98308
  0.0 12.6 %copy-start.9 = (f32[4,2,3,128]{3,2,1,0:T(4,128)S(1)}, f32[4,2,3,128]{3,2,1,0:T(4,128)}, u32[]{:S(2)}) copy-start(f32[4,2,3,128]{3,2,1,0:T(4,128)} %constant.56.clone.ft_hbm) | copy-start | bytes 36868
  0.0 12.7 %copy-start.10 = (f32[2,2,8,128]{3,2,1,0:T(8,128)S(1)}, f32[2,2,8,128]{3,2,1,0:T(8,128)}, u32[]{:S(2)}) copy-start(f32[2,2,8,128]{3,2,1,0:T(8,128)} %constant.58.clone.ct_hbm) | copy-start | bytes 49156
  0.0 12.7 %copy-start.11 = (f32[1536]{0:T(1024)S(1)}, f32[1536]{0:T(1024)}, u32[]{:S(2)}) copy-start(f32[1536]{0:T(1024)} %nq_hbm.1) | copy-start | bytes 18436
  5.7 15.2 %copy-start.3 = (bf16[2,3,192,128]{3,2,1,0:T(8,128)(2,1)}, bf16[2,3,192,128]{3,2,1,0:T(8,128)(2,1)S(1)}, u32[]{:S(2)}) copy-start(bf16[2,3,192,128]{3,2,1,0:T(8,128)(2,1)S(1)} %get-tuple-element.33.refs_4_) | copy-start | bytes 884740
  5.7 6.9 %collective-permute-start = (bf16[2,3,192,128]{3,2,1,0:T(8,128)(2,1)S(1)}, bf16[2,3,192,128]{3,2,1,0:T(8,128)(2,1)S(1)}, u32[]{:S(2)}, u32[]{:S(2)}) collective-permute-start(bf16[2,3,192,128]{3,2,1,0:T(8,128)(2,1)S(1)} %get-tuple-element.33.refs_4_), channel_id=1, source_target_pairs={{0,8},{8,0},{16,24},{24,16},{1,9},{9,1},{17,25},{25,17},{2,10},{10... | collective-permute-start | bytes 884744 | tf_op jit(solution)/shard_map/ppermute | solution.py:539
  6.2 10.3 %collective-permute-start.3 = (bf16[2,3,192,128]{3,2,1,0:T(8,128)(2,1)S(1)}, bf16[2,3,192,128]{3,2,1,0:T(8,128)(2,1)S(1)}, u32[]{:S(2)}, u32[]{:S(2)}) collective-permute-start(bf16[2,3,192,128]{3,2,1,0:T(8,128)(2,1)S(1)} %get-tuple-element.33.refs_4_), channel_id=1, source_target_pairs={{0,2},{2,0},{4,6},{6,4},{1,3},{3,1},{5,7},{7,5},{8,10},{10,8},{12,... | collective-permute-start | bytes 884744 | tf_op jit(solution)/shard_map/ppermute | solution.py:544
  8.9 9.3 %collective-permute-start.4 = (bf16[2,3,192,128]{3,2,1,0:T(8,128)(2,1)S(1)}, bf16[2,3,192,128]{3,2,1,0:T(8,128)(2,1)S(1)}, u32[]{:S(2)}, u32[]{:S(2)}) collective-permute-start(bf16[2,3,192,128]{3,2,1,0:T(8,128)(2,1)S(1)} %get-tuple-element.33.refs_4_), channel_id=1, source_target_pairs={{2,4},{4,2},{3,5},{5,3},{10,12},{12,10},{11,13},{13,11},{18,20},{2... | collective-permute-start | bytes 884744 | tf_op jit(solution)/shard_map/ppermute | solution.py:544
  9.6 9.6 %collective-permute-start.1 = (bf16[2,3,192,128]{3,2,1,0:T(8,128)(2,1)S(1)}, bf16[2,3,192,128]{3,2,1,0:T(8,128)(2,1)S(1)}, u32[]{:S(2)}, u32[]{:S(2)}) collective-permute-start(bf16[2,3,192,128]{3,2,1,0:T(8,128)(2,1)S(1)} %get-tuple-element.36), channel_id=1, source_target_pairs={{0,1},{1,0},{8,9},{9,8},{16,17},{17,16},{24,25},{25,24},{2,3},{3,2... | collective-permute-start | bytes 884744 | tf_op jit(solution)/shard_map/ppermute | solution.py:535
  11.1 9.7 %collective-permute-start.2 = (bf16[2,3,192,128]{3,2,1,0:T(8,128)(2,1)S(1)}, bf16[2,3,192,128]{3,2,1,0:T(8,128)(2,1)S(1)}, u32[]{:S(2)}, u32[]{:S(2)}) collective-permute-start(bf16[2,3,192,128]{3,2,1,0:T(8,128)(2,1)S(1)} %get-tuple-element.37), channel_id=1, source_target_pairs={{0,16},{1,17},{8,24},{9,25},{16,0},{17,1},{24,8},{25,9},{2,18},{3,... | collective-permute-start | bytes 884744 | tf_op jit(solution)/shard_map/ppermute | solution.py:535
  12.6 8.3 %copy-start.5 = (bf16[2,3,192,128]{3,2,1,0:T(8,128)(2,1)}, bf16[2,3,192,128]{3,2,1,0:T(8,128)(2,1)S(1)}, u32[]{:S(2)}) copy-start(bf16[2,3,192,128]{3,2,1,0:T(8,128)(2,1)S(1)} %collective-permute-done.refs_6_) | copy-start | bytes 884740
  15.9 9.7 %collective-permute-start.7 = (bf16[3,192,128]{2,1,0:T(8,128)(2,1)S(1)}, bf16[3,192,128]{2,1,0:T(8,128)(2,1)S(1)}, u32[]{:S(2)}, u32[]{:S(2)}) collective-permute-start(bf16[3,192,128]{2,1,0:T(8,128)(2,1)S(1)} %get-tuple-element.41), channel_id=1, source_target_pairs={{0,1},{1,0},{8,9},{9,8},{16,17},{17,16},{24,25},{25,24},{2,3},{3,2... | collective-permute-start | bytes 442376 | tf_op jit(solution)/shard_map/ppermute | solution.py:535
  16.5 9.1 %collective-permute-start.8 = (bf16[3,192,128]{2,1,0:T(8,128)(2,1)S(1)}, bf16[3,192,128]{2,1,0:T(8,128)(2,1)S(1)}, u32[]{:S(2)}, u32[]{:S(2)}) collective-permute-start(bf16[3,192,128]{2,1,0:T(8,128)(2,1)S(1)} %get-tuple-element.42), channel_id=1, source_target_pairs={{0,16},{1,17},{8,24},{9,25},{16,0},{17,1},{24,8},{25,9},{2,18},{3,... | collective-permute-start | bytes 442376 | tf_op jit(solution)/shard_map/ppermute | solution.py:535
  18.2 7.5 %copy-start.1 = (bf16[2,3,192,128]{3,2,1,0:T(8,128)(2,1)}, bf16[2,3,192,128]{3,2,1,0:T(8,128)(2,1)S(1)}, u32[]{:S(2)}) copy-start(bf16[2,3,192,128]{3,2,1,0:T(8,128)(2,1)S(1)} %collective-permute-done.4.refs_8_) | copy-start | bytes 884740
  21.0 19.0 %collective-permute-start.5 = (bf16[2,2,3,192,128]{4,3,2,1,0:T(8,128)(2,1)S(1)}, bf16[2,2,3,192,128]{4,3,2,1,0:T(8,128)(2,1)S(1)}, u32[]{:S(2)}, u32[]{:S(2)}) collective-permute-start(bf16[2,2,3,192,128]{4,3,2,1,0:T(8,128)(2,1)S(1)} %pad_maximum_fusion.refs_5_), channel_id=1, source_target_pairs={{0,2},{2,0},{4,6},{6,4},{1,3},{3,1},{5,7},{7,5},{8,10},{10,8},{12,... | collective-permute-start | bytes 1769480 | tf_op jit(solution)/shard_map/ppermute | solution.py:544
  25.7 10.0 %collective-permute-start.9 = (bf16[3,3,192,128]{3,2,1,0:T(8,128)(2,1)S(1)}, bf16[3,3,192,128]{3,2,1,0:T(8,128)(2,1)S(1)}, u32[]{:S(2)}, u32[]{:S(2)}) collective-permute-start(bf16[3,3,192,128]{3,2,1,0:T(8,128)(2,1)S(1)} %pad_maximum_fusion.1), channel_id=1, source_target_pairs={{0,17},{1,16},{8,25},{9,24},{16,1},{17,0},{24,9},{25,8},{2,19},{3,... | collective-permute-start | bytes 1327112 | tf_op jit(solution)/shard_map/ppermute | solution.py:535
  27.2 14.4 %collective-permute-start.6 = (bf16[2,2,3,192,128]{4,3,2,1,0:T(8,128)(2,1)S(1)}, bf16[2,2,3,192,128]{4,3,2,1,0:T(8,128)(2,1)S(1)}, u32[]{:S(2)}, u32[]{:S(2)}) collective-permute-start(bf16[2,2,3,192,128]{4,3,2,1,0:T(8,128)(2,1)S(1)} %pad_maximum_fusion.refs_5_), channel_id=1, source_target_pairs={{2,4},{4,2},{3,5},{5,3},{10,12},{12,10},{11,13},{13,11},{18,20},{2... | collective-permute-start | bytes 1769480 | tf_op jit(solution)/shard_map/ppermute | solution.py:544
  27.8 14.0 %collective-permute-start.11 = (bf16[2,2,3,192,128]{4,3,2,1,0:T(8,128)(2,1)S(1)}, bf16[2,2,3,192,128]{4,3,2,1,0:T(8,128)(2,1)S(1)}, u32[]{:S(2)}, u32[]{:S(2)}) collective-permute-start(bf16[2,2,3,192,128]{4,3,2,1,0:T(8,128)(2,1)S(1)} %pad_maximum_fusion.refs_5_), channel_id=1, source_target_pairs={{0,8},{8,0},{16,24},{24,16},{1,9},{9,1},{17,25},{25,17},{2,10},{10... | collective-permute-start | bytes 1769480 | tf_op jit(solution)/shard_map/ppermute | solution.py:539
  35.7 0.8 %copy-start.12 = (bf16[3,3,192,128]{3,2,1,0:T(8,128)(2,1)}, bf16[3,3,192,128]{3,2,1,0:T(8,128)(2,1)S(1)}, u32[]{:S(2)}) copy-start(bf16[3,3,192,128]{3,2,1,0:T(8,128)(2,1)S(1)} %collective-permute-done.9) | copy-start | bytes 1327108
  36.5 5.7 %collective-permute-start.12 = (bf16[2,3,192,128]{3,2,1,0:T(8,128)(2,1)S(1)}, bf16[2,3,192,128]{3,2,1,0:T(8,128)(2,1)}, u32[]{:S(2)}, u32[]{:S(2)}) collective-permute-start(bf16[2,3,192,128]{3,2,1,0:T(8,128)(2,1)S(1)} %slice.14.refs_9_), channel_id=1, source_target_pairs={{0,8},{8,0},{16,24},{24,16},{1,9},{9,1},{17,25},{25,17},{2,10},{10... | collective-permute-start | bytes 884744 | tf_op jit(solution)/shard_map/ppermute | solution.py:539
  36.7 12.0 %collective-permute-start.13 = (bf16[2,3,192,128]{3,2,1,0:T(8,128)(2,1)S(1)}, bf16[2,3,192,128]{3,2,1,0:T(8,128)(2,1)S(1)}, u32[]{:S(2)}, u32[]{:S(2)}) collective-permute-start(bf16[2,3,192,128]{3,2,1,0:T(8,128)(2,1)S(1)} %slice.14.refs_9_), channel_id=1, source_target_pairs={{0,2},{2,0},{4,6},{6,4},{1,3},{3,1},{5,7},{7,5},{8,10},{10,8},{12,... | collective-permute-start | bytes 884744 | tf_op jit(solution)/shard_map/ppermute | solution.py:544
  40.0 8.8 %collective-permute-start.16 = (bf16[2,3,192,128]{3,2,1,0:T(8,128)(2,1)S(1)}, bf16[2,3,192,128]{3,2,1,0:T(8,128)(2,1)S(1)}, u32[]{:S(2)}, u32[]{:S(2)}) collective-permute-start(bf16[2,3,192,128]{3,2,1,0:T(8,128)(2,1)S(1)} %slice.14.refs_9_), channel_id=1, source_target_pairs={{2,4},{4,2},{3,5},{5,3},{10,12},{12,10},{11,13},{13,11},{18,20},{2... | collective-permute-start | bytes 884744 | tf_op jit(solution)/shard_map/ppermute | solution.py:544
  41.6 7.8 %collective-permute-start.18 = (bf16[2,3,192,128]{3,2,1,0:T(8,128)(2,1)S(1)}, bf16[2,3,192,128]{3,2,1,0:T(8,128)(2,1)S(1)}, u32[]{:S(2)}, u32[]{:S(2)}) collective-permute-start(bf16[2,3,192,128]{3,2,1,0:T(8,128)(2,1)S(1)} %collective-permute-done.3.refs_4_), channel_id=1, source_target_pairs={{0,8},{8,0},{16,24},{24,16},{1,9},{9,1},{17,25},{25,17},{2,10},{10... | collective-permute-start | bytes 884744 | tf_op jit(solution)/shard_map/ppermute | solution.py:539
  41.9 8.7 %collective-permute-start.10 = (bf16[2,2,3,192,128]{4,3,2,1,0:T(8,128)(2,1)S(1)}, bf16[2,2,3,192,128]{4,3,2,1,0:T(8,128)(2,1)S(1)}, u32[]{:S(2)}, u32[]{:S(2)}) collective-permute-start(bf16[2,2,3,192,128]{4,3,2,1,0:T(8,128)(2,1)S(1)} %collective-permute-done.5.refs_5_.refs_8_), channel_id=1, source_target_pairs={{0,8},{8,0},{16,24},{24,16},{1,9},{9,1},{17,25},{25,17},{2,10},{10... | collective-permute-start | bytes 1769480 | tf_op jit(solution)/shard_map/ppermute | solution.py:539
  42.2 8.3 %collective-permute-start.15 = (bf16[2,2,3,192,128]{4,3,2,1,0:T(8,128)(2,1)S(1)}, bf16[2,2,3,192,128]{4,3,2,1,0:T(8,128)(2,1)S(1)}, u32[]{:S(2)}, u32[]{:S(2)}) collective-permute-start(bf16[2,2,3,192,128]{4,3,2,1,0:T(8,128)(2,1)S(1)} %collective-permute-done.6.refs_9_.refs_10_), channel_id=1, source_target_pairs={{0,8},{8,0},{16,24},{24,16},{1,9},{9,1},{17,25},{25,17},{2,10},{10... | collective-permute-start | bytes 1769480 | tf_op jit(solution)/shard_map/ppermute | solution.py:539
  42.4 1.0 %copy-start.4 = (bf16[2,3,192,128]{3,2,1,0:T(8,128)(2,1)S(1)}, bf16[2,3,192,128]{3,2,1,0:T(8,128)(2,1)}, u32[]{:S(2)}) copy-start(bf16[2,3,192,128]{3,2,1,0:T(8,128)(2,1)} %copy-done.3) | copy-start | bytes 884740
  43.3 1.0 %copy-start.6 = (bf16[2,3,192,128]{3,2,1,0:T(8,128)(2,1)S(1)}, bf16[2,3,192,128]{3,2,1,0:T(8,128)(2,1)}, u32[]{:S(2)}) copy-start(bf16[2,3,192,128]{3,2,1,0:T(8,128)(2,1)} %copy-done.5) | copy-start | bytes 884740
  48.7 1.9 %collective-permute-start.19 = (bf16[2,3,192,128]{3,2,1,0:T(8,128)(2,1)}, bf16[2,3,192,128]{3,2,1,0:T(8,128)(2,1)S(1)}, u32[]{:S(2)}, u32[]{:S(2)}) collective-permute-start(bf16[2,3,192,128]{3,2,1,0:T(8,128)(2,1)} %copy-done.1), channel_id=1, source_target_pairs={{0,8},{8,0},{16,24},{24,16},{1,9},{9,1},{17,25},{25,17},{2,10},{10... | collective-permute-start | bytes 884744 | tf_op jit(solution)/shard_map/ppermute | solution.py:539
  48.8 20.3 %slice-start = ((s8[4718592]{0:T(1024)(128)(4,1)}), s8[4194304]{0:T(1024)(128)(4,1)S(1)}, s32[]{:S(2)}) async-start(s8[4718592]{0:T(1024)(128)(4,1)} %bitcast.16), calls=%async_computation | async-start | bytes 8388608
  48.8 7.2 %collective-permute-start.14 = (bf16[2,3,192,128]{3,2,1,0:T(8,128)(2,1)S(1)}, bf16[2,3,192,128]{3,2,1,0:T(8,128)(2,1)S(1)}, u32[]{:S(2)}, u32[]{:S(2)}) collective-permute-start(bf16[2,3,192,128]{3,2,1,0:T(8,128)(2,1)S(1)} %get-tuple-element.60), channel_id=1, source_target_pairs={{0,8},{8,0},{16,24},{24,16},{1,9},{9,1},{17,25},{25,17},{2,10},{10... | collective-permute-start | bytes 884744 | tf_op jit(solution)/shard_map/ppermute | solution.py:539
  49.4 6.6 %collective-permute-start.17 = (bf16[2,3,192,128]{3,2,1,0:T(8,128)(2,1)S(1)}, bf16[2,3,192,128]{3,2,1,0:T(8,128)(2,1)S(1)}, u32[]{:S(2)}, u32[]{:S(2)}) collective-permute-start(bf16[2,3,192,128]{3,2,1,0:T(8,128)(2,1)S(1)} %get-tuple-element.59), channel_id=1, source_target_pairs={{0,8},{8,0},{16,24},{24,16},{1,9},{9,1},{17,25},{25,17},{2,10},{10... | collective-permute-start | bytes 884744 | tf_op jit(solution)/shard_map/ppermute | solution.py:539
  50.5 1.0 %copy-start.2 = (bf16[2,3,192,128]{3,2,1,0:T(8,128)(2,1)S(1)}, bf16[2,3,192,128]{3,2,1,0:T(8,128)(2,1)}, u32[]{:S(2)}) copy-start(bf16[2,3,192,128]{3,2,1,0:T(8,128)(2,1)} %copy-done.1) | copy-start | bytes 884740
  51.5 17.5 %slice-start.1 = ((s8[4718592]{0:T(1024)(128)(4,1)}), s8[524288]{0:T(1024)(128)(4,1)S(1)}, s32[]{:S(2)}) async-start(s8[4718592]{0:T(1024)(128)(4,1)} %bitcast.16), calls=%async_computation.1 | async-start | bytes 1048576
  61.7 10.6 %copy-start.8 = (f32[3,1536]{1,0:T(4,128)S(1)}, f32[3,1536]{1,0:T(4,128)}, u32[]{:S(2)}) copy-start(f32[3,1536]{1,0:T(4,128)} %mod_ref.1) | copy-start | bytes 55300
  61.8 6.2 %collective-permute-start.20 = (bf16[3,192,128]{2,1,0:T(8,128)(2,1)S(1)}, bf16[3,192,128]{2,1,0:T(8,128)(2,1)S(1)}, u32[]{:S(2)}, u32[]{:S(2)}) collective-permute-start(bf16[3,192,128]{2,1,0:T(8,128)(2,1)S(1)} %get-tuple-element.56), channel_id=1, source_target_pairs={{0,1},{1,0},{8,9},{9,8},{16,17},{17,16},{24,25},{25,24},{2,3},{3,2... | collective-permute-start | bytes 442376 | tf_op jit(solution)/shard_map/ppermute | solution.py:535
  62.4 6.7 %collective-permute-start.21 = (bf16[3,192,128]{2,1,0:T(8,128)(2,1)S(1)}, bf16[3,192,128]{2,1,0:T(8,128)(2,1)S(1)}, u32[]{:S(2)}, u32[]{:S(2)}) collective-permute-start(bf16[3,192,128]{2,1,0:T(8,128)(2,1)S(1)} %get-tuple-element.57), channel_id=1, source_target_pairs={{0,16},{1,17},{8,24},{9,25},{16,0},{17,1},{24,8},{25,9},{2,18},{3,... | collective-permute-start | bytes 442376 | tf_op jit(solution)/shard_map/ppermute | solution.py:535
  64.1 8.2 %collective-permute-start.22 = (bf16[3,192,128]{2,1,0:T(8,128)(2,1)S(1)}, bf16[3,192,128]{2,1,0:T(8,128)(2,1)S(1)}, u32[]{:S(2)}, u32[]{:S(2)}) collective-permute-start(bf16[3,192,128]{2,1,0:T(8,128)(2,1)S(1)} %get-tuple-element.58), channel_id=1, source_target_pairs={{0,17},{1,16},{8,25},{9,24},{16,1},{17,0},{24,9},{25,8},{2,19},{3,... | collective-permute-start | bytes 442376 | tf_op jit(solution)/shard_map/ppermute | solution.py:535

commit v6 on v5

--- a/solution.py
+++ b/solution.py
@@ -410,7 +410,7 @@
 
 
 def attend_kernel(plan, arrays_n, state_slots, final, sc_ref, *refs):
-    q, arrays, refs = refs[:4], refs[4 : 4 + arrays_n], refs[4 + arrays_n :]
+    q, arrays, refs = [*refs[:3], refs[3].at[2]], refs[4 : 4 + arrays_n], refs[4 + arrays_n :]
     state_in = {s: refs[2 * n : 2 * n + 2] for n, s in enumerate(state_slots)}
     *refs, token_ref = refs[2 * len(state_slots) :]
     token_ref[...] = jnp.zeros_like(token_ref)
@@ -573,15 +573,15 @@
     def rows_of(tile):
         return [row_swap(tile, first, rows_n) for first in range(2)]
 
+    halo0 = rows_of(kv[0])
     other0 = core_swap(kv[0])
-    halo0 = rows_of(kv[0])
     side = [square_swap(kv[1], 1), square_swap(kv[2], 2)]
     *queries, made = project_q(after(normed, other0), norm_q, tables, w_query, normed)
     middle = jnp.stack(after(side, queries[0], *halo0))
     halo12, other12 = rows_of(middle), core_swap(middle)
     mine3 = queries[3][None]
     queries[1:3] = [square_swap(queries[m], m) for m in range(1, 3)]
-    corner = square_swap(jnp.concatenate([kv[3], after(mine3, queries[1], queries[2])]), 3)
+    corner = square_swap(jnp.concatenate([kv[3], mine3]), 3)
     queries[0] = after(queries[0], *halo12)
     swapped0 = [core_swap(tile) for tile in halo0]
     halo_parts = {"same": [halo0, halo12, None], "other": [swapped0, None, None]}
@@ -619,7 +619,7 @@
                         ids.append(numbers[key])
                     made[s] += ((tuple(ids), row),)
             numbered.append(made)
-        return attend_call(name, tuple(numbered), sc, queries, arrays, state)
+        return attend_call(name, tuple(numbered), sc, [*queries[:3], bundle], arrays, state)
 
     def both(*places):
         return [(kind, m) for kind in ("same", "other") for m in places]
@@ -628,8 +628,8 @@
         return [row_keys(kinds, r) for r in range(2)]
 
     cross = [("other", 2), ("other", 3)], [("other", 0), ("other", 1)]
-    queries[3], corner = corner[2], corner[:2]
-    own["same"][3], own["other"][3] = (corner, ()), (core_swap(corner), ())
+    queries[3], bundle, corner = None, corner, corner[:2]
+    own["same"][3], own["other"][3] = (bundle, ()), (core_swap(bundle), ())
     halo_parts["other"][1] = [core_swap(tile) for tile in halo12]
     *state, made = call(
         "attend_own",
@@ -650,7 +650,7 @@
         ({0: rows_keys(cross[0]), 1: rows_keys(both(2, 3))}, {0: [], 1: rows_keys(both(2, 3) + cross[1])}),
         {0: state[:2], 1: state[2:]},
     )
-    attended = [square_swap(attended[m], m) for m in range(GROUPS)]
+    attended = [square_swap(attended[m], m) for m in reversed(range(GROUPS))][::-1]
     branch = project_out(attended, modulation, w_out)
     return branch.reshape(CT, CH, CW, D)
 

time: 73.9 us -> 73.3 us (level)
  local copies, waits for them, and re-layouts: 4.72 us -> 1.83 us
  waiting for transfers between devices: 17.6 us -> 19.1 us
  Pallas kernels: 25.8 us -> 26.7 us
    unnamed x30 -> x28, local copies, waits for them, and re-layouts: 3.69 us -> 1.01 us
    ppermute x8, waiting for transfers between devices: 16.5 us -> 18 us  [square_swap(): return lax.ppermute(value, ('ta', 'wa'), [(i, i ^ flip) for i in range(8)])]
    squeeze x1 -> x0, local copies, waits for them, and re-layouts: 0.92 us -> none  [square_body(): queries[3], corner = (corner[2], corner[:2])]
  transfers between devices with their start and end apart: 23 -> 23, of which waited for: 7 -> 8; matrix products, arithmetic and copies ran while one was open for 2% -> 1% of each run, Pallas kernels for 18% -> 19%
where the time goes in v6:
time: 73.3 us; the launch traced here: 73.1 us
  Pallas kernels  26.7 us (36%)
  starting transfers between devices  25 us (34%)
  waiting for transfers between devices  19.1 us (26%)
  local copies, waits for them, and re-layouts  1.83 us (2%)
    ppermute x8, waiting for transfers between devices, square_swap(): return lax.ppermute(value, ('ta', 'wa'), [(i, i ^ flip) for i in range(8)])  18 us
    pallas_call x3, Pallas kernels, attend_call(): pl.pallas_call(functools.partial(attend_kernel, plan, len(arrays), tuple(...  14.9 us
    ppermute x6, starting transfers between devices, row_swap(): lax.ppermute(value, 'ha', [edge for i, j in pairs for edge in ((i, j), (j...  12.9 us
    ppermute x8, starting transfers between devices, square_swap(): return lax.ppermute(value, ('ta', 'wa'), [(i, i ^ flip) for i in range(8)])  10.1 us
    pallas_call x1, Pallas kernels, project_kv(): pl.pallas_call(kv_kernel, in_specs=[HBM] * 8, out_specs=[VMEM] * (GROUPS...  5.67 us
    pallas_call x1, Pallas kernels, project_q(): pl.pallas_call(q_kernel, in_specs=[HBM] * 7, out_specs=[VMEM] * (GROUPS +...  3.88 us
    ppermute x9, starting transfers between devices, core_swap(): return lax.ppermute(value, 'ta', [(i, i ^ 1) for i in range(4)])  1.96 us
  transfers between devices with their start and end apart: 23, of which 8 were waited for; matrix products, arithmetic and copies ran while one was open for 1% of the time, Pallas kernels for 19%

profile of v6, /device:TPU:0, one launch (start us, length us, event | category | flops | bytes accessed | tf_op | source)
XLA Modules:
  0.0 73.1 jit_solution(2096352718840575119)
XLA Ops:
  0.0 5.7 %project_kv.1 = (bf16[2,3,192,128]{3,2,1,0:T(8,128)(2,1)S(1)}, bf16[2,3,192,128]{3,2,1,0:T(8,128)(2,1)S(1)}, bf16[2,3,192,128]{3,2,1,0:T(8,128)(2,1)S(1)}, bf16[...) custom-call(bf16[192,1536]{1,0:T(8,128)(2,1)} %bitcast.17, f32[3,1536]{1,0:T(4,128)} %mod_ref.1, f32[1536]{0:T(1024)} %nk_hbm.1, ...), custom_call_target="tpu_custom_call" | custom-call | flops 1811939328 | bytes 9437184 | tf_op jit(solution)/shard_map/project_kv/pallas_call | solution.py:332
  5.7 0.5 collective-permute-start
  6.2 2.7 %collective-permute-start.3 = (bf16[2,3,192,128]{3,2,1,0:T(8,128)(2,1)S(1)}, bf16[2,3,192,128]{3,2,1,0:T(8,128)(2,1)S(1)}, u32[]{:S(2)}, u32[]{:S(2)}) collective-permute-start(bf16[2,3,192,128]{3,2,1,0:T(8,128)(2,1)S(1)} %get-tuple-element.32.refs_4_), channel_id=1, source_target_pairs={{0,2},{2,0},{4,6},{6,4},{1,3},{3,1},{5,7},{7,5},{8,10},{10,8},{12,... | collective-permute-start | bytes 884744 | tf_op jit(solution)/shard_map/ppermute | solution.py:544
  8.9 0.7 collective-permute-start.4
  9.6 1.6 %collective-permute-start.1 = (bf16[2,3,192,128]{3,2,1,0:T(8,128)(2,1)S(1)}, bf16[2,3,192,128]{3,2,1,0:T(8,128)(2,1)S(1)}, u32[]{:S(2)}, u32[]{:S(2)}) collective-permute-start(bf16[2,3,192,128]{3,2,1,0:T(8,128)(2,1)S(1)} %get-tuple-element.35), channel_id=1, source_target_pairs={{0,1},{1,0},{8,9},{9,8},{16,17},{17,16},{24,25},{25,24},{2,3},{3,2... | collective-permute-start | bytes 884744 | tf_op jit(solution)/shard_map/ppermute | solution.py:535
  11.1 1.5 %collective-permute-start.2 = (bf16[2,3,192,128]{3,2,1,0:T(8,128)(2,1)S(1)}, bf16[2,3,192,128]{3,2,1,0:T(8,128)(2,1)S(1)}, u32[]{:S(2)}, u32[]{:S(2)}) collective-permute-start(bf16[2,3,192,128]{3,2,1,0:T(8,128)(2,1)S(1)} %get-tuple-element.36), channel_id=1, source_target_pairs={{0,16},{1,17},{8,24},{9,25},{16,0},{17,1},{24,8},{25,9},{2,18},{3,... | collective-permute-start | bytes 884744 | tf_op jit(solution)/shard_map/ppermute | solution.py:535
  12.6 0.0 collective-permute-done.refs_6_
  12.7 3.9 %project_q.1 = (bf16[3,192,128]{2,1,0:T(8,128)(2,1)S(1)}, bf16[3,192,128]{2,1,0:T(8,128)(2,1)S(1)}, bf16[3,192,128]{2,1,0:T(8,128)(2,1)}, bf16[3,192,128]{2,1,0:T(8,128)(2,1)S(1)}, f32[8,128]{1,0:T(8,128)}) custom-call(bf16[192,1536]{1,0:T(8,128)(2,1)S(1)} %get-tuple-element.33.normed_hbm.token_hbm, f32[1536]{0:T(1024)S(1)} %copy-done.11, ...), custom_call_target="tpu_custom_call" | custom-call | flops 905969664 | bytes 4718592 | tf_op jit(solution)/shard_map/project_q/pallas_call | solution.py:355
  16.6 0.5 collective-permute-start.9
  17.2 0.0 collective-permute-done.3.refs_4_
  17.2 0.0 collective-permute-done.4.refs_8_
  17.2 1.5 %collective-permute-done.1 = bf16[2,3,192,128]{3,2,1,0:T(8,128)(2,1)S(1)} collective-permute-done((bf16[2,3,192,128]{3,2,1,0:T(8,128)(2,1)S(1)}, bf16[2,3,192,128]{3,2,1,0:T(8,128)(2,1)S(1)}, u32[]{:S(2)}, u32[]{:S(2)}) %collective-permute-start.1) | collective-permute-done | bytes 294944 | tf_op jit(solution)/shard_map/ppermute | solution.py:535
  18.7 2.3 %collective-permute-done.2 = bf16[2,3,192,128]{3,2,1,0:T(8,128)(2,1)S(1)} collective-permute-done((bf16[2,3,192,128]{3,2,1,0:T(8,128)(2,1)S(1)}, bf16[2,3,192,128]{3,2,1,0:T(8,128)(2,1)S(1)}, u32[]{:S(2)}, u32[]{:S(2)}) %collective-permute-start.2) | collective-permute-done | bytes 294944 | tf_op jit(solution)/shard_map/ppermute | solution.py:535
  21.0 0.1 pad_maximum_fusion.refs_5_
  21.1 4.1 %collective-permute-start.5 = (bf16[2,2,3,192,128]{4,3,2,1,0:T(8,128)(2,1)S(1)}, bf16[2,2,3,192,128]{4,3,2,1,0:T(8,128)(2,1)S(1)}, u32[]{:S(2)}, u32[]{:S(2)}) collective-permute-start(bf16[2,2,3,192,128]{4,3,2,1,0:T(8,128)(2,1)S(1)} %pad_maximum_fusion.refs_5_), channel_id=1, source_target_pairs={{0,2},{2,0},{4,6},{6,4},{1,3},{3,1},{5,7},{7,5},{8,10},{10,8},{12,... | collective-permute-start | bytes 1769480 | tf_op jit(solution)/shard_map/ppermute | solution.py:544
  25.2 0.7 collective-permute-start.6
  25.9 0.1 collective-permute-start.11
  26.0 3.4 %collective-permute-done.9.refs_3_.refs_9_ = bf16[3,3,192,128]{3,2,1,0:T(8,128)(2,1)S(1)} collective-permute-done((bf16[3,3,192,128]{3,2,1,0:T(8,128)(2,1)S(1)}, bf16[3,3,192,128]{3,2,1,0:T(8,128)(2,1)S(1)}, u32[]{:S(2)}, u32[]{:S(2)}) %collective-permute-start.9) | collective-permute-done | bytes 442400 | tf_op jit(solution)/shard_map/ppermute | solution.py:535
  29.4 0.0 collective-permute-start.12
  29.4 1.5 %collective-permute-start.7 = (bf16[3,192,128]{2,1,0:T(8,128)(2,1)S(1)}, bf16[3,192,128]{2,1,0:T(8,128)(2,1)S(1)}, u32[]{:S(2)}, u32[]{:S(2)}) collective-permute-start(bf16[3,192,128]{2,1,0:T(8,128)(2,1)S(1)} %get-tuple-element.40), channel_id=1, source_target_pairs={{0,1},{1,0},{8,9},{9,8},{16,17},{17,16},{24,25},{25,24},{2,3},{3,2... | collective-permute-start | bytes 442376 | tf_op jit(solution)/shard_map/ppermute | solution.py:535
  30.9 4.7 %collective-permute-done.7.refs_1_ = bf16[3,192,128]{2,1,0:T(8,128)(2,1)S(1)} collective-permute-done((bf16[3,192,128]{2,1,0:T(8,128)(2,1)S(1)}, bf16[3,192,128]{2,1,0:T(8,128)(2,1)S(1)}, u32[]{:S(2)}, u32[]{:S(2)}) %collective-permute-start.7) | collective-permute-done | bytes 147488 | tf_op jit(solution)/shard_map/ppermute | solution.py:535
  35.6 1.5 %collective-permute-start.8 = (bf16[3,192,128]{2,1,0:T(8,128)(2,1)}, bf16[3,192,128]{2,1,0:T(8,128)(2,1)S(1)}, u32[]{:S(2)}, u32[]{:S(2)}) collective-permute-start(bf16[3,192,128]{2,1,0:T(8,128)(2,1)} %get-tuple-element.41), channel_id=1, source_target_pairs={{0,16},{1,17},{8,24},{9,25},{16,0},{17,1},{24,8},{25,9},{2,18},{3,... | collective-permute-start | bytes 442376 | tf_op jit(solution)/shard_map/ppermute | solution.py:535
  37.1 0.7 %slice.9 = bf16[2,3,192,128]{3,2,1,0:T(8,128)(2,1)} slice(bf16[3,3,192,128]{3,2,1,0:T(8,128)(2,1)S(1)} %collective-permute-done.9.refs_3_.refs_9_), slice={[0:2], [0:3], [0:192], [0:128]} | slice | bytes 589824 | tf_op jit(solution)/shard_map/slice | solution.py:631
  37.8 0.0 collective-permute-done.5.refs_5_.refs_8_
  37.9 4.1 %collective-permute-start.13 = (bf16[2,3,192,128]{3,2,1,0:T(8,128)(2,1)}, bf16[2,3,192,128]{3,2,1,0:T(8,128)(2,1)S(1)}, u32[]{:S(2)}, u32[]{:S(2)}) collective-permute-start(bf16[2,3,192,128]{3,2,1,0:T(8,128)(2,1)} %slice.9), channel_id=1, source_target_pairs={{0,2},{2,0},{4,6},{6,4},{1,3},{3,1},{5,7},{7,5},{8,10},{10,8},{12,... | collective-permute-start | bytes 884744 | tf_op jit(solution)/shard_map/ppermute | solution.py:544
  42.0 0.7 collective-permute-start.16
  42.7 0.1 stack.48.sc_ref
  42.8 0.0 collective-permute-start.18
  42.8 0.5 collective-permute-start.10
  43.3 0.0 collective-permute-done.12.refs_8_
  43.3 0.1 collective-permute-start.15
  43.4 1.0 %copy-done.2 = bf16[2,3,192,128]{3,2,1,0:T(8,128)(2,1)S(1)} copy-done((bf16[2,3,192,128]{3,2,1,0:T(8,128)(2,1)S(1)}, bf16[2,3,192,128]{3,2,1,0:T(8,128)(2,1)}, u32[]{:S(2)}) %copy-start.2) | copy-done | bytes 294936
  44.4 4.6 %attend_own.1 = (f32[3,384,128]{2,1,0:T(8,128)S(1)}, f32[3,384,128]{2,1,0:T(8,128)S(1)}, f32[3,384,128]{2,1,0:T(8,128)S(1)}, f32[3,384,128]{2,1,0:T(8,128)S(1)}, f32[8,128]{1,0:T(8,128)S(1)}) custom-call(s32[7]{0:T(128)S(1)} %stack.48.sc_ref, bf16[3,192,128]{2,1,0:T(8,128)(2,1)S(1)} %get-tuple-element.39.refs_0_, ...), custom_call_target="tpu_custom_call" | custom-call | flops 1000 | bytes 1000 | tf_op jit(solution)/shard_map/attend_own/pallas_call | solution.py:467
  49.0 0.1 collective-permute-start.19
  49.2 0.5 collective-permute-start.14
  49.7 0.1 collective-permute-start.17
  49.8 1.1 %collective-permute-done.19.refs_10_.refs_13_ = bf16[2,3,192,128]{3,2,1,0:T(8,128)(2,1)S(1)} collective-permute-done((bf16[2,3,192,128]{3,2,1,0:T(8,128)(2,1)}, bf16[2,3,192,128]{3,2,1,0:T(8,128)(2,1)S(1)}, u32[]{:S(2)}, u32[]{:S(2)}) %collective-permute-start.19) | collective-permute-done | bytes 294944 | tf_op jit(solution)/shard_map/ppermute | solution.py:539
  50.9 0.0 slice-start.1
  50.9 4.5 %attend_halo.1 = (f32[3,384,128]{2,1,0:T(8,128)S(1)}, f32[3,384,128]{2,1,0:T(8,128)S(1)}, f32[3,384,128]{2,1,0:T(8,128)S(1)}, f32[3,384,128]{2,1,0:T(8,128)S(1)}, f32[8,128]{1,0:T(8,128)}) custom-call(s32[7]{0:T(128)S(1)} %stack.48.sc_ref, bf16[3,192,128]{2,1,0:T(8,128)(2,1)S(1)} %get-tuple-element.39.refs_0_, ...), custom_call_target="tpu_custom_call" | custom-call | flops 1000 | bytes 1000 | tf_op jit(solution)/shard_map/attend_halo/pallas_call | solution.py:467
  55.4 5.8 %attend_last.1 = (bf16[3,192,128]{2,1,0:T(8,128)(2,1)S(1)}, bf16[3,192,128]{2,1,0:T(8,128)(2,1)S(1)}, bf16[3,192,128]{2,1,0:T(8,128)(2,1)S(1)}, bf16[3,192,128]{2,1,0:T(8,128)(2,1)S(1)}, f32[8,128]{1,0:T(8,128)}) custom-call(s32[7]{0:T(128)S(1)} %stack.48.sc_ref, bf16[3,192,128]{2,1,0:T(8,128)(2,1)S(1)} %get-tuple-element.39.refs_0_, ...), custom_call_target="tpu_custom_call" | custom-call | flops 1000 | bytes 1000 | tf_op jit(solution)/shard_map/attend_last/pallas_call | solution.py:467
  61.2 1.5 %collective-permute-start.20 = (bf16[3,192,128]{2,1,0:T(8,128)(2,1)S(1)}, bf16[3,192,128]{2,1,0:T(8,128)(2,1)S(1)}, u32[]{:S(2)}, u32[]{:S(2)}) collective-permute-start(bf16[3,192,128]{2,1,0:T(8,128)(2,1)S(1)} %get-tuple-element.54), channel_id=1, source_target_pairs={{0,1},{1,0},{8,9},{9,8},{16,17},{17,16},{24,25},{25,24},{2,3},{3,2... | collective-permute-start | bytes 442376 | tf_op jit(solution)/shard_map/ppermute | solution.py:535
  62.7 0.9 %collective-permute-start.21 = (bf16[3,192,128]{2,1,0:T(8,128)(2,1)S(1)}, bf16[3,192,128]{2,1,0:T(8,128)(2,1)S(1)}, u32[]{:S(2)}, u32[]{:S(2)}) collective-permute-start(bf16[3,192,128]{2,1,0:T(8,128)(2,1)S(1)} %get-tuple-element.55), channel_id=1, source_target_pairs={{0,16},{1,17},{8,24},{9,25},{16,0},{17,1},{24,8},{25,9},{2,18},{3,... | collective-permute-start | bytes 442376 | tf_op jit(solution)/shard_map/ppermute | solution.py:535
  63.6 1.0 %collective-permute-start.22 = (bf16[3,192,128]{2,1,0:T(8,128)(2,1)S(1)}, bf16[3,192,128]{2,1,0:T(8,128)(2,1)S(1)}, u32[]{:S(2)}, u32[]{:S(2)}) collective-permute-start(bf16[3,192,128]{2,1,0:T(8,128)(2,1)S(1)} %get-tuple-element.56), channel_id=1, source_target_pairs={{0,17},{1,16},{8,25},{9,24},{16,1},{17,0},{24,9},{25,8},{2,19},{3,... | collective-permute-start | bytes 442376 | tf_op jit(solution)/shard_map/ppermute | solution.py:535
  64.7 2.7 %collective-permute-done.20.a1 = bf16[3,192,128]{2,1,0:T(8,128)(2,1)S(1)} collective-permute-done((bf16[3,192,128]{2,1,0:T(8,128)(2,1)S(1)}, bf16[3,192,128]{2,1,0:T(8,128)(2,1)S(1)}, u32[]{:S(2)}, u32[]{:S(2)}) %collective-permute-start.20) | collective-permute-done | bytes 147488 | tf_op jit(solution)/shard_map/ppermute | solution.py:535
  67.4 2.0 %collective-permute-done.21.a2 = bf16[3,192,128]{2,1,0:T(8,128)(2,1)S(1)} collective-permute-done((bf16[3,192,128]{2,1,0:T(8,128)(2,1)S(1)}, bf16[3,192,128]{2,1,0:T(8,128)(2,1)S(1)}, u32[]{:S(2)}, u32[]{:S(2)}) %collective-permute-start.21) | collective-permute-done | bytes 147488 | tf_op jit(solution)/shard_map/ppermute | solution.py:535
  69.4 1.1 %project_part.1.part_ref = f32[192,1536]{1,0:T(8,128)S(1)} custom-call(bf16[3,192,128]{2,1,0:T(8,128)(2,1)S(1)} %get-tuple-element.53.a0, bf16[3,192,128]{2,1,0:T(8,128)(2,1)S(1)} %collective-permute-done.20.a1, bf16[3,192,128]{2,1,0:T(8,128)(2,1)S(1)} %collective-permute-done.21.a2, bf16[1536,1536]{1,0:T(8,128)(2,1)S(1)} %bitcast.15), custom_call_target="tpu_custom_call" | custom-call | flops 905969664 | bytes 4718592 | tf_op jit(solution)/shard_map/project_part/pallas_call | solution.py:510
  70.5 1.3 %collective-permute-done.22.a3 = bf16[3,192,128]{2,1,0:T(8,128)(2,1)S(1)} collective-permute-done((bf16[3,192,128]{2,1,0:T(8,128)(2,1)S(1)}, bf16[3,192,128]{2,1,0:T(8,128)(2,1)S(1)}, u32[]{:S(2)}, u32[]{:S(2)}) %collective-permute-start.22) | collective-permute-done | bytes 147488 | tf_op jit(solution)/shard_map/ppermute | solution.py:535
  71.8 1.2 %project_out.1 = bf16[192,1536]{1,0:T(8,128)(2,1)} custom-call(f32[192,1536]{1,0:T(8,128)S(1)} %project_part.1.part_ref, bf16[3,192,128]{2,1,0:T(8,128)(2,1)S(1)} %collective-permute-done.22.a3, f32[3,1536]{1,0:T(4,128)S(1)} %copy-done.8, bf16[1536,1536]{1,0:T(8,128)(2,1)S(1)} %bitcast.15), custom_call_target="tpu_custom_call" | custom-call | flops 226492416 | bytes 1179648 | tf_op jit(solution)/shard_map/project_out/pallas_call | solution.py:519
  (40 shorter events, 0.2 us)
Async XLA Ops:
  0.0 12.6 %copy-start = (bf16[1536,1536]{1,0:T(8,128)(2,1)S(1)}, bf16[1536,1536]{1,0:T(8,128)(2,1)}, u32[]{:S(2)}) copy-start(bf16[1536,1536]{1,0:T(8,128)(2,1)} %wq_hbm.1) | copy-start | bytes 14155780
  0.0 12.6 %copy-start.7 = (f32[4,2,8,128]{3,2,1,0:T(8,128)S(1)}, f32[4,2,8,128]{3,2,1,0:T(8,128)}, u32[]{:S(2)}) copy-start(f32[4,2,8,128]{3,2,1,0:T(8,128)} %constant.57.clone.rt_hbm) | copy-start | bytes 98308
  0.0 12.6 %copy-start.9 = (f32[4,2,3,128]{3,2,1,0:T(4,128)S(1)}, f32[4,2,3,128]{3,2,1,0:T(4,128)}, u32[]{:S(2)}) copy-start(f32[4,2,3,128]{3,2,1,0:T(4,128)} %constant.56.clone.ft_hbm) | copy-start | bytes 36868
  0.0 12.6 %copy-start.10 = (f32[2,2,8,128]{3,2,1,0:T(8,128)S(1)}, f32[2,2,8,128]{3,2,1,0:T(8,128)}, u32[]{:S(2)}) copy-start(f32[2,2,8,128]{3,2,1,0:T(8,128)} %constant.58.clone.ct_hbm) | copy-start | bytes 49156
  0.0 12.7 %copy-start.11 = (f32[1536]{0:T(1024)S(1)}, f32[1536]{0:T(1024)}, u32[]{:S(2)}) copy-start(f32[1536]{0:T(1024)} %nq_hbm.1) | copy-start | bytes 18436
  5.7 6.9 %collective-permute-start = (bf16[2,3,192,128]{3,2,1,0:T(8,128)(2,1)S(1)}, bf16[2,3,192,128]{3,2,1,0:T(8,128)(2,1)S(1)}, u32[]{:S(2)}, u32[]{:S(2)}) collective-permute-start(bf16[2,3,192,128]{3,2,1,0:T(8,128)(2,1)S(1)} %get-tuple-element.32.refs_4_), channel_id=1, source_target_pairs={{0,8},{8,0},{16,24},{24,16},{1,9},{9,1},{17,25},{25,17},{2,10},{10... | collective-permute-start | bytes 884744 | tf_op jit(solution)/shard_map/ppermute | solution.py:539
  6.2 10.9 %collective-permute-start.3 = (bf16[2,3,192,128]{3,2,1,0:T(8,128)(2,1)S(1)}, bf16[2,3,192,128]{3,2,1,0:T(8,128)(2,1)S(1)}, u32[]{:S(2)}, u32[]{:S(2)}) collective-permute-start(bf16[2,3,192,128]{3,2,1,0:T(8,128)(2,1)S(1)} %get-tuple-element.32.refs_4_), channel_id=1, source_target_pairs={{0,2},{2,0},{4,6},{6,4},{1,3},{3,1},{5,7},{7,5},{8,10},{10,8},{12,... | collective-permute-start | bytes 884744 | tf_op jit(solution)/shard_map/ppermute | solution.py:544
  8.9 8.3 %collective-permute-start.4 = (bf16[2,3,192,128]{3,2,1,0:T(8,128)(2,1)S(1)}, bf16[2,3,192,128]{3,2,1,0:T(8,128)(2,1)S(1)}, u32[]{:S(2)}, u32[]{:S(2)}) collective-permute-start(bf16[2,3,192,128]{3,2,1,0:T(8,128)(2,1)S(1)} %get-tuple-element.32.refs_4_), channel_id=1, source_target_pairs={{2,4},{4,2},{3,5},{5,3},{10,12},{12,10},{11,13},{13,11},{18,20},{2... | collective-permute-start | bytes 884744 | tf_op jit(solution)/shard_map/ppermute | solution.py:544
  9.6 9.1 %collective-permute-start.1 = (bf16[2,3,192,128]{3,2,1,0:T(8,128)(2,1)S(1)}, bf16[2,3,192,128]{3,2,1,0:T(8,128)(2,1)S(1)}, u32[]{:S(2)}, u32[]{:S(2)}) collective-permute-start(bf16[2,3,192,128]{3,2,1,0:T(8,128)(2,1)S(1)} %get-tuple-element.35), channel_id=1, source_target_pairs={{0,1},{1,0},{8,9},{9,8},{16,17},{17,16},{24,25},{25,24},{2,3},{3,2... | collective-permute-start | bytes 884744 | tf_op jit(solution)/shard_map/ppermute | solution.py:535
  11.1 9.9 %collective-permute-start.2 = (bf16[2,3,192,128]{3,2,1,0:T(8,128)(2,1)S(1)}, bf16[2,3,192,128]{3,2,1,0:T(8,128)(2,1)S(1)}, u32[]{:S(2)}, u32[]{:S(2)}) collective-permute-start(bf16[2,3,192,128]{3,2,1,0:T(8,128)(2,1)S(1)} %get-tuple-element.36), channel_id=1, source_target_pairs={{0,16},{1,17},{8,24},{9,25},{16,0},{17,1},{24,8},{25,9},{2,18},{3,... | collective-permute-start | bytes 884744 | tf_op jit(solution)/shard_map/ppermute | solution.py:535
  12.6 29.3 %copy-start.1 = (bf16[2,3,192,128]{3,2,1,0:T(8,128)(2,1)}, bf16[2,3,192,128]{3,2,1,0:T(8,128)(2,1)S(1)}, u32[]{:S(2)}) copy-start(bf16[2,3,192,128]{3,2,1,0:T(8,128)(2,1)S(1)} %collective-permute-done.refs_6_) | copy-start | bytes 884740
  16.6 12.7 %collective-permute-start.9 = (bf16[3,3,192,128]{3,2,1,0:T(8,128)(2,1)S(1)}, bf16[3,3,192,128]{3,2,1,0:T(8,128)(2,1)S(1)}, u32[]{:S(2)}, u32[]{:S(2)}) collective-permute-start(bf16[3,3,192,128]{3,2,1,0:T(8,128)(2,1)S(1)} %pad_maximum_fusion.1), channel_id=1, source_target_pairs={{0,17},{1,16},{8,25},{9,24},{16,1},{17,0},{24,9},{25,8},{2,19},{3,... | collective-permute-start | bytes 1327112 | tf_op jit(solution)/shard_map/ppermute | solution.py:535
  17.2 3.9 %copy-start.3 = (bf16[2,3,192,128]{3,2,1,0:T(8,128)(2,1)}, bf16[2,3,192,128]{3,2,1,0:T(8,128)(2,1)S(1)}, u32[]{:S(2)}) copy-start(bf16[2,3,192,128]{3,2,1,0:T(8,128)(2,1)S(1)} %collective-permute-done.3.refs_4_) | copy-start | bytes 884740
  17.2 3.9 %copy-start.5 = (bf16[2,3,192,128]{3,2,1,0:T(8,128)(2,1)}, bf16[2,3,192,128]{3,2,1,0:T(8,128)(2,1)S(1)}, u32[]{:S(2)}) copy-start(bf16[2,3,192,128]{3,2,1,0:T(8,128)(2,1)S(1)} %collective-permute-done.4.refs_8_) | copy-start | bytes 884740
  21.1 16.8 %collective-permute-start.5 = (bf16[2,2,3,192,128]{4,3,2,1,0:T(8,128)(2,1)S(1)}, bf16[2,2,3,192,128]{4,3,2,1,0:T(8,128)(2,1)S(1)}, u32[]{:S(2)}, u32[]{:S(2)}) collective-permute-start(bf16[2,2,3,192,128]{4,3,2,1,0:T(8,128)(2,1)S(1)} %pad_maximum_fusion.refs_5_), channel_id=1, source_target_pairs={{0,2},{2,0},{4,6},{6,4},{1,3},{3,1},{5,7},{7,5},{8,10},{10,8},{12,... | collective-permute-start | bytes 1769480 | tf_op jit(solution)/shard_map/ppermute | solution.py:544
  25.2 16.7 %collective-permute-start.6 = (bf16[2,2,3,192,128]{4,3,2,1,0:T(8,128)(2,1)S(1)}, bf16[2,2,3,192,128]{4,3,2,1,0:T(8,128)(2,1)S(1)}, u32[]{:S(2)}, u32[]{:S(2)}) collective-permute-start(bf16[2,2,3,192,128]{4,3,2,1,0:T(8,128)(2,1)S(1)} %pad_maximum_fusion.refs_5_), channel_id=1, source_target_pairs={{2,4},{4,2},{3,5},{5,3},{10,12},{12,10},{11,13},{13,11},{18,20},{2... | collective-permute-start | bytes 1769480 | tf_op jit(solution)/shard_map/ppermute | solution.py:544
  25.9 16.9 %collective-permute-start.11 = (bf16[2,2,3,192,128]{4,3,2,1,0:T(8,128)(2,1)S(1)}, bf16[2,2,3,192,128]{4,3,2,1,0:T(8,128)(2,1)}, u32[]{:S(2)}, u32[]{:S(2)}) collective-permute-start(bf16[2,2,3,192,128]{4,3,2,1,0:T(8,128)(2,1)S(1)} %pad_maximum_fusion.refs_5_), channel_id=1, source_target_pairs={{0,8},{8,0},{16,24},{24,16},{1,9},{9,1},{17,25},{25,17},{2,10},{10... | collective-permute-start | bytes 1769480 | tf_op jit(solution)/shard_map/ppermute | solution.py:539
  29.4 14.0 %collective-permute-start.12 = (bf16[3,3,192,128]{3,2,1,0:T(8,128)(2,1)S(1)}, bf16[3,3,192,128]{3,2,1,0:T(8,128)(2,1)}, u32[]{:S(2)}, u32[]{:S(2)}) collective-permute-start(bf16[3,3,192,128]{3,2,1,0:T(8,128)(2,1)S(1)} %collective-permute-done.9.refs_3_.refs_9_), channel_id=1, source_target_pairs={{0,8},{8,0},{16,24},{24,16},{1,9},{9,1},{17,25},{25,17},{2,10},{10... | collective-permute-start | bytes 1327112 | tf_op jit(solution)/shard_map/ppermute | solution.py:539
  29.4 6.3 %collective-permute-start.7 = (bf16[3,192,128]{2,1,0:T(8,128)(2,1)S(1)}, bf16[3,192,128]{2,1,0:T(8,128)(2,1)S(1)}, u32[]{:S(2)}, u32[]{:S(2)}) collective-permute-start(bf16[3,192,128]{2,1,0:T(8,128)(2,1)S(1)} %get-tuple-element.40), channel_id=1, source_target_pairs={{0,1},{1,0},{8,9},{9,8},{16,17},{17,16},{24,25},{25,24},{2,3},{3,2... | collective-permute-start | bytes 442376 | tf_op jit(solution)/shard_map/ppermute | solution.py:535
  35.6 7.1 %collective-permute-start.8 = (bf16[3,192,128]{2,1,0:T(8,128)(2,1)}, bf16[3,192,128]{2,1,0:T(8,128)(2,1)S(1)}, u32[]{:S(2)}, u32[]{:S(2)}) collective-permute-start(bf16[3,192,128]{2,1,0:T(8,128)(2,1)} %get-tuple-element.41), channel_id=1, source_target_pairs={{0,16},{1,17},{8,24},{9,25},{16,0},{17,1},{24,8},{25,9},{2,18},{3,... | collective-permute-start | bytes 442376 | tf_op jit(solution)/shard_map/ppermute | solution.py:535
  37.9 11.2 %collective-permute-start.13 = (bf16[2,3,192,128]{3,2,1,0:T(8,128)(2,1)}, bf16[2,3,192,128]{3,2,1,0:T(8,128)(2,1)S(1)}, u32[]{:S(2)}, u32[]{:S(2)}) collective-permute-start(bf16[2,3,192,128]{3,2,1,0:T(8,128)(2,1)} %slice.9), channel_id=1, source_target_pairs={{0,2},{2,0},{4,6},{6,4},{1,3},{3,1},{5,7},{7,5},{8,10},{10,8},{12,... | collective-permute-start | bytes 884744 | tf_op jit(solution)/shard_map/ppermute | solution.py:544
  42.0 7.2 %collective-permute-start.16 = (bf16[2,3,192,128]{3,2,1,0:T(8,128)(2,1)}, bf16[2,3,192,128]{3,2,1,0:T(8,128)(2,1)S(1)}, u32[]{:S(2)}, u32[]{:S(2)}) collective-permute-start(bf16[2,3,192,128]{3,2,1,0:T(8,128)(2,1)} %slice.9), channel_id=1, source_target_pairs={{2,4},{4,2},{3,5},{5,3},{10,12},{12,10},{11,13},{13,11},{18,20},{2... | collective-permute-start | bytes 884744 | tf_op jit(solution)/shard_map/ppermute | solution.py:544
  42.8 6.9 %collective-permute-start.18 = (bf16[2,3,192,128]{3,2,1,0:T(8,128)(2,1)}, bf16[2,3,192,128]{3,2,1,0:T(8,128)(2,1)S(1)}, u32[]{:S(2)}, u32[]{:S(2)}) collective-permute-start(bf16[2,3,192,128]{3,2,1,0:T(8,128)(2,1)} %copy-done.3), channel_id=1, source_target_pairs={{0,8},{8,0},{16,24},{24,16},{1,9},{9,1},{17,25},{25,17},{2,10},{10... | collective-permute-start | bytes 884744 | tf_op jit(solution)/shard_map/ppermute | solution.py:539
  42.8 8.0 %collective-permute-start.10 = (bf16[2,2,3,192,128]{4,3,2,1,0:T(8,128)(2,1)S(1)}, bf16[2,2,3,192,128]{4,3,2,1,0:T(8,128)(2,1)S(1)}, u32[]{:S(2)}, u32[]{:S(2)}) collective-permute-start(bf16[2,2,3,192,128]{4,3,2,1,0:T(8,128)(2,1)S(1)} %collective-permute-done.5.refs_5_.refs_8_), channel_id=1, source_target_pairs={{0,8},{8,0},{16,24},{24,16},{1,9},{9,1},{17,25},{25,17},{2,10},{10... | collective-permute-start | bytes 1769480 | tf_op jit(solution)/shard_map/ppermute | solution.py:539
  43.3 7.6 %collective-permute-start.15 = (bf16[2,2,3,192,128]{4,3,2,1,0:T(8,128)(2,1)S(1)}, bf16[2,2,3,192,128]{4,3,2,1,0:T(8,128)(2,1)S(1)}, u32[]{:S(2)}, u32[]{:S(2)}) collective-permute-start(bf16[2,2,3,192,128]{4,3,2,1,0:T(8,128)(2,1)S(1)} %collective-permute-done.6.refs_9_.refs_10_), channel_id=1, source_target_pairs={{0,8},{8,0},{16,24},{24,16},{1,9},{9,1},{17,25},{25,17},{2,10},{10... | collective-permute-start | bytes 1769480 | tf_op jit(solution)/shard_map/ppermute | solution.py:539
  43.4 1.0 %copy-start.2 = (bf16[2,3,192,128]{3,2,1,0:T(8,128)(2,1)S(1)}, bf16[2,3,192,128]{3,2,1,0:T(8,128)(2,1)}, u32[]{:S(2)}) copy-start(bf16[2,3,192,128]{3,2,1,0:T(8,128)(2,1)} %copy-done.1) | copy-start | bytes 884740
  44.4 6.5 %copy-start.4 = (bf16[2,3,192,128]{3,2,1,0:T(8,128)(2,1)S(1)}, bf16[2,3,192,128]{3,2,1,0:T(8,128)(2,1)}, u32[]{:S(2)}) copy-start(bf16[2,3,192,128]{3,2,1,0:T(8,128)(2,1)} %copy-done.3) | copy-start | bytes 884740
  44.4 6.5 %copy-start.6 = (bf16[2,3,192,128]{3,2,1,0:T(8,128)(2,1)S(1)}, bf16[2,3,192,128]{3,2,1,0:T(8,128)(2,1)}, u32[]{:S(2)}) copy-start(bf16[2,3,192,128]{3,2,1,0:T(8,128)(2,1)} %copy-done.5) | copy-start | bytes 884740
  49.0 1.9 %collective-permute-start.19 = (bf16[2,3,192,128]{3,2,1,0:T(8,128)(2,1)}, bf16[2,3,192,128]{3,2,1,0:T(8,128)(2,1)S(1)}, u32[]{:S(2)}, u32[]{:S(2)}) collective-permute-start(bf16[2,3,192,128]{3,2,1,0:T(8,128)(2,1)} %copy-done.5), channel_id=1, source_target_pairs={{0,8},{8,0},{16,24},{24,16},{1,9},{9,1},{17,25},{25,17},{2,10},{10... | collective-permute-start | bytes 884744 | tf_op jit(solution)/shard_map/ppermute | solution.py:539
  49.2 20.2 %slice-start = ((s8[4718592]{0:T(1024)(128)(4,1)}), s8[4194304]{0:T(1024)(128)(4,1)S(1)}, s32[]{:S(2)}) async-start(s8[4718592]{0:T(1024)(128)(4,1)} %bitcast.14), calls=%async_computation | async-start | bytes 8388608
  49.2 6.2 %collective-permute-start.14 = (bf16[2,3,192,128]{3,2,1,0:T(8,128)(2,1)S(1)}, bf16[2,3,192,128]{3,2,1,0:T(8,128)(2,1)S(1)}, u32[]{:S(2)}, u32[]{:S(2)}) collective-permute-start(bf16[2,3,192,128]{3,2,1,0:T(8,128)(2,1)S(1)} %get-tuple-element.58), channel_id=1, source_target_pairs={{0,8},{8,0},{16,24},{24,16},{1,9},{9,1},{17,25},{25,17},{2,10},{10... | collective-permute-start | bytes 884744 | tf_op jit(solution)/shard_map/ppermute | solution.py:539
  49.7 5.7 %collective-permute-start.17 = (bf16[2,3,192,128]{3,2,1,0:T(8,128)(2,1)S(1)}, bf16[2,3,192,128]{3,2,1,0:T(8,128)(2,1)S(1)}, u32[]{:S(2)}, u32[]{:S(2)}) collective-permute-start(bf16[2,3,192,128]{3,2,1,0:T(8,128)(2,1)S(1)} %get-tuple-element.57), channel_id=1, source_target_pairs={{0,8},{8,0},{16,24},{24,16},{1,9},{9,1},{17,25},{25,17},{2,10},{10... | collective-permute-start | bytes 884744 | tf_op jit(solution)/shard_map/ppermute | solution.py:539
  50.9 18.5 %slice-start.1 = ((s8[4718592]{0:T(1024)(128)(4,1)}), s8[524288]{0:T(1024)(128)(4,1)S(1)}, s32[]{:S(2)}) async-start(s8[4718592]{0:T(1024)(128)(4,1)} %bitcast.14), calls=%async_computation.1 | async-start | bytes 1048576
  61.2 10.6 %copy-start.8 = (f32[3,1536]{1,0:T(4,128)S(1)}, f32[3,1536]{1,0:T(4,128)}, u32[]{:S(2)}) copy-start(f32[3,1536]{1,0:T(4,128)} %mod_ref.1) | copy-start | bytes 55300
  61.2 6.2 %collective-permute-start.20 = (bf16[3,192,128]{2,1,0:T(8,128)(2,1)S(1)}, bf16[3,192,128]{2,1,0:T(8,128)(2,1)S(1)}, u32[]{:S(2)}, u32[]{:S(2)}) collective-permute-start(bf16[3,192,128]{2,1,0:T(8,128)(2,1)S(1)} %get-tuple-element.54), channel_id=1, source_target_pairs={{0,1},{1,0},{8,9},{9,8},{16,17},{17,16},{24,25},{25,24},{2,3},{3,2... | collective-permute-start | bytes 442376 | tf_op jit(solution)/shard_map/ppermute | solution.py:535
  62.7 6.7 %collective-permute-start.21 = (bf16[3,192,128]{2,1,0:T(8,128)(2,1)S(1)}, bf16[3,192,128]{2,1,0:T(8,128)(2,1)S(1)}, u32[]{:S(2)}, u32[]{:S(2)}) collective-permute-start(bf16[3,192,128]{2,1,0:T(8,128)(2,1)S(1)} %get-tuple-element.55), channel_id=1, source_target_pairs={{0,16},{1,17},{8,24},{9,25},{16,0},{17,1},{24,8},{25,9},{2,18},{3,... | collective-permute-start | bytes 442376 | tf_op jit(solution)/shard_map/ppermute | solution.py:535
  63.6 8.1 %collective-permute-start.22 = (bf16[3,192,128]{2,1,0:T(8,128)(2,1)S(1)}, bf16[3,192,128]{2,1,0:T(8,128)(2,1)S(1)}, u32[]{:S(2)}, u32[]{:S(2)}) collective-permute-start(bf16[3,192,128]{2,1,0:T(8,128)(2,1)S(1)} %get-tuple-element.56), channel_id=1, source_target_pairs={{0,17},{1,16},{8,25},{9,24},{16,1},{17,0},{24,9},{25,8},{2,19},{3,... | collective-permute-start | bytes 442376 | tf_op jit(solution)/shard_map/ppermute | solution.py:535

commit v7 on v6

--- a/solution.py
+++ b/solution.py
@@ -469,7 +469,7 @@
         in_specs=[SMEM] + [VMEM] * (GROUPS + len(arrays) + len(states)),
         out_specs=[VMEM] * (5 if final else 2 * len(plan[0]) + 1),
         out_shape=[*([jax.ShapeDtypeStruct(Q_SHAPE, jnp.bfloat16)] * 4 if final else [STATE_SHAPE] * (2 * len(plan[0]))), TOKEN],
-        compiler_params=limit(32),
+        compiler_params=limit(24),
         cost_estimate=pl.CostEstimate(flops=1000, bytes_accessed=1000, transcendentals=0),
         name=name,
     )(sc, *queries, *arrays, *states)

time: 73.3 us -> 73.3 us (level)
  no operation moved by 1% of the time
where the time goes in v7:
time: 73.3 us; the launch traced here: 73.1 us
  Pallas kernels  26.7 us (36%)
  starting transfers between devices  25 us (34%)
  waiting for transfers between devices  19.1 us (26%)
  local copies, waits for them, and re-layouts  1.83 us (2%)
    ppermute x8, waiting for transfers between devices, square_swap(): return lax.ppermute(value, ('ta', 'wa'), [(i, i ^ flip) for i in range(8)])  18 us
    pallas_call x3, Pallas kernels, attend_call(): pl.pallas_call(functools.partial(attend_kernel, plan, len(arrays), tuple(...  14.9 us
    ppermute x6, starting transfers between devices, row_swap(): lax.ppermute(value, 'ha', [edge for i, j in pairs for edge in ((i, j), (j...  12.9 us
    ppermute x8, starting transfers between devices, square_swap(): return lax.ppermute(value, ('ta', 'wa'), [(i, i ^ flip) for i in range(8)])  10.1 us
    pallas_call x1, Pallas kernels, project_kv(): pl.pallas_call(kv_kernel, in_specs=[HBM] * 8, out_specs=[VMEM] * (GROUPS...  5.67 us
    pallas_call x1, Pallas kernels, project_q(): pl.pallas_call(q_kernel, in_specs=[HBM] * 7, out_specs=[VMEM] * (GROUPS +...  3.88 us
    ppermute x9, starting transfers between devices, core_swap(): return lax.ppermute(value, 'ta', [(i, i ^ 1) for i in range(4)])  1.96 us
  transfers between devices with their start and end apart: 23, of which 8 were waited for; matrix products, arithmetic and copies ran while one was open for 1% of the time, Pallas kernels for 19%

profile of v7, /device:TPU:0, one launch (start us, length us, event | category | flops | bytes accessed | tf_op | source)
XLA Modules:
  0.0 73.1 jit_solution(11016376398183340487)
XLA Ops:
  0.0 5.7 %project_kv.1 = (bf16[2,3,192,128]{3,2,1,0:T(8,128)(2,1)S(1)}, bf16[2,3,192,128]{3,2,1,0:T(8,128)(2,1)S(1)}, bf16[2,3,192,128]{3,2,1,0:T(8,128)(2,1)S(1)}, bf16[...) custom-call(bf16[192,1536]{1,0:T(8,128)(2,1)} %bitcast.17, f32[3,1536]{1,0:T(4,128)} %mod_ref.1, f32[1536]{0:T(1024)} %nk_hbm.1, ...), custom_call_target="tpu_custom_call" | custom-call | flops 1811939328 | bytes 9437184 | tf_op jit(solution)/shard_map/project_kv/pallas_call | solution.py:332
  5.7 0.5 collective-permute-start
  6.2 2.7 %collective-permute-start.3 = (bf16[2,3,192,128]{3,2,1,0:T(8,128)(2,1)S(1)}, bf16[2,3,192,128]{3,2,1,0:T(8,128)(2,1)S(1)}, u32[]{:S(2)}, u32[]{:S(2)}) collective-permute-start(bf16[2,3,192,128]{3,2,1,0:T(8,128)(2,1)S(1)} %get-tuple-element.32.refs_4_), channel_id=1, source_target_pairs={{0,2},{2,0},{4,6},{6,4},{1,3},{3,1},{5,7},{7,5},{8,10},{10,8},{12,... | collective-permute-start | bytes 884744 | tf_op jit(solution)/shard_map/ppermute | solution.py:544
  8.9 0.7 collective-permute-start.4
  9.6 1.6 %collective-permute-start.1 = (bf16[2,3,192,128]{3,2,1,0:T(8,128)(2,1)S(1)}, bf16[2,3,192,128]{3,2,1,0:T(8,128)(2,1)S(1)}, u32[]{:S(2)}, u32[]{:S(2)}) collective-permute-start(bf16[2,3,192,128]{3,2,1,0:T(8,128)(2,1)S(1)} %get-tuple-element.35), channel_id=1, source_target_pairs={{0,1},{1,0},{8,9},{9,8},{16,17},{17,16},{24,25},{25,24},{2,3},{3,2... | collective-permute-start | bytes 884744 | tf_op jit(solution)/shard_map/ppermute | solution.py:535
  11.1 1.5 %collective-permute-start.2 = (bf16[2,3,192,128]{3,2,1,0:T(8,128)(2,1)S(1)}, bf16[2,3,192,128]{3,2,1,0:T(8,128)(2,1)S(1)}, u32[]{:S(2)}, u32[]{:S(2)}) collective-permute-start(bf16[2,3,192,128]{3,2,1,0:T(8,128)(2,1)S(1)} %get-tuple-element.36), channel_id=1, source_target_pairs={{0,16},{1,17},{8,24},{9,25},{16,0},{17,1},{24,8},{25,9},{2,18},{3,... | collective-permute-start | bytes 884744 | tf_op jit(solution)/shard_map/ppermute | solution.py:535
  12.6 0.0 collective-permute-done.refs_6_
  12.7 3.9 %project_q.1 = (bf16[3,192,128]{2,1,0:T(8,128)(2,1)S(1)}, bf16[3,192,128]{2,1,0:T(8,128)(2,1)S(1)}, bf16[3,192,128]{2,1,0:T(8,128)(2,1)}, bf16[3,192,128]{2,1,0:T(8,128)(2,1)S(1)}, f32[8,128]{1,0:T(8,128)}) custom-call(bf16[192,1536]{1,0:T(8,128)(2,1)S(1)} %get-tuple-element.33.normed_hbm.token_hbm, f32[1536]{0:T(1024)S(1)} %copy-done.11, ...), custom_call_target="tpu_custom_call" | custom-call | flops 905969664 | bytes 4718592 | tf_op jit(solution)/shard_map/project_q/pallas_call | solution.py:355
  16.6 0.5 collective-permute-start.9
  17.2 0.0 collective-permute-done.3.refs_4_
  17.2 0.0 collective-permute-done.4.refs_8_
  17.2 1.5 %collective-permute-done.1 = bf16[2,3,192,128]{3,2,1,0:T(8,128)(2,1)S(1)} collective-permute-done((bf16[2,3,192,128]{3,2,1,0:T(8,128)(2,1)S(1)}, bf16[2,3,192,128]{3,2,1,0:T(8,128)(2,1)S(1)}, u32[]{:S(2)}, u32[]{:S(2)}) %collective-permute-start.1) | collective-permute-done | bytes 294944 | tf_op jit(solution)/shard_map/ppermute | solution.py:535
  18.7 2.3 %collective-permute-done.2 = bf16[2,3,192,128]{3,2,1,0:T(8,128)(2,1)S(1)} collective-permute-done((bf16[2,3,192,128]{3,2,1,0:T(8,128)(2,1)S(1)}, bf16[2,3,192,128]{3,2,1,0:T(8,128)(2,1)S(1)}, u32[]{:S(2)}, u32[]{:S(2)}) %collective-permute-start.2) | collective-permute-done | bytes 294944 | tf_op jit(solution)/shard_map/ppermute | solution.py:535
  21.0 0.1 pad_maximum_fusion.refs_5_
  21.1 4.1 %collective-permute-start.5 = (bf16[2,2,3,192,128]{4,3,2,1,0:T(8,128)(2,1)S(1)}, bf16[2,2,3,192,128]{4,3,2,1,0:T(8,128)(2,1)S(1)}, u32[]{:S(2)}, u32[]{:S(2)}) collective-permute-start(bf16[2,2,3,192,128]{4,3,2,1,0:T(8,128)(2,1)S(1)} %pad_maximum_fusion.refs_5_), channel_id=1, source_target_pairs={{0,2},{2,0},{4,6},{6,4},{1,3},{3,1},{5,7},{7,5},{8,10},{10,8},{12,... | collective-permute-start | bytes 1769480 | tf_op jit(solution)/shard_map/ppermute | solution.py:544
  25.2 0.7 collective-permute-start.6
  25.9 0.1 collective-permute-start.11
  26.0 3.4 %collective-permute-done.9.refs_3_.refs_9_ = bf16[3,3,192,128]{3,2,1,0:T(8,128)(2,1)S(1)} collective-permute-done((bf16[3,3,192,128]{3,2,1,0:T(8,128)(2,1)S(1)}, bf16[3,3,192,128]{3,2,1,0:T(8,128)(2,1)S(1)}, u32[]{:S(2)}, u32[]{:S(2)}) %collective-permute-start.9) | collective-permute-done | bytes 442400 | tf_op jit(solution)/shard_map/ppermute | solution.py:535
  29.4 0.0 collective-permute-start.12
  29.4 1.5 %collective-permute-start.7 = (bf16[3,192,128]{2,1,0:T(8,128)(2,1)S(1)}, bf16[3,192,128]{2,1,0:T(8,128)(2,1)S(1)}, u32[]{:S(2)}, u32[]{:S(2)}) collective-permute-start(bf16[3,192,128]{2,1,0:T(8,128)(2,1)S(1)} %get-tuple-element.40), channel_id=1, source_target_pairs={{0,1},{1,0},{8,9},{9,8},{16,17},{17,16},{24,25},{25,24},{2,3},{3,2... | collective-permute-start | bytes 442376 | tf_op jit(solution)/shard_map/ppermute | solution.py:535
  30.9 4.7 %collective-permute-done.7.refs_1_ = bf16[3,192,128]{2,1,0:T(8,128)(2,1)S(1)} collective-permute-done((bf16[3,192,128]{2,1,0:T(8,128)(2,1)S(1)}, bf16[3,192,128]{2,1,0:T(8,128)(2,1)S(1)}, u32[]{:S(2)}, u32[]{:S(2)}) %collective-permute-start.7) | collective-permute-done | bytes 147488 | tf_op jit(solution)/shard_map/ppermute | solution.py:535
  35.6 1.5 %collective-permute-start.8 = (bf16[3,192,128]{2,1,0:T(8,128)(2,1)}, bf16[3,192,128]{2,1,0:T(8,128)(2,1)S(1)}, u32[]{:S(2)}, u32[]{:S(2)}) collective-permute-start(bf16[3,192,128]{2,1,0:T(8,128)(2,1)} %get-tuple-element.41), channel_id=1, source_target_pairs={{0,16},{1,17},{8,24},{9,25},{16,0},{17,1},{24,8},{25,9},{2,18},{3,... | collective-permute-start | bytes 442376 | tf_op jit(solution)/shard_map/ppermute | solution.py:535
  37.1 0.7 %slice.9 = bf16[2,3,192,128]{3,2,1,0:T(8,128)(2,1)} slice(bf16[3,3,192,128]{3,2,1,0:T(8,128)(2,1)S(1)} %collective-permute-done.9.refs_3_.refs_9_), slice={[0:2], [0:3], [0:192], [0:128]} | slice | bytes 589824 | tf_op jit(solution)/shard_map/slice | solution.py:631
  37.8 0.0 collective-permute-done.5.refs_5_.refs_8_
  37.9 4.1 %collective-permute-start.13 = (bf16[2,3,192,128]{3,2,1,0:T(8,128)(2,1)}, bf16[2,3,192,128]{3,2,1,0:T(8,128)(2,1)S(1)}, u32[]{:S(2)}, u32[]{:S(2)}) collective-permute-start(bf16[2,3,192,128]{3,2,1,0:T(8,128)(2,1)} %slice.9), channel_id=1, source_target_pairs={{0,2},{2,0},{4,6},{6,4},{1,3},{3,1},{5,7},{7,5},{8,10},{10,8},{12,... | collective-permute-start | bytes 884744 | tf_op jit(solution)/shard_map/ppermute | solution.py:544
  42.0 0.7 collective-permute-start.16
  42.7 0.1 stack.48.sc_ref
  42.8 0.0 collective-permute-start.18
  42.8 0.5 collective-permute-start.10
  43.3 0.0 collective-permute-done.12.refs_8_
  43.3 0.1 collective-permute-start.15
  43.4 1.0 %copy-done.2 = bf16[2,3,192,128]{3,2,1,0:T(8,128)(2,1)S(1)} copy-done((bf16[2,3,192,128]{3,2,1,0:T(8,128)(2,1)S(1)}, bf16[2,3,192,128]{3,2,1,0:T(8,128)(2,1)}, u32[]{:S(2)}) %copy-start.2) | copy-done | bytes 294936
  44.4 4.6 %attend_own.1 = (f32[3,384,128]{2,1,0:T(8,128)S(1)}, f32[3,384,128]{2,1,0:T(8,128)S(1)}, f32[3,384,128]{2,1,0:T(8,128)S(1)}, f32[3,384,128]{2,1,0:T(8,128)S(1)}, f32[8,128]{1,0:T(8,128)S(1)}) custom-call(s32[7]{0:T(128)S(1)} %stack.48.sc_ref, bf16[3,192,128]{2,1,0:T(8,128)(2,1)S(1)} %get-tuple-element.39.refs_0_, ...), custom_call_target="tpu_custom_call" | custom-call | flops 1000 | bytes 1000 | tf_op jit(solution)/shard_map/attend_own/pallas_call | solution.py:467
  49.0 0.1 collective-permute-start.19
  49.2 0.5 collective-permute-start.14
  49.7 0.1 collective-permute-start.17
  49.8 1.1 %collective-permute-done.19.refs_10_.refs_13_ = bf16[2,3,192,128]{3,2,1,0:T(8,128)(2,1)S(1)} collective-permute-done((bf16[2,3,192,128]{3,2,1,0:T(8,128)(2,1)}, bf16[2,3,192,128]{3,2,1,0:T(8,128)(2,1)S(1)}, u32[]{:S(2)}, u32[]{:S(2)}) %collective-permute-start.19) | collective-permute-done | bytes 294944 | tf_op jit(solution)/shard_map/ppermute | solution.py:539
  50.9 0.0 slice-start.1
  50.9 4.5 %attend_halo.1 = (f32[3,384,128]{2,1,0:T(8,128)S(1)}, f32[3,384,128]{2,1,0:T(8,128)S(1)}, f32[3,384,128]{2,1,0:T(8,128)S(1)}, f32[3,384,128]{2,1,0:T(8,128)S(1)}, f32[8,128]{1,0:T(8,128)}) custom-call(s32[7]{0:T(128)S(1)} %stack.48.sc_ref, bf16[3,192,128]{2,1,0:T(8,128)(2,1)S(1)} %get-tuple-element.39.refs_0_, ...), custom_call_target="tpu_custom_call" | custom-call | flops 1000 | bytes 1000 | tf_op jit(solution)/shard_map/attend_halo/pallas_call | solution.py:467
  55.4 5.8 %attend_last.1 = (bf16[3,192,128]{2,1,0:T(8,128)(2,1)S(1)}, bf16[3,192,128]{2,1,0:T(8,128)(2,1)S(1)}, bf16[3,192,128]{2,1,0:T(8,128)(2,1)S(1)}, bf16[3,192,128]{2,1,0:T(8,128)(2,1)S(1)}, f32[8,128]{1,0:T(8,128)}) custom-call(s32[7]{0:T(128)S(1)} %stack.48.sc_ref, bf16[3,192,128]{2,1,0:T(8,128)(2,1)S(1)} %get-tuple-element.39.refs_0_, ...), custom_call_target="tpu_custom_call" | custom-call | flops 1000 | bytes 1000 | tf_op jit(solution)/shard_map/attend_last/pallas_call | solution.py:467
  61.2 1.5 %collective-permute-start.20 = (bf16[3,192,128]{2,1,0:T(8,128)(2,1)S(1)}, bf16[3,192,128]{2,1,0:T(8,128)(2,1)S(1)}, u32[]{:S(2)}, u32[]{:S(2)}) collective-permute-start(bf16[3,192,128]{2,1,0:T(8,128)(2,1)S(1)} %get-tuple-element.54), channel_id=1, source_target_pairs={{0,1},{1,0},{8,9},{9,8},{16,17},{17,16},{24,25},{25,24},{2,3},{3,2... | collective-permute-start | bytes 442376 | tf_op jit(solution)/shard_map/ppermute | solution.py:535
  62.7 0.9 %collective-permute-start.21 = (bf16[3,192,128]{2,1,0:T(8,128)(2,1)S(1)}, bf16[3,192,128]{2,1,0:T(8,128)(2,1)S(1)}, u32[]{:S(2)}, u32[]{:S(2)}) collective-permute-start(bf16[3,192,128]{2,1,0:T(8,128)(2,1)S(1)} %get-tuple-element.55), channel_id=1, source_target_pairs={{0,16},{1,17},{8,24},{9,25},{16,0},{17,1},{24,8},{25,9},{2,18},{3,... | collective-permute-start | bytes 442376 | tf_op jit(solution)/shard_map/ppermute | solution.py:535
  63.6 1.0 %collective-permute-start.22 = (bf16[3,192,128]{2,1,0:T(8,128)(2,1)S(1)}, bf16[3,192,128]{2,1,0:T(8,128)(2,1)S(1)}, u32[]{:S(2)}, u32[]{:S(2)}) collective-permute-start(bf16[3,192,128]{2,1,0:T(8,128)(2,1)S(1)} %get-tuple-element.56), channel_id=1, source_target_pairs={{0,17},{1,16},{8,25},{9,24},{16,1},{17,0},{24,9},{25,8},{2,19},{3,... | collective-permute-start | bytes 442376 | tf_op jit(solution)/shard_map/ppermute | solution.py:535
  64.7 2.7 %collective-permute-done.20.a1 = bf16[3,192,128]{2,1,0:T(8,128)(2,1)S(1)} collective-permute-done((bf16[3,192,128]{2,1,0:T(8,128)(2,1)S(1)}, bf16[3,192,128]{2,1,0:T(8,128)(2,1)S(1)}, u32[]{:S(2)}, u32[]{:S(2)}) %collective-permute-start.20) | collective-permute-done | bytes 147488 | tf_op jit(solution)/shard_map/ppermute | solution.py:535
  67.4 2.0 %collective-permute-done.21.a2 = bf16[3,192,128]{2,1,0:T(8,128)(2,1)S(1)} collective-permute-done((bf16[3,192,128]{2,1,0:T(8,128)(2,1)S(1)}, bf16[3,192,128]{2,1,0:T(8,128)(2,1)S(1)}, u32[]{:S(2)}, u32[]{:S(2)}) %collective-permute-start.21) | collective-permute-done | bytes 147488 | tf_op jit(solution)/shard_map/ppermute | solution.py:535
  69.4 1.1 %project_part.1.part_ref = f32[192,1536]{1,0:T(8,128)S(1)} custom-call(bf16[3,192,128]{2,1,0:T(8,128)(2,1)S(1)} %get-tuple-element.53.a0, bf16[3,192,128]{2,1,0:T(8,128)(2,1)S(1)} %collective-permute-done.20.a1, bf16[3,192,128]{2,1,0:T(8,128)(2,1)S(1)} %collective-permute-done.21.a2, bf16[1536,1536]{1,0:T(8,128)(2,1)S(1)} %bitcast.15), custom_call_target="tpu_custom_call" | custom-call | flops 905969664 | bytes 4718592 | tf_op jit(solution)/shard_map/project_part/pallas_call | solution.py:510
  70.5 1.3 %collective-permute-done.22.a3 = bf16[3,192,128]{2,1,0:T(8,128)(2,1)S(1)} collective-permute-done((bf16[3,192,128]{2,1,0:T(8,128)(2,1)S(1)}, bf16[3,192,128]{2,1,0:T(8,128)(2,1)S(1)}, u32[]{:S(2)}, u32[]{:S(2)}) %collective-permute-start.22) | collective-permute-done | bytes 147488 | tf_op jit(solution)/shard_map/ppermute | solution.py:535
  71.8 1.2 %project_out.1 = bf16[192,1536]{1,0:T(8,128)(2,1)} custom-call(f32[192,1536]{1,0:T(8,128)S(1)} %project_part.1.part_ref, bf16[3,192,128]{2,1,0:T(8,128)(2,1)S(1)} %collective-permute-done.22.a3, f32[3,1536]{1,0:T(4,128)S(1)} %copy-done.8, bf16[1536,1536]{1,0:T(8,128)(2,1)S(1)} %bitcast.15), custom_call_target="tpu_custom_call" | custom-call | flops 226492416 | bytes 1179648 | tf_op jit(solution)/shard_map/project_out/pallas_call | solution.py:519
  (40 shorter events, 0.2 us)
Async XLA Ops:
  0.0 12.6 %copy-start = (bf16[1536,1536]{1,0:T(8,128)(2,1)S(1)}, bf16[1536,1536]{1,0:T(8,128)(2,1)}, u32[]{:S(2)}) copy-start(bf16[1536,1536]{1,0:T(8,128)(2,1)} %wq_hbm.1) | copy-start | bytes 14155780
  0.0 12.6 %copy-start.7 = (f32[4,2,8,128]{3,2,1,0:T(8,128)S(1)}, f32[4,2,8,128]{3,2,1,0:T(8,128)}, u32[]{:S(2)}) copy-start(f32[4,2,8,128]{3,2,1,0:T(8,128)} %constant.57.clone.rt_hbm) | copy-start | bytes 98308
  0.0 12.6 %copy-start.9 = (f32[4,2,3,128]{3,2,1,0:T(4,128)S(1)}, f32[4,2,3,128]{3,2,1,0:T(4,128)}, u32[]{:S(2)}) copy-start(f32[4,2,3,128]{3,2,1,0:T(4,128)} %constant.56.clone.ft_hbm) | copy-start | bytes 36868
  0.0 12.6 %copy-start.10 = (f32[2,2,8,128]{3,2,1,0:T(8,128)S(1)}, f32[2,2,8,128]{3,2,1,0:T(8,128)}, u32[]{:S(2)}) copy-start(f32[2,2,8,128]{3,2,1,0:T(8,128)} %constant.58.clone.ct_hbm) | copy-start | bytes 49156
  0.0 12.7 %copy-start.11 = (f32[1536]{0:T(1024)S(1)}, f32[1536]{0:T(1024)}, u32[]{:S(2)}) copy-start(f32[1536]{0:T(1024)} %nq_hbm.1) | copy-start | bytes 18436
  5.7 6.9 %collective-permute-start = (bf16[2,3,192,128]{3,2,1,0:T(8,128)(2,1)S(1)}, bf16[2,3,192,128]{3,2,1,0:T(8,128)(2,1)S(1)}, u32[]{:S(2)}, u32[]{:S(2)}) collective-permute-start(bf16[2,3,192,128]{3,2,1,0:T(8,128)(2,1)S(1)} %get-tuple-element.32.refs_4_), channel_id=1, source_target_pairs={{0,8},{8,0},{16,24},{24,16},{1,9},{9,1},{17,25},{25,17},{2,10},{10... | collective-permute-start | bytes 884744 | tf_op jit(solution)/shard_map/ppermute | solution.py:539
  6.2 10.9 %collective-permute-start.3 = (bf16[2,3,192,128]{3,2,1,0:T(8,128)(2,1)S(1)}, bf16[2,3,192,128]{3,2,1,0:T(8,128)(2,1)S(1)}, u32[]{:S(2)}, u32[]{:S(2)}) collective-permute-start(bf16[2,3,192,128]{3,2,1,0:T(8,128)(2,1)S(1)} %get-tuple-element.32.refs_4_), channel_id=1, source_target_pairs={{0,2},{2,0},{4,6},{6,4},{1,3},{3,1},{5,7},{7,5},{8,10},{10,8},{12,... | collective-permute-start | bytes 884744 | tf_op jit(solution)/shard_map/ppermute | solution.py:544
  8.9 8.3 %collective-permute-start.4 = (bf16[2,3,192,128]{3,2,1,0:T(8,128)(2,1)S(1)}, bf16[2,3,192,128]{3,2,1,0:T(8,128)(2,1)S(1)}, u32[]{:S(2)}, u32[]{:S(2)}) collective-permute-start(bf16[2,3,192,128]{3,2,1,0:T(8,128)(2,1)S(1)} %get-tuple-element.32.refs_4_), channel_id=1, source_target_pairs={{2,4},{4,2},{3,5},{5,3},{10,12},{12,10},{11,13},{13,11},{18,20},{2... | collective-permute-start | bytes 884744 | tf_op jit(solution)/shard_map/ppermute | solution.py:544
  9.6 9.1 %collective-permute-start.1 = (bf16[2,3,192,128]{3,2,1,0:T(8,128)(2,1)S(1)}, bf16[2,3,192,128]{3,2,1,0:T(8,128)(2,1)S(1)}, u32[]{:S(2)}, u32[]{:S(2)}) collective-permute-start(bf16[2,3,192,128]{3,2,1,0:T(8,128)(2,1)S(1)} %get-tuple-element.35), channel_id=1, source_target_pairs={{0,1},{1,0},{8,9},{9,8},{16,17},{17,16},{24,25},{25,24},{2,3},{3,2... | collective-permute-start | bytes 884744 | tf_op jit(solution)/shard_map/ppermute | solution.py:535
  11.1 9.9 %collective-permute-start.2 = (bf16[2,3,192,128]{3,2,1,0:T(8,128)(2,1)S(1)}, bf16[2,3,192,128]{3,2,1,0:T(8,128)(2,1)S(1)}, u32[]{:S(2)}, u32[]{:S(2)}) collective-permute-start(bf16[2,3,192,128]{3,2,1,0:T(8,128)(2,1)S(1)} %get-tuple-element.36), channel_id=1, source_target_pairs={{0,16},{1,17},{8,24},{9,25},{16,0},{17,1},{24,8},{25,9},{2,18},{3,... | collective-permute-start | bytes 884744 | tf_op jit(solution)/shard_map/ppermute | solution.py:535
  12.6 29.3 %copy-start.1 = (bf16[2,3,192,128]{3,2,1,0:T(8,128)(2,1)}, bf16[2,3,192,128]{3,2,1,0:T(8,128)(2,1)S(1)}, u32[]{:S(2)}) copy-start(bf16[2,3,192,128]{3,2,1,0:T(8,128)(2,1)S(1)} %collective-permute-done.refs_6_) | copy-start | bytes 884740
  16.6 12.7 %collective-permute-start.9 = (bf16[3,3,192,128]{3,2,1,0:T(8,128)(2,1)S(1)}, bf16[3,3,192,128]{3,2,1,0:T(8,128)(2,1)S(1)}, u32[]{:S(2)}, u32[]{:S(2)}) collective-permute-start(bf16[3,3,192,128]{3,2,1,0:T(8,128)(2,1)S(1)} %pad_maximum_fusion.1), channel_id=1, source_target_pairs={{0,17},{1,16},{8,25},{9,24},{16,1},{17,0},{24,9},{25,8},{2,19},{3,... | collective-permute-start | bytes 1327112 | tf_op jit(solution)/shard_map/ppermute | solution.py:535
  17.2 3.9 %copy-start.3 = (bf16[2,3,192,128]{3,2,1,0:T(8,128)(2,1)}, bf16[2,3,192,128]{3,2,1,0:T(8,128)(2,1)S(1)}, u32[]{:S(2)}) copy-start(bf16[2,3,192,128]{3,2,1,0:T(8,128)(2,1)S(1)} %collective-permute-done.3.refs_4_) | copy-start | bytes 884740
  17.2 3.9 %copy-start.5 = (bf16[2,3,192,128]{3,2,1,0:T(8,128)(2,1)}, bf16[2,3,192,128]{3,2,1,0:T(8,128)(2,1)S(1)}, u32[]{:S(2)}) copy-start(bf16[2,3,192,128]{3,2,1,0:T(8,128)(2,1)S(1)} %collective-permute-done.4.refs_8_) | copy-start | bytes 884740
  21.1 16.8 %collective-permute-start.5 = (bf16[2,2,3,192,128]{4,3,2,1,0:T(8,128)(2,1)S(1)}, bf16[2,2,3,192,128]{4,3,2,1,0:T(8,128)(2,1)S(1)}, u32[]{:S(2)}, u32[]{:S(2)}) collective-permute-start(bf16[2,2,3,192,128]{4,3,2,1,0:T(8,128)(2,1)S(1)} %pad_maximum_fusion.refs_5_), channel_id=1, source_target_pairs={{0,2},{2,0},{4,6},{6,4},{1,3},{3,1},{5,7},{7,5},{8,10},{10,8},{12,... | collective-permute-start | bytes 1769480 | tf_op jit(solution)/shard_map/ppermute | solution.py:544
  25.2 16.7 %collective-permute-start.6 = (bf16[2,2,3,192,128]{4,3,2,1,0:T(8,128)(2,1)S(1)}, bf16[2,2,3,192,128]{4,3,2,1,0:T(8,128)(2,1)S(1)}, u32[]{:S(2)}, u32[]{:S(2)}) collective-permute-start(bf16[2,2,3,192,128]{4,3,2,1,0:T(8,128)(2,1)S(1)} %pad_maximum_fusion.refs_5_), channel_id=1, source_target_pairs={{2,4},{4,2},{3,5},{5,3},{10,12},{12,10},{11,13},{13,11},{18,20},{2... | collective-permute-start | bytes 1769480 | tf_op jit(solution)/shard_map/ppermute | solution.py:544
  25.9 16.9 %collective-permute-start.11 = (bf16[2,2,3,192,128]{4,3,2,1,0:T(8,128)(2,1)S(1)}, bf16[2,2,3,192,128]{4,3,2,1,0:T(8,128)(2,1)}, u32[]{:S(2)}, u32[]{:S(2)}) collective-permute-start(bf16[2,2,3,192,128]{4,3,2,1,0:T(8,128)(2,1)S(1)} %pad_maximum_fusion.refs_5_), channel_id=1, source_target_pairs={{0,8},{8,0},{16,24},{24,16},{1,9},{9,1},{17,25},{25,17},{2,10},{10... | collective-permute-start | bytes 1769480 | tf_op jit(solution)/shard_map/ppermute | solution.py:539
  29.4 14.0 %collective-permute-start.12 = (bf16[3,3,192,128]{3,2,1,0:T(8,128)(2,1)S(1)}, bf16[3,3,192,128]{3,2,1,0:T(8,128)(2,1)}, u32[]{:S(2)}, u32[]{:S(2)}) collective-permute-start(bf16[3,3,192,128]{3,2,1,0:T(8,128)(2,1)S(1)} %collective-permute-done.9.refs_3_.refs_9_), channel_id=1, source_target_pairs={{0,8},{8,0},{16,24},{24,16},{1,9},{9,1},{17,25},{25,17},{2,10},{10... | collective-permute-start | bytes 1327112 | tf_op jit(solution)/shard_map/ppermute | solution.py:539
  29.4 6.3 %collective-permute-start.7 = (bf16[3,192,128]{2,1,0:T(8,128)(2,1)S(1)}, bf16[3,192,128]{2,1,0:T(8,128)(2,1)S(1)}, u32[]{:S(2)}, u32[]{:S(2)}) collective-permute-start(bf16[3,192,128]{2,1,0:T(8,128)(2,1)S(1)} %get-tuple-element.40), channel_id=1, source_target_pairs={{0,1},{1,0},{8,9},{9,8},{16,17},{17,16},{24,25},{25,24},{2,3},{3,2... | collective-permute-start | bytes 442376 | tf_op jit(solution)/shard_map/ppermute | solution.py:535
  35.6 7.1 %collective-permute-start.8 = (bf16[3,192,128]{2,1,0:T(8,128)(2,1)}, bf16[3,192,128]{2,1,0:T(8,128)(2,1)S(1)}, u32[]{:S(2)}, u32[]{:S(2)}) collective-permute-start(bf16[3,192,128]{2,1,0:T(8,128)(2,1)} %get-tuple-element.41), channel_id=1, source_target_pairs={{0,16},{1,17},{8,24},{9,25},{16,0},{17,1},{24,8},{25,9},{2,18},{3,... | collective-permute-start | bytes 442376 | tf_op jit(solution)/shard_map/ppermute | solution.py:535
  37.9 11.2 %collective-permute-start.13 = (bf16[2,3,192,128]{3,2,1,0:T(8,128)(2,1)}, bf16[2,3,192,128]{3,2,1,0:T(8,128)(2,1)S(1)}, u32[]{:S(2)}, u32[]{:S(2)}) collective-permute-start(bf16[2,3,192,128]{3,2,1,0:T(8,128)(2,1)} %slice.9), channel_id=1, source_target_pairs={{0,2},{2,0},{4,6},{6,4},{1,3},{3,1},{5,7},{7,5},{8,10},{10,8},{12,... | collective-permute-start | bytes 884744 | tf_op jit(solution)/shard_map/ppermute | solution.py:544
  42.0 7.2 %collective-permute-start.16 = (bf16[2,3,192,128]{3,2,1,0:T(8,128)(2,1)}, bf16[2,3,192,128]{3,2,1,0:T(8,128)(2,1)S(1)}, u32[]{:S(2)}, u32[]{:S(2)}) collective-permute-start(bf16[2,3,192,128]{3,2,1,0:T(8,128)(2,1)} %slice.9), channel_id=1, source_target_pairs={{2,4},{4,2},{3,5},{5,3},{10,12},{12,10},{11,13},{13,11},{18,20},{2... | collective-permute-start | bytes 884744 | tf_op jit(solution)/shard_map/ppermute | solution.py:544
  42.8 6.9 %collective-permute-start.18 = (bf16[2,3,192,128]{3,2,1,0:T(8,128)(2,1)}, bf16[2,3,192,128]{3,2,1,0:T(8,128)(2,1)S(1)}, u32[]{:S(2)}, u32[]{:S(2)}) collective-permute-start(bf16[2,3,192,128]{3,2,1,0:T(8,128)(2,1)} %copy-done.3), channel_id=1, source_target_pairs={{0,8},{8,0},{16,24},{24,16},{1,9},{9,1},{17,25},{25,17},{2,10},{10... | collective-permute-start | bytes 884744 | tf_op jit(solution)/shard_map/ppermute | solution.py:539
  42.8 8.0 %collective-permute-start.10 = (bf16[2,2,3,192,128]{4,3,2,1,0:T(8,128)(2,1)S(1)}, bf16[2,2,3,192,128]{4,3,2,1,0:T(8,128)(2,1)S(1)}, u32[]{:S(2)}, u32[]{:S(2)}) collective-permute-start(bf16[2,2,3,192,128]{4,3,2,1,0:T(8,128)(2,1)S(1)} %collective-permute-done.5.refs_5_.refs_8_), channel_id=1, source_target_pairs={{0,8},{8,0},{16,24},{24,16},{1,9},{9,1},{17,25},{25,17},{2,10},{10... | collective-permute-start | bytes 1769480 | tf_op jit(solution)/shard_map/ppermute | solution.py:539
  43.3 7.6 %collective-permute-start.15 = (bf16[2,2,3,192,128]{4,3,2,1,0:T(8,128)(2,1)S(1)}, bf16[2,2,3,192,128]{4,3,2,1,0:T(8,128)(2,1)S(1)}, u32[]{:S(2)}, u32[]{:S(2)}) collective-permute-start(bf16[2,2,3,192,128]{4,3,2,1,0:T(8,128)(2,1)S(1)} %collective-permute-done.6.refs_9_.refs_10_), channel_id=1, source_target_pairs={{0,8},{8,0},{16,24},{24,16},{1,9},{9,1},{17,25},{25,17},{2,10},{10... | collective-permute-start | bytes 1769480 | tf_op jit(solution)/shard_map/ppermute | solution.py:539
  43.4 1.0 %copy-start.2 = (bf16[2,3,192,128]{3,2,1,0:T(8,128)(2,1)S(1)}, bf16[2,3,192,128]{3,2,1,0:T(8,128)(2,1)}, u32[]{:S(2)}) copy-start(bf16[2,3,192,128]{3,2,1,0:T(8,128)(2,1)} %copy-done.1) | copy-start | bytes 884740
  44.4 6.5 %copy-start.4 = (bf16[2,3,192,128]{3,2,1,0:T(8,128)(2,1)S(1)}, bf16[2,3,192,128]{3,2,1,0:T(8,128)(2,1)}, u32[]{:S(2)}) copy-start(bf16[2,3,192,128]{3,2,1,0:T(8,128)(2,1)} %copy-done.3) | copy-start | bytes 884740
  44.4 6.5 %copy-start.6 = (bf16[2,3,192,128]{3,2,1,0:T(8,128)(2,1)S(1)}, bf16[2,3,192,128]{3,2,1,0:T(8,128)(2,1)}, u32[]{:S(2)}) copy-start(bf16[2,3,192,128]{3,2,1,0:T(8,128)(2,1)} %copy-done.5) | copy-start | bytes 884740
  49.0 1.9 %collective-permute-start.19 = (bf16[2,3,192,128]{3,2,1,0:T(8,128)(2,1)}, bf16[2,3,192,128]{3,2,1,0:T(8,128)(2,1)S(1)}, u32[]{:S(2)}, u32[]{:S(2)}) collective-permute-start(bf16[2,3,192,128]{3,2,1,0:T(8,128)(2,1)} %copy-done.5), channel_id=1, source_target_pairs={{0,8},{8,0},{16,24},{24,16},{1,9},{9,1},{17,25},{25,17},{2,10},{10... | collective-permute-start | bytes 884744 | tf_op jit(solution)/shard_map/ppermute | solution.py:539
  49.2 20.2 %slice-start = ((s8[4718592]{0:T(1024)(128)(4,1)}), s8[4194304]{0:T(1024)(128)(4,1)S(1)}, s32[]{:S(2)}) async-start(s8[4718592]{0:T(1024)(128)(4,1)} %bitcast.14), calls=%async_computation | async-start | bytes 8388608
  49.2 6.2 %collective-permute-start.14 = (bf16[2,3,192,128]{3,2,1,0:T(8,128)(2,1)S(1)}, bf16[2,3,192,128]{3,2,1,0:T(8,128)(2,1)S(1)}, u32[]{:S(2)}, u32[]{:S(2)}) collective-permute-start(bf16[2,3,192,128]{3,2,1,0:T(8,128)(2,1)S(1)} %get-tuple-element.58), channel_id=1, source_target_pairs={{0,8},{8,0},{16,24},{24,16},{1,9},{9,1},{17,25},{25,17},{2,10},{10... | collective-permute-start | bytes 884744 | tf_op jit(solution)/shard_map/ppermute | solution.py:539
  49.7 5.7 %collective-permute-start.17 = (bf16[2,3,192,128]{3,2,1,0:T(8,128)(2,1)S(1)}, bf16[2,3,192,128]{3,2,1,0:T(8,128)(2,1)S(1)}, u32[]{:S(2)}, u32[]{:S(2)}) collective-permute-start(bf16[2,3,192,128]{3,2,1,0:T(8,128)(2,1)S(1)} %get-tuple-element.57), channel_id=1, source_target_pairs={{0,8},{8,0},{16,24},{24,16},{1,9},{9,1},{17,25},{25,17},{2,10},{10... | collective-permute-start | bytes 884744 | tf_op jit(solution)/shard_map/ppermute | solution.py:539
  50.9 18.5 %slice-start.1 = ((s8[4718592]{0:T(1024)(128)(4,1)}), s8[524288]{0:T(1024)(128)(4,1)S(1)}, s32[]{:S(2)}) async-start(s8[4718592]{0:T(1024)(128)(4,1)} %bitcast.14), calls=%async_computation.1 | async-start | bytes 1048576
  61.2 10.6 %copy-start.8 = (f32[3,1536]{1,0:T(4,128)S(1)}, f32[3,1536]{1,0:T(4,128)}, u32[]{:S(2)}) copy-start(f32[3,1536]{1,0:T(4,128)} %mod_ref.1) | copy-start | bytes 55300
  61.2 6.2 %collective-permute-start.20 = (bf16[3,192,128]{2,1,0:T(8,128)(2,1)S(1)}, bf16[3,192,128]{2,1,0:T(8,128)(2,1)S(1)}, u32[]{:S(2)}, u32[]{:S(2)}) collective-permute-start(bf16[3,192,128]{2,1,0:T(8,128)(2,1)S(1)} %get-tuple-element.54), channel_id=1, source_target_pairs={{0,1},{1,0},{8,9},{9,8},{16,17},{17,16},{24,25},{25,24},{2,3},{3,2... | collective-permute-start | bytes 442376 | tf_op jit(solution)/shard_map/ppermute | solution.py:535
  62.7 6.7 %collective-permute-start.21 = (bf16[3,192,128]{2,1,0:T(8,128)(2,1)S(1)}, bf16[3,192,128]{2,1,0:T(8,128)(2,1)S(1)}, u32[]{:S(2)}, u32[]{:S(2)}) collective-permute-start(bf16[3,192,128]{2,1,0:T(8,128)(2,1)S(1)} %get-tuple-element.55), channel_id=1, source_target_pairs={{0,16},{1,17},{8,24},{9,25},{16,0},{17,1},{24,8},{25,9},{2,18},{3,... | collective-permute-start | bytes 442376 | tf_op jit(solution)/shard_map/ppermute | solution.py:535
  63.6 8.1 %collective-permute-start.22 = (bf16[3,192,128]{2,1,0:T(8,128)(2,1)S(1)}, bf16[3,192,128]{2,1,0:T(8,128)(2,1)S(1)}, u32[]{:S(2)}, u32[]{:S(2)}) collective-permute-start(bf16[3,192,128]{2,1,0:T(8,128)(2,1)S(1)} %get-tuple-element.56), channel_id=1, source_target_pairs={{0,17},{1,16},{8,25},{9,24},{16,1},{17,0},{24,9},{25,8},{2,19},{3,... | collective-permute-start | bytes 442376 | tf_op jit(solution)/shard_map/ppermute | solution.py:535
